TPU v7x, 32 devices: a whole 2x2x4 slice. The times are simulated.
32 devices in a mesh: frames: 8 (over z, x), mp: 4 (over y, core).
Axes of the slice: x: 2, y: 2, z: 4, core: 2. Of those that a mesh axis runs over, the one named last changes fastest.
Arguments:
- video_tokens: bfloat16 [8, 256, 1024], P('frames', 'mp'), may hold values from -64 to 64
- grad_output: bfloat16 [8, 256, 1024], P('frames', 'mp'), may hold values from -6 to 6
- spatial_qkv: bfloat16 [3, 1024, 1024], P(None, None, 'mp'), may hold values from -1 to 1
- spatial_out: bfloat16 [1024, 1024], P('mp'), may hold values from -0.1875 to 0.1875
- temporal_qkv: bfloat16 [3, 1024, 1024], P(None, None, 'mp'), may hold values from -1 to 1
- temporal_out: bfloat16 [1024, 1024], P('mp'), may hold values from -0.1875 to 0.1875
- clip_frames: int32 [4], replicated, may hold values from 1 to 4, 8 in all
Outputs:
- grad_tokens: bfloat16 [8, 256, 1024], P('frames', 'mp')
- grad_spatial_qkv: float32 [3, 1024, 1024], P(None, 'frames', 'mp')
- grad_spatial_out: float32 [1024, 1024], P('mp', 'frames')
- grad_temporal_qkv: float32 [3, 1024, 1024], P(None, 'frames', 'mp')
- grad_temporal_out: float32 [1024, 1024], P('mp', 'frames')
Inputs may be any that keep to these rules, and one draw needn't show every extreme that they name: `clip_frames`: 4 clip lengths that sum to 8; the longest is exactly 4.
All inputs are finite; a program needn't handle non-finite values.
Results may differ from a plain program's by a relative error of at most 0.015.
Values may be sent and summed in bfloat16 or wider, within the bound.
No kernel may reach another device: no remote copies, remote signals or barrier semaphores. Data moves between devices by JAX's collectives and lax.ppermute only.
A program may use at most 128 MiB of HBM per device.

v0:
```python
import jax
import jax.numpy as jnp
from jax import lax
from jax.sharding import PartitionSpec as P

HD = 64


EPS = 1e-06
NEGATIVE = -1e30


def normed(values_in):
    inv_rms = lax.rsqrt(jnp.mean(values_in * values_in, -1, keepdims=True) + EPS)
    return ((values_in * inv_rms).astype(jnp.bfloat16), inv_rms)


def norm_back(values_in, inv_rms, upstream):
    return inv_rms * (
        upstream
        - values_in * (inv_rms * inv_rms) * jnp.mean(upstream * values_in, -1, keepdims=True)
    )


def probs_of(queries, keys_in, mask_bias, layout):
    key_layout = layout.replace("l", "m")
    scores = jnp.einsum(
        layout + "," + key_layout + "->bhlm", queries, keys_in, preferred_element_type=jnp.float32
    )
    scores = scores * queries.shape[-1] ** (-0.5) + mask_bias
    scores = scores - jnp.max(scores, -1, keepdims=True)
    expo = jnp.exp(scores)
    return expo / jnp.sum(expo, -1, keepdims=True)


def attend(queries, keys_in, values_in, mask_bias, layout):
    key_layout = layout.replace("l", "m")
    probs_f = probs_of(queries, keys_in, mask_bias, layout)
    result = jnp.einsum(
        "bhlm," + key_layout + "->" + layout,
        probs_f.astype(jnp.bfloat16),
        values_in,
        preferred_element_type=jnp.float32,
    )
    return result.astype(jnp.bfloat16)


def attend_back(queries, keys_in, values_in, mask_bias, upstream, layout):
    key_layout = layout.replace("l", "m")
    probs_f = probs_of(queries, keys_in, mask_bias, layout)
    d_values = jnp.einsum(
        "bhlm," + layout + "->" + key_layout,
        probs_f.astype(jnp.bfloat16),
        upstream,
        preferred_element_type=jnp.float32,
    )
    d_probs = jnp.einsum(
        layout + "," + key_layout + "->bhlm",
        upstream,
        values_in,
        preferred_element_type=jnp.float32,
    )
    row_delta = jnp.sum(probs_f * d_probs, -1, keepdims=True)
    d_scores = (probs_f * (d_probs - row_delta) * queries.shape[-1] ** (-0.5)).astype(jnp.bfloat16)
    d_queries = jnp.einsum(
        "bhlm," + key_layout + "->" + layout, d_scores, keys_in, preferred_element_type=jnp.float32
    )
    d_keys = jnp.einsum(
        "bhlm," + layout + "->" + key_layout, d_scores, queries, preferred_element_type=jnp.float32
    )
    return (d_queries, d_keys, d_values)


def shards(
    video_tokens, grad_output, spatial_qkv, spatial_out, temporal_qkv, temporal_out, clip_frames
):
    frames_dev, rows_mp, model_width = video_tokens.shape
    local_width = spatial_out.shape[0]
    heads_loc = local_width // HD
    groups = lax.axis_size("frames")
    patches = rows_mp * lax.axis_size("mp")
    all_frames = frames_dev * groups
    tokens = frames_dev * patches

    def patch_rows(tensor):
        return lax.all_gather(tensor, "mp", axis=1, tiled=True)

    def heads_of(tensor):
        return tensor.reshape(tensor.shape[:-1] + (heads_loc, HD))

    def patch_sums(tensor):
        return lax.psum_scatter(
            tensor.reshape(frames_dev, patches, model_width), "mp", scatter_dimension=1, tiled=True
        )

    def back_sum(d_flat, weights_local):
        return patch_sums(
            jnp.einsum("jne,jde->nd", d_flat, weights_local, preferred_element_type=jnp.float32)
        )

    clip_ends = jnp.cumsum(clip_frames)
    x_float = video_tokens.astype(jnp.float32)
    normed_x, inv_x = normed(x_float)
    normed_x_all = patch_rows(normed_x).reshape(tokens, model_width)
    qkv_s = jnp.einsum(
        "nd,jde->jne", normed_x_all, spatial_qkv, preferred_element_type=jnp.float32
    ).astype(jnp.bfloat16)
    qkv_s = qkv_s.reshape(3, frames_dev, patches, heads_loc, HD)
    attn_s = attend(qkv_s[0], qkv_s[1], qkv_s[2], 0.0, "blhd").reshape(tokens, local_width)
    hidden = x_float + patch_sums(jnp.dot(attn_s, spatial_out, preferred_element_type=jnp.float32))
    normed_h, inv_h = normed(hidden)
    normed_h_all = patch_rows(normed_h).reshape(tokens, model_width)
    qkv_t = jnp.einsum(
        "nd,jde->jne", normed_h_all, temporal_qkv, preferred_element_type=jnp.float32
    ).astype(jnp.bfloat16)
    qkv_t = qkv_t.reshape(3, frames_dev, patches, local_width)
    grad_all = patch_rows(grad_output).reshape(tokens, model_width)

    def to_owners(tensor):
        return lax.all_to_all(tensor, "frames", split_axis=2, concat_axis=1, tiled=True)

    def from_owners(tensor):
        return lax.all_to_all(tensor, "frames", split_axis=1, concat_axis=2, tiled=True)

    at_owners = to_owners(qkv_t)
    clip_ids = jnp.sum(
        (jnp.arange(all_frames, dtype=jnp.int32)[:, None] >= clip_ends[None, :]).astype(jnp.int32),
        axis=1,
    )
    mask_bias = jnp.where(clip_ids[:, None] == clip_ids[None, :], 0.0, NEGATIVE).astype(jnp.float32)
    own_queries = heads_of(at_owners[0])
    own_keys = heads_of(at_owners[1])
    own_values = heads_of(at_owners[2])
    attn_owned = attend(own_queries, own_keys, own_values, mask_bias, "lbhd")
    attn_t = from_owners(attn_owned.reshape((1,) + at_owners.shape[1:]))[0].reshape(
        tokens, local_width
    )
    d_attn_t = jnp.einsum(
        "nd,ed->ne", grad_all, temporal_out, preferred_element_type=jnp.float32
    ).astype(jnp.bfloat16)
    d_owned = to_owners(d_attn_t.reshape(1, frames_dev, patches, local_width))[0]
    d_queries, d_keys, d_values = attend_back(
        own_queries, own_keys, own_values, mask_bias, heads_of(d_owned), "lbhd"
    )
    d_stack = jnp.stack([d_queries, d_keys, d_values]).astype(jnp.bfloat16).reshape(at_owners.shape)
    d_qkv_t = from_owners(d_stack)
    grad_temporal_out = jnp.einsum(
        "ne,nd->ed", attn_t, grad_all, preferred_element_type=jnp.float32
    )
    d_qkv_t_flat = d_qkv_t.reshape(3, tokens, local_width)
    grad_temporal_qkv = jnp.einsum(
        "nd,jne->jde", normed_h_all, d_qkv_t_flat, preferred_element_type=jnp.float32
    )
    d_normed_h = back_sum(d_qkv_t_flat, temporal_qkv)
    d_hidden = grad_output.astype(jnp.float32) + norm_back(hidden, inv_h, d_normed_h)
    d_hidden_all = patch_rows(d_hidden.astype(jnp.bfloat16)).reshape(tokens, model_width)
    grad_spatial_out = jnp.einsum(
        "ne,nd->ed", attn_s, d_hidden_all, preferred_element_type=jnp.float32
    )
    d_attn_s = jnp.einsum(
        "nd,ed->ne", d_hidden_all, spatial_out, preferred_element_type=jnp.float32
    ).astype(jnp.bfloat16)
    d_attn_s = d_attn_s.reshape(frames_dev, patches, heads_loc, HD)
    d_queries_s, d_keys_s, d_values_s = attend_back(
        qkv_s[0], qkv_s[1], qkv_s[2], 0.0, d_attn_s, "blhd"
    )
    d_qkv_s = (
        jnp.stack([d_queries_s, d_keys_s, d_values_s])
        .astype(jnp.bfloat16)
        .reshape(3, tokens, local_width)
    )
    grad_spatial_qkv = jnp.einsum(
        "nd,jne->jde", normed_x_all, d_qkv_s, preferred_element_type=jnp.float32
    )
    d_normed_x = back_sum(d_qkv_s, spatial_qkv)
    grad_tokens = (d_hidden + norm_back(x_float, inv_x, d_normed_x)).astype(jnp.bfloat16)
    reduced = (
        lax.psum_scatter(grad_spatial_qkv, "frames", scatter_dimension=1, tiled=True),
        lax.psum_scatter(grad_spatial_out, "frames", scatter_dimension=1, tiled=True),
        lax.psum_scatter(grad_temporal_qkv, "frames", scatter_dimension=1, tiled=True),
        lax.psum_scatter(grad_temporal_out, "frames", scatter_dimension=1, tiled=True),
    )
    return (grad_tokens, reduced[0], reduced[1], reduced[2], reduced[3])


def solution(mesh):
    placed = (
        P("frames", "mp", None),
        P("frames", "mp", None),
        P(None, None, "mp"),
        P("mp", None),
        P(None, None, "mp"),
        P("mp", None),
        P(),
    )
    return jax.shard_map(
        shards,
        mesh=mesh,
        in_specs=placed,
        out_specs=(
            P("frames", "mp", None),
            P(None, "frames", "mp"),
            P("mp", "frames"),
            P(None, "frames", "mp"),
            P("mp", "frames"),
        ),
        check_vma=False,
    )
```

profile of v0, /device:TPU:0, one launch (start us, length us, event | category | flops | bytes accessed | tf_op | source)
XLA Modules:
  0.0 490.2 jit_solution(1501687964953269562)
XLA Ops:
  7.2 1.1 fusion.44
  8.4 0.6 fusion.79
  9.0 1.0 fusion.45
  10.0 8.6 %all_gather.12 = bf16[1,256,1024]{2,1,0:T(8,128)(2,1)S(1)} all-gather(bf16[1,64,1024]{2,1,0:T(8,128)(2,1)S(1)} %fusion.45), channel_id=1, replica_groups=mesh['frames'=8,'mp'=4] {'mp'}, dimensions={1}, use_global_device_ids=true | all-gather | bytes 655360 | tf_op jit(solution)/shard_map/all_gather | solution.py:86
  18.6 2.3 fusion.17
  21.0 1.5 fusion.83
  22.5 0.7 convolution_convert_fusion.11
  23.6 1.4 convolution_bitcast_fusion.4
  25.0 7.4 %all_gather.14 = bf16[1,256,1024]{2,1,0:T(8,128)(2,1)S(1)} all-gather(bf16[1,64,1024]{2,1,0:T(8,128)(2,1)S(1)} %copy-done.14), channel_id=1, replica_groups=mesh['frames'=8,'mp'=4] {'mp'}, dimensions={1}, use_global_device_ids=true | all-gather | bytes 655360 | tf_op jit(solution)/shard_map/all_gather | solution.py:86
  32.4 0.3 fusion.23
  33.0 0.5 broadcast.159
  33.5 1.4 reduce.18
  34.9 0.7 reshape.316
  35.6 5.8 %all-to-all-start.1 = ((bf16[8,2,4096]{2,1,0:T(2,128)(2,1)}), bf16[8,2,4096]{2,1,0:T(2,128)(2,1)S(1)}, u32[]{:S(2)}, u32[]{:S(2)}) async-start(bf16[8,2,4096]{2,1,0:T(2,128)(2,1)} %reshape.316), calls=%async_computation.2 | async-start | bytes 262144 | tf_op jit(solution)/shard_map/all_to_all | solution.py:120
  41.4 9.5 %reduce-scatter.8.cloned.1.call-done = f32[1,64,1024]{2,1,0:T(8,128)} async-done(((f32[1,256,1024]{2,1,0:T(8,128)}), f32[1,64,1024]{2,1,0:T(8,128)}) %reduce-scatter.8.cloned.1.call-update) | async-done | bytes 262160 | tf_op jit(solution)/shard_map/reduce_scatter | solution.py:92
  50.9 1.1 multiply_reduce_fusion.3
  52.0 1.0 multiply_convert_fusion
  53.0 6.8 %all_gather.13 = bf16[1,256,1024]{2,1,0:T(8,128)(2,1)S(1)} all-gather(bf16[1,64,1024]{2,1,0:T(8,128)(2,1)S(1)} %multiply_convert_fusion), channel_id=1, replica_groups=mesh['frames'=8,'mp'=4] {'mp'}, dimensions={1}, use_global_device_ids=true | all-gather | bytes 655360 | tf_op jit(solution)/shard_map/all_gather | solution.py:86
  59.8 0.8 copy-done.8
  60.6 0.6 fusion.18
  61.2 1.2 copy.116
  62.3 5.5 %all-to-all-start = ((bf16[3,1,256,256]{3,0,1,2:T(4,128)(2,1)}), bf16[3,1,256,256]{3,0,1,2:T(4,128)(2,1)S(1)}, u32[]{:S(2)}, u32[]{:S(2)}) async-start(bf16[3,1,256,256]{3,0,1,2:T(4,128)(2,1)} %copy.116), calls=%async_computation.1 | async-start | bytes 1048576 | tf_op jit(solution)/shard_map/all_to_all | solution.py:120
  68.6 0.7 bitcast_reduce_fusion
  69.5 13.4 %all-to-all-done = bf16[3,1,256,256]{3,0,1,2:T(4,128)(2,1)S(1)} async-done(((bf16[3,1,256,256]{3,0,1,2:T(4,128)(2,1)}), bf16[3,1,256,256]{3,0,1,2:T(4,128)(2,1)S(1)}, u32[]{:S(2)}, u32[]{:S(2)}) %all-to-all-start) | async-done | bytes 393248 | tf_op jit(solution)/shard_map/all_to_all | solution.py:120
  82.9 2.3 slice_reduce_fusion
  85.3 1.2 reshape_squeeze.16
  86.5 1.8 reshape_squeeze.15
  88.3 1.3 fusion.15
  89.7 1.7 fusion.84
  91.3 1.2 fusion.59
  92.5 2.9 fusion.20
  95.4 2.9 fusion.19
  98.3 1.3 fusion.21
  99.6 1.1 copy.124
  101.7 15.7 %all_to_all.16 = bf16[3,8,32,256]{3,2,0,1:T(8,128)(2,1)S(1)} all-to-all(bf16[3,8,32,256]{3,2,0,1:T(8,128)(2,1)S(1)} %copy.129), channel_id=1, replica_groups=mesh['frames'=8,'mp'=4] {'frames'}, dimensions={1} | all-to-all | bytes 786432 | tf_op jit(solution)/shard_map/all_to_all | solution.py:123
  117.4 1.6 convolution_bitcast_fusion.3
  119.1 23.1 %reduce-scatter.10.cloned.1.call-done = f32[1,64,1024]{2,1,0:T(8,128)} async-done(((f32[1,256,1024]{2,1,0:T(8,128)}), f32[1,64,1024]{2,1,0:T(8,128)}) %reduce-scatter.10.cloned.1.call-update) | async-done | bytes 262160 | tf_op jit(solution)/shard_map/reduce_scatter | solution.py:92
  142.2 1.1 multiply_reduce_fusion.2
  143.3 1.8 fusion.81
  145.1 6.7 %all_gather.15 = bf16[1,256,1024]{2,1,0:T(8,128)(2,1)S(1)} all-gather(bf16[1,64,1024]{2,1,0:T(8,128)(2,1)S(1)} %get-tuple-element.33), channel_id=1, replica_groups=mesh['frames'=8,'mp'=4] {'mp'}, dimensions={1}, use_global_device_ids=true | all-gather | bytes 655360 | tf_op jit(solution)/shard_map/all_gather | solution.py:86
  151.9 1.4 convolution_convert_fusion.9
  153.3 1.7 convolution_convert_fusion.6
  155.0 1.4 fusion.85
  156.4 3.4 convolution_convert_fusion.8
  159.8 2.6 convolution_convert_fusion.7
  162.7 1.0 copy.134
  163.7 3.1 convolution_bitcast_fusion.2
  166.8 3.3 convolution_bitcast_fusion
  170.2 1.0 copy-done.7
  171.2 3.2 convolution_bitcast_fusion.1
  174.5 1.0 copy-done.5
  175.6 2.0 fusion.22
  177.6 1.1 copy.141
  178.9 13.0 %all_to_all.17 = bf16[1,8,32,256]{3,2,0,1:T(8,128)(2,1)S(1)} all-to-all(bf16[1,8,32,256]{3,2,0,1:T(8,128)(2,1)S(1)} %bitcast.116), channel_id=1, replica_groups=mesh['frames'=8,'mp'=4] {'frames'}, dimensions={1} | all-to-all | bytes 262144 | tf_op jit(solution)/shard_map/all_to_all | solution.py:123
  191.8 1.3 fusion.35
  193.2 1.4 fusion.32
  194.7 1.1 fusion.51
  195.8 1.7 fusion.50
  197.5 73.4 %reduce-scatter.18.cloned.1.call-done = f32[3,128,256]{1,2,0:T(8,128)} async-done(((f32[3,1024,256]{1,2,0:T(8,128)}), f32[3,128,256]{1,2,0:T(8,128)}) %reduce-scatter.18.cloned.1.call-update) | async-done | bytes 393232 | tf_op jit(solution)/shard_map/reduce_scatter | solution.py:180
  270.9 1.9 copy.144
  272.9 76.1 %reduce-scatter.14.cloned.1.call-done = f32[3,128,256]{1,2,0:T(8,128)} async-done(((f32[3,1024,256]{1,2,0:T(8,128)}), f32[3,128,256]{1,2,0:T(8,128)}) %reduce-scatter.14.cloned.1.call-update) | async-done | bytes 393232 | tf_op jit(solution)/shard_map/reduce_scatter | solution.py:178
  348.9 1.9 copy.143
  350.8 65.5 %reduce-scatter.20.cloned.1.call-done = f32[256,128]{1,0:T(8,128)} async-done(((f32[256,1024]{1,0:T(8,128)}), f32[256,128]{1,0:T(8,128)}) %reduce-scatter.20.cloned.1.call-update) | async-done | bytes 131088 | tf_op jit(solution)/shard_map/reduce_scatter | solution.py:181
  416.3 67.0 %reduce-scatter.16.cloned.1.call-done = f32[256,128]{1,0:T(8,128)} async-done(((f32[256,1024]{1,0:T(8,128)}), f32[256,128]{1,0:T(8,128)}) %reduce-scatter.16.cloned.1.call-update) | async-done | bytes 131088 | tf_op jit(solution)/shard_map/reduce_scatter | solution.py:179
  (93 shorter events, 3.5 us)
Async XLA Ops:
  7.2 53.4 %copy-start = (bf16[3,1024,256]{2,1,0:T(8,128)(2,1)S(1)}, bf16[3,1024,256]{2,1,0:T(8,128)(2,1)}, u32[]{:S(2)}) copy-start(bf16[3,1024,256]{2,1,0:T(8,128)(2,1)} %param.11) | copy-start | bytes 4718596
  7.2 43.7 %reduce-scatter.8.cloned.1.call-start = ((), (), s32[]{:S(2)}) async-start(), calls=%async_computation.11 | async-start | bytes 1310720 | tf_op jit(solution)/shard_map/reduce_scatter | solution.py:92
  18.6 2.4 copy-start.6
  21.0 1.5 copy-start.22
  21.0 2.2 copy-start.17
  21.0 2.2 copy-start.24
  22.5 0.7 copy-start.27
  22.5 1.0 copy-start.3
  23.2 9.1 %copy-start.19 = (bf16[4,64,256]{2,1,0:T(8,128)(2,1)}, bf16[4,64,256]{2,1,0:T(8,128)(2,1)S(1)}, u32[]{:S(2)}) copy-start(bf16[4,64,256]{2,1,0:T(8,128)(2,1)S(1)} %convolution_convert_fusion.11) | copy-start | bytes 393220
  23.3 1.7 copy-start.14
  23.6 8.8 %copy-start.16 = (bf16[256,1024]{1,0:T(8,128)(2,1)S(1)}, bf16[256,1024]{1,0:T(8,128)(2,1)}, u32[]{:S(2)}) copy-start(bf16[256,1024]{1,0:T(8,128)(2,1)} %param.12) | copy-start | bytes 1572868
  24.9 25.9 %copy-start.1 = (bf16[1,64,1024]{2,1,0:T(8,128)(2,1)S(1)}, bf16[1,64,1024]{2,1,0:T(8,128)(2,1)}, u32[]{:S(2)}) copy-start(bf16[1,64,1024]{2,1,0:T(8,128)(2,1)} %param.7) | copy-start | bytes 393220
  35.6 26.8 %all-to-all-start.1 = ((bf16[8,2,4096]{2,1,0:T(2,128)(2,1)}), bf16[8,2,4096]{2,1,0:T(2,128)(2,1)S(1)}, u32[]{:S(2)}, u32[]{:S(2)}) async-start(bf16[8,2,4096]{2,1,0:T(2,128)(2,1)} %reshape.316), calls=%async_computation.2 | async-start | bytes 262144 | tf_op jit(solution)/shard_map/all_to_all | solution.py:120
  59.8 0.8 copy-start.8
  61.2 6.9 %copy-start.26 = (s32[4]{0:T(128)S(1)}, s32[4]{0:T(128)}, u32[]{:S(2)}) copy-start(s32[4]{0:T(128)} %param.13) | copy-start | bytes 52
  62.3 20.5 %all-to-all-start = ((bf16[3,1,256,256]{3,0,1,2:T(4,128)(2,1)}), bf16[3,1,256,256]{3,0,1,2:T(4,128)(2,1)S(1)}, u32[]{:S(2)}, u32[]{:S(2)}) async-start(bf16[3,1,256,256]{3,0,1,2:T(4,128)(2,1)} %copy.116), calls=%async_computation.1 | async-start | bytes 1048576 | tf_op jit(solution)/shard_map/all_to_all | solution.py:120
  67.9 74.4 %reduce-scatter.10.cloned.1.call-start = ((), (), s32[]{:S(2)}) async-start(), calls=%async_computation.12 | async-start | bytes 1310720 | tf_op jit(solution)/shard_map/reduce_scatter | solution.py:92
  85.3 7.2 %copy-start.11 = (bf16[8,32,4,64]{3,2,1,0:T(4,128)(2,1)}, bf16[8,32,4,64]{3,2,1,0:T(4,128)(2,1)S(1)}, u32[]{:S(2)}) copy-start(bf16[8,32,4,64]{3,2,1,0:T(4,128)(2,1)S(1)} %reshape_squeeze.18) | copy-start | bytes 393220
  89.7 8.7 %copy-start.4 = (f32[32,4,8,8]{2,3,1,0:T(8,128)}, f32[32,4,8,8]{2,3,1,0:T(8,128)S(1)}, u32[]{:S(2)}) copy-start(f32[32,4,8,8]{2,3,1,0:T(8,128)S(1)} %fusion.15) | copy-start | bytes 98308
  92.5 2.9 copy-start.13
  98.3 2.6 copy-start.21
  117.4 24.8 %copy-start.2 = (f32[1,64,1024]{2,1,0:T(8,128)S(1)}, f32[1,64,1024]{2,1,0:T(8,128)}, u32[]{:S(2)}) copy-start(f32[1,64,1024]{2,1,0:T(8,128)} %reduce-scatter.8.cloned.1.call-done) | copy-start | bytes 786436
  119.0 24.3 %copy-start.15 = (bf16[1,64,1024]{2,1,0:T(8,128)(2,1)S(1)}, bf16[1,64,1024]{2,1,0:T(8,128)(2,1)}, u32[]{:S(2)}) copy-start(bf16[1,64,1024]{2,1,0:T(8,128)(2,1)} %param.8) | copy-start | bytes 393220
  119.1 75.6 %reduce-scatter.12.cloned.1.call-start = ((), (), s32[]{:S(2)}) async-start(), calls=%async_computation.13 | async-start | bytes 1310720 | tf_op jit(solution)/shard_map/reduce_scatter | solution.py:92
  143.3 9.9 %copy-start.28 = (f32[4,256]{1,0:T(4,128)S(1)}, f32[4,256]{1,0:T(4,128)}, u32[]{:S(2)}) copy-start(f32[4,256]{1,0:T(4,128)} %copy-done.27) | copy-start | bytes 12292
  153.3 1.7 copy-start.18
  156.4 3.4 copy-start.23
  163.7 3.1 copy-start.9
  166.8 104.2 %reduce-scatter.18.cloned.1.call-start = ((), (), s32[]{:S(2)}) async-start(), calls=%async_computation.16 | async-start | bytes 3538944 | tf_op jit(solution)/shard_map/reduce_scatter | solution.py:180
  170.2 1.0 copy-start.7
  170.2 178.7 %reduce-scatter.14.cloned.1.call-start = ((), (), s32[]{:S(2)}) async-start(), calls=%async_computation.14 | async-start | bytes 3538944 | tf_op jit(solution)/shard_map/reduce_scatter | solution.py:178
  174.4 1.1 copy-start.5
  174.4 1.2 copy-start.12
  174.4 241.9 %reduce-scatter.20.cloned.1.call-start = ((), (), s32[]{:S(2)}) async-start(), calls=%async_computation.17 | async-start | bytes 1179648 | tf_op jit(solution)/shard_map/reduce_scatter | solution.py:181
  178.9 14.4 %copy-start.20 = (bf16[4,64,256]{2,1,0:T(8,128)(2,1)S(1)}, bf16[4,64,256]{2,1,0:T(8,128)(2,1)}, u32[]{:S(2)}) copy-start(bf16[4,64,256]{2,1,0:T(8,128)(2,1)} %copy-done.19) | copy-start | bytes 393220
  193.1 2.6 copy-start.10
  193.2 2.6 copy-start.25
  193.2 290.2 %reduce-scatter.16.cloned.1.call-start = ((), (), s32[]{:S(2)}) async-start(), calls=%async_computation.15 | async-start | bytes 1179648 | tf_op jit(solution)/shard_map/reduce_scatter | solution.py:179
Sparse Core Ops, SparseCore 0:
  25.1 25.7 reduce-scatter.7
  119.2 22.9 reduce-scatter.9
  166.9 25.2 reduce-scatter.11
  196.1 74.7 reduce-scatter.17
  274.8 74.0 reduce-scatter.13
  353.1 63.1 reduce-scatter.19
  420.3 62.9 reduce-scatter.15
where the time goes:
time: 491 us; the launch traced here: 490 us
  waiting for transfers between devices  328 us (67%)
  blocking collectives  58.2 us (12%)
  matrix products  42.9 us (9%)
  local copies, waits for them, and re-layouts  20.5 us (4%)
  between operations  14.6 us (3%)
  other arithmetic  14 us (3%)
  starting transfers between devices  11.8 us (2%)
    reduce_scatter x1, waiting for transfers between devices, shards(): lax.psum_scatter(grad_spatial_qkv, 'frames', scatter_dimension=1, tiled=T...  76.1 us
    reduce_scatter x1, waiting for transfers between devices, shards(): lax.psum_scatter(grad_temporal_qkv, 'frames', scatter_dimension=1, tiled=...  73.4 us
    reduce_scatter x1, waiting for transfers between devices, shards(): lax.psum_scatter(grad_spatial_out, 'frames', scatter_dimension=1, tiled=T...  67 us
    reduce_scatter x1, waiting for transfers between devices, shards(): lax.psum_scatter(grad_temporal_out, 'frames', scatter_dimension=1, tiled=...  65.5 us
    reduce_scatter x3, waiting for transfers between devices, patch_sums(): lax.psum_scatter(tensor.reshape(frames_dev, patches, model_width), 'mp',...  32.6 us
    all_gather x4, blocking collectives, patch_rows(): return lax.all_gather(tensor, 'mp', axis=1, tiled=True)  29.6 us
    all_to_all x2, blocking collectives, from_owners(): lax.all_to_all(tensor, 'frames', split_axis=1, concat_axis=2, tiled=True)  28.6 us
    all_to_all x2, waiting for transfers between devices, to_owners(): lax.all_to_all(tensor, 'frames', split_axis=2, concat_axis=1, tiled=True)  13.4 us
  transfers between devices with their start and end apart: 9, of which 7 were waited for; matrix products, arithmetic and copies ran while one was open for 6% of the time, Pallas kernels for 0%

commit v1 on v0

v1 whole, which is shorter than its diff:
```python
import jax
import jax.numpy as jnp
from jax import lax
from jax.experimental import pallas as pl
from jax.experimental.pallas import tpu as pltpu
from jax.sharding import PartitionSpec as P

HD = 64
EPS = 1e-06
NEGATIVE = -1e30
BF = jnp.bfloat16
F32 = jnp.float32
VMEM_LIMIT = 20 * 1024 * 1024


def mm(a, b, ca, cb):
    return lax.dot_general(a, b, (((ca,), (cb,)), ((), ())), preferred_element_type=F32)


def shape(dims, dtype=BF):
    return jax.ShapeDtypeStruct(dims, dtype)


def flipped(index, by, bits):
    total = index
    for b in range(bits):
        if (by >> b) & 1:
            total = total + (1 << b) * (1 - 2 * ((index // (1 << b)) % 2))
    return total


def swap(value, axis, by):
    size = lax.axis_size(axis)
    return lax.ppermute(value, axis, [(i, i ^ by) for i in range(size)])


class Kernel:
    def __init__(self, get, outs, put, smem, scratch, sems, early):
        self.get, self.outs, self.put = get, outs, put
        self.smem, self.scratch, self.sems, self.early = smem, scratch, sems, early

    def copy(self, src, dst):
        made = pltpu.make_async_copy(src, dst, self.sems.pop(0))
        made.start()
        return made


def run(
    body, ins, where, outs, out_where, smem=(), scratch=(), copies=0, early=None, flops=1000
):
    n, k, s = len(ins), len(outs), len(smem)
    staged_in = [i for i in range(n) if where[i] in "ha"]
    staged_out = [i for i in range(k) if out_where[i] in "ha"]

    def wrapped(*refs):
        refs = list(refs)

        def take(count):
            part = refs[:count]
            del refs[:count]
            return part

        scalars, src, dst = take(s), take(n), take(k)
        in_bufs, out_bufs = take(len(staged_in)), take(len(staged_out))
        in_sem, out_sem, own_sem = take(3)
        loads, stores = {}, {}
        results = list(dst)
        for at, i in enumerate(staged_out):
            results[i] = out_bufs[at]
        held = {i: in_bufs[at] for at, i in enumerate(staged_in)}
        waited = set()

        def get(i):
            if i not in held:
                return src[i]
            if i not in waited:
                loads[i].wait()
                waited.add(i)
            return held[i]

        def put(i):
            if i in staged_out and i not in stores:
                at = staged_out.index(i)
                stores[i] = pltpu.make_async_copy(out_bufs[at], dst[i], out_sem.at[at])
                stores[i].start()

        sems = [own_sem.at[i] for i in range(copies)]
        tools = Kernel(get, results, put, scalars, refs, sems, None)
        if early is not None:
            tools.early = early(tools)
        for at, i in enumerate(staged_in):
            loads[i] = pltpu.make_async_copy(src[i], in_bufs[at], in_sem.at[at])
            loads[i].start()
        body(tools)
        for i in staged_in:
            get(i)
        for i in range(k):
            put(i)
        for copy in stores.values():
            copy.wait()

    specs = {"v": pltpu.VMEM, "h": pltpu.HBM, "a": pl.ANY, "n": pl.ANY, "x": pltpu.HBM}
    specs = {key: pl.BlockSpec(memory_space=space) for key, space in specs.items()}
    buffers = [pltpu.VMEM(ins[i].shape, ins[i].dtype) for i in staged_in]
    buffers += [pltpu.VMEM(outs[i].shape, outs[i].dtype) for i in staged_out]
    ins = [
        pltpu.with_memory_space_constraint(a, pltpu.HBM) if w in "hx" else a
        for a, w in zip(ins, where)
    ]
    return pl.pallas_call(
        wrapped,
        out_shape=tuple(
            pltpu.HBM(o.shape, o.dtype) if w in "hx" else o for o, w in zip(outs, out_where)
        ),
        in_specs=[pl.BlockSpec(memory_space=pltpu.SMEM)] * s
        + [specs[w] for w in where],
        out_specs=tuple(specs[w] for w in out_where),
        scratch_shapes=buffers
        + [pltpu.SemaphoreType.DMA((max(1, c),)) for c in (len(staged_in), len(staged_out), copies)]
        + list(scratch),
        compiler_params=pltpu.CompilerParams(vmem_limit_bytes=VMEM_LIMIT),
        cost_estimate=pl.CostEstimate(flops=flops, bytes_accessed=1000, transcendentals=0),
    )(*smem, *ins)


def inv_rms(v):
    return lax.rsqrt(jnp.mean(v * v, -1, keepdims=True) + EPS)


SCALE = HD ** (-0.5)
assert SCALE == 0.125


def head_mask(width, head, scale=1.0):
    lane = lax.broadcasted_iota(jnp.int32, (1, width), 1)
    mask = ((lane >= head * HD) & (lane < (head + 1) * HD)).astype(F32)
    return (mask * scale).astype(BF)


def probs_of(q, k, head, allowed):
    scores = mm(q * head_mask(q.shape[1], head, SCALE), k, 1, 1)
    if allowed is not None:
        scores = jnp.where(allowed, scores, NEGATIVE)
    expo = jnp.exp(scores - jnp.max(scores, -1, keepdims=True))
    return expo * (1.0 / jnp.sum(expo, -1, keepdims=True))


def attend(q, k, v, heads):
    total = jnp.zeros(q.shape, F32)
    for h in range(heads):
        mask = head_mask(q.shape[1], h)
        probs = probs_of(q, k, h, None)
        total += mm(probs.astype(BF), v * mask, 1, 0)
    return total.astype(BF)


def attend_back(q, k, v, up, heads, probs_at, with_out):
    zero = jnp.zeros(q.shape, F32)
    out, dq, dk, dv = zero, zero, zero, zero
    v_scaled = v * jnp.full((1, 1), SCALE, BF)
    for h in range(heads):
        mask = head_mask(q.shape[1], h)
        up_head = up * mask
        probs = probs_at(h)
        probs_b = probs.astype(BF)
        if with_out:
            out += mm(probs_b, v * mask, 1, 0)
        dv += mm(probs_b, up_head, 0, 0)
        dp = mm(up_head, v_scaled, 1, 1)
        delta = jnp.sum(probs * dp, -1, keepdims=True)
        ds = (probs * (dp - delta)).astype(BF)
        dq += mm(ds, k * mask, 1, 0)
        dk += mm(ds, q * mask, 0, 0)
    return dq.astype(BF), dk.astype(BF), dv.astype(BF), out.astype(BF)


def row_order(rows, outer, middle, inner):
    to = lax.broadcasted_iota(jnp.int32, (rows, 1), 0)
    at = lax.broadcasted_iota(jnp.int32, (1, rows), 1)
    o, m, i = to // (middle * inner), (to // inner) % middle, to % inner
    return (at == (m * outer + o) * inner + i).astype(F32).astype(BF)


def own_block(r, rows):
    start = flipped(lax.axis_index("mp"), r, 2) * rows
    return pl.ds(pl.multiple_of(start, rows), rows)


def joined(x, grad):
    rows, dim = x.shape

    def body(t):
        for i in range(2):
            t.outs[0][:, i * dim : (i + 1) * dim] = t.get(i)[...]

    return run(body, (x, grad), "hh", (shape((rows, 2 * dim)),), "v")[0]


def spatial_forward(parts, weights, heads, groups):
    own_rows, dim = parts[0].shape
    mp, width = len(parts), weights.shape[2]
    rows = mp * own_rows

    def body(t):
        for r in (*range(1, mp), 0):
            xf = t.get(r)[...].astype(F32)
            t.outs[0][own_block(r, own_rows), :] = (xf * inv_rms(xf)).astype(BF)
        nx = t.outs[0][...]
        t.put(0)
        w = t.get(mp)
        q, k, v = [mm(nx, w[j], 1, 0).astype(BF) for j in range(3)]
        for j, part in enumerate((q, k, v)):
            t.outs[1][j] = part
        t.put(1)
        attn = attend(q, k, v, heads)
        order = row_order(rows, groups, mp, rows // (groups * mp))
        t.outs[2][...] = mm(order, attn, 1, 0).astype(BF)

    outs = (shape((rows, dim)), shape((3, rows, width)), shape((rows, width)))
    return run(
        body, (*parts, weights), "h" + "v" * (mp - 1) + "h", outs, "hhv"
    )


def owner_rows(xg, w_to):
    own_rows, mp = xg[0].shape[0], len(xg)
    rows, (width, dim) = mp * own_rows, w_to.shape

    def body(t):
        for r in range(mp):
            at = own_block(r, own_rows)
            t.outs[0][at, :] = t.get(r)[:, :dim]
            t.outs[1][at, :] = t.get(r)[:, dim:]
        t.outs[2][...] = mm(t.outs[1][...], t.get(mp)[...], 1, 1).astype(BF)

    whole = shape((rows, dim))
    return run(
        body, (*xg, w_to), "v" * mp + "h", (whole, whole, shape((rows, width))), "vvv"
    )


SENT = ((1, 3, 5, 7), (2, 3, 6, 7))
KEPT = ((0, 2, 4, 6), (0, 1, 4, 5))
OUT_SENT, OUT_KEPT = (1, 5, 3, 7), (0, 4, 2, 6)


def chunk_of(flat, right, r, groups):
    chunk = right.shape[1] // groups
    start = pl.multiple_of(flipped(lax.axis_index("frames"), r, 3) * chunk, chunk)
    return mm(flat, right[:, pl.ds(start, chunk)], 1, 0).astype(BF)


def chunk_grads(t, first, chosen, grads, normed, other, groups):
    flat = [grad.T for grad in grads]
    right = (normed, normed, normed, other)
    for pair, relative in enumerate(chosen):
        for i, r in enumerate(relative):
            for j in range(2):
                at = 2 * pair + j
                t.outs[first + pair][i, j] = chunk_of(flat[at], right[at], r, groups)


def half_shape(width, dim, groups):
    return shape((groups // 2, 2, width, dim // groups))


def temporal_stage(attn, x_all, g_all, up, w_so, w_qkv, clips, heads, frames, per):
    mp, (rows, width) = len(attn), attn[0].shape
    own_rows = rows // mp
    dim = x_all.shape[1]
    halves = frames == 8

    def rows_of(r):
        return own_block(r, own_rows)

    def body(t):
        (clip_ref,) = t.smem
        back, inv_buf = t.scratch
        total = t.get(mp)[...].astype(F32)
        order = row_order(rows, mp, frames, per)
        for r in range(mp):
            part = mm(order, t.get(r)[...], 1, 0).astype(BF)
            total += mm(part, t.get(mp + 2 + r)[...], 1, 0)
        inv = inv_rms(total)
        nh = (total * inv).astype(BF)
        t.outs[2][...] = nh
        inv_buf[...] = jnp.broadcast_to(inv, inv_buf.shape)
        t.outs[3][...] = t.outs[2][rows_of(0), :]
        t.outs[4][...] = inv_buf[rows_of(0), :]

        def key_of(axis):
            dims = (rows, 1) if axis == 0 else (1, rows)
            token = lax.broadcasted_iota(jnp.int32, dims, axis)
            block = token // per
            frame = block % frames
            patch = (block // frames) * per + token % per
            end = jnp.int32(0)
            clip = jnp.zeros(dims, jnp.int32)
            for c in range(clips.shape[0]):
                end = end + clip_ref[c]
                clip += (frame >= end).astype(jnp.int32)
            return clip * rows + patch

        allowed = key_of(0) == key_of(1)
        w = t.get(2 * mp + 2)
        q, k, v = [mm(nh, w[j], 1, 0).astype(BF) for j in range(3)]
        grads = attend_back(
            q, k, v, t.get(mp + 1)[...], heads, lambda h: probs_of(q, k, h, allowed), True
        )
        for j in range(4):
            t.outs[5][j] = grads[j]
        d_normed = jnp.zeros((rows, dim), F32)
        for j in range(3):
            d_normed += mm(grads[j], w[j], 1, 1)
        back[...] = d_normed.astype(BF)
        for r in range(mp):
            t.outs[1 - r % 2][r // 2] = back[rows_of(r), :]
        if halves:
            chunk_grads(t, 6, SENT, grads, t.outs[2], t.get(2 * mp + 3), frames)

    half = shape((mp // 2, own_rows, dim))
    outs = (
        half,
        half,
        shape((rows, dim)),
        shape((own_rows, dim)),
        shape((own_rows, 128), F32),
        shape((4, rows, width)),
    )
    if halves:
        outs += (half_shape(width, dim, frames),) * 2
    ins = (*attn, x_all, up, *w_so, w_qkv, g_all)
    return run(
        body, ins, "v" * len(ins), outs, "v" * len(outs), smem=(clips,),
        scratch=(pltpu.VMEM((rows, dim), BF), pltpu.VMEM((rows, 128), F32)),
    )


def head_sums(send, keep):
    def body(t):
        t.outs[0][...] = (t.get(0)[1].astype(F32) + t.get(1)[1].astype(F32)).astype(BF)

    came = swap(send, "mp", 1)
    (pair,) = run(body, (keep, came), "vv", (shape(keep.shape[1:]),), "v")
    return keep, came, swap(pair, "mp", 2)


def summed(t):
    return t.get(0)[0].astype(F32) + t.get(1)[0].astype(F32) + t.get(2)[...].astype(F32)


def hidden_back(parts, unit, inv, grad):
    dim = unit.shape[1]

    def body(t):
        total, nh = summed(t), t.get(3)[...].astype(F32)
        rest = total - nh * jnp.mean(total * nh, -1, keepdims=True)
        g = t.get(5)[:, dim:].astype(F32)
        t.outs[0][...] = (g + t.get(4)[:, :1] * rest).astype(BF)

    return run(body, (*parts, unit, inv, grad), "vvvvvv", (shape(unit.shape),), "v")[0]


def tokens_back(parts, x, grad):
    def body(t):
        total, xf = summed(t), t.get(3)[...].astype(F32)
        inv = inv_rms(xf)
        nx = xf * inv
        rest = total - nx * jnp.mean(total * nx, -1, keepdims=True)
        t.outs[0][...] = (t.get(4)[...].astype(F32) + inv * rest).astype(BF)

    return run(body, (*parts, x, grad), "vvvvv", (shape(x.shape),), "v")[0]


def weight_grads_half(grads, normed, other, groups, flops=1000):
    def body(t):
        left = [t.get(0)[j] for j in range(4)]
        chunk_grads(t, 0, KEPT, left, t.get(1), t.get(2), groups)

    half = half_shape(grads.shape[2], normed.shape[1], groups)
    return run(body, (grads, normed, other), "vvv", (half, half), "vv", flops=flops)


def weight_grads_whole(grads, normed, other):
    def body(t):
        for j in range(4):
            right = t.get(2) if j == 3 else t.get(1)
            t.outs[0][j] = mm(t.get(0)[j], right[...], 0, 0)

    whole = shape((4, grads.shape[2], normed.shape[1]), F32)
    return run(body, (grads, normed, other), "vhh", (whole,), "h")[0]


def spatial_probs(qkv, attn_moved, heads, groups, mp):
    rows, width = attn_moved.shape

    def body(t):
        q, k = t.get(0)[0], t.get(0)[1]
        for h in range(heads):
            t.outs[0][h] = probs_of(q, k, h, None)
        order = row_order(rows, mp, groups, rows // (groups * mp))
        t.outs[1][...] = mm(order, t.get(1)[...], 1, 0).astype(BF)

    outs = (shape((heads, rows, rows), F32), shape((rows, width)))
    return run(body, (qkv, attn_moved), "vv", outs, "vv")


def out_chunks(parts, attn, groups):
    own_rows, dim = parts[0].shape
    mp, width = len(parts), attn.shape[1]

    def body(t):
        dh = t.outs[0]
        for r in range(mp):
            dh[own_block(r, own_rows), :] = t.get(r)[...]
        if groups == 8:
            flat = t.get(mp)[...].T
            for at, relative in ((1, OUT_SENT), (2, OUT_KEPT)):
                for i, r in enumerate(relative):
                    t.outs[at][i] = chunk_of(flat, dh, r, groups)

    outs = (shape((mp * own_rows, dim)),)
    if groups == 8:
        outs += (shape((groups // 2, width, dim // groups)),) * 2
    return run(body, (*parts, attn), "v" * (mp + 1), outs, "v" * len(outs))


def qkv_parts(grads):
    flat = jnp.concatenate([grad.T for grad in grads], 0)
    first = 7 * flat.shape[0] // 12
    return flat[:first], flat[first:]


def qkv_chunks(t, first, chosen, grads, normed, groups):
    for at, (flat, relative) in enumerate(zip(qkv_parts(grads), chosen)):
        for i, r in enumerate(relative):
            t.outs[first + at][i] = chunk_of(flat, normed, r, groups)


def qkv_part_shapes(width, dim, groups):
    first = 7 * 3 * width // 12
    return tuple(
        shape((groups // 2, rows, dim // groups)) for rows in (first, 3 * width - first)
    )


def spatial_back(dh, w_so, qkv, probs, normed, heads, groups):
    rows, dim = dh.shape
    width = w_so.shape[0]

    def body(t):
        up = mm(t.get(0)[...], t.get(1)[...], 1, 1).astype(BF)
        qkv_ref = t.get(2)
        grads = attend_back(
            qkv_ref[0], qkv_ref[1], qkv_ref[2], up, heads, lambda h: t.get(3)[h], False
        )[:3]
        for j in range(3):
            t.outs[0][j] = grads[j]
        if groups == 8:
            qkv_chunks(t, 1, SENT, grads, t.get(4), groups)

    outs = (shape((3, rows, width)),)
    if groups == 8:
        outs += qkv_part_shapes(width, dim, groups)
    return run(body, (dh, w_so, qkv, probs, normed), "vvvvh", outs, "v" * len(outs))


def qkv_keeps(grads, normed, groups, flops):
    def body(t):
        qkv_chunks(t, 0, KEPT, [t.get(0)[j] for j in range(3)], t.get(1), groups)

    outs = qkv_part_shapes(grads.shape[2], normed.shape[1], groups)
    return run(body, (grads, normed), "vv", outs, "vv", flops=flops)


def normed_back(grads, w_qkv, mp):
    rows, dim = grads.shape[1], w_qkv.shape[1]
    own_rows = rows // mp

    def body(t):
        (back,) = t.scratch
        total = jnp.zeros((rows, dim), F32)
        for j in range(3):
            total += mm(t.get(0)[j], t.get(1)[j], 1, 1)
        back[...] = total.astype(BF)
        for r in range(mp):
            t.outs[1 - r % 2][r // 2] = back[own_block(r, own_rows), :]

    half = shape((mp // 2, own_rows, dim))
    return run(
        body, (grads, w_qkv), "vv", (half, half), "vv", scratch=(pltpu.VMEM((rows, dim), BF),)
    )


def halve(keeps, cames, keep_in="v", out="v", merged=False):
    n, depth = len(keeps), keeps[0].shape[0]

    def body(t):
        for i in range(depth - 1, -1, -1):
            for at in range(n):
                total = t.get(at)[i].astype(F32) + t.get(n + at)[i].astype(F32)
                kept = 1 - i % 2
                if merged:
                    t.outs[kept][at] = total.astype(BF)
                else:
                    t.outs[n * kept + at][i // 2] = total.astype(BF)

    if merged:
        outs = (shape((n, *keeps[0].shape[1:])),) * 2
    else:
        outs = tuple(shape((depth // 2, *keep.shape[1:])) for keep in keeps) * 2
    where = keep_in * n + "v" * n
    return run(body, (*keeps, *cames), where, outs, out * len(outs))


def last_sums(pairs):
    chunk, size = pairs[0][0].shape[-1], HD
    blocks = [tuple(part.reshape(-1, size, chunk) for part in pair) for pair in pairs]
    width = sum(pair[0].shape[0] for pair in blocks) * size // 4
    per = width // size

    def body(t):
        b = 0
        for at, (keep, _) in enumerate(blocks):
            for i in range(keep.shape[0]):
                total = t.get(2 * at)[i].astype(F32) + t.get(2 * at + 1)[i].astype(F32)
                side = slice((b % per) * size, (b % per + 1) * size)
                if b < 3 * per:
                    t.outs[0][b // per, :, side] = total.T
                else:
                    t.outs[1][side, :] = total
                b += 1

    ins = [part for pair in blocks for part in pair]
    outs = (shape((3, chunk, width), F32), shape((width, chunk), F32))
    return run(body, ins, "v" * len(ins), outs, "hh")


def reduce_whole(flat, normed, other):
    whole = weight_grads_whole(flat, normed, other)
    mine = lax.psum_scatter(whole, "frames", scatter_dimension=2, tiled=True)
    return jnp.swapaxes(mine[:3], 1, 2), mine[3]


def shards(
    video_tokens, grad_output, spatial_qkv, spatial_out, temporal_qkv, temporal_out, clip_frames
):
    frames_dev, rows_mp, dim = video_tokens.shape
    width = spatial_out.shape[0]
    heads = width // HD
    groups = lax.axis_size("frames")
    mp = lax.axis_size("mp")
    patches = rows_mp * mp
    per = rows_mp // groups
    assert frames_dev == 1 and rows_mp % groups == 0 and mp == 4

    halves = groups == 8
    x_own, g_own = video_tokens[0], grad_output[0]
    x_one, x_two = swap(x_own, "mp", 1), swap(x_own, "mp", 2)
    xg, x_one, x_two, so_own = lax.optimization_barrier(
        (joined(x_own, g_own), x_one, x_two, spatial_out)
    )
    x_three = swap(x_two, "mp", 1)
    xg = lax.all_to_all(xg.reshape(groups, per, 2 * dim), "frames", 0, 0, tiled=True)
    xg = xg.reshape(rows_mp, 2 * dim)
    so_two = swap(so_own, "mp", 2)

    normed_x, qkv_s, attn_send = spatial_forward(
        (x_own, x_one, x_two, x_three), spatial_qkv, heads, groups
    )
    attn_send, xg = lax.optimization_barrier((attn_send, xg))
    xg_two = swap(xg, "mp", 2)
    moved = lax.all_to_all(
        attn_send.reshape(groups, mp * per, width), "frames", 0, 0, tiled=True
    ).reshape(patches, width)
    so_two, moved = lax.optimization_barrier((so_two, moved))
    moved_two = swap(moved, "mp", 2)
    w_so = spatial_out, swap(spatial_out, "mp", 1), so_two, swap(so_two, "mp", 1)
    xg_all = xg, swap(xg, "mp", 1), xg_two, swap(xg_two, "mp", 1)
    moved_two, rows_own = lax.optimization_barrier((moved_two, owner_rows(xg_all, temporal_out)))
    x_rows, g_rows, d_attn_t = rows_own
    attn_owned = moved, swap(moved, "mp", 1), moved_two, swap(moved_two, "mp", 1)

    send_h, keep_h, normed_h, unit_own, inv_own, t_grads, *t_sent = temporal_stage(
        attn_owned, x_rows, g_rows, d_attn_t, w_so, temporal_qkv, clip_frames, heads, groups, per
    )
    parts = head_sums(send_h, keep_h)
    if halves:
        t_kept = weight_grads_half(t_grads, normed_h, g_rows, groups)
        parts, t_kept = lax.optimization_barrier((parts, t_kept))
        came = [swap(t_sent[0], "frames", 1), swap(t_sent[1], "frames", 2)]
        t_sums = halve(t_kept, came, out="h")
    d_hidden = hidden_back(parts, unit_own, inv_own, xg)
    d_hidden = lax.all_to_all(
        d_hidden.reshape(groups, per, dim), "frames", 0, 0, tiled=True
    ).reshape(rows_mp, dim)
    if halves:
        d_hidden, t_sums = lax.optimization_barrier((d_hidden, t_sums))
        t_second = [swap(t_sums[0], "frames", 2), swap(t_sums[1], "frames", 1)]
    dh_one, dh_two = swap(d_hidden, "mp", 1), swap(d_hidden, "mp", 2)
    d_hidden, qkv_s, attn_send = lax.optimization_barrier((d_hidden, qkv_s, attn_send))
    probs_s, attn_s = spatial_probs(qkv_s, attn_send, heads, groups, mp)
    dh_two, probs_s, attn_s = lax.optimization_barrier((dh_two, probs_s, attn_s))
    dh_three = swap(dh_two, "mp", 1)
    d_hidden_all, *o_chunks = out_chunks((d_hidden, dh_one, dh_two, dh_three), attn_s, groups)
    dh_ready = d_hidden_all
    if halves:
        dh_ready, t_second = lax.optimization_barrier((dh_ready, t_second))
        t_send, t_keep = halve(t_sums[2:], t_second, keep_in="h", merged=True)
        dh_ready, t_send, t_keep = lax.optimization_barrier((dh_ready, t_send, t_keep))
        t_came = swap(t_send, "frames", 4)
    else:
        t_qkv, t_out = reduce_whole(t_grads, normed_h, g_rows)
    s_grads, *s_sent = spatial_back(
        dh_ready, spatial_out, qkv_s, probs_s, normed_x, heads, groups
    )
    if halves:
        after = lax.optimization_barrier
        o_send, o_keep = halve([o_chunks[1]], [swap(o_chunks[0], "frames", 1)])
        send_x, keep_x = normed_back(s_grads, spatial_qkv, mp)
        s_grads, t_came, o_send, o_keep = after((s_grads, t_came, o_send, o_keep))
        t_qkv, t_out = last_sums([(t_keep, t_came)])
        s_kept = qkv_keeps(s_grads, normed_x, groups, 50_000_000_000)
        a_came, b_came = swap(s_sent[0], "frames", 1), swap(s_sent[1], "frames", 2)
        o_came = swap(o_send, "frames", 4)
        a_sums = halve([s_kept[0]], [a_came])
        a_sums, b_came = after((a_sums, b_came))
        b_sums = halve([s_kept[1]], [b_came])
        b_sums, o_came = after((b_sums, o_came))
        o_sums = halve([o_keep], [o_came])
        a_came, b_came = swap(a_sums[0], "frames", 2), swap(b_sums[0], "frames", 1)
        o_sums, a_came = after((o_sums, a_came))
        a_sums = halve([a_sums[1]], [a_came])
        a_sums, b_came = after((a_sums, b_came))
        b_sums = halve([b_sums[1]], [b_came])
        s_qkv, s_out = last_sums([
            (a_sums[1], swap(a_sums[0], "frames", 4)),
            (b_sums[1], swap(b_sums[0], "frames", 4)),
            (o_sums[1], swap(o_sums[0], "frames", 2)),
        ])
    else:
        send_x, keep_x = normed_back(s_grads, spatial_qkv, mp)
        all_grads = jnp.concatenate([s_grads, attn_s[None]], 0)
        s_qkv, s_out = reduce_whole(all_grads, normed_x, d_hidden_all)
    grad_tokens = tokens_back(head_sums(send_x, keep_x), x_own, d_hidden)
    return grad_tokens[None], s_qkv, s_out, t_qkv, t_out


def solution(mesh):
    placed = (
        P("frames", "mp", None),
        P("frames", "mp", None),
        P(None, None, "mp"),
        P("mp", None),
        P(None, None, "mp"),
        P("mp", None),
        P(),
    )
    return jax.shard_map(
        shards,
        mesh=mesh,
        in_specs=placed,
        out_specs=(
            P("frames", "mp", None),
            P(None, "frames", "mp"),
            P("mp", "frames"),
            P(None, "frames", "mp"),
            P("mp", "frames"),
        ),
        check_vma=False,
    )
```

time: 491 us -> 119 us (0.24)
  waiting for transfers between devices: 328 us -> 51.6 us
  blocking collectives: 58.2 us -> 0 us
  matrix products: 42.9 us -> 0 us
  Pallas kernels: 0 us -> 28.6 us
  starting transfers between devices: 11.8 us -> 37 us
  local copies, waits for them, and re-layouts: 20.5 us -> 0.04 us
  other arithmetic: 14 us -> 0 us
  between operations: 14.6 us -> 1.1 us
    reduce_scatter x7 -> x0, waiting for transfers between devices: 315 us -> none  [the longest x1 76.1 us: shards(): lax.psum_scatter(grad_spatial_qkv, 'frames', scatter_dimension=1, tiled=T...]
    dot_general x22 -> x0, matrix products: 41.4 us -> none  [the longest x2 6.33 us: attend_back(): jnp.einsum('bhlm,' + key_layout + '->' + layout, d_scores, keys_in, prefe...]
    ppermute x0 -> x33, waiting for transfers between devices: none -> 39.6 us  [swap(): return lax.ppermute(value, axis, [(i, i ^ by) for i in range(size)])]
    all_gather x4 -> x0, blocking collectives: 29.6 us -> none  [patch_rows(): return lax.all_gather(tensor, 'mp', axis=1, tiled=True)]
    all_to_all x2 -> x0, blocking collectives: 28.6 us -> none  [from_owners(): lax.all_to_all(tensor, 'frames', split_axis=1, concat_axis=2, tiled=True)]
    pallas_call x0 -> x24, Pallas kernels: none -> 28.6 us  [run(): pl.pallas_call(wrapped, out_shape=tuple((pltpu.HBM(o.shape, o.dtype) if w...]
    ppermute x0 -> x33, starting transfers between devices: none -> 22.3 us  [swap(): return lax.ppermute(value, axis, [(i, i ^ by) for i in range(size)])]
    unnamed x63 -> x14, local copies, waits for them, and re-layouts: 8.41 us -> 0.04 us
  transfers between devices with their start and end apart: 9 -> 36, of which waited for: 7 -> 24; matrix products, arithmetic and copies ran while one was open for 6% -> 0% of each run, Pallas kernels for 0% -> 17%
where the time goes in v1:
time: 119 us; the launch traced here: 118 us
  waiting for transfers between devices  51.6 us (43%)
  starting transfers between devices  37 us (31%)
  Pallas kernels  28.6 us (24%)
    ppermute x33, waiting for transfers between devices, swap(): return lax.ppermute(value, axis, [(i, i ^ by) for i in range(size)])  39.6 us
    pallas_call x24, Pallas kernels, run(): pl.pallas_call(wrapped, out_shape=tuple((pltpu.HBM(o.shape, o.dtype) if w...  28.6 us
    ppermute x33, starting transfers between devices, swap(): return lax.ppermute(value, axis, [(i, i ^ by) for i in range(size)])  22.3 us
    all_to_all x1, waiting for transfers between devices, shards(): lax.all_to_all(attn_send.reshape(groups, mp * per, width), 'frames', 0, 0...  6.81 us
    all_to_all x1, starting transfers between devices, shards(): lax.all_to_all(xg.reshape(groups, per, 2 * dim), 'frames', 0, 0, tiled=True)  6.03 us
    all_to_all x1, starting transfers between devices, shards(): lax.all_to_all(attn_send.reshape(groups, mp * per, width), 'frames', 0, 0...  4.48 us
    all_to_all x1, starting transfers between devices, shards(): lax.all_to_all(d_hidden.reshape(groups, per, dim), 'frames', 0, 0, tiled=...  4.24 us
    all_to_all x1, waiting for transfers between devices, shards(): lax.all_to_all(d_hidden.reshape(groups, per, dim), 'frames', 0, 0, tiled=...  3.77 us
  transfers between devices with their start and end apart: 36, of which 24 were waited for; matrix products, arithmetic and copies ran while one was open for 0% of the time, Pallas kernels for 17%

profile of v1, /device:TPU:0, one launch (start us, length us, event | category | flops | bytes accessed | tf_op | source)
XLA Modules:
  0.0 118.3 jit_solution(3212691228860314230)
XLA Ops:
  0.6 3.0 %collective-permute-start.1 = (bf16[64,1024]{1,0:T(8,128)(2,1)}, bf16[64,1024]{1,0:T(8,128)(2,1)S(1)}, u32[]{:S(2)}, u32[]{:S(2)}) collective-permute-start(bf16[64,1024]{1,0:T(8,128)(2,1)} %bitcast.25), channel_id=1, source_target_pairs={{0,2},{1,3},{2,0},{3,1},{4,6},{5,7},{6,4},{7,5},{8,10},{9,11},{10,... | collective-permute-start | bytes 393224 | tf_op jit(solution)/shard_map/ppermute | solution.py:34
  3.7 1.7 %shard_map.110 = bf16[64,2048]{1,0:T(8,128)(2,1)} custom-call(bf16[64,1024]{1,0:T(8,128)(2,1)} %bitcast.27, bf16[64,1024]{1,0:T(8,128)(2,1)} %bitcast.41), custom_call_target="tpu_custom_call" | custom-call | flops 1000 | bytes 1000 | tf_op jit(solution)/shard_map/pallas_call | solution.py:110
  5.4 2.0 %collective-permute-done.1.refs_2_ = bf16[64,1024]{1,0:T(8,128)(2,1)S(1)} collective-permute-done((bf16[64,1024]{1,0:T(8,128)(2,1)}, bf16[64,1024]{1,0:T(8,128)(2,1)S(1)}, u32[]{:S(2)}, u32[]{:S(2)}) %collective-permute-start.1) | collective-permute-done | bytes 131104 | tf_op jit(solution)/shard_map/ppermute | solution.py:34
  7.4 6.0 %all-to-all-start = ((bf16[8,8,2048]{2,1,0:T(8,128)(2,1)}), bf16[8,8,2048]{2,1,0:T(8,128)(2,1)S(1)}, u32[]{:S(2)}, u32[]{:S(2)}) async-start(bf16[8,8,2048]{2,1,0:T(8,128)(2,1)} %bitcast.2), calls=%async_computation | async-start | bytes 524288 | tf_op jit(solution)/shard_map/all_to_all | solution.py:564
  13.4 1.6 %collective-permute-start.2 = (bf16[256,1024]{1,0:T(8,128)(2,1)}, bf16[256,1024]{1,0:T(8,128)(2,1)S(1)}, u32[]{:S(2)}, u32[]{:S(2)}) collective-permute-start(bf16[256,1024]{1,0:T(8,128)(2,1)} %refs_1_.2), channel_id=1, source_target_pairs={{0,2},{1,3},{2,0},{3,1},{4,6},{5,7},{6,4},{7,5},{8,10},{9,11},{10,... | collective-permute-start | bytes 1572872 | tf_op jit(solution)/shard_map/ppermute | solution.py:34
  15.0 1.3 %collective-permute-done.3.refs_3_ = bf16[64,1024]{1,0:T(8,128)(2,1)S(1)} collective-permute-done((bf16[64,1024]{1,0:T(8,128)(2,1)S(1)}, bf16[64,1024]{1,0:T(8,128)(2,1)S(1)}, u32[]{:S(2)}, u32[]{:S(2)}) %collective-permute-start.3) | collective-permute-done | bytes 131104 | tf_op jit(solution)/shard_map/ppermute | solution.py:34
  16.4 3.8 %shard_map.111 = (bf16[256,1024]{1,0:T(8,128)(2,1)}, bf16[3,256,256]{2,1,0:T(8,128)(2,1)}, bf16[256,256]{1,0:T(8,128)(2,1)}) custom-call(bf16[64,1024]{1,0:T(8,128)(2,1)} %bitcast.28, bf16[64,1024]{1,0:T(8,128)(2,1)S(1)} %collective-permute-done.refs_1_, bf16[64,1024]{1,0:T(8,128)(2,1)S(1)} %collective-permute-done.1.refs_2_, ...), custom_call_target="tpu_custom_call" | custom-call | flops 1000 | bytes 1000 | tf_op jit(solution)/shard_map/pallas_call | solution.py:110
  20.2 1.5 %all-to-all-done = bf16[8,8,2048]{2,1,0:T(8,128)(2,1)S(1)} async-done(((bf16[8,8,2048]{2,1,0:T(8,128)(2,1)}), bf16[8,8,2048]{2,1,0:T(8,128)(2,1)S(1)}, u32[]{:S(2)}, u32[]{:S(2)}) %all-to-all-start) | async-done | bytes 262176 | tf_op jit(solution)/shard_map/all_to_all | solution.py:564
  21.6 4.5 %all-to-all-start.1 = ((bf16[8,32,256]{2,1,0:T(8,128)(2,1)}), bf16[8,32,256]{2,1,0:T(8,128)(2,1)S(1)}, u32[]{:S(2)}, u32[]{:S(2)}) async-start(bf16[8,32,256]{2,1,0:T(8,128)(2,1)} %bitcast.4), calls=%async_computation.1 | async-start | bytes 262144 | tf_op jit(solution)/shard_map/all_to_all | solution.py:573
  26.1 0.5 collective-permute-start.7
  26.6 6.8 %all-to-all-done.1 = bf16[8,32,256]{2,1,0:T(8,128)(2,1)S(1)} async-done(((bf16[8,32,256]{2,1,0:T(8,128)(2,1)}), bf16[8,32,256]{2,1,0:T(8,128)(2,1)S(1)}, u32[]{:S(2)}, u32[]{:S(2)}) %all-to-all-start.1) | async-done | bytes 131104 | tf_op jit(solution)/shard_map/all_to_all | solution.py:573
  33.5 0.5 collective-permute-start.6
  34.0 0.3 collective-permute-done.7.refs_2_
  34.3 0.5 collective-permute-start.5
  34.8 0.9 collective-permute-done.6.refs_1_
  35.7 0.1 collective-permute-start.4
  35.9 0.4 collective-permute-done.8.refs_3_
  36.3 2.4 %shard_map.112 = (bf16[256,1024]{1,0:T(8,128)(2,1)S(1)}, bf16[256,1024]{1,0:T(8,128)(2,1)S(1)}, bf16[256,256]{1,0:T(8,128)(2,1)S(1)}) custom-call(bf16[64,2048]{1,0:T(8,128)(2,1)S(1)} %bitcast.19, bf16[64,2048]{1,0:T(8,128)(2,1)S(1)} %collective-permute-done.6.refs_1_, bf16[64,2048]{1,0:T(8,128)(2,1)} %collective-permute-done.7.refs_2_, ...), custom_call_target="tpu_custom_call" | custom-call | flops 1000 | bytes 1000 | tf_op jit(solution)/shard_map/pallas_call | solution.py:110
  38.7 1.5 %collective-permute-done.5.refs_3_ = bf16[256,256]{1,0:T(8,128)(2,1)S(1)} collective-permute-done((bf16[256,256]{1,0:T(8,128)(2,1)S(1)}, bf16[256,256]{1,0:T(8,128)(2,1)S(1)}, u32[]{:S(2)}, u32[]{:S(2)}) %collective-permute-start.5) | collective-permute-done | bytes 131104 | tf_op jit(solution)/shard_map/ppermute | solution.py:34
  40.2 1.3 %collective-permute-done.9.refs_4_ = bf16[256,256]{1,0:T(8,128)(2,1)S(1)} collective-permute-done((bf16[256,256]{1,0:T(8,128)(2,1)S(1)}, bf16[256,256]{1,0:T(8,128)(2,1)S(1)}, u32[]{:S(2)}, u32[]{:S(2)}) %collective-permute-start.9) | collective-permute-done | bytes 131104 | tf_op jit(solution)/shard_map/ppermute | solution.py:34
  41.6 7.0 %shard_map.113 = (bf16[2,64,1024]{2,1,0:T(8,128)(2,1)S(1)}, bf16[2,64,1024]{2,1,0:T(8,128)(2,1)S(1)}, bf16[256,1024]{1,0:T(8,128)(2,1)S(1)}, bf16[64,1024]{1,0:T...) custom-call(s32[4]{0:T(128)S(1)} %copy-done.6, ...), custom_call_target="tpu_custom_call" | custom-call | flops 1000 | bytes 1000 | tf_op jit(solution)/shard_map/pallas_call | solution.py:110
  48.6 0.2 collective-permute-start.12
  48.8 1.7 %collective-permute-start.14 = (bf16[4,2,256,128]{3,2,1,0:T(8,128)(2,1)}, bf16[4,2,256,128]{3,2,1,0:T(8,128)(2,1)S(1)}, u32[]{:S(2)}, u32[]{:S(2)}) collective-permute-start(bf16[4,2,256,128]{3,2,1,0:T(8,128)(2,1)} %get-tuple-element.134), channel_id=1, source_target_pairs={{0,4},{4,0},{8,12},{12,8},{16,20},{20,16},{24,28},{28,24},{1,5},{5... | collective-permute-start | bytes 1572872 | tf_op jit(solution)/shard_map/ppermute | solution.py:34
  50.5 1.5 %collective-permute-start.15 = (bf16[4,2,256,128]{3,2,1,0:T(8,128)(2,1)}, bf16[4,2,256,128]{3,2,1,0:T(8,128)(2,1)S(1)}, u32[]{:S(2)}, u32[]{:S(2)}) collective-permute-start(bf16[4,2,256,128]{3,2,1,0:T(8,128)(2,1)} %get-tuple-element.135), channel_id=1, source_target_pairs={{0,8},{4,12},{8,0},{12,4},{16,24},{20,28},{24,16},{28,20},{1,9},{5... | collective-permute-start | bytes 1572872 | tf_op jit(solution)/shard_map/ppermute | solution.py:34
  52.1 0.6 collective-permute-start.13
  52.7 0.8 shard_map.115
  53.5 3.9 %collective-permute-done.13.refs_2_ = bf16[64,1024]{1,0:T(8,128)(2,1)S(1)} collective-permute-done((bf16[64,1024]{1,0:T(8,128)(2,1)S(1)}, bf16[64,1024]{1,0:T(8,128)(2,1)S(1)}, u32[]{:S(2)}, u32[]{:S(2)}) %collective-permute-start.13) | collective-permute-done | bytes 131104 | tf_op jit(solution)/shard_map/ppermute | solution.py:34
  57.4 0.9 shard_map.116
  58.2 4.2 %all-to-all-start.2 = ((bf16[8,8,1024]{2,1,0:T(8,128)(2,1)}), bf16[8,8,1024]{2,1,0:T(8,128)(2,1)S(1)}, u32[]{:S(2)}, u32[]{:S(2)}) async-start(bf16[8,8,1024]{2,1,0:T(8,128)(2,1)} %bitcast.6), calls=%async_computation.2 | async-start | bytes 262144 | tf_op jit(solution)/shard_map/all_to_all | solution.py:594
  62.5 0.7 collective-permute-done.14.refs_2_
  63.2 1.7 %collective-permute-done.15.refs_3_ = bf16[4,2,256,128]{3,2,1,0:T(8,128)(2,1)S(1)} collective-permute-done((bf16[4,2,256,128]{3,2,1,0:T(8,128)(2,1)}, bf16[4,2,256,128]{3,2,1,0:T(8,128)(2,1)S(1)}, u32[]{:S(2)}, u32[]{:S(2)}) %collective-permute-start.15) | collective-permute-done | bytes 524320 | tf_op jit(solution)/shard_map/ppermute | solution.py:34
  64.9 1.1 shard_map.117
  66.1 3.8 %all-to-all-done.2 = bf16[8,8,1024]{2,1,0:T(8,128)(2,1)S(1)} async-done(((bf16[8,8,1024]{2,1,0:T(8,128)(2,1)}), bf16[8,8,1024]{2,1,0:T(8,128)(2,1)S(1)}, u32[]{:S(2)}, u32[]{:S(2)}) %all-to-all-start.2) | async-done | bytes 131104 | tf_op jit(solution)/shard_map/all_to_all | solution.py:594
  69.8 0.5 collective-permute-start.17
  70.3 1.3 %collective-permute-start.20 = (bf16[2,2,256,128]{3,2,1,0:T(8,128)(2,1)}, bf16[2,2,256,128]{3,2,1,0:T(8,128)(2,1)S(1)}, u32[]{:S(2)}, u32[]{:S(2)}) collective-permute-start(bf16[2,2,256,128]{3,2,1,0:T(8,128)(2,1)} %get-tuple-element.151), channel_id=1, source_target_pairs={{0,4},{4,0},{8,12},{12,8},{16,20},{20,16},{24,28},{28,24},{1,5},{5... | collective-permute-start | bytes 786440 | tf_op jit(solution)/shard_map/ppermute | solution.py:34
  71.7 1.5 %shard_map.118 = (f32[4,256,256]{2,1,0:T(8,128)S(1)}, bf16[256,256]{1,0:T(8,128)(2,1)S(1)}) custom-call(bf16[3,256,256]{2,1,0:T(8,128)(2,1)S(1)} %copy-done.3, bf16[256,256]{1,0:T(8,128)(2,1)} %get-tuple-element.144.refs_1_), custom_call_target="tpu_custom_call" | custom-call | flops 1000 | bytes 1000 | tf_op jit(solution)/shard_map/pallas_call | solution.py:110
  73.2 1.6 %collective-permute-done.17.refs_2_ = bf16[64,1024]{1,0:T(8,128)(2,1)S(1)} collective-permute-done((bf16[64,1024]{1,0:T(8,128)(2,1)S(1)}, bf16[64,1024]{1,0:T(8,128)(2,1)S(1)}, u32[]{:S(2)}, u32[]{:S(2)}) %collective-permute-start.17) | collective-permute-done | bytes 131104 | tf_op jit(solution)/shard_map/ppermute | solution.py:34
  74.8 1.3 %collective-permute-done.18.refs_3_ = bf16[64,1024]{1,0:T(8,128)(2,1)S(1)} collective-permute-done((bf16[64,1024]{1,0:T(8,128)(2,1)S(1)}, bf16[64,1024]{1,0:T(8,128)(2,1)S(1)}, u32[]{:S(2)}, u32[]{:S(2)}) %collective-permute-start.18) | collective-permute-done | bytes 131104 | tf_op jit(solution)/shard_map/ppermute | solution.py:34
  76.1 0.5 shard_map.119
  76.7 0.3 collective-permute-done.19.refs_2_
  76.9 1.3 %collective-permute-start.24 = (bf16[4,256,128]{2,1,0:T(8,128)(2,1)S(1)}, bf16[4,256,128]{2,1,0:T(8,128)(2,1)S(1)}, u32[]{:S(2)}, u32[]{:S(2)}) collective-permute-start(bf16[4,256,128]{2,1,0:T(8,128)(2,1)S(1)} %get-tuple-element.167), channel_id=1, source_target_pairs={{0,4},{4,0},{8,12},{12,8},{16,20},{20,16},{24,28},{28,24},{1,5},{5... | collective-permute-start | bytes 786440 | tf_op jit(solution)/shard_map/ppermute | solution.py:34
  78.2 1.2 shard_map.120
  79.4 1.1 collective-permute-start.23
  80.5 2.4 %shard_map.121 = (bf16[3,256,256]{2,1,0:T(8,128)(2,1)S(1)}, bf16[4,448,128]{2,1,0:T(8,128)(2,1)S(1)}, bf16[4,320,128]{2,1,0:T(8,128)(2,1)S(1)}) custom-call(bf16[256,1024]{1,0:T(8,128)(2,1)S(1)} %get-tuple-element.159.refs_0_, bf16[256,1024]{1,0:T(8,128)(2,1)S(1)} %copy-done.1, bf16[3,256,256]{2,1,0:T(8,128)(2,1)S(1)} %copy-done.3, ...), custom_call_target="tpu_custom_call" | custom-call | flops 1000 | bytes 1000 | tf_op jit(solution)/shard_map/pallas_call | solution.py:110
  82.9 0.4 collective-permute-start.26
  83.3 1.8 %collective-permute-start.25 = (bf16[4,448,128]{2,1,0:T(8,128)(2,1)S(1)}, bf16[4,448,128]{2,1,0:T(8,128)(2,1)S(1)}, u32[]{:S(2)}, u32[]{:S(2)}) collective-permute-start(bf16[4,448,128]{2,1,0:T(8,128)(2,1)S(1)} %get-tuple-element.172), channel_id=1, source_target_pairs={{0,4},{4,0},{8,12},{12,8},{16,20},{20,16},{24,28},{28,24},{1,5},{5... | collective-permute-start | bytes 1376264 | tf_op jit(solution)/shard_map/ppermute | solution.py:34
  85.1 0.7 shard_map.122
  85.9 7.0 %collective-permute-done.23 = bf16[2,2,256,128]{3,2,1,0:T(8,128)(2,1)S(1)} collective-permute-done((bf16[2,2,256,128]{3,2,1,0:T(8,128)(2,1)S(1)}, bf16[2,2,256,128]{3,2,1,0:T(8,128)(2,1)S(1)}, u32[]{:S(2)}, u32[]{:S(2)}) %collective-permute-start.23) | collective-permute-done | bytes 262176 | tf_op jit(solution)/shard_map/ppermute | solution.py:34
  93.0 0.6 shard_map.126
  93.6 1.3 %collective-permute-done.25.refs_1_ = bf16[4,448,128]{2,1,0:T(8,128)(2,1)S(1)} collective-permute-done((bf16[4,448,128]{2,1,0:T(8,128)(2,1)S(1)}, bf16[4,448,128]{2,1,0:T(8,128)(2,1)S(1)}, u32[]{:S(2)}, u32[]{:S(2)}) %collective-permute-start.25) | collective-permute-done | bytes 458784 | tf_op jit(solution)/shard_map/ppermute | solution.py:34
  94.9 0.1 shard_map.127
  95.2 0.6 collective-permute-start.28
  95.7 0.1 shard_map.128
  95.8 5.0 %collective-permute-done.27.refs_1_ = bf16[2,256,128]{2,1,0:T(8,128)(2,1)S(1)} collective-permute-done((bf16[2,256,128]{2,1,0:T(8,128)(2,1)S(1)}, bf16[2,256,128]{2,1,0:T(8,128)(2,1)S(1)}, u32[]{:S(2)}, u32[]{:S(2)}) %collective-permute-start.27) | collective-permute-done | bytes 131104 | tf_op jit(solution)/shard_map/ppermute | solution.py:34
  100.8 0.9 collective-permute-start.29
  101.7 1.1 collective-permute-start.22
  102.9 1.1 collective-permute-done.28.refs_1_
  104.0 2.8 %collective-permute-done.29.refs_1_ = bf16[2,320,128]{2,1,0:T(8,128)(2,1)S(1)} collective-permute-done((bf16[2,320,128]{2,1,0:T(8,128)(2,1)S(1)}, bf16[2,320,128]{2,1,0:T(8,128)(2,1)S(1)}, u32[]{:S(2)}, u32[]{:S(2)}) %collective-permute-start.29) | collective-permute-done | bytes 163872 | tf_op jit(solution)/shard_map/ppermute | solution.py:34
  106.9 3.0 %collective-permute-start.31 = (bf16[1,320,128]{2,1,0:T(8,128)(2,1)S(1)}, bf16[1,320,128]{2,1,0:T(8,128)(2,1)S(1)}, u32[]{:S(2)}, u32[]{:S(2)}) collective-permute-start(bf16[1,320,128]{2,1,0:T(8,128)(2,1)S(1)} %get-tuple-element.196), channel_id=1, source_target_pairs={{0,16},{4,20},{8,24},{12,28},{16,0},{20,4},{24,8},{28,12},{1,17},{... | collective-permute-start | bytes 245768 | tf_op jit(solution)/shard_map/ppermute | solution.py:34
  109.9 1.2 %shard_map.133 = (f32[3,128,256]{2,1,0:T(8,128)}, f32[256,128]{1,0:T(8,128)}) custom-call(bf16[16,64,128]{2,1,0:T(8,128)(2,1)S(1)} %bitcast.33, bf16[16,64,128]{2,1,0:T(8,128)(2,1)S(1)} %bitcast.34), custom_call_target="tpu_custom_call" | custom-call | flops 1000 | bytes 1000 | tf_op jit(solution)/shard_map/pallas_call | solution.py:110
  111.2 0.9 shard_map.124
  112.1 2.1 %collective-permute-done.32 = bf16[1,256,128]{2,1,0:T(8,128)(2,1)S(1)} collective-permute-done((bf16[1,256,128]{2,1,0:T(8,128)(2,1)S(1)}, bf16[1,256,128]{2,1,0:T(8,128)(2,1)S(1)}, u32[]{:S(2)}, u32[]{:S(2)}) %collective-permute-start.32) | collective-permute-done | bytes 65568 | tf_op jit(solution)/shard_map/ppermute | solution.py:34
  114.2 2.8 %collective-permute-done.31 = bf16[1,320,128]{2,1,0:T(8,128)(2,1)S(1)} collective-permute-done((bf16[1,320,128]{2,1,0:T(8,128)(2,1)S(1)}, bf16[1,320,128]{2,1,0:T(8,128)(2,1)S(1)}, u32[]{:S(2)}, u32[]{:S(2)}) %collective-permute-start.31) | collective-permute-done | bytes 81952 | tf_op jit(solution)/shard_map/ppermute | solution.py:34
  117.0 1.2 %shard_map.132 = (f32[3,128,256]{2,1,0:T(8,128)}, f32[256,128]{1,0:T(8,128)}) custom-call(bf16[7,64,128]{2,1,0:T(8,128)(2,1)S(1)} %bitcast.35, bf16[7,64,128]{2,1,0:T(8,128)(2,1)S(1)} %bitcast.36, bf16[5,64,128]{2,1,0:T(8,128)(2,1)S(1)} %bitcast.37, bf16[5,64,128]{2,1,0:T(8,128)(2,1)S(1)} %bitcast.38, bf16[4,64,128]{2,1,0:T(8,128)(2,1)S(1)} %bitcast.39, ...), custom_call_target="tpu_custom_call" | custom-call | flops 1000 | bytes 1000 | tf_op jit(solution)/shard_map/pallas_call | solution.py:110
  (46 shorter events, 0.6 us)
Async XLA Ops:
  0.6 6.7 %collective-permute-start.1 = (bf16[64,1024]{1,0:T(8,128)(2,1)}, bf16[64,1024]{1,0:T(8,128)(2,1)S(1)}, u32[]{:S(2)}, u32[]{:S(2)}) collective-permute-start(bf16[64,1024]{1,0:T(8,128)(2,1)} %bitcast.25), channel_id=1, source_target_pairs={{0,2},{1,3},{2,0},{3,1},{4,6},{5,7},{6,4},{7,5},{8,10},{9,11},{10,... | collective-permute-start | bytes 393224 | tf_op jit(solution)/shard_map/ppermute | solution.py:34
  3.7 3.7 %collective-permute-start = (bf16[64,1024]{1,0:T(8,128)(2,1)}, bf16[64,1024]{1,0:T(8,128)(2,1)S(1)}, u32[]{:S(2)}, u32[]{:S(2)}) collective-permute-start(bf16[64,1024]{1,0:T(8,128)(2,1)} %bitcast.26), channel_id=1, source_target_pairs={{0,1},{1,0},{2,3},{3,2},{4,5},{5,4},{6,7},{7,6},{8,9},{9,8},{10,11... | collective-permute-start | bytes 393224 | tf_op jit(solution)/shard_map/ppermute | solution.py:34
  5.4 21.3 %copy-start.1 = (bf16[256,1024]{1,0:T(8,128)(2,1)S(1)}, bf16[256,1024]{1,0:T(8,128)(2,1)}, u32[]{:S(2)}) copy-start(bf16[256,1024]{1,0:T(8,128)(2,1)} %refs_1_.2) | copy-start | bytes 1572868
  7.4 14.3 %all-to-all-start = ((bf16[8,8,2048]{2,1,0:T(8,128)(2,1)}), bf16[8,8,2048]{2,1,0:T(8,128)(2,1)S(1)}, u32[]{:S(2)}, u32[]{:S(2)}) async-start(bf16[8,8,2048]{2,1,0:T(8,128)(2,1)} %bitcast.2), calls=%async_computation | async-start | bytes 524288 | tf_op jit(solution)/shard_map/all_to_all | solution.py:564
  13.4 28.2 %copy-start.2 = (bf16[3,1024,256]{2,1,0:T(8,128)(2,1)S(1)}, bf16[3,1024,256]{2,1,0:T(8,128)(2,1)}, u32[]{:S(2)}) copy-start(bf16[3,1024,256]{2,1,0:T(8,128)(2,1)} %refs_11_.1) | copy-start | bytes 4718596
  13.4 28.2 %copy-start.6 = (s32[4]{0:T(128)S(1)}, s32[4]{0:T(128)}, u32[]{:S(2)}) copy-start(s32[4]{0:T(128)} %refs_0_.1) | copy-start | bytes 52
  13.4 13.2 %collective-permute-start.2 = (bf16[256,1024]{1,0:T(8,128)(2,1)}, bf16[256,1024]{1,0:T(8,128)(2,1)S(1)}, u32[]{:S(2)}, u32[]{:S(2)}) collective-permute-start(bf16[256,1024]{1,0:T(8,128)(2,1)} %refs_1_.2), channel_id=1, source_target_pairs={{0,2},{1,3},{2,0},{3,1},{4,6},{5,7},{6,4},{7,5},{8,10},{9,11},{10,... | collective-permute-start | bytes 1572872 | tf_op jit(solution)/shard_map/ppermute | solution.py:34
  15.0 1.3 %collective-permute-start.3 = (bf16[64,1024]{1,0:T(8,128)(2,1)S(1)}, bf16[64,1024]{1,0:T(8,128)(2,1)S(1)}, u32[]{:S(2)}, u32[]{:S(2)}) collective-permute-start(bf16[64,1024]{1,0:T(8,128)(2,1)S(1)} %collective-permute-done.1.refs_2_), channel_id=1, source_target_pairs={{0,1},{1,0},{2,3},{3,2},{4,5},{5,4},{6,7},{7,6},{8,9},{9,8},{10,11... | collective-permute-start | bytes 393224 | tf_op jit(solution)/shard_map/ppermute | solution.py:34
  21.6 11.8 %all-to-all-start.1 = ((bf16[8,32,256]{2,1,0:T(8,128)(2,1)}), bf16[8,32,256]{2,1,0:T(8,128)(2,1)S(1)}, u32[]{:S(2)}, u32[]{:S(2)}) async-start(bf16[8,32,256]{2,1,0:T(8,128)(2,1)} %bitcast.4), calls=%async_computation.1 | async-start | bytes 262144 | tf_op jit(solution)/shard_map/all_to_all | solution.py:573
  26.1 8.2 %collective-permute-start.7 = (bf16[64,2048]{1,0:T(8,128)(2,1)S(1)}, bf16[64,2048]{1,0:T(8,128)(2,1)}, u32[]{:S(2)}, u32[]{:S(2)}) collective-permute-start(bf16[64,2048]{1,0:T(8,128)(2,1)S(1)} %bitcast.17), channel_id=1, source_target_pairs={{0,2},{1,3},{2,0},{3,1},{4,6},{5,7},{6,4},{7,5},{8,10},{9,11},{10,... | collective-permute-start | bytes 786440 | tf_op jit(solution)/shard_map/ppermute | solution.py:34
  26.6 13.6 %collective-permute-start.10 = (bf16[256,1024]{1,0:T(8,128)(2,1)S(1)}, bf16[256,1024]{1,0:T(8,128)(2,1)S(1)}, u32[]{:S(2)}, u32[]{:S(2)}) collective-permute-start(bf16[256,1024]{1,0:T(8,128)(2,1)S(1)} %copy-done.1), channel_id=1, source_target_pairs={{0,1},{1,0},{2,3},{3,2},{4,5},{5,4},{6,7},{7,6},{8,9},{9,8},{10,11... | collective-permute-start | bytes 1572872 | tf_op jit(solution)/shard_map/ppermute | solution.py:34
  33.5 8.1 %collective-permute-start.11 = (bf16[256,1024]{1,0:T(8,128)(2,1)S(1)}, bf16[256,1024]{1,0:T(8,128)(2,1)S(1)}, u32[]{:S(2)}, u32[]{:S(2)}) collective-permute-start(bf16[256,1024]{1,0:T(8,128)(2,1)S(1)} %collective-permute-done.2.refs_9_), channel_id=1, source_target_pairs={{0,1},{1,0},{2,3},{3,2},{4,5},{5,4},{6,7},{7,6},{8,9},{9,8},{10,11... | collective-permute-start | bytes 1572872 | tf_op jit(solution)/shard_map/ppermute | solution.py:34
  33.5 2.3 %collective-permute-start.6 = (bf16[64,2048]{1,0:T(8,128)(2,1)S(1)}, bf16[64,2048]{1,0:T(8,128)(2,1)S(1)}, u32[]{:S(2)}, u32[]{:S(2)}) collective-permute-start(bf16[64,2048]{1,0:T(8,128)(2,1)S(1)} %bitcast.18), channel_id=1, source_target_pairs={{0,1},{1,0},{2,3},{3,2},{4,5},{5,4},{6,7},{7,6},{8,9},{9,8},{10,11... | collective-permute-start | bytes 786440 | tf_op jit(solution)/shard_map/ppermute | solution.py:34
  34.3 2.0 %collective-permute-start.8 = (bf16[64,2048]{1,0:T(8,128)(2,1)}, bf16[64,2048]{1,0:T(8,128)(2,1)S(1)}, u32[]{:S(2)}, u32[]{:S(2)}) collective-permute-start(bf16[64,2048]{1,0:T(8,128)(2,1)} %collective-permute-done.7.refs_2_), channel_id=1, source_target_pairs={{0,1},{1,0},{2,3},{3,2},{4,5},{5,4},{6,7},{7,6},{8,9},{9,8},{10,11... | collective-permute-start | bytes 786440 | tf_op jit(solution)/shard_map/ppermute | solution.py:34
  34.3 5.9 %collective-permute-start.5 = (bf16[256,256]{1,0:T(8,128)(2,1)S(1)}, bf16[256,256]{1,0:T(8,128)(2,1)S(1)}, u32[]{:S(2)}, u32[]{:S(2)}) collective-permute-start(bf16[256,256]{1,0:T(8,128)(2,1)S(1)} %bitcast.30), channel_id=1, source_target_pairs={{0,2},{1,3},{2,0},{3,1},{4,6},{5,7},{6,4},{7,5},{8,10},{9,11},{10,... | collective-permute-start | bytes 393224 | tf_op jit(solution)/shard_map/ppermute | solution.py:34
  35.7 4.5 %collective-permute-start.4 = (bf16[256,256]{1,0:T(8,128)(2,1)S(1)}, bf16[256,256]{1,0:T(8,128)(2,1)S(1)}, u32[]{:S(2)}, u32[]{:S(2)}) collective-permute-start(bf16[256,256]{1,0:T(8,128)(2,1)S(1)} %bitcast.31), channel_id=1, source_target_pairs={{0,1},{1,0},{2,3},{3,2},{4,5},{5,4},{6,7},{7,6},{8,9},{9,8},{10,11... | collective-permute-start | bytes 393224 | tf_op jit(solution)/shard_map/ppermute | solution.py:34
  40.2 1.3 %collective-permute-start.9 = (bf16[256,256]{1,0:T(8,128)(2,1)S(1)}, bf16[256,256]{1,0:T(8,128)(2,1)S(1)}, u32[]{:S(2)}, u32[]{:S(2)}) collective-permute-start(bf16[256,256]{1,0:T(8,128)(2,1)S(1)} %collective-permute-done.5.refs_3_), channel_id=1, source_target_pairs={{0,1},{1,0},{2,3},{3,2},{4,5},{5,4},{6,7},{7,6},{8,9},{9,8},{10,11... | collective-permute-start | bytes 393224 | tf_op jit(solution)/shard_map/ppermute | solution.py:34
  48.6 3.4 %collective-permute-start.12 = (bf16[2,64,1024]{2,1,0:T(8,128)(2,1)S(1)}, bf16[2,64,1024]{2,1,0:T(8,128)(2,1)S(1)}, u32[]{:S(2)}, u32[]{:S(2)}) collective-permute-start(bf16[2,64,1024]{2,1,0:T(8,128)(2,1)S(1)} %get-tuple-element.122), channel_id=1, source_target_pairs={{0,1},{1,0},{2,3},{3,2},{4,5},{5,4},{6,7},{7,6},{8,9},{9,8},{10,11... | collective-permute-start | bytes 786440 | tf_op jit(solution)/shard_map/ppermute | solution.py:34
  48.8 14.4 %collective-permute-start.14 = (bf16[4,2,256,128]{3,2,1,0:T(8,128)(2,1)}, bf16[4,2,256,128]{3,2,1,0:T(8,128)(2,1)S(1)}, u32[]{:S(2)}, u32[]{:S(2)}) collective-permute-start(bf16[4,2,256,128]{3,2,1,0:T(8,128)(2,1)} %get-tuple-element.134), channel_id=1, source_target_pairs={{0,4},{4,0},{8,12},{12,8},{16,20},{20,16},{24,28},{28,24},{1,5},{5... | collective-permute-start | bytes 1572872 | tf_op jit(solution)/shard_map/ppermute | solution.py:34
  50.5 14.4 %collective-permute-start.15 = (bf16[4,2,256,128]{3,2,1,0:T(8,128)(2,1)}, bf16[4,2,256,128]{3,2,1,0:T(8,128)(2,1)S(1)}, u32[]{:S(2)}, u32[]{:S(2)}) collective-permute-start(bf16[4,2,256,128]{3,2,1,0:T(8,128)(2,1)} %get-tuple-element.135), channel_id=1, source_target_pairs={{0,8},{4,12},{8,0},{12,4},{16,24},{20,28},{24,16},{28,20},{1,9},{5... | collective-permute-start | bytes 1572872 | tf_op jit(solution)/shard_map/ppermute | solution.py:34
  52.1 5.3 %collective-permute-start.13 = (bf16[64,1024]{1,0:T(8,128)(2,1)S(1)}, bf16[64,1024]{1,0:T(8,128)(2,1)S(1)}, u32[]{:S(2)}, u32[]{:S(2)}) collective-permute-start(bf16[64,1024]{1,0:T(8,128)(2,1)S(1)} %shard_map.114), channel_id=1, source_target_pairs={{0,2},{1,3},{2,0},{3,1},{4,6},{5,7},{6,4},{7,5},{8,10},{9,11},{10,... | collective-permute-start | bytes 393224 | tf_op jit(solution)/shard_map/ppermute | solution.py:34
  57.4 14.3 %copy-start.3 = (bf16[3,256,256]{2,1,0:T(8,128)(2,1)S(1)}, bf16[3,256,256]{2,1,0:T(8,128)(2,1)}, u32[]{:S(2)}) copy-start(bf16[3,256,256]{2,1,0:T(8,128)(2,1)} %get-tuple-element.143.refs_0_.refs_2_) | copy-start | bytes 1179652
  58.2 11.6 %all-to-all-start.2 = ((bf16[8,8,1024]{2,1,0:T(8,128)(2,1)}), bf16[8,8,1024]{2,1,0:T(8,128)(2,1)S(1)}, u32[]{:S(2)}, u32[]{:S(2)}) async-start(bf16[8,8,1024]{2,1,0:T(8,128)(2,1)} %bitcast.6), calls=%async_computation.2 | async-start | bytes 262144 | tf_op jit(solution)/shard_map/all_to_all | solution.py:594
  69.8 5.0 %collective-permute-start.17 = (bf16[64,1024]{1,0:T(8,128)(2,1)S(1)}, bf16[64,1024]{1,0:T(8,128)(2,1)S(1)}, u32[]{:S(2)}, u32[]{:S(2)}) collective-permute-start(bf16[64,1024]{1,0:T(8,128)(2,1)S(1)} %bitcast.21), channel_id=1, source_target_pairs={{0,2},{1,3},{2,0},{3,1},{4,6},{5,7},{6,4},{7,5},{8,10},{9,11},{10,... | collective-permute-start | bytes 393224 | tf_op jit(solution)/shard_map/ppermute | solution.py:34
  70.3 6.6 %collective-permute-start.19 = (bf16[2,2,256,128]{3,2,1,0:T(8,128)(2,1)}, bf16[2,2,256,128]{3,2,1,0:T(8,128)(2,1)S(1)}, u32[]{:S(2)}, u32[]{:S(2)}) collective-permute-start(bf16[2,2,256,128]{3,2,1,0:T(8,128)(2,1)} %get-tuple-element.150), channel_id=1, source_target_pairs={{0,8},{4,12},{8,0},{12,4},{16,24},{20,28},{24,16},{28,20},{1,9},{5... | collective-permute-start | bytes 786440 | tf_op jit(solution)/shard_map/ppermute | solution.py:34
  70.3 6.6 %collective-permute-start.20 = (bf16[2,2,256,128]{3,2,1,0:T(8,128)(2,1)}, bf16[2,2,256,128]{3,2,1,0:T(8,128)(2,1)S(1)}, u32[]{:S(2)}, u32[]{:S(2)}) collective-permute-start(bf16[2,2,256,128]{3,2,1,0:T(8,128)(2,1)} %get-tuple-element.151), channel_id=1, source_target_pairs={{0,4},{4,0},{8,12},{12,8},{16,20},{20,16},{24,28},{28,24},{1,5},{5... | collective-permute-start | bytes 786440 | tf_op jit(solution)/shard_map/ppermute | solution.py:34
  71.6 3.2 %collective-permute-start.16 = (bf16[64,1024]{1,0:T(8,128)(2,1)S(1)}, bf16[64,1024]{1,0:T(8,128)(2,1)S(1)}, u32[]{:S(2)}, u32[]{:S(2)}) collective-permute-start(bf16[64,1024]{1,0:T(8,128)(2,1)S(1)} %bitcast.22), channel_id=1, source_target_pairs={{0,1},{1,0},{2,3},{3,2},{4,5},{5,4},{6,7},{7,6},{8,9},{9,8},{10,11... | collective-permute-start | bytes 393224 | tf_op jit(solution)/shard_map/ppermute | solution.py:34
  74.8 1.3 %collective-permute-start.18 = (bf16[64,1024]{1,0:T(8,128)(2,1)S(1)}, bf16[64,1024]{1,0:T(8,128)(2,1)S(1)}, u32[]{:S(2)}, u32[]{:S(2)}) collective-permute-start(bf16[64,1024]{1,0:T(8,128)(2,1)S(1)} %collective-permute-done.17.refs_2_), channel_id=1, source_target_pairs={{0,1},{1,0},{2,3},{3,2},{4,5},{5,4},{6,7},{7,6},{8,9},{9,8},{10,11... | collective-permute-start | bytes 393224 | tf_op jit(solution)/shard_map/ppermute | solution.py:34
  76.9 8.9 %collective-permute-start.24 = (bf16[4,256,128]{2,1,0:T(8,128)(2,1)S(1)}, bf16[4,256,128]{2,1,0:T(8,128)(2,1)S(1)}, u32[]{:S(2)}, u32[]{:S(2)}) collective-permute-start(bf16[4,256,128]{2,1,0:T(8,128)(2,1)S(1)} %get-tuple-element.167), channel_id=1, source_target_pairs={{0,4},{4,0},{8,12},{12,8},{16,20},{20,16},{24,28},{28,24},{1,5},{5... | collective-permute-start | bytes 786440 | tf_op jit(solution)/shard_map/ppermute | solution.py:34
  79.4 5.7 %copy-start = (bf16[3,1024,256]{2,1,0:T(8,128)(2,1)S(1)}, bf16[3,1024,256]{2,1,0:T(8,128)(2,1)}, u32[]{:S(2)}) copy-start(bf16[3,1024,256]{2,1,0:T(8,128)(2,1)} %refs_1_.3) | copy-start | bytes 4718596
  79.4 13.6 %collective-permute-start.23 = (bf16[2,2,256,128]{3,2,1,0:T(8,128)(2,1)S(1)}, bf16[2,2,256,128]{3,2,1,0:T(8,128)(2,1)S(1)}, u32[]{:S(2)}, u32[]{:S(2)}) collective-permute-start(bf16[2,2,256,128]{3,2,1,0:T(8,128)(2,1)S(1)} %get-tuple-element.165), channel_id=1, source_target_pairs={{0,16},{4,20},{8,24},{12,28},{16,0},{20,4},{24,8},{28,12},{1,17},{... | collective-permute-start | bytes 786440 | tf_op jit(solution)/shard_map/ppermute | solution.py:34
  82.9 10.1 %copy-start.5 = (bf16[256,1024]{1,0:T(8,128)(2,1)S(1)}, bf16[256,1024]{1,0:T(8,128)(2,1)}, u32[]{:S(2)}) copy-start(bf16[256,1024]{1,0:T(8,128)(2,1)} %get-tuple-element.161.refs_4_.refs_1_) | copy-start | bytes 1572868
  82.9 12.3 %collective-permute-start.26 = (bf16[4,320,128]{2,1,0:T(8,128)(2,1)S(1)}, bf16[4,320,128]{2,1,0:T(8,128)(2,1)S(1)}, u32[]{:S(2)}, u32[]{:S(2)}) collective-permute-start(bf16[4,320,128]{2,1,0:T(8,128)(2,1)S(1)} %get-tuple-element.175), channel_id=1, source_target_pairs={{0,8},{4,12},{8,0},{12,4},{16,24},{20,28},{24,16},{28,20},{1,9},{5... | collective-permute-start | bytes 983048 | tf_op jit(solution)/shard_map/ppermute | solution.py:34
  83.3 11.6 %collective-permute-start.25 = (bf16[4,448,128]{2,1,0:T(8,128)(2,1)S(1)}, bf16[4,448,128]{2,1,0:T(8,128)(2,1)S(1)}, u32[]{:S(2)}, u32[]{:S(2)}) collective-permute-start(bf16[4,448,128]{2,1,0:T(8,128)(2,1)S(1)} %get-tuple-element.172), channel_id=1, source_target_pairs={{0,4},{4,0},{8,12},{12,8},{16,20},{20,16},{24,28},{28,24},{1,5},{5... | collective-permute-start | bytes 1376264 | tf_op jit(solution)/shard_map/ppermute | solution.py:34
  85.8 15.9 %collective-permute-start.21 = (bf16[2,64,1024]{2,1,0:T(8,128)(2,1)S(1)}, bf16[2,64,1024]{2,1,0:T(8,128)(2,1)S(1)}, u32[]{:S(2)}, u32[]{:S(2)}) collective-permute-start(bf16[2,64,1024]{2,1,0:T(8,128)(2,1)S(1)} %get-tuple-element.164), channel_id=1, source_target_pairs={{0,1},{1,0},{2,3},{3,2},{4,5},{5,4},{6,7},{7,6},{8,9},{9,8},{10,11... | collective-permute-start | bytes 786440 | tf_op jit(solution)/shard_map/ppermute | solution.py:34
  93.0 7.8 %collective-permute-start.27 = (bf16[2,256,128]{2,1,0:T(8,128)(2,1)S(1)}, bf16[2,256,128]{2,1,0:T(8,128)(2,1)S(1)}, u32[]{:S(2)}, u32[]{:S(2)}) collective-permute-start(bf16[2,256,128]{2,1,0:T(8,128)(2,1)S(1)} %get-tuple-element.182), channel_id=1, source_target_pairs={{0,16},{4,20},{8,24},{12,28},{16,0},{20,4},{24,8},{28,12},{1,17},{... | collective-permute-start | bytes 393224 | tf_op jit(solution)/shard_map/ppermute | solution.py:34
  95.1 16.1 %copy-start.4 = (bf16[1,64,1024]{2,1,0:T(8,128)(2,1)S(1)}, bf16[1,64,1024]{2,1,0:T(8,128)(2,1)}, u32[]{:S(2)}) copy-start(bf16[1,64,1024]{2,1,0:T(8,128)(2,1)} %param.7) | copy-start | bytes 393220
  95.2 8.8 %collective-permute-start.28 = (bf16[2,448,128]{2,1,0:T(8,128)(2,1)S(1)}, bf16[2,448,128]{2,1,0:T(8,128)(2,1)S(1)}, u32[]{:S(2)}, u32[]{:S(2)}) collective-permute-start(bf16[2,448,128]{2,1,0:T(8,128)(2,1)S(1)} %get-tuple-element.186), channel_id=1, source_target_pairs={{0,8},{4,12},{8,0},{12,4},{16,24},{20,28},{24,16},{28,20},{1,9},{5... | collective-permute-start | bytes 688136 | tf_op jit(solution)/shard_map/ppermute | solution.py:34
  100.8 6.1 %collective-permute-start.29 = (bf16[2,320,128]{2,1,0:T(8,128)(2,1)S(1)}, bf16[2,320,128]{2,1,0:T(8,128)(2,1)S(1)}, u32[]{:S(2)}, u32[]{:S(2)}) collective-permute-start(bf16[2,320,128]{2,1,0:T(8,128)(2,1)S(1)} %get-tuple-element.190), channel_id=1, source_target_pairs={{0,4},{4,0},{8,12},{12,8},{16,20},{20,16},{24,28},{28,24},{1,5},{5... | collective-permute-start | bytes 491528 | tf_op jit(solution)/shard_map/ppermute | solution.py:34
  101.7 9.4 %collective-permute-start.22 = (bf16[64,1024]{1,0:T(8,128)(2,1)S(1)}, bf16[64,1024]{1,0:T(8,128)(2,1)S(1)}, u32[]{:S(2)}, u32[]{:S(2)}) collective-permute-start(bf16[64,1024]{1,0:T(8,128)(2,1)S(1)} %shard_map.123), channel_id=1, source_target_pairs={{0,2},{1,3},{2,0},{3,1},{4,6},{5,7},{6,4},{7,5},{8,10},{9,11},{10,... | collective-permute-start | bytes 393224 | tf_op jit(solution)/shard_map/ppermute | solution.py:34
  106.9 10.1 %collective-permute-start.30 = (bf16[1,448,128]{2,1,0:T(8,128)(2,1)S(1)}, bf16[1,448,128]{2,1,0:T(8,128)(2,1)S(1)}, u32[]{:S(2)}, u32[]{:S(2)}) collective-permute-start(bf16[1,448,128]{2,1,0:T(8,128)(2,1)S(1)} %get-tuple-element.192), channel_id=1, source_target_pairs={{0,16},{4,20},{8,24},{12,28},{16,0},{20,4},{24,8},{28,12},{1,17},{... | collective-permute-start | bytes 344072 | tf_op jit(solution)/shard_map/ppermute | solution.py:34
  106.9 10.0 %collective-permute-start.31 = (bf16[1,320,128]{2,1,0:T(8,128)(2,1)S(1)}, bf16[1,320,128]{2,1,0:T(8,128)(2,1)S(1)}, u32[]{:S(2)}, u32[]{:S(2)}) collective-permute-start(bf16[1,320,128]{2,1,0:T(8,128)(2,1)S(1)} %get-tuple-element.196), channel_id=1, source_target_pairs={{0,16},{4,20},{8,24},{12,28},{16,0},{20,4},{24,8},{28,12},{1,17},{... | collective-permute-start | bytes 245768 | tf_op jit(solution)/shard_map/ppermute | solution.py:34
  109.9 4.3 %collective-permute-start.32 = (bf16[1,256,128]{2,1,0:T(8,128)(2,1)S(1)}, bf16[1,256,128]{2,1,0:T(8,128)(2,1)S(1)}, u32[]{:S(2)}, u32[]{:S(2)}) collective-permute-start(bf16[1,256,128]{2,1,0:T(8,128)(2,1)S(1)} %get-tuple-element.198), channel_id=1, source_target_pairs={{0,8},{4,12},{8,0},{12,4},{16,24},{20,28},{24,16},{28,20},{1,9},{5... | collective-permute-start | bytes 196616 | tf_op jit(solution)/shard_map/ppermute | solution.py:34

commit v2 on v1

--- a/solution.py
+++ b/solution.py
@@ -222,21 +222,28 @@
     )
 
 
-def owner_rows(xg, w_to):
+def owner_rows(xg, w_to, attn, w_so, frames, per):
     own_rows, mp = xg[0].shape[0], len(xg)
     rows, (width, dim) = mp * own_rows, w_to.shape
 
     def body(t):
+        x_buf = t.scratch[0]
         for r in range(mp):
             at = own_block(r, own_rows)
-            t.outs[0][at, :] = t.get(r)[:, :dim]
+            x_buf[at, :] = t.get(r)[:, :dim]
             t.outs[1][at, :] = t.get(r)[:, dim:]
+        total = x_buf[...].astype(F32)
+        order = row_order(rows, mp, frames, per)
+        for i in range(len(attn)):
+            part = mm(order, t.get(mp + 1 + i)[...], 1, 0).astype(BF)
+            total += mm(part, t.get(mp + 1 + len(attn) + i)[...], 1, 0)
+        t.outs[0][...] = total
         t.outs[2][...] = mm(t.outs[1][...], t.get(mp)[...], 1, 1).astype(BF)
 
-    whole = shape((rows, dim))
-    return run(
-        body, (*xg, w_to), "v" * mp + "h", (whole, whole, shape((rows, width))), "vvv"
-    )
+    outs = (shape((rows, dim), F32), shape((rows, dim)), shape((rows, width)))
+    ins = (*xg, w_to, *attn, *w_so)
+    where = "v" * mp + "h" + "v" * len(attn) + "h" + "v" * (len(w_so) - 1)
+    return run(body, ins, where, outs, "vvv", scratch=(pltpu.VMEM((rows, dim), BF),))
 
 
 SENT = ((1, 3, 5, 7), (2, 3, 6, 7))
@@ -257,17 +264,18 @@
         for i, r in enumerate(relative):
             for j in range(2):
                 at = 2 * pair + j
-                t.outs[first + pair][i, j] = chunk_of(flat[at], right[at], r, groups)
+                side = slice(j * flat[at].shape[0], (j + 1) * flat[at].shape[0])
+                t.outs[first + pair][i, side] = chunk_of(flat[at], right[at], r, groups)
 
 
 def half_shape(width, dim, groups):
-    return shape((groups // 2, 2, width, dim // groups))
-
-
-def temporal_stage(attn, x_all, g_all, up, w_so, w_qkv, clips, heads, frames, per):
-    mp, (rows, width) = len(attn), attn[0].shape
+    return shape((groups // 2, 2 * width, dim // groups))
+
+
+def temporal_stage(attn, so_far, g_all, up, w_so, w_qkv, clips, heads, frames, per, mp):
+    n, (rows, width) = len(attn), attn[0].shape
     own_rows = rows // mp
-    dim = x_all.shape[1]
+    dim = so_far.shape[1]
     halves = frames == 8
 
     def rows_of(r):
@@ -276,11 +284,11 @@
     def body(t):
         (clip_ref,) = t.smem
         back, inv_buf = t.scratch
-        total = t.get(mp)[...].astype(F32)
+        total = t.get(n)[...]
         order = row_order(rows, mp, frames, per)
-        for r in range(mp):
+        for r in range(n):
             part = mm(order, t.get(r)[...], 1, 0).astype(BF)
-            total += mm(part, t.get(mp + 2 + r)[...], 1, 0)
+            total += mm(part, t.get(n + 2 + r)[...], 1, 0)
         inv = inv_rms(total)
         nh = (total * inv).astype(BF)
         t.outs[2][...] = nh
@@ -302,10 +310,10 @@
             return clip * rows + patch
 
         allowed = key_of(0) == key_of(1)
-        w = t.get(2 * mp + 2)
+        w = t.get(2 * n + 2)
         q, k, v = [mm(nh, w[j], 1, 0).astype(BF) for j in range(3)]
         grads = attend_back(
-            q, k, v, t.get(mp + 1)[...], heads, lambda h: probs_of(q, k, h, allowed), True
+            q, k, v, t.get(n + 1)[...], heads, lambda h: probs_of(q, k, h, allowed), True
         )
         for j in range(4):
             t.outs[5][j] = grads[j]
@@ -316,7 +324,7 @@
         for r in range(mp):
             t.outs[1 - r % 2][r // 2] = back[rows_of(r), :]
         if halves:
-            chunk_grads(t, 6, SENT, grads, t.outs[2], t.get(2 * mp + 3), frames)
+            chunk_grads(t, 6, SENT, grads, t.outs[2], t.get(2 * n + 3), frames)
 
     half = shape((mp // 2, own_rows, dim))
     outs = (
@@ -329,7 +337,7 @@
     )
     if halves:
         outs += (half_shape(width, dim, frames),) * 2
-    ins = (*attn, x_all, up, *w_so, w_qkv, g_all)
+    ins = (*attn, so_far, up, *w_so, w_qkv, g_all)
     return run(
         body, ins, "v" * len(ins), outs, "v" * len(outs), smem=(clips,),
         scratch=(pltpu.VMEM((rows, dim), BF), pltpu.VMEM((rows, 128), F32)),
@@ -494,44 +502,48 @@
 
 def halve(keeps, cames, keep_in="v", out="v", merged=False):
     n, depth = len(keeps), keeps[0].shape[0]
+    rows = [keep.shape[1] for keep in keeps]
+    chunk = keeps[0].shape[2]
 
     def body(t):
         for i in range(depth - 1, -1, -1):
             for at in range(n):
                 total = t.get(at)[i].astype(F32) + t.get(n + at)[i].astype(F32)
-                kept = 1 - i % 2
+                kept, first = 1 - i % 2, sum(rows[:at])
                 if merged:
-                    t.outs[kept][at] = total.astype(BF)
+                    t.outs[kept][first : first + rows[at]] = total.astype(BF)
                 else:
                     t.outs[n * kept + at][i // 2] = total.astype(BF)
 
     if merged:
-        outs = (shape((n, *keeps[0].shape[1:])),) * 2
+        outs = (shape((sum(rows), chunk)),) * 2
     else:
-        outs = tuple(shape((depth // 2, *keep.shape[1:])) for keep in keeps) * 2
+        outs = tuple(shape((depth // 2, r, chunk)) for r in rows) * 2
     where = keep_in * n + "v" * n
     return run(body, (*keeps, *cames), where, outs, out * len(outs))
 
 
 def last_sums(pairs):
-    chunk, size = pairs[0][0].shape[-1], HD
-    blocks = [tuple(part.reshape(-1, size, chunk) for part in pair) for pair in pairs]
-    width = sum(pair[0].shape[0] for pair in blocks) * size // 4
-    per = width // size
-
-    def body(t):
-        b = 0
-        for at, (keep, _) in enumerate(blocks):
-            for i in range(keep.shape[0]):
-                total = t.get(2 * at)[i].astype(F32) + t.get(2 * at + 1)[i].astype(F32)
-                side = slice((b % per) * size, (b % per + 1) * size)
-                if b < 3 * per:
-                    t.outs[0][b // per, :, side] = total.T
+    chunk = pairs[0][0].shape[-1]
+    pairs = [tuple(part.reshape(-1, chunk) for part in pair) for pair in pairs]
+    width = sum(pair[0].shape[0] for pair in pairs) // 4
+
+    def body(t):
+        row = 0
+        for at, (keep, _) in enumerate(pairs):
+            start = 0
+            while start < keep.shape[0]:
+                size = min(width - row % width, keep.shape[0] - start)
+                here = slice(start, start + size)
+                total = t.get(2 * at)[here].astype(F32) + t.get(2 * at + 1)[here].astype(F32)
+                side = slice(row % width, row % width + size)
+                if row < 3 * width:
+                    t.outs[0][row // width, :, side] = total.T
                 else:
                     t.outs[1][side, :] = total
-                b += 1
-
-    ins = [part for pair in blocks for part in pair]
+                start, row = start + size, row + size
+
+    ins = [part for pair in pairs for part in pair]
     outs = (shape((3, chunk, width), F32), shape((width, chunk), F32))
     return run(body, ins, "v" * len(ins), outs, "hh")
 
@@ -574,15 +586,18 @@
         attn_send.reshape(groups, mp * per, width), "frames", 0, 0, tiled=True
     ).reshape(patches, width)
     so_two, moved = lax.optimization_barrier((so_two, moved))
-    moved_two = swap(moved, "mp", 2)
-    w_so = spatial_out, swap(spatial_out, "mp", 1), so_two, swap(so_two, "mp", 1)
+    moved_one, moved_two = swap(moved, "mp", 1), swap(moved, "mp", 2)
+    so_one = swap(spatial_out, "mp", 1)
     xg_all = xg, swap(xg, "mp", 1), xg_two, swap(xg_two, "mp", 1)
-    moved_two, rows_own = lax.optimization_barrier((moved_two, owner_rows(xg_all, temporal_out)))
-    x_rows, g_rows, d_attn_t = rows_own
-    attn_owned = moved, swap(moved, "mp", 1), moved_two, swap(moved_two, "mp", 1)
+    rows_own = owner_rows(
+        xg_all, temporal_out, (moved, moved_one), (spatial_out, so_one), groups, per
+    )
+    moved_two, rows_own = lax.optimization_barrier((moved_two, rows_own))
+    so_far, g_rows, d_attn_t = rows_own
 
     send_h, keep_h, normed_h, unit_own, inv_own, t_grads, *t_sent = temporal_stage(
-        attn_owned, x_rows, g_rows, d_attn_t, w_so, temporal_qkv, clip_frames, heads, groups, per
+        (moved_two, swap(moved_two, "mp", 1)), so_far, g_rows, d_attn_t,
+        (so_two, swap(so_two, "mp", 1)), temporal_qkv, clip_frames, heads, groups, per, mp,
     )
     parts = head_sums(send_h, keep_h)
     if halves:
@@ -616,27 +631,18 @@
     )
     if halves:
         after = lax.optimization_barrier
-        o_send, o_keep = halve([o_chunks[1]], [swap(o_chunks[0], "frames", 1)])
         send_x, keep_x = normed_back(s_grads, spatial_qkv, mp)
-        s_grads, t_came, o_send, o_keep = after((s_grads, t_came, o_send, o_keep))
+        s_grads, t_came = after((s_grads, t_came))
         t_qkv, t_out = last_sums([(t_keep, t_came)])
         s_kept = qkv_keeps(s_grads, normed_x, groups, 50_000_000_000)
-        a_came, b_came = swap(s_sent[0], "frames", 1), swap(s_sent[1], "frames", 2)
-        o_came = swap(o_send, "frames", 4)
-        a_sums = halve([s_kept[0]], [a_came])
-        a_sums, b_came = after((a_sums, b_came))
-        b_sums = halve([s_kept[1]], [b_came])
-        b_sums, o_came = after((b_sums, o_came))
-        o_sums = halve([o_keep], [o_came])
-        a_came, b_came = swap(a_sums[0], "frames", 2), swap(b_sums[0], "frames", 1)
-        o_sums, a_came = after((o_sums, a_came))
-        a_sums = halve([a_sums[1]], [a_came])
-        a_sums, b_came = after((a_sums, b_came))
-        b_sums = halve([b_sums[1]], [b_came])
+        came = [swap(s_sent[0], "frames", 1), swap(s_sent[1], "frames", 2)]
+        came.append(swap(o_chunks[0], "frames", 1))
+        *sends, keep_a, keep_b, o_keep = halve([*s_kept, o_chunks[1]], came)
+        came = [swap(send, "frames", by) for send, by in zip(sends, (2, 1, 4))]
+        s_send, s_keep = halve([keep_a, keep_b], came[:2], merged=True)
+        o_send, o_keep = halve([o_keep], came[2:])
         s_qkv, s_out = last_sums([
-            (a_sums[1], swap(a_sums[0], "frames", 4)),
-            (b_sums[1], swap(b_sums[0], "frames", 4)),
-            (o_sums[1], swap(o_sums[0], "frames", 2)),
+            (s_keep, swap(s_send, "frames", 4)), (o_keep, swap(o_send, "frames", 2))
         ])
     else:
         send_x, keep_x = normed_back(s_grads, spatial_qkv, mp)

time: 119 us -> 119 us (level)
  starting transfers between devices: 37 us -> 41 us
  waiting for transfers between devices: 51.6 us -> 49 us
    ppermute x33 -> x32, starting transfers between devices: 22.3 us -> 25.9 us  [swap(): return lax.ppermute(value, axis, [(i, i ^ by) for i in range(size)])]
    ppermute x33 -> x32, waiting for transfers between devices: 39.6 us -> 37 us  [swap(): return lax.ppermute(value, axis, [(i, i ^ by) for i in range(size)])]
    pallas_call x24 -> x21, Pallas kernels: 28.6 us -> 27.5 us  [run(): pl.pallas_call(wrapped, out_shape=tuple((pltpu.HBM(o.shape, o.dtype) if w...]
  transfers between devices with their start and end apart: 36 -> 35, of which waited for: 24 -> 22; matrix products, arithmetic and copies ran while one was open for 0% -> 0% of each run, Pallas kernels for 17% -> 16%
where the time goes in v2:
time: 119 us; the launch traced here: 118 us
  waiting for transfers between devices  49 us (41%)
  starting transfers between devices  41 us (34%)
  Pallas kernels  27.5 us (23%)
    ppermute x32, waiting for transfers between devices, swap(): return lax.ppermute(value, axis, [(i, i ^ by) for i in range(size)])  37 us
    pallas_call x21, Pallas kernels, run(): pl.pallas_call(wrapped, out_shape=tuple((pltpu.HBM(o.shape, o.dtype) if w...  27.5 us
    ppermute x32, starting transfers between devices, swap(): return lax.ppermute(value, axis, [(i, i ^ by) for i in range(size)])  25.9 us
    all_to_all x1, waiting for transfers between devices, shards(): lax.all_to_all(attn_send.reshape(groups, mp * per, width), 'frames', 0, 0...  6.83 us
    all_to_all x1, starting transfers between devices, shards(): lax.all_to_all(xg.reshape(groups, per, 2 * dim), 'frames', 0, 0, tiled=True)  6.03 us
    all_to_all x1, starting transfers between devices, shards(): lax.all_to_all(attn_send.reshape(groups, mp * per, width), 'frames', 0, 0...  4.78 us
    all_to_all x1, starting transfers between devices, shards(): lax.all_to_all(d_hidden.reshape(groups, per, dim), 'frames', 0, 0, tiled=...  4.24 us
    all_to_all x1, waiting for transfers between devices, shards(): lax.all_to_all(d_hidden.reshape(groups, per, dim), 'frames', 0, 0, tiled=...  3.76 us
  transfers between devices with their start and end apart: 35, of which 22 were waited for; matrix products, arithmetic and copies ran while one was open for 0% of the time, Pallas kernels for 16%

profile of v2, /device:TPU:0, one launch (start us, length us, event | category | flops | bytes accessed | tf_op | source)
XLA Modules:
  0.0 118.5 jit_solution(17511957798104611415)
XLA Ops:
  0.6 3.0 %collective-permute-start.1 = (bf16[64,1024]{1,0:T(8,128)(2,1)}, bf16[64,1024]{1,0:T(8,128)(2,1)S(1)}, u32[]{:S(2)}, u32[]{:S(2)}) collective-permute-start(bf16[64,1024]{1,0:T(8,128)(2,1)} %bitcast.19), channel_id=1, source_target_pairs={{0,2},{1,3},{2,0},{3,1},{4,6},{5,7},{6,4},{7,5},{8,10},{9,11},{10,... | collective-permute-start | bytes 393224 | tf_op jit(solution)/shard_map/ppermute | solution.py:34
  3.7 1.7 %shard_map.110 = bf16[64,2048]{1,0:T(8,128)(2,1)} custom-call(bf16[64,1024]{1,0:T(8,128)(2,1)} %bitcast.21, bf16[64,1024]{1,0:T(8,128)(2,1)} %bitcast.29), custom_call_target="tpu_custom_call" | custom-call | flops 1000 | bytes 1000 | tf_op jit(solution)/shard_map/pallas_call | solution.py:110
  5.4 2.0 %collective-permute-done.1.refs_2_ = bf16[64,1024]{1,0:T(8,128)(2,1)S(1)} collective-permute-done((bf16[64,1024]{1,0:T(8,128)(2,1)}, bf16[64,1024]{1,0:T(8,128)(2,1)S(1)}, u32[]{:S(2)}, u32[]{:S(2)}) %collective-permute-start.1) | collective-permute-done | bytes 131104 | tf_op jit(solution)/shard_map/ppermute | solution.py:34
  7.4 6.0 %all-to-all-start = ((bf16[8,8,2048]{2,1,0:T(8,128)(2,1)}), bf16[8,8,2048]{2,1,0:T(8,128)(2,1)S(1)}, u32[]{:S(2)}, u32[]{:S(2)}) async-start(bf16[8,8,2048]{2,1,0:T(8,128)(2,1)} %bitcast.2), calls=%async_computation | async-start | bytes 524288 | tf_op jit(solution)/shard_map/all_to_all | solution.py:576
  13.4 1.5 %collective-permute-start.2 = (bf16[256,1024]{1,0:T(8,128)(2,1)}, bf16[256,1024]{1,0:T(8,128)(2,1)S(1)}, u32[]{:S(2)}, u32[]{:S(2)}) collective-permute-start(bf16[256,1024]{1,0:T(8,128)(2,1)} %refs_1_.2), channel_id=1, source_target_pairs={{0,2},{1,3},{2,0},{3,1},{4,6},{5,7},{6,4},{7,5},{8,10},{9,11},{10,... | collective-permute-start | bytes 1572872 | tf_op jit(solution)/shard_map/ppermute | solution.py:34
  14.9 0.5 collective-permute-start.9
  15.4 1.0 collective-permute-done.3.refs_3_
  16.4 3.8 %shard_map.111 = (bf16[256,1024]{1,0:T(8,128)(2,1)}, bf16[3,256,256]{2,1,0:T(8,128)(2,1)}, bf16[256,256]{1,0:T(8,128)(2,1)}) custom-call(bf16[64,1024]{1,0:T(8,128)(2,1)} %bitcast.22, bf16[64,1024]{1,0:T(8,128)(2,1)S(1)} %collective-permute-done.refs_1_, bf16[64,1024]{1,0:T(8,128)(2,1)S(1)} %collective-permute-done.1.refs_2_, ...), custom_call_target="tpu_custom_call" | custom-call | flops 1000 | bytes 1000 | tf_op jit(solution)/shard_map/pallas_call | solution.py:110
  20.2 1.4 %all-to-all-done = bf16[8,8,2048]{2,1,0:T(8,128)(2,1)S(1)} async-done(((bf16[8,8,2048]{2,1,0:T(8,128)(2,1)}), bf16[8,8,2048]{2,1,0:T(8,128)(2,1)S(1)}, u32[]{:S(2)}, u32[]{:S(2)}) %all-to-all-start) | async-done | bytes 262176 | tf_op jit(solution)/shard_map/all_to_all | solution.py:576
  21.6 4.8 %all-to-all-start.1 = ((bf16[8,32,256]{2,1,0:T(8,128)(2,1)}), bf16[8,32,256]{2,1,0:T(8,128)(2,1)S(1)}, u32[]{:S(2)}, u32[]{:S(2)}) async-start(bf16[8,32,256]{2,1,0:T(8,128)(2,1)} %bitcast.4), calls=%async_computation.1 | async-start | bytes 262144 | tf_op jit(solution)/shard_map/all_to_all | solution.py:585
  26.4 0.5 collective-permute-start.6
  26.9 6.8 %all-to-all-done.1 = bf16[8,32,256]{2,1,0:T(8,128)(2,1)S(1)} async-done(((bf16[8,32,256]{2,1,0:T(8,128)(2,1)}), bf16[8,32,256]{2,1,0:T(8,128)(2,1)S(1)}, u32[]{:S(2)}, u32[]{:S(2)}) %all-to-all-start.1) | async-done | bytes 131104 | tf_op jit(solution)/shard_map/all_to_all | solution.py:585
  33.8 0.5 collective-permute-start.5
  34.3 0.2 collective-permute-done.6.refs_2_
  34.5 0.5 collective-permute-start.8
  35.0 0.5 collective-permute-start.4
  35.5 0.5 collective-permute-done.5.refs_1_
  36.0 0.6 collective-permute-done.8.refs_6_
  36.6 2.4 %shard_map.112 = (f32[256,1024]{1,0:T(8,128)S(1)}, bf16[256,1024]{1,0:T(8,128)(2,1)S(1)}, bf16[256,256]{1,0:T(8,128)(2,1)S(1)}) custom-call(bf16[64,2048]{1,0:T(8,128)(2,1)S(1)} %bitcast.13, bf16[64,2048]{1,0:T(8,128)(2,1)S(1)} %collective-permute-done.5.refs_1_, bf16[64,2048]{1,0:T(8,128)(2,1)S(1)} %collective-permute-done.6.refs_2_, ...), custom_call_target="tpu_custom_call" | custom-call | flops 1000 | bytes 1000 | tf_op jit(solution)/shard_map/pallas_call | solution.py:110
  39.0 1.4 %collective-permute-done.4.refs_1_ = bf16[256,256]{1,0:T(8,128)(2,1)S(1)} collective-permute-done((bf16[256,256]{1,0:T(8,128)(2,1)S(1)}, bf16[256,256]{1,0:T(8,128)(2,1)S(1)}, u32[]{:S(2)}, u32[]{:S(2)}) %collective-permute-start.4) | collective-permute-done | bytes 131104 | tf_op jit(solution)/shard_map/ppermute | solution.py:34
  40.4 1.3 %collective-permute-done.10.refs_2_ = bf16[256,256]{1,0:T(8,128)(2,1)S(1)} collective-permute-done((bf16[256,256]{1,0:T(8,128)(2,1)S(1)}, bf16[256,256]{1,0:T(8,128)(2,1)S(1)}, u32[]{:S(2)}, u32[]{:S(2)}) %collective-permute-start.10) | collective-permute-done | bytes 131104 | tf_op jit(solution)/shard_map/ppermute | solution.py:34
  41.8 6.4 %shard_map.113 = (bf16[2,64,1024]{2,1,0:T(8,128)(2,1)S(1)}, bf16[2,64,1024]{2,1,0:T(8,128)(2,1)S(1)}, bf16[256,1024]{1,0:T(8,128)(2,1)S(1)}, bf16[64,1024]{1,0:T...) custom-call(s32[4]{0:T(128)S(1)} %copy-done.6, ...), custom_call_target="tpu_custom_call" | custom-call | flops 1000 | bytes 1000 | tf_op jit(solution)/shard_map/pallas_call | solution.py:110
  48.2 0.2 collective-permute-start.12
  48.4 1.8 %collective-permute-start.14 = (bf16[4,512,128]{2,1,0:T(8,128)(2,1)}, bf16[4,512,128]{2,1,0:T(8,128)(2,1)S(1)}, u32[]{:S(2)}, u32[]{:S(2)}) collective-permute-start(bf16[4,512,128]{2,1,0:T(8,128)(2,1)} %get-tuple-element.118), channel_id=1, source_target_pairs={{0,4},{4,0},{8,12},{12,8},{16,20},{20,16},{24,28},{28,24},{1,5},{5... | collective-permute-start | bytes 1572872 | tf_op jit(solution)/shard_map/ppermute | solution.py:34
  50.1 1.5 %collective-permute-start.15 = (bf16[4,512,128]{2,1,0:T(8,128)(2,1)}, bf16[4,512,128]{2,1,0:T(8,128)(2,1)S(1)}, u32[]{:S(2)}, u32[]{:S(2)}) collective-permute-start(bf16[4,512,128]{2,1,0:T(8,128)(2,1)} %get-tuple-element.119), channel_id=1, source_target_pairs={{0,8},{4,12},{8,0},{12,4},{16,24},{20,28},{24,16},{28,20},{1,9},{5... | collective-permute-start | bytes 1572872 | tf_op jit(solution)/shard_map/ppermute | solution.py:34
  51.7 0.6 collective-permute-start.13
  52.3 0.8 shard_map.115
  53.1 3.9 %collective-permute-done.13.refs_2_ = bf16[64,1024]{1,0:T(8,128)(2,1)S(1)} collective-permute-done((bf16[64,1024]{1,0:T(8,128)(2,1)S(1)}, bf16[64,1024]{1,0:T(8,128)(2,1)S(1)}, u32[]{:S(2)}, u32[]{:S(2)}) %collective-permute-start.13) | collective-permute-done | bytes 131104 | tf_op jit(solution)/shard_map/ppermute | solution.py:34
  57.0 0.9 shard_map.116
  57.8 4.2 %all-to-all-start.2 = ((bf16[8,8,1024]{2,1,0:T(8,128)(2,1)}), bf16[8,8,1024]{2,1,0:T(8,128)(2,1)S(1)}, u32[]{:S(2)}, u32[]{:S(2)}) async-start(bf16[8,8,1024]{2,1,0:T(8,128)(2,1)} %bitcast.6), calls=%async_computation.2 | async-start | bytes 262144 | tf_op jit(solution)/shard_map/all_to_all | solution.py:609
  62.1 0.7 collective-permute-done.14.refs_2_
  62.8 1.7 %collective-permute-done.15.refs_3_ = bf16[4,512,128]{2,1,0:T(8,128)(2,1)S(1)} collective-permute-done((bf16[4,512,128]{2,1,0:T(8,128)(2,1)}, bf16[4,512,128]{2,1,0:T(8,128)(2,1)S(1)}, u32[]{:S(2)}, u32[]{:S(2)}) %collective-permute-start.15) | collective-permute-done | bytes 524320 | tf_op jit(solution)/shard_map/ppermute | solution.py:34
  64.5 1.1 shard_map.117
  65.7 3.8 %all-to-all-done.2 = bf16[8,8,1024]{2,1,0:T(8,128)(2,1)S(1)} async-done(((bf16[8,8,1024]{2,1,0:T(8,128)(2,1)}), bf16[8,8,1024]{2,1,0:T(8,128)(2,1)S(1)}, u32[]{:S(2)}, u32[]{:S(2)}) %all-to-all-start.2) | async-done | bytes 131104 | tf_op jit(solution)/shard_map/all_to_all | solution.py:609
  69.4 0.5 collective-permute-start.17
  69.9 1.3 %collective-permute-start.20 = (bf16[2,512,128]{2,1,0:T(8,128)(2,1)}, bf16[2,512,128]{2,1,0:T(8,128)(2,1)S(1)}, u32[]{:S(2)}, u32[]{:S(2)}) collective-permute-start(bf16[2,512,128]{2,1,0:T(8,128)(2,1)} %get-tuple-element.135), channel_id=1, source_target_pairs={{0,4},{4,0},{8,12},{12,8},{16,20},{20,16},{24,28},{28,24},{1,5},{5... | collective-permute-start | bytes 786440 | tf_op jit(solution)/shard_map/ppermute | solution.py:34
  71.2 1.5 %shard_map.118 = (f32[4,256,256]{2,1,0:T(8,128)S(1)}, bf16[256,256]{1,0:T(8,128)(2,1)S(1)}) custom-call(bf16[3,256,256]{2,1,0:T(8,128)(2,1)S(1)} %copy-done.3, bf16[256,256]{1,0:T(8,128)(2,1)} %get-tuple-element.128.refs_1_), custom_call_target="tpu_custom_call" | custom-call | flops 1000 | bytes 1000 | tf_op jit(solution)/shard_map/pallas_call | solution.py:110
  72.8 1.6 %collective-permute-done.17.refs_2_ = bf16[64,1024]{1,0:T(8,128)(2,1)S(1)} collective-permute-done((bf16[64,1024]{1,0:T(8,128)(2,1)S(1)}, bf16[64,1024]{1,0:T(8,128)(2,1)S(1)}, u32[]{:S(2)}, u32[]{:S(2)}) %collective-permute-start.17) | collective-permute-done | bytes 131104 | tf_op jit(solution)/shard_map/ppermute | solution.py:34
  74.4 1.3 %collective-permute-done.18.refs_3_ = bf16[64,1024]{1,0:T(8,128)(2,1)S(1)} collective-permute-done((bf16[64,1024]{1,0:T(8,128)(2,1)S(1)}, bf16[64,1024]{1,0:T(8,128)(2,1)S(1)}, u32[]{:S(2)}, u32[]{:S(2)}) %collective-permute-start.18) | collective-permute-done | bytes 131104 | tf_op jit(solution)/shard_map/ppermute | solution.py:34
  75.7 0.5 shard_map.119
  76.3 0.3 collective-permute-done.19.refs_2_
  76.5 1.2 shard_map.120
  77.7 1.2 %collective-permute-start.23 = (bf16[1024,128]{1,0:T(8,128)(2,1)S(1)}, bf16[1024,128]{1,0:T(8,128)(2,1)S(1)}, u32[]{:S(2)}, u32[]{:S(2)}) collective-permute-start(bf16[1024,128]{1,0:T(8,128)(2,1)S(1)} %get-tuple-element.149), channel_id=1, source_target_pairs={{0,16},{4,20},{8,24},{12,28},{16,0},{20,4},{24,8},{28,12},{1,17},{... | collective-permute-start | bytes 786440 | tf_op jit(solution)/shard_map/ppermute | solution.py:34
  78.9 1.2 %collective-permute-start.26 = (bf16[4,256,128]{2,1,0:T(8,128)(2,1)S(1)}, bf16[4,256,128]{2,1,0:T(8,128)(2,1)S(1)}, u32[]{:S(2)}, u32[]{:S(2)}) collective-permute-start(bf16[4,256,128]{2,1,0:T(8,128)(2,1)S(1)} %get-tuple-element.156), channel_id=1, source_target_pairs={{0,4},{4,0},{8,12},{12,8},{16,20},{20,16},{24,28},{28,24},{1,5},{5... | collective-permute-start | bytes 786440 | tf_op jit(solution)/shard_map/ppermute | solution.py:34
  80.1 2.4 %shard_map.121 = (bf16[3,256,256]{2,1,0:T(8,128)(2,1)S(1)}, bf16[4,448,128]{2,1,0:T(8,128)(2,1)S(1)}, bf16[4,320,128]{2,1,0:T(8,128)(2,1)S(1)}) custom-call(bf16[256,1024]{1,0:T(8,128)(2,1)S(1)} %get-tuple-element.143.refs_0_, bf16[256,1024]{1,0:T(8,128)(2,1)S(1)} %copy-done.1, bf16[3,256,256]{2,1,0:T(8,128)(2,1)S(1)} %copy-done.3, ...), custom_call_target="tpu_custom_call" | custom-call | flops 1000 | bytes 1000 | tf_op jit(solution)/shard_map/pallas_call | solution.py:110
  82.5 0.4 collective-permute-start.25
  82.9 1.8 %collective-permute-start.24 = (bf16[4,448,128]{2,1,0:T(8,128)(2,1)S(1)}, bf16[4,448,128]{2,1,0:T(8,128)(2,1)S(1)}, u32[]{:S(2)}, u32[]{:S(2)}) collective-permute-start(bf16[4,448,128]{2,1,0:T(8,128)(2,1)S(1)} %get-tuple-element.154), channel_id=1, source_target_pairs={{0,4},{4,0},{8,12},{12,8},{16,20},{20,16},{24,28},{28,24},{1,5},{5... | collective-permute-start | bytes 1376264 | tf_op jit(solution)/shard_map/ppermute | solution.py:34
  84.7 7.1 %collective-permute-done.23.refs_1_ = bf16[1024,128]{1,0:T(8,128)(2,1)S(1)} collective-permute-done((bf16[1024,128]{1,0:T(8,128)(2,1)S(1)}, bf16[1024,128]{1,0:T(8,128)(2,1)S(1)}, u32[]{:S(2)}, u32[]{:S(2)}) %collective-permute-start.23) | collective-permute-done | bytes 262176 | tf_op jit(solution)/shard_map/ppermute | solution.py:34
  91.8 0.6 shard_map.125
  92.5 2.9 %collective-permute-done.25.refs_4_ = bf16[4,320,128]{2,1,0:T(8,128)(2,1)S(1)} collective-permute-done((bf16[4,320,128]{2,1,0:T(8,128)(2,1)S(1)}, bf16[4,320,128]{2,1,0:T(8,128)(2,1)S(1)}, u32[]{:S(2)}, u32[]{:S(2)}) %collective-permute-start.25) | collective-permute-done | bytes 327712 | tf_op jit(solution)/shard_map/ppermute | solution.py:34
  95.4 0.4 collective-permute-done.24.refs_3_
  95.8 0.3 shard_map.126
  96.1 0.8 collective-permute-start.27
  96.9 0.7 shard_map.122
  97.7 1.3 %collective-permute-start.28 = (bf16[2,320,128]{2,1,0:T(8,128)(2,1)S(1)}, bf16[2,320,128]{2,1,0:T(8,128)(2,1)S(1)}, u32[]{:S(2)}, u32[]{:S(2)}) collective-permute-start(bf16[2,320,128]{2,1,0:T(8,128)(2,1)S(1)} %get-tuple-element.160), channel_id=1, source_target_pairs={{0,4},{4,0},{8,12},{12,8},{16,20},{20,16},{24,28},{28,24},{1,5},{5... | collective-permute-start | bytes 491528 | tf_op jit(solution)/shard_map/ppermute | solution.py:34
  98.9 2.2 %collective-permute-start.30 = (bf16[2,256,128]{2,1,0:T(8,128)(2,1)S(1)}, bf16[2,256,128]{2,1,0:T(8,128)(2,1)S(1)}, u32[]{:S(2)}, u32[]{:S(2)}) collective-permute-start(bf16[2,256,128]{2,1,0:T(8,128)(2,1)S(1)} %get-tuple-element.164), channel_id=1, source_target_pairs={{0,16},{4,20},{8,24},{12,28},{16,0},{20,4},{24,8},{28,12},{1,17},{... | collective-permute-start | bytes 393224 | tf_op jit(solution)/shard_map/ppermute | solution.py:34
  101.1 3.2 %collective-permute-done.28.refs_3_ = bf16[2,320,128]{2,1,0:T(8,128)(2,1)S(1)} collective-permute-done((bf16[2,320,128]{2,1,0:T(8,128)(2,1)S(1)}, bf16[2,320,128]{2,1,0:T(8,128)(2,1)S(1)}, u32[]{:S(2)}, u32[]{:S(2)}) %collective-permute-start.28) | collective-permute-done | bytes 163872 | tf_op jit(solution)/shard_map/ppermute | solution.py:34
  104.4 2.4 %collective-permute-start.29 = (bf16[768,128]{1,0:T(8,128)(2,1)S(1)}, bf16[768,128]{1,0:T(8,128)(2,1)S(1)}, u32[]{:S(2)}, u32[]{:S(2)}) collective-permute-start(bf16[768,128]{1,0:T(8,128)(2,1)S(1)} %get-tuple-element.162), channel_id=1, source_target_pairs={{0,16},{4,20},{8,24},{12,28},{16,0},{20,4},{24,8},{28,12},{1,17},{... | collective-permute-start | bytes 589832 | tf_op jit(solution)/shard_map/ppermute | solution.py:34
  106.9 1.6 %collective-permute-start.22 = (bf16[64,1024]{1,0:T(8,128)(2,1)S(1)}, bf16[64,1024]{1,0:T(8,128)(2,1)S(1)}, u32[]{:S(2)}, u32[]{:S(2)}) collective-permute-start(bf16[64,1024]{1,0:T(8,128)(2,1)S(1)} %shard_map.123), channel_id=1, source_target_pairs={{0,2},{1,3},{2,0},{3,1},{4,6},{5,7},{6,4},{7,5},{8,10},{9,11},{10,... | collective-permute-start | bytes 393224 | tf_op jit(solution)/shard_map/ppermute | solution.py:34
  108.5 3.2 %collective-permute-done.30.refs_1_ = bf16[2,256,128]{2,1,0:T(8,128)(2,1)S(1)} collective-permute-done((bf16[2,256,128]{2,1,0:T(8,128)(2,1)S(1)}, bf16[2,256,128]{2,1,0:T(8,128)(2,1)S(1)}, u32[]{:S(2)}, u32[]{:S(2)}) %collective-permute-start.30) | collective-permute-done | bytes 131104 | tf_op jit(solution)/shard_map/ppermute | solution.py:34
  111.8 1.0 shard_map.130
  112.8 0.9 shard_map.124
  113.8 3.6 %collective-permute-done.31 = bf16[1,256,128]{2,1,0:T(8,128)(2,1)S(1)} collective-permute-done((bf16[1,256,128]{2,1,0:T(8,128)(2,1)S(1)}, bf16[1,256,128]{2,1,0:T(8,128)(2,1)S(1)}, u32[]{:S(2)}, u32[]{:S(2)}) %collective-permute-start.31) | collective-permute-done | bytes 65568 | tf_op jit(solution)/shard_map/ppermute | solution.py:34
  117.3 1.0 shard_map.129
  (41 shorter events, 0.5 us)
Async XLA Ops:
  0.6 6.7 %collective-permute-start.1 = (bf16[64,1024]{1,0:T(8,128)(2,1)}, bf16[64,1024]{1,0:T(8,128)(2,1)S(1)}, u32[]{:S(2)}, u32[]{:S(2)}) collective-permute-start(bf16[64,1024]{1,0:T(8,128)(2,1)} %bitcast.19), channel_id=1, source_target_pairs={{0,2},{1,3},{2,0},{3,1},{4,6},{5,7},{6,4},{7,5},{8,10},{9,11},{10,... | collective-permute-start | bytes 393224 | tf_op jit(solution)/shard_map/ppermute | solution.py:34
  3.7 3.7 %collective-permute-start = (bf16[64,1024]{1,0:T(8,128)(2,1)}, bf16[64,1024]{1,0:T(8,128)(2,1)S(1)}, u32[]{:S(2)}, u32[]{:S(2)}) collective-permute-start(bf16[64,1024]{1,0:T(8,128)(2,1)} %bitcast.20), channel_id=1, source_target_pairs={{0,1},{1,0},{2,3},{3,2},{4,5},{5,4},{6,7},{7,6},{8,9},{9,8},{10,11... | collective-permute-start | bytes 393224 | tf_op jit(solution)/shard_map/ppermute | solution.py:34
  7.4 14.3 %all-to-all-start = ((bf16[8,8,2048]{2,1,0:T(8,128)(2,1)}), bf16[8,8,2048]{2,1,0:T(8,128)(2,1)S(1)}, u32[]{:S(2)}, u32[]{:S(2)}) async-start(bf16[8,8,2048]{2,1,0:T(8,128)(2,1)} %bitcast.2), calls=%async_computation | async-start | bytes 524288 | tf_op jit(solution)/shard_map/all_to_all | solution.py:576
  13.4 13.5 %collective-permute-start.2 = (bf16[256,1024]{1,0:T(8,128)(2,1)}, bf16[256,1024]{1,0:T(8,128)(2,1)S(1)}, u32[]{:S(2)}, u32[]{:S(2)}) collective-permute-start(bf16[256,1024]{1,0:T(8,128)(2,1)} %refs_1_.2), channel_id=1, source_target_pairs={{0,2},{1,3},{2,0},{3,1},{4,6},{5,7},{6,4},{7,5},{8,10},{9,11},{10,... | collective-permute-start | bytes 1572872 | tf_op jit(solution)/shard_map/ppermute | solution.py:34
  14.9 1.5 %collective-permute-start.3 = (bf16[64,1024]{1,0:T(8,128)(2,1)S(1)}, bf16[64,1024]{1,0:T(8,128)(2,1)S(1)}, u32[]{:S(2)}, u32[]{:S(2)}) collective-permute-start(bf16[64,1024]{1,0:T(8,128)(2,1)S(1)} %collective-permute-done.1.refs_2_), channel_id=1, source_target_pairs={{0,1},{1,0},{2,3},{3,2},{4,5},{5,4},{6,7},{7,6},{8,9},{9,8},{10,11... | collective-permute-start | bytes 393224 | tf_op jit(solution)/shard_map/ppermute | solution.py:34
  14.9 20.1 %collective-permute-start.9 = (bf16[256,1024]{1,0:T(8,128)(2,1)}, bf16[256,1024]{1,0:T(8,128)(2,1)S(1)}, u32[]{:S(2)}, u32[]{:S(2)}) collective-permute-start(bf16[256,1024]{1,0:T(8,128)(2,1)} %refs_1_.2), channel_id=1, source_target_pairs={{0,1},{1,0},{2,3},{3,2},{4,5},{5,4},{6,7},{7,6},{8,9},{9,8},{10,11... | collective-permute-start | bytes 1572872 | tf_op jit(solution)/shard_map/ppermute | solution.py:34
  21.6 20.1 %copy-start.2 = (bf16[3,1024,256]{2,1,0:T(8,128)(2,1)S(1)}, bf16[3,1024,256]{2,1,0:T(8,128)(2,1)}, u32[]{:S(2)}) copy-start(bf16[3,1024,256]{2,1,0:T(8,128)(2,1)} %refs_7_.3) | copy-start | bytes 4718596
  21.6 20.1 %copy-start.6 = (s32[4]{0:T(128)S(1)}, s32[4]{0:T(128)}, u32[]{:S(2)}) copy-start(s32[4]{0:T(128)} %refs_0_.1) | copy-start | bytes 52
  21.6 12.1 %all-to-all-start.1 = ((bf16[8,32,256]{2,1,0:T(8,128)(2,1)}), bf16[8,32,256]{2,1,0:T(8,128)(2,1)S(1)}, u32[]{:S(2)}, u32[]{:S(2)}) async-start(bf16[8,32,256]{2,1,0:T(8,128)(2,1)} %bitcast.4), calls=%async_computation.1 | async-start | bytes 262144 | tf_op jit(solution)/shard_map/all_to_all | solution.py:585
  26.4 8.1 %collective-permute-start.6 = (bf16[64,2048]{1,0:T(8,128)(2,1)S(1)}, bf16[64,2048]{1,0:T(8,128)(2,1)S(1)}, u32[]{:S(2)}, u32[]{:S(2)}) collective-permute-start(bf16[64,2048]{1,0:T(8,128)(2,1)S(1)} %bitcast.11), channel_id=1, source_target_pairs={{0,2},{1,3},{2,0},{3,1},{4,6},{5,7},{6,4},{7,5},{8,10},{9,11},{10,... | collective-permute-start | bytes 786440 | tf_op jit(solution)/shard_map/ppermute | solution.py:34
  33.8 8.0 %collective-permute-start.11 = (bf16[256,1024]{1,0:T(8,128)(2,1)S(1)}, bf16[256,1024]{1,0:T(8,128)(2,1)S(1)}, u32[]{:S(2)}, u32[]{:S(2)}) collective-permute-start(bf16[256,1024]{1,0:T(8,128)(2,1)S(1)} %collective-permute-done.2.refs_5_), channel_id=1, source_target_pairs={{0,1},{1,0},{2,3},{3,2},{4,5},{5,4},{6,7},{7,6},{8,9},{9,8},{10,11... | collective-permute-start | bytes 1572872 | tf_op jit(solution)/shard_map/ppermute | solution.py:34
  33.8 2.3 %collective-permute-start.5 = (bf16[64,2048]{1,0:T(8,128)(2,1)S(1)}, bf16[64,2048]{1,0:T(8,128)(2,1)S(1)}, u32[]{:S(2)}, u32[]{:S(2)}) collective-permute-start(bf16[64,2048]{1,0:T(8,128)(2,1)S(1)} %bitcast.12), channel_id=1, source_target_pairs={{0,1},{1,0},{2,3},{3,2},{4,5},{5,4},{6,7},{7,6},{8,9},{9,8},{10,11... | collective-permute-start | bytes 786440 | tf_op jit(solution)/shard_map/ppermute | solution.py:34
  34.5 2.1 %collective-permute-start.7 = (bf16[64,2048]{1,0:T(8,128)(2,1)S(1)}, bf16[64,2048]{1,0:T(8,128)(2,1)S(1)}, u32[]{:S(2)}, u32[]{:S(2)}) collective-permute-start(bf16[64,2048]{1,0:T(8,128)(2,1)S(1)} %collective-permute-done.6.refs_2_), channel_id=1, source_target_pairs={{0,1},{1,0},{2,3},{3,2},{4,5},{5,4},{6,7},{7,6},{8,9},{9,8},{10,11... | collective-permute-start | bytes 786440 | tf_op jit(solution)/shard_map/ppermute | solution.py:34
  34.5 2.1 %collective-permute-start.8 = (bf16[256,256]{1,0:T(8,128)(2,1)S(1)}, bf16[256,256]{1,0:T(8,128)(2,1)S(1)}, u32[]{:S(2)}, u32[]{:S(2)}) collective-permute-start(bf16[256,256]{1,0:T(8,128)(2,1)S(1)} %bitcast.24), channel_id=1, source_target_pairs={{0,1},{1,0},{2,3},{3,2},{4,5},{5,4},{6,7},{7,6},{8,9},{9,8},{10,11... | collective-permute-start | bytes 393224 | tf_op jit(solution)/shard_map/ppermute | solution.py:34
  35.0 5.4 %collective-permute-start.4 = (bf16[256,256]{1,0:T(8,128)(2,1)S(1)}, bf16[256,256]{1,0:T(8,128)(2,1)S(1)}, u32[]{:S(2)}, u32[]{:S(2)}) collective-permute-start(bf16[256,256]{1,0:T(8,128)(2,1)S(1)} %bitcast.25), channel_id=1, source_target_pairs={{0,2},{1,3},{2,0},{3,1},{4,6},{5,7},{6,4},{7,5},{8,10},{9,11},{10,... | collective-permute-start | bytes 393224 | tf_op jit(solution)/shard_map/ppermute | solution.py:34
  40.4 1.3 %collective-permute-start.10 = (bf16[256,256]{1,0:T(8,128)(2,1)S(1)}, bf16[256,256]{1,0:T(8,128)(2,1)S(1)}, u32[]{:S(2)}, u32[]{:S(2)}) collective-permute-start(bf16[256,256]{1,0:T(8,128)(2,1)S(1)} %collective-permute-done.4.refs_1_), channel_id=1, source_target_pairs={{0,1},{1,0},{2,3},{3,2},{4,5},{5,4},{6,7},{7,6},{8,9},{9,8},{10,11... | collective-permute-start | bytes 393224 | tf_op jit(solution)/shard_map/ppermute | solution.py:34
  48.2 3.4 %collective-permute-start.12 = (bf16[2,64,1024]{2,1,0:T(8,128)(2,1)S(1)}, bf16[2,64,1024]{2,1,0:T(8,128)(2,1)S(1)}, u32[]{:S(2)}, u32[]{:S(2)}) collective-permute-start(bf16[2,64,1024]{2,1,0:T(8,128)(2,1)S(1)} %get-tuple-element.106), channel_id=1, source_target_pairs={{0,1},{1,0},{2,3},{3,2},{4,5},{5,4},{6,7},{7,6},{8,9},{9,8},{10,11... | collective-permute-start | bytes 786440 | tf_op jit(solution)/shard_map/ppermute | solution.py:34
  48.4 14.4 %collective-permute-start.14 = (bf16[4,512,128]{2,1,0:T(8,128)(2,1)}, bf16[4,512,128]{2,1,0:T(8,128)(2,1)S(1)}, u32[]{:S(2)}, u32[]{:S(2)}) collective-permute-start(bf16[4,512,128]{2,1,0:T(8,128)(2,1)} %get-tuple-element.118), channel_id=1, source_target_pairs={{0,4},{4,0},{8,12},{12,8},{16,20},{20,16},{24,28},{28,24},{1,5},{5... | collective-permute-start | bytes 1572872 | tf_op jit(solution)/shard_map/ppermute | solution.py:34
  50.1 14.4 %collective-permute-start.15 = (bf16[4,512,128]{2,1,0:T(8,128)(2,1)}, bf16[4,512,128]{2,1,0:T(8,128)(2,1)S(1)}, u32[]{:S(2)}, u32[]{:S(2)}) collective-permute-start(bf16[4,512,128]{2,1,0:T(8,128)(2,1)} %get-tuple-element.119), channel_id=1, source_target_pairs={{0,8},{4,12},{8,0},{12,4},{16,24},{20,28},{24,16},{28,20},{1,9},{5... | collective-permute-start | bytes 1572872 | tf_op jit(solution)/shard_map/ppermute | solution.py:34
  51.7 5.3 %collective-permute-start.13 = (bf16[64,1024]{1,0:T(8,128)(2,1)S(1)}, bf16[64,1024]{1,0:T(8,128)(2,1)S(1)}, u32[]{:S(2)}, u32[]{:S(2)}) collective-permute-start(bf16[64,1024]{1,0:T(8,128)(2,1)S(1)} %shard_map.114), channel_id=1, source_target_pairs={{0,2},{1,3},{2,0},{3,1},{4,6},{5,7},{6,4},{7,5},{8,10},{9,11},{10,... | collective-permute-start | bytes 393224 | tf_op jit(solution)/shard_map/ppermute | solution.py:34
  56.9 14.3 %copy-start.3 = (bf16[3,256,256]{2,1,0:T(8,128)(2,1)S(1)}, bf16[3,256,256]{2,1,0:T(8,128)(2,1)}, u32[]{:S(2)}) copy-start(bf16[3,256,256]{2,1,0:T(8,128)(2,1)} %get-tuple-element.127.refs_0_.refs_2_) | copy-start | bytes 1179652
  57.8 11.6 %all-to-all-start.2 = ((bf16[8,8,1024]{2,1,0:T(8,128)(2,1)}), bf16[8,8,1024]{2,1,0:T(8,128)(2,1)S(1)}, u32[]{:S(2)}, u32[]{:S(2)}) async-start(bf16[8,8,1024]{2,1,0:T(8,128)(2,1)} %bitcast.6), calls=%async_computation.2 | async-start | bytes 262144 | tf_op jit(solution)/shard_map/all_to_all | solution.py:609
  65.7 14.4 %copy-start.1 = (bf16[256,1024]{1,0:T(8,128)(2,1)S(1)}, bf16[256,1024]{1,0:T(8,128)(2,1)}, u32[]{:S(2)}) copy-start(bf16[256,1024]{1,0:T(8,128)(2,1)} %refs_1_.2) | copy-start | bytes 1572868
  69.4 5.0 %collective-permute-start.17 = (bf16[64,1024]{1,0:T(8,128)(2,1)S(1)}, bf16[64,1024]{1,0:T(8,128)(2,1)S(1)}, u32[]{:S(2)}, u32[]{:S(2)}) collective-permute-start(bf16[64,1024]{1,0:T(8,128)(2,1)S(1)} %bitcast.15), channel_id=1, source_target_pairs={{0,2},{1,3},{2,0},{3,1},{4,6},{5,7},{6,4},{7,5},{8,10},{9,11},{10,... | collective-permute-start | bytes 393224 | tf_op jit(solution)/shard_map/ppermute | solution.py:34
  69.9 6.6 %collective-permute-start.19 = (bf16[2,512,128]{2,1,0:T(8,128)(2,1)}, bf16[2,512,128]{2,1,0:T(8,128)(2,1)S(1)}, u32[]{:S(2)}, u32[]{:S(2)}) collective-permute-start(bf16[2,512,128]{2,1,0:T(8,128)(2,1)} %get-tuple-element.134), channel_id=1, source_target_pairs={{0,8},{4,12},{8,0},{12,4},{16,24},{20,28},{24,16},{28,20},{1,9},{5... | collective-permute-start | bytes 786440 | tf_op jit(solution)/shard_map/ppermute | solution.py:34
  69.9 6.6 %collective-permute-start.20 = (bf16[2,512,128]{2,1,0:T(8,128)(2,1)}, bf16[2,512,128]{2,1,0:T(8,128)(2,1)S(1)}, u32[]{:S(2)}, u32[]{:S(2)}) collective-permute-start(bf16[2,512,128]{2,1,0:T(8,128)(2,1)} %get-tuple-element.135), channel_id=1, source_target_pairs={{0,4},{4,0},{8,12},{12,8},{16,20},{20,16},{24,28},{28,24},{1,5},{5... | collective-permute-start | bytes 786440 | tf_op jit(solution)/shard_map/ppermute | solution.py:34
  71.2 3.2 %collective-permute-start.16 = (bf16[64,1024]{1,0:T(8,128)(2,1)S(1)}, bf16[64,1024]{1,0:T(8,128)(2,1)S(1)}, u32[]{:S(2)}, u32[]{:S(2)}) collective-permute-start(bf16[64,1024]{1,0:T(8,128)(2,1)S(1)} %bitcast.16), channel_id=1, source_target_pairs={{0,1},{1,0},{2,3},{3,2},{4,5},{5,4},{6,7},{7,6},{8,9},{9,8},{10,11... | collective-permute-start | bytes 393224 | tf_op jit(solution)/shard_map/ppermute | solution.py:34
  74.4 1.3 %collective-permute-start.18 = (bf16[64,1024]{1,0:T(8,128)(2,1)S(1)}, bf16[64,1024]{1,0:T(8,128)(2,1)S(1)}, u32[]{:S(2)}, u32[]{:S(2)}) collective-permute-start(bf16[64,1024]{1,0:T(8,128)(2,1)S(1)} %collective-permute-done.17.refs_2_), channel_id=1, source_target_pairs={{0,1},{1,0},{2,3},{3,2},{4,5},{5,4},{6,7},{7,6},{8,9},{9,8},{10,11... | collective-permute-start | bytes 393224 | tf_op jit(solution)/shard_map/ppermute | solution.py:34
  77.7 14.1 %copy-start.5 = (bf16[256,1024]{1,0:T(8,128)(2,1)S(1)}, bf16[256,1024]{1,0:T(8,128)(2,1)}, u32[]{:S(2)}) copy-start(bf16[256,1024]{1,0:T(8,128)(2,1)} %get-tuple-element.145.refs_4_.refs_1_) | copy-start | bytes 1572868
  77.7 14.1 %collective-permute-start.23 = (bf16[1024,128]{1,0:T(8,128)(2,1)S(1)}, bf16[1024,128]{1,0:T(8,128)(2,1)S(1)}, u32[]{:S(2)}, u32[]{:S(2)}) collective-permute-start(bf16[1024,128]{1,0:T(8,128)(2,1)S(1)} %get-tuple-element.149), channel_id=1, source_target_pairs={{0,16},{4,20},{8,24},{12,28},{16,0},{20,4},{24,8},{28,12},{1,17},{... | collective-permute-start | bytes 786440 | tf_op jit(solution)/shard_map/ppermute | solution.py:34
  78.9 13.6 %collective-permute-start.26 = (bf16[4,256,128]{2,1,0:T(8,128)(2,1)S(1)}, bf16[4,256,128]{2,1,0:T(8,128)(2,1)S(1)}, u32[]{:S(2)}, u32[]{:S(2)}) collective-permute-start(bf16[4,256,128]{2,1,0:T(8,128)(2,1)S(1)} %get-tuple-element.156), channel_id=1, source_target_pairs={{0,4},{4,0},{8,12},{12,8},{16,20},{20,16},{24,28},{28,24},{1,5},{5... | collective-permute-start | bytes 786440 | tf_op jit(solution)/shard_map/ppermute | solution.py:34
  82.5 12.9 %collective-permute-start.25 = (bf16[4,320,128]{2,1,0:T(8,128)(2,1)S(1)}, bf16[4,320,128]{2,1,0:T(8,128)(2,1)S(1)}, u32[]{:S(2)}, u32[]{:S(2)}) collective-permute-start(bf16[4,320,128]{2,1,0:T(8,128)(2,1)S(1)} %get-tuple-element.155), channel_id=1, source_target_pairs={{0,8},{4,12},{8,0},{12,4},{16,24},{20,28},{24,16},{28,20},{1,9},{5... | collective-permute-start | bytes 983048 | tf_op jit(solution)/shard_map/ppermute | solution.py:34
  82.9 12.9 %collective-permute-start.24 = (bf16[4,448,128]{2,1,0:T(8,128)(2,1)S(1)}, bf16[4,448,128]{2,1,0:T(8,128)(2,1)S(1)}, u32[]{:S(2)}, u32[]{:S(2)}) collective-permute-start(bf16[4,448,128]{2,1,0:T(8,128)(2,1)S(1)} %get-tuple-element.154), channel_id=1, source_target_pairs={{0,4},{4,0},{8,12},{12,8},{16,20},{20,16},{24,28},{28,24},{1,5},{5... | collective-permute-start | bytes 1376264 | tf_op jit(solution)/shard_map/ppermute | solution.py:34
  92.5 4.4 %copy-start = (bf16[3,1024,256]{2,1,0:T(8,128)(2,1)S(1)}, bf16[3,1024,256]{2,1,0:T(8,128)(2,1)}, u32[]{:S(2)}) copy-start(bf16[3,1024,256]{2,1,0:T(8,128)(2,1)} %refs_1_.3) | copy-start | bytes 4718596
  96.1 8.2 %collective-permute-start.27 = (bf16[2,448,128]{2,1,0:T(8,128)(2,1)S(1)}, bf16[2,448,128]{2,1,0:T(8,128)(2,1)S(1)}, u32[]{:S(2)}, u32[]{:S(2)}) collective-permute-start(bf16[2,448,128]{2,1,0:T(8,128)(2,1)S(1)} %get-tuple-element.159), channel_id=1, source_target_pairs={{0,8},{4,12},{8,0},{12,4},{16,24},{20,28},{24,16},{28,20},{1,9},{5... | collective-permute-start | bytes 688136 | tf_op jit(solution)/shard_map/ppermute | solution.py:34
  97.6 15.2 %copy-start.4 = (bf16[1,64,1024]{2,1,0:T(8,128)(2,1)S(1)}, bf16[1,64,1024]{2,1,0:T(8,128)(2,1)}, u32[]{:S(2)}) copy-start(bf16[1,64,1024]{2,1,0:T(8,128)(2,1)} %param.7) | copy-start | bytes 393220
  97.6 9.2 %collective-permute-start.21 = (bf16[2,64,1024]{2,1,0:T(8,128)(2,1)S(1)}, bf16[2,64,1024]{2,1,0:T(8,128)(2,1)S(1)}, u32[]{:S(2)}, u32[]{:S(2)}) collective-permute-start(bf16[2,64,1024]{2,1,0:T(8,128)(2,1)S(1)} %get-tuple-element.148), channel_id=1, source_target_pairs={{0,1},{1,0},{2,3},{3,2},{4,5},{5,4},{6,7},{7,6},{8,9},{9,8},{10,11... | collective-permute-start | bytes 786440 | tf_op jit(solution)/shard_map/ppermute | solution.py:34
  97.7 6.6 %collective-permute-start.28 = (bf16[2,320,128]{2,1,0:T(8,128)(2,1)S(1)}, bf16[2,320,128]{2,1,0:T(8,128)(2,1)S(1)}, u32[]{:S(2)}, u32[]{:S(2)}) collective-permute-start(bf16[2,320,128]{2,1,0:T(8,128)(2,1)S(1)} %get-tuple-element.160), channel_id=1, source_target_pairs={{0,4},{4,0},{8,12},{12,8},{16,20},{20,16},{24,28},{28,24},{1,5},{5... | collective-permute-start | bytes 491528 | tf_op jit(solution)/shard_map/ppermute | solution.py:34
  98.9 12.7 %collective-permute-start.30 = (bf16[2,256,128]{2,1,0:T(8,128)(2,1)S(1)}, bf16[2,256,128]{2,1,0:T(8,128)(2,1)S(1)}, u32[]{:S(2)}, u32[]{:S(2)}) collective-permute-start(bf16[2,256,128]{2,1,0:T(8,128)(2,1)S(1)} %get-tuple-element.164), channel_id=1, source_target_pairs={{0,16},{4,20},{8,24},{12,28},{16,0},{20,4},{24,8},{28,12},{1,17},{... | collective-permute-start | bytes 393224 | tf_op jit(solution)/shard_map/ppermute | solution.py:34
  104.4 12.9 %collective-permute-start.29 = (bf16[768,128]{1,0:T(8,128)(2,1)S(1)}, bf16[768,128]{1,0:T(8,128)(2,1)S(1)}, u32[]{:S(2)}, u32[]{:S(2)}) collective-permute-start(bf16[768,128]{1,0:T(8,128)(2,1)S(1)} %get-tuple-element.162), channel_id=1, source_target_pairs={{0,16},{4,20},{8,24},{12,28},{16,0},{20,4},{24,8},{28,12},{1,17},{... | collective-permute-start | bytes 589832 | tf_op jit(solution)/shard_map/ppermute | solution.py:34
  106.9 5.9 %collective-permute-start.22 = (bf16[64,1024]{1,0:T(8,128)(2,1)S(1)}, bf16[64,1024]{1,0:T(8,128)(2,1)S(1)}, u32[]{:S(2)}, u32[]{:S(2)}) collective-permute-start(bf16[64,1024]{1,0:T(8,128)(2,1)S(1)} %shard_map.123), channel_id=1, source_target_pairs={{0,2},{1,3},{2,0},{3,1},{4,6},{5,7},{6,4},{7,5},{8,10},{9,11},{10,... | collective-permute-start | bytes 393224 | tf_op jit(solution)/shard_map/ppermute | solution.py:34
  111.7 5.6 %collective-permute-start.31 = (bf16[1,256,128]{2,1,0:T(8,128)(2,1)S(1)}, bf16[1,256,128]{2,1,0:T(8,128)(2,1)S(1)}, u32[]{:S(2)}, u32[]{:S(2)}) collective-permute-start(bf16[1,256,128]{2,1,0:T(8,128)(2,1)S(1)} %get-tuple-element.166), channel_id=1, source_target_pairs={{0,8},{4,12},{8,0},{12,4},{16,24},{20,28},{24,16},{28,20},{1,9},{5... | collective-permute-start | bytes 196616 | tf_op jit(solution)/shard_map/ppermute | solution.py:34

commit v3 on v2

--- a/solution.py
+++ b/solution.py
@@ -186,14 +186,17 @@
     return pl.ds(pl.multiple_of(start, rows), rows)
 
 
-def joined(x, grad):
+def joined(x, grad, weights):
     rows, dim = x.shape
 
     def body(t):
+        brought = t.copy(t.get(2), t.outs[1])
         for i in range(2):
             t.outs[0][:, i * dim : (i + 1) * dim] = t.get(i)[...]
-
-    return run(body, (x, grad), "hh", (shape((rows, 2 * dim)),), "v")[0]
+        brought.wait()
+
+    outs = (shape((rows, 2 * dim)), shape(weights.shape))
+    return run(body, (x, grad, weights), "hhx", outs, "vv", copies=1)
 
 
 def spatial_forward(parts, weights, heads, groups):
@@ -218,7 +221,7 @@
 
     outs = (shape((rows, dim)), shape((3, rows, width)), shape((rows, width)))
     return run(
-        body, (*parts, weights), "h" + "v" * (mp - 1) + "h", outs, "hhv"
+        body, (*parts, weights), "h" + "v" * mp, outs, "hhv"
     )
 
 
@@ -344,13 +347,15 @@
     )
 
 
-def head_sums(send, keep):
+def head_sums(send, keep, later=()):
     def body(t):
         t.outs[0][...] = (t.get(0)[1].astype(F32) + t.get(1)[1].astype(F32)).astype(BF)
 
     came = swap(send, "mp", 1)
     (pair,) = run(body, (keep, came), "vv", (shape(keep.shape[1:]),), "v")
-    return keep, came, swap(pair, "mp", 2)
+    if later:
+        pair, later = lax.optimization_barrier((pair, later))
+    return (keep, came, swap(pair, "mp", 2)), later
 
 
 def summed(t):
@@ -569,16 +574,15 @@
     halves = groups == 8
     x_own, g_own = video_tokens[0], grad_output[0]
     x_one, x_two = swap(x_own, "mp", 1), swap(x_own, "mp", 2)
-    xg, x_one, x_two, so_own = lax.optimization_barrier(
-        (joined(x_own, g_own), x_one, x_two, spatial_out)
-    )
+    xg, w_spatial = joined(x_own, g_own, spatial_qkv)
+    xg, x_one, x_two, so_own = lax.optimization_barrier((xg, x_one, x_two, spatial_out))
     x_three = swap(x_two, "mp", 1)
     xg = lax.all_to_all(xg.reshape(groups, per, 2 * dim), "frames", 0, 0, tiled=True)
     xg = xg.reshape(rows_mp, 2 * dim)
     so_two = swap(so_own, "mp", 2)
 
     normed_x, qkv_s, attn_send = spatial_forward(
-        (x_own, x_one, x_two, x_three), spatial_qkv, heads, groups
+        (x_own, x_one, x_two, x_three), w_spatial, heads, groups
     )
     attn_send, xg = lax.optimization_barrier((attn_send, xg))
     xg_two = swap(xg, "mp", 2)
@@ -599,9 +603,9 @@
         (moved_two, swap(moved_two, "mp", 1)), so_far, g_rows, d_attn_t,
         (so_two, swap(so_two, "mp", 1)), temporal_qkv, clip_frames, heads, groups, per, mp,
     )
-    parts = head_sums(send_h, keep_h)
+    parts, t_sent = head_sums(send_h, keep_h, t_sent)
     if halves:
-        t_kept = weight_grads_half(t_grads, normed_h, g_rows, groups)
+        t_kept = weight_grads_half(t_grads, normed_h, g_rows, groups, 50_000_000_000)
         parts, t_kept = lax.optimization_barrier((parts, t_kept))
         came = [swap(t_sent[0], "frames", 1), swap(t_sent[1], "frames", 2)]
         t_sums = halve(t_kept, came, out="h")
@@ -632,7 +636,7 @@
     if halves:
         after = lax.optimization_barrier
         send_x, keep_x = normed_back(s_grads, spatial_qkv, mp)
-        s_grads, t_came = after((s_grads, t_came))
+        s_grads, send_x, keep_x, t_came = after((s_grads, send_x, keep_x, t_came))
         t_qkv, t_out = last_sums([(t_keep, t_came)])
         s_kept = qkv_keeps(s_grads, normed_x, groups, 50_000_000_000)
         came = [swap(s_sent[0], "frames", 1), swap(s_sent[1], "frames", 2)]
@@ -648,7 +652,7 @@
         send_x, keep_x = normed_back(s_grads, spatial_qkv, mp)
         all_grads = jnp.concatenate([s_grads, attn_s[None]], 0)
         s_qkv, s_out = reduce_whole(all_grads, normed_x, d_hidden_all)
-    grad_tokens = tokens_back(head_sums(send_x, keep_x), x_own, d_hidden)
+    grad_tokens = tokens_back(head_sums(send_x, keep_x)[0], x_own, d_hidden)
     return grad_tokens[None], s_qkv, s_out, t_qkv, t_out
 
 

time: 119 us -> 120 us (level)
  waiting for transfers between devices: 49 us -> 46.3 us
  local copies, waits for them, and re-layouts: 0.03 us -> 1.6 us
    all_to_all x1, waiting for transfers between devices: 3.76 us -> 1.9 us  [shards(): lax.all_to_all(d_hidden.reshape(groups, per, dim), 'frames', 0, 0, tiled=...]
    unnamed x14 -> x20, local copies, waits for them, and re-layouts: 0.03 us -> 1.6 us
    all_to_all x1, starting transfers between devices: 4.24 us -> 5.72 us  [shards(): lax.all_to_all(d_hidden.reshape(groups, per, dim), 'frames', 0, 0, tiled=...]
  transfers between devices with their start and end apart: 35 -> 35, of which waited for: 22 -> 27; matrix products, arithmetic and copies ran while one was open for 0% -> 0% of each run, Pallas kernels for 16% -> 16%
where the time goes in v3:
time: 120 us
  waiting for transfers between devices  46.3 us (39%)
  starting transfers between devices  42 us (35%)
  Pallas kernels  28.6 us (24%)
  local copies, waits for them, and re-layouts  1.6 us (1%)
    ppermute x32, waiting for transfers between devices, swap(): return lax.ppermute(value, axis, [(i, i ^ by) for i in range(size)])  36.5 us
    pallas_call x21, Pallas kernels, run(): pl.pallas_call(wrapped, out_shape=tuple((pltpu.HBM(o.shape, o.dtype) if w...  28.6 us
    ppermute x32, starting transfers between devices, swap(): return lax.ppermute(value, axis, [(i, i ^ by) for i in range(size)])  25.2 us
    all_to_all x1, waiting for transfers between devices, shards(): lax.all_to_all(attn_send.reshape(groups, mp * per, width), 'frames', 0, 0...  6.83 us
    all_to_all x1, starting transfers between devices, shards(): lax.all_to_all(xg.reshape(groups, per, 2 * dim), 'frames', 0, 0, tiled=True)  6.02 us
    all_to_all x1, starting transfers between devices, shards(): lax.all_to_all(d_hidden.reshape(groups, per, dim), 'frames', 0, 0, tiled=...  5.72 us
    all_to_all x1, starting transfers between devices, shards(): lax.all_to_all(attn_send.reshape(groups, mp * per, width), 'frames', 0, 0...  5.03 us
  transfers between devices with their start and end apart: 35, of which 27 were waited for; matrix products, arithmetic and copies ran while one was open for 0% of the time, Pallas kernels for 16%

profile of v3, /device:TPU:0, one launch (start us, length us, event | category | flops | bytes accessed | tf_op | source)
XLA Modules:
  0.0 119.6 jit_solution(18205133490708731128)
XLA Ops:
  0.6 3.0 %collective-permute-start.1 = (bf16[64,1024]{1,0:T(8,128)(2,1)}, bf16[64,1024]{1,0:T(8,128)(2,1)S(1)}, u32[]{:S(2)}, u32[]{:S(2)}) collective-permute-start(bf16[64,1024]{1,0:T(8,128)(2,1)} %bitcast.15), channel_id=1, source_target_pairs={{0,2},{1,3},{2,0},{3,1},{4,6},{5,7},{6,4},{7,5},{8,10},{9,11},{10,... | collective-permute-start | bytes 393224 | tf_op jit(solution)/shard_map/ppermute | solution.py:34
  3.7 2.3 %shard_map.110 = (bf16[64,2048]{1,0:T(8,128)(2,1)}, bf16[3,1024,256]{2,1,0:T(8,128)(2,1)S(1)}) custom-call(bf16[64,1024]{1,0:T(8,128)(2,1)} %bitcast.17, bf16[64,1024]{1,0:T(8,128)(2,1)} %bitcast.29, bf16[3,1024,256]{2,1,0:T(8,128)(2,1)} %refs_1_.3), custom_call_target="tpu_custom_call" | custom-call | flops 1000 | bytes 1000 | tf_op jit(solution)/shard_map/pallas_call | solution.py:110
  6.0 1.4 %collective-permute-done.1.refs_2_ = bf16[64,1024]{1,0:T(8,128)(2,1)S(1)} collective-permute-done((bf16[64,1024]{1,0:T(8,128)(2,1)}, bf16[64,1024]{1,0:T(8,128)(2,1)S(1)}, u32[]{:S(2)}, u32[]{:S(2)}) %collective-permute-start.1) | collective-permute-done | bytes 131104 | tf_op jit(solution)/shard_map/ppermute | solution.py:34
  7.4 0.7 copy-done.7
  8.0 6.0 %all-to-all-start = ((bf16[8,8,2048]{2,1,0:T(8,128)(2,1)}), bf16[8,8,2048]{2,1,0:T(8,128)(2,1)S(1)}, u32[]{:S(2)}, u32[]{:S(2)}) async-start(bf16[8,8,2048]{2,1,0:T(8,128)(2,1)} %bitcast.2), calls=%async_computation | async-start | bytes 524288 | tf_op jit(solution)/shard_map/all_to_all | solution.py:580
  14.1 1.6 %collective-permute-start.2 = (bf16[256,1024]{1,0:T(8,128)(2,1)S(1)}, bf16[256,1024]{1,0:T(8,128)(2,1)S(1)}, u32[]{:S(2)}, u32[]{:S(2)}) collective-permute-start(bf16[256,1024]{1,0:T(8,128)(2,1)S(1)} %copy-done.1), channel_id=1, source_target_pairs={{0,2},{1,3},{2,0},{3,1},{4,6},{5,7},{6,4},{7,5},{8,10},{9,11},{10,... | collective-permute-start | bytes 1572872 | tf_op jit(solution)/shard_map/ppermute | solution.py:34
  15.7 0.5 collective-permute-start.9
  16.2 0.8 collective-permute-done.3.refs_3_
  17.0 0.9 copy-done.8
  17.9 3.3 %shard_map.111 = (bf16[256,1024]{1,0:T(8,128)(2,1)}, bf16[3,256,256]{2,1,0:T(8,128)(2,1)}, bf16[256,256]{1,0:T(8,128)(2,1)}) custom-call(bf16[64,1024]{1,0:T(8,128)(2,1)} %bitcast.18, bf16[64,1024]{1,0:T(8,128)(2,1)S(1)} %copy-done.8, bf16[64,1024]{1,0:T(8,128)(2,1)S(1)} %collective-permute-done.1.refs_2_, ...), custom_call_target="tpu_custom_call" | custom-call | flops 1000 | bytes 1000 | tf_op jit(solution)/shard_map/pallas_call | solution.py:110
  21.2 1.1 all-to-all-done
  22.3 5.0 %all-to-all-start.1 = ((bf16[8,32,256]{2,1,0:T(8,128)(2,1)}), bf16[8,32,256]{2,1,0:T(8,128)(2,1)S(1)}, u32[]{:S(2)}, u32[]{:S(2)}) async-start(bf16[8,32,256]{2,1,0:T(8,128)(2,1)} %bitcast.4), calls=%async_computation.1 | async-start | bytes 262144 | tf_op jit(solution)/shard_map/all_to_all | solution.py:589
  27.3 0.5 collective-permute-start.6
  27.8 6.8 %all-to-all-done.1 = bf16[8,32,256]{2,1,0:T(8,128)(2,1)S(1)} async-done(((bf16[8,32,256]{2,1,0:T(8,128)(2,1)}), bf16[8,32,256]{2,1,0:T(8,128)(2,1)S(1)}, u32[]{:S(2)}, u32[]{:S(2)}) %all-to-all-start.1) | async-done | bytes 131104 | tf_op jit(solution)/shard_map/all_to_all | solution.py:589
  34.7 0.5 collective-permute-start.5
  35.5 0.5 collective-permute-start.8
  36.0 0.5 collective-permute-start.4
  37.7 3.5 %shard_map.112 = (f32[256,1024]{1,0:T(8,128)S(1)}, bf16[256,1024]{1,0:T(8,128)(2,1)S(1)}, bf16[256,256]{1,0:T(8,128)(2,1)S(1)}) custom-call(bf16[64,2048]{1,0:T(8,128)(2,1)S(1)} %bitcast.13, bf16[64,2048]{1,0:T(8,128)(2,1)S(1)} %collective-permute-done.5.refs_1_, bf16[64,2048]{1,0:T(8,128)(2,1)} %collective-permute-done.6.refs_2_, ...), custom_call_target="tpu_custom_call" | custom-call | flops 1000 | bytes 1000 | tf_op jit(solution)/shard_map/pallas_call | solution.py:110
  41.4 1.3 %collective-permute-done.10.refs_2_ = bf16[256,256]{1,0:T(8,128)(2,1)S(1)} collective-permute-done((bf16[256,256]{1,0:T(8,128)(2,1)S(1)}, bf16[256,256]{1,0:T(8,128)(2,1)S(1)}, u32[]{:S(2)}, u32[]{:S(2)}) %collective-permute-start.10) | collective-permute-done | bytes 131104 | tf_op jit(solution)/shard_map/ppermute | solution.py:34
  42.8 6.4 %shard_map.113 = (bf16[2,64,1024]{2,1,0:T(8,128)(2,1)S(1)}, bf16[2,64,1024]{2,1,0:T(8,128)(2,1)S(1)}, bf16[256,1024]{1,0:T(8,128)(2,1)S(1)}, bf16[64,1024]{1,0:T...) custom-call(s32[4]{0:T(128)S(1)} %copy-done.9, ...), custom_call_target="tpu_custom_call" | custom-call | flops 1000 | bytes 1000 | tf_op jit(solution)/shard_map/pallas_call | solution.py:110
  49.4 1.4 %collective-permute-done.12.refs_1_ = bf16[2,64,1024]{2,1,0:T(8,128)(2,1)S(1)} collective-permute-done((bf16[2,64,1024]{2,1,0:T(8,128)(2,1)S(1)}, bf16[2,64,1024]{2,1,0:T(8,128)(2,1)S(1)}, u32[]{:S(2)}, u32[]{:S(2)}) %collective-permute-start.12) | collective-permute-done | bytes 262176 | tf_op jit(solution)/shard_map/ppermute | solution.py:34
  50.9 0.6 collective-permute-start.13
  51.5 1.7 %collective-permute-start.14 = (bf16[4,512,128]{2,1,0:T(8,128)(2,1)}, bf16[4,512,128]{2,1,0:T(8,128)(2,1)S(1)}, u32[]{:S(2)}, u32[]{:S(2)}) collective-permute-start(bf16[4,512,128]{2,1,0:T(8,128)(2,1)} %get-tuple-element.130), channel_id=1, source_target_pairs={{0,4},{4,0},{8,12},{12,8},{16,20},{20,16},{24,28},{28,24},{1,5},{5... | collective-permute-start | bytes 1572872 | tf_op jit(solution)/shard_map/ppermute | solution.py:34
  53.2 1.5 %collective-permute-start.15 = (bf16[4,512,128]{2,1,0:T(8,128)(2,1)}, bf16[4,512,128]{2,1,0:T(8,128)(2,1)S(1)}, u32[]{:S(2)}, u32[]{:S(2)}) collective-permute-start(bf16[4,512,128]{2,1,0:T(8,128)(2,1)} %get-tuple-element.131), channel_id=1, source_target_pairs={{0,8},{4,12},{8,0},{12,4},{16,24},{20,28},{24,16},{28,20},{1,9},{5... | collective-permute-start | bytes 1572872 | tf_op jit(solution)/shard_map/ppermute | solution.py:34
  54.7 0.8 shard_map.115
  55.5 1.0 collective-permute-done.13.refs_2_
  56.5 0.9 shard_map.116
  57.4 5.7 %all-to-all-start.2 = ((bf16[8,8,1024]{2,1,0:T(8,128)(2,1)}), bf16[8,8,1024]{2,1,0:T(8,128)(2,1)S(1)}, u32[]{:S(2)}, u32[]{:S(2)}) async-start(bf16[8,8,1024]{2,1,0:T(8,128)(2,1)} %bitcast.6), calls=%async_computation.2 | async-start | bytes 262144 | tf_op jit(solution)/shard_map/all_to_all | solution.py:613
  63.1 2.4 %collective-permute-done.14.refs_2_ = bf16[4,512,128]{2,1,0:T(8,128)(2,1)S(1)} collective-permute-done((bf16[4,512,128]{2,1,0:T(8,128)(2,1)}, bf16[4,512,128]{2,1,0:T(8,128)(2,1)S(1)}, u32[]{:S(2)}, u32[]{:S(2)}) %collective-permute-start.14) | collective-permute-done | bytes 524320 | tf_op jit(solution)/shard_map/ppermute | solution.py:34
  65.5 2.0 %collective-permute-done.15.refs_3_ = bf16[4,512,128]{2,1,0:T(8,128)(2,1)S(1)} collective-permute-done((bf16[4,512,128]{2,1,0:T(8,128)(2,1)}, bf16[4,512,128]{2,1,0:T(8,128)(2,1)S(1)}, u32[]{:S(2)}, u32[]{:S(2)}) %collective-permute-start.15) | collective-permute-done | bytes 524320 | tf_op jit(solution)/shard_map/ppermute | solution.py:34
  67.5 1.1 shard_map.117
  68.7 1.9 %all-to-all-done.2 = bf16[8,8,1024]{2,1,0:T(8,128)(2,1)S(1)} async-done(((bf16[8,8,1024]{2,1,0:T(8,128)(2,1)}), bf16[8,8,1024]{2,1,0:T(8,128)(2,1)S(1)}, u32[]{:S(2)}, u32[]{:S(2)}) %all-to-all-start.2) | async-done | bytes 131104 | tf_op jit(solution)/shard_map/all_to_all | solution.py:613
  70.6 1.5 %collective-permute-start.17 = (bf16[64,1024]{1,0:T(8,128)(2,1)S(1)}, bf16[64,1024]{1,0:T(8,128)(2,1)S(1)}, u32[]{:S(2)}, u32[]{:S(2)}) collective-permute-start(bf16[64,1024]{1,0:T(8,128)(2,1)S(1)} %bitcast.20), channel_id=1, source_target_pairs={{0,2},{1,3},{2,0},{3,1},{4,6},{5,7},{6,4},{7,5},{8,10},{9,11},{10,... | collective-permute-start | bytes 393224 | tf_op jit(solution)/shard_map/ppermute | solution.py:34
  72.1 0.7 collective-permute-start.19
  72.8 1.3 %collective-permute-start.20 = (bf16[2,512,128]{2,1,0:T(8,128)(2,1)}, bf16[2,512,128]{2,1,0:T(8,128)(2,1)S(1)}, u32[]{:S(2)}, u32[]{:S(2)}) collective-permute-start(bf16[2,512,128]{2,1,0:T(8,128)(2,1)} %get-tuple-element.147), channel_id=1, source_target_pairs={{0,4},{4,0},{8,12},{12,8},{16,20},{20,16},{24,28},{28,24},{1,5},{5... | collective-permute-start | bytes 786440 | tf_op jit(solution)/shard_map/ppermute | solution.py:34
  74.1 1.5 %shard_map.118 = (f32[4,256,256]{2,1,0:T(8,128)S(1)}, bf16[256,256]{1,0:T(8,128)(2,1)S(1)}) custom-call(bf16[3,256,256]{2,1,0:T(8,128)(2,1)S(1)} %copy-done.4, bf16[256,256]{1,0:T(8,128)(2,1)} %get-tuple-element.140.refs_1_), custom_call_target="tpu_custom_call" | custom-call | flops 1000 | bytes 1000 | tf_op jit(solution)/shard_map/pallas_call | solution.py:110
  75.7 0.6 collective-permute-start.18
  76.2 1.0 collective-permute-done.18.refs_3_
  77.2 0.5 shard_map.119
  77.7 0.9 collective-permute-done.19.refs_2_
  78.7 0.7 collective-permute-done.20.refs_3_
  79.4 1.2 shard_map.120
  80.6 2.4 %collective-permute-start.21 = (bf16[1024,128]{1,0:T(8,128)(2,1)S(1)}, bf16[1024,128]{1,0:T(8,128)(2,1)S(1)}, u32[]{:S(2)}, u32[]{:S(2)}) collective-permute-start(bf16[1024,128]{1,0:T(8,128)(2,1)S(1)} %get-tuple-element.161), channel_id=1, source_target_pairs={{0,16},{4,20},{8,24},{12,28},{16,0},{20,4},{24,8},{28,12},{1,17},{... | collective-permute-start | bytes 786440 | tf_op jit(solution)/shard_map/ppermute | solution.py:34
  83.0 0.4 collective-permute-start.26
  83.4 2.4 %shard_map.121 = (bf16[3,256,256]{2,1,0:T(8,128)(2,1)S(1)}, bf16[4,448,128]{2,1,0:T(8,128)(2,1)S(1)}, bf16[4,320,128]{2,1,0:T(8,128)(2,1)S(1)}) custom-call(bf16[256,1024]{1,0:T(8,128)(2,1)S(1)} %get-tuple-element.155.refs_0_, bf16[256,1024]{1,0:T(8,128)(2,1)S(1)} %copy-done.2, bf16[3,256,256]{2,1,0:T(8,128)(2,1)S(1)} %copy-done.4, ...), custom_call_target="tpu_custom_call" | custom-call | flops 1000 | bytes 1000 | tf_op jit(solution)/shard_map/pallas_call | solution.py:110
  85.8 0.6 collective-permute-start.25
  86.4 1.1 collective-permute-start.24
  87.5 0.7 shard_map.122
  88.2 6.0 %collective-permute-done.21.refs_1_ = bf16[1024,128]{1,0:T(8,128)(2,1)S(1)} collective-permute-done((bf16[1024,128]{1,0:T(8,128)(2,1)S(1)}, bf16[1024,128]{1,0:T(8,128)(2,1)S(1)}, u32[]{:S(2)}, u32[]{:S(2)}) %collective-permute-start.21) | collective-permute-done | bytes 262176 | tf_op jit(solution)/shard_map/ppermute | solution.py:34
  94.2 0.6 shard_map.125
  94.9 4.2 %collective-permute-done.25.refs_4_ = bf16[4,320,128]{2,1,0:T(8,128)(2,1)S(1)} collective-permute-done((bf16[4,320,128]{2,1,0:T(8,128)(2,1)S(1)}, bf16[4,320,128]{2,1,0:T(8,128)(2,1)S(1)}, u32[]{:S(2)}, u32[]{:S(2)}) %collective-permute-start.25) | collective-permute-done | bytes 327712 | tf_op jit(solution)/shard_map/ppermute | solution.py:34
  99.4 0.5 collective-permute-start.27
  100.0 0.7 collective-permute-start.28
  100.7 1.8 %collective-permute-start.30 = (bf16[2,256,128]{2,1,0:T(8,128)(2,1)S(1)}, bf16[2,256,128]{2,1,0:T(8,128)(2,1)S(1)}, u32[]{:S(2)}, u32[]{:S(2)}) collective-permute-start(bf16[2,256,128]{2,1,0:T(8,128)(2,1)S(1)} %get-tuple-element.178), channel_id=1, source_target_pairs={{0,16},{4,20},{8,24},{12,28},{16,0},{20,4},{24,8},{28,12},{1,17},{... | collective-permute-start | bytes 393224 | tf_op jit(solution)/shard_map/ppermute | solution.py:34
  102.4 4.2 %collective-permute-done.28.refs_3_ = bf16[2,320,128]{2,1,0:T(8,128)(2,1)S(1)} collective-permute-done((bf16[2,320,128]{2,1,0:T(8,128)(2,1)S(1)}, bf16[2,320,128]{2,1,0:T(8,128)(2,1)S(1)}, u32[]{:S(2)}, u32[]{:S(2)}) %collective-permute-start.28) | collective-permute-done | bytes 163872 | tf_op jit(solution)/shard_map/ppermute | solution.py:34
  106.6 0.6 collective-permute-done.27.refs_2_
  107.4 0.9 collective-permute-start.29
  108.3 1.1 collective-permute-start.23
  109.4 0.6 collective-permute-done.30.refs_1_
  110.5 1.0 shard_map.130
  111.5 1.8 %collective-permute-done.23.refs_2_ = bf16[64,1024]{1,0:T(8,128)(2,1)S(1)} collective-permute-done((bf16[64,1024]{1,0:T(8,128)(2,1)S(1)}, bf16[64,1024]{1,0:T(8,128)(2,1)S(1)}, u32[]{:S(2)}, u32[]{:S(2)}) %collective-permute-start.23) | collective-permute-done | bytes 131104 | tf_op jit(solution)/shard_map/ppermute | solution.py:34
  113.3 0.9 shard_map.124
  114.7 3.8 %collective-permute-done.29.refs_1_ = bf16[768,128]{1,0:T(8,128)(2,1)S(1)} collective-permute-done((bf16[768,128]{1,0:T(8,128)(2,1)S(1)}, bf16[768,128]{1,0:T(8,128)(2,1)S(1)}, u32[]{:S(2)}, u32[]{:S(2)}) %collective-permute-start.29) | collective-permute-done | bytes 196640 | tf_op jit(solution)/shard_map/ppermute | solution.py:34
  118.4 1.0 shard_map.129
  (47 shorter events, 3.5 us)
Async XLA Ops:
  0.6 13.4 %copy-start.1 = (bf16[256,1024]{1,0:T(8,128)(2,1)S(1)}, bf16[256,1024]{1,0:T(8,128)(2,1)}, u32[]{:S(2)}) copy-start(bf16[256,1024]{1,0:T(8,128)(2,1)} %refs_1_.2) | copy-start | bytes 1572868
  0.6 6.7 %collective-permute-start.1 = (bf16[64,1024]{1,0:T(8,128)(2,1)}, bf16[64,1024]{1,0:T(8,128)(2,1)S(1)}, u32[]{:S(2)}, u32[]{:S(2)}) collective-permute-start(bf16[64,1024]{1,0:T(8,128)(2,1)} %bitcast.15), channel_id=1, source_target_pairs={{0,2},{1,3},{2,0},{3,1},{4,6},{5,7},{6,4},{7,5},{8,10},{9,11},{10,... | collective-permute-start | bytes 393224 | tf_op jit(solution)/shard_map/ppermute | solution.py:34
  3.7 3.7 %collective-permute-start = (bf16[64,1024]{1,0:T(8,128)(2,1)}, bf16[64,1024]{1,0:T(8,128)(2,1)S(1)}, u32[]{:S(2)}, u32[]{:S(2)}) collective-permute-start(bf16[64,1024]{1,0:T(8,128)(2,1)} %bitcast.16), channel_id=1, source_target_pairs={{0,1},{1,0},{2,3},{3,2},{4,5},{5,4},{6,7},{7,6},{8,9},{9,8},{10,11... | collective-permute-start | bytes 393224 | tf_op jit(solution)/shard_map/ppermute | solution.py:34
  7.4 0.7 copy-start.7
  8.0 14.3 %all-to-all-start = ((bf16[8,8,2048]{2,1,0:T(8,128)(2,1)}), bf16[8,8,2048]{2,1,0:T(8,128)(2,1)S(1)}, u32[]{:S(2)}, u32[]{:S(2)}) async-start(bf16[8,8,2048]{2,1,0:T(8,128)(2,1)} %bitcast.2), calls=%async_computation | async-start | bytes 524288 | tf_op jit(solution)/shard_map/all_to_all | solution.py:580
  14.1 13.8 %collective-permute-start.2 = (bf16[256,1024]{1,0:T(8,128)(2,1)S(1)}, bf16[256,1024]{1,0:T(8,128)(2,1)S(1)}, u32[]{:S(2)}, u32[]{:S(2)}) collective-permute-start(bf16[256,1024]{1,0:T(8,128)(2,1)S(1)} %copy-done.1), channel_id=1, source_target_pairs={{0,2},{1,3},{2,0},{3,1},{4,6},{5,7},{6,4},{7,5},{8,10},{9,11},{10,... | collective-permute-start | bytes 1572872 | tf_op jit(solution)/shard_map/ppermute | solution.py:34
  15.7 1.3 %collective-permute-start.3 = (bf16[64,1024]{1,0:T(8,128)(2,1)S(1)}, bf16[64,1024]{1,0:T(8,128)(2,1)S(1)}, u32[]{:S(2)}, u32[]{:S(2)}) collective-permute-start(bf16[64,1024]{1,0:T(8,128)(2,1)S(1)} %collective-permute-done.1.refs_2_), channel_id=1, source_target_pairs={{0,1},{1,0},{2,3},{3,2},{4,5},{5,4},{6,7},{7,6},{8,9},{9,8},{10,11... | collective-permute-start | bytes 393224 | tf_op jit(solution)/shard_map/ppermute | solution.py:34
  15.7 20.4 %collective-permute-start.9 = (bf16[256,1024]{1,0:T(8,128)(2,1)S(1)}, bf16[256,1024]{1,0:T(8,128)(2,1)S(1)}, u32[]{:S(2)}, u32[]{:S(2)}) collective-permute-start(bf16[256,1024]{1,0:T(8,128)(2,1)S(1)} %copy-done.1), channel_id=1, source_target_pairs={{0,1},{1,0},{2,3},{3,2},{4,5},{5,4},{6,7},{7,6},{8,9},{9,8},{10,11... | collective-permute-start | bytes 1572872 | tf_op jit(solution)/shard_map/ppermute | solution.py:34
  17.0 0.9 copy-start.8
  22.3 20.5 %copy-start.3 = (bf16[3,1024,256]{2,1,0:T(8,128)(2,1)S(1)}, bf16[3,1024,256]{2,1,0:T(8,128)(2,1)}, u32[]{:S(2)}) copy-start(bf16[3,1024,256]{2,1,0:T(8,128)(2,1)} %refs_7_.3) | copy-start | bytes 4718596
  22.3 20.5 %copy-start.9 = (s32[4]{0:T(128)S(1)}, s32[4]{0:T(128)}, u32[]{:S(2)}) copy-start(s32[4]{0:T(128)} %refs_0_.1) | copy-start | bytes 52
  22.3 12.4 %all-to-all-start.1 = ((bf16[8,32,256]{2,1,0:T(8,128)(2,1)}), bf16[8,32,256]{2,1,0:T(8,128)(2,1)S(1)}, u32[]{:S(2)}, u32[]{:S(2)}) async-start(bf16[8,32,256]{2,1,0:T(8,128)(2,1)} %bitcast.4), calls=%async_computation.1 | async-start | bytes 262144 | tf_op jit(solution)/shard_map/all_to_all | solution.py:589
  27.3 8.2 %collective-permute-start.6 = (bf16[64,2048]{1,0:T(8,128)(2,1)S(1)}, bf16[64,2048]{1,0:T(8,128)(2,1)}, u32[]{:S(2)}, u32[]{:S(2)}) collective-permute-start(bf16[64,2048]{1,0:T(8,128)(2,1)S(1)} %bitcast.11), channel_id=1, source_target_pairs={{0,2},{1,3},{2,0},{3,1},{4,6},{5,7},{6,4},{7,5},{8,10},{9,11},{10,... | collective-permute-start | bytes 786440 | tf_op jit(solution)/shard_map/ppermute | solution.py:34
  34.7 8.1 %collective-permute-start.11 = (bf16[256,1024]{1,0:T(8,128)(2,1)S(1)}, bf16[256,1024]{1,0:T(8,128)(2,1)S(1)}, u32[]{:S(2)}, u32[]{:S(2)}) collective-permute-start(bf16[256,1024]{1,0:T(8,128)(2,1)S(1)} %collective-permute-done.2.refs_5_), channel_id=1, source_target_pairs={{0,1},{1,0},{2,3},{3,2},{4,5},{5,4},{6,7},{7,6},{8,9},{9,8},{10,11... | collective-permute-start | bytes 1572872 | tf_op jit(solution)/shard_map/ppermute | solution.py:34
  34.7 2.3 %collective-permute-start.5 = (bf16[64,2048]{1,0:T(8,128)(2,1)S(1)}, bf16[64,2048]{1,0:T(8,128)(2,1)S(1)}, u32[]{:S(2)}, u32[]{:S(2)}) collective-permute-start(bf16[64,2048]{1,0:T(8,128)(2,1)S(1)} %bitcast.12), channel_id=1, source_target_pairs={{0,1},{1,0},{2,3},{3,2},{4,5},{5,4},{6,7},{7,6},{8,9},{9,8},{10,11... | collective-permute-start | bytes 786440 | tf_op jit(solution)/shard_map/ppermute | solution.py:34
  35.5 2.2 %collective-permute-start.7 = (bf16[64,2048]{1,0:T(8,128)(2,1)}, bf16[64,2048]{1,0:T(8,128)(2,1)S(1)}, u32[]{:S(2)}, u32[]{:S(2)}) collective-permute-start(bf16[64,2048]{1,0:T(8,128)(2,1)} %collective-permute-done.6.refs_2_), channel_id=1, source_target_pairs={{0,1},{1,0},{2,3},{3,2},{4,5},{5,4},{6,7},{7,6},{8,9},{9,8},{10,11... | collective-permute-start | bytes 786440 | tf_op jit(solution)/shard_map/ppermute | solution.py:34
  35.5 1.8 %collective-permute-start.8 = (bf16[256,256]{1,0:T(8,128)(2,1)S(1)}, bf16[256,256]{1,0:T(8,128)(2,1)S(1)}, u32[]{:S(2)}, u32[]{:S(2)}) collective-permute-start(bf16[256,256]{1,0:T(8,128)(2,1)S(1)} %bitcast.24), channel_id=1, source_target_pairs={{0,1},{1,0},{2,3},{3,2},{4,5},{5,4},{6,7},{7,6},{8,9},{9,8},{10,11... | collective-permute-start | bytes 393224 | tf_op jit(solution)/shard_map/ppermute | solution.py:34
  36.0 5.4 %collective-permute-start.4 = (bf16[256,256]{1,0:T(8,128)(2,1)S(1)}, bf16[256,256]{1,0:T(8,128)(2,1)S(1)}, u32[]{:S(2)}, u32[]{:S(2)}) collective-permute-start(bf16[256,256]{1,0:T(8,128)(2,1)S(1)} %bitcast.25), channel_id=1, source_target_pairs={{0,2},{1,3},{2,0},{3,1},{4,6},{5,7},{6,4},{7,5},{8,10},{9,11},{10,... | collective-permute-start | bytes 393224 | tf_op jit(solution)/shard_map/ppermute | solution.py:34
  41.4 1.3 %collective-permute-start.10 = (bf16[256,256]{1,0:T(8,128)(2,1)S(1)}, bf16[256,256]{1,0:T(8,128)(2,1)S(1)}, u32[]{:S(2)}, u32[]{:S(2)}) collective-permute-start(bf16[256,256]{1,0:T(8,128)(2,1)S(1)} %collective-permute-done.4.refs_1_), channel_id=1, source_target_pairs={{0,1},{1,0},{2,3},{3,2},{4,5},{5,4},{6,7},{7,6},{8,9},{9,8},{10,11... | collective-permute-start | bytes 393224 | tf_op jit(solution)/shard_map/ppermute | solution.py:34
  49.2 1.6 %collective-permute-start.12 = (bf16[2,64,1024]{2,1,0:T(8,128)(2,1)S(1)}, bf16[2,64,1024]{2,1,0:T(8,128)(2,1)S(1)}, u32[]{:S(2)}, u32[]{:S(2)}) collective-permute-start(bf16[2,64,1024]{2,1,0:T(8,128)(2,1)S(1)} %get-tuple-element.115), channel_id=1, source_target_pairs={{0,1},{1,0},{2,3},{3,2},{4,5},{5,4},{6,7},{7,6},{8,9},{9,8},{10,11... | collective-permute-start | bytes 786440 | tf_op jit(solution)/shard_map/ppermute | solution.py:34
  50.9 5.6 %collective-permute-start.13 = (bf16[64,1024]{1,0:T(8,128)(2,1)S(1)}, bf16[64,1024]{1,0:T(8,128)(2,1)S(1)}, u32[]{:S(2)}, u32[]{:S(2)}) collective-permute-start(bf16[64,1024]{1,0:T(8,128)(2,1)S(1)} %shard_map.114), channel_id=1, source_target_pairs={{0,2},{1,3},{2,0},{3,1},{4,6},{5,7},{6,4},{7,5},{8,10},{9,11},{10,... | collective-permute-start | bytes 393224 | tf_op jit(solution)/shard_map/ppermute | solution.py:34
  51.5 14.1 %collective-permute-start.14 = (bf16[4,512,128]{2,1,0:T(8,128)(2,1)}, bf16[4,512,128]{2,1,0:T(8,128)(2,1)S(1)}, u32[]{:S(2)}, u32[]{:S(2)}) collective-permute-start(bf16[4,512,128]{2,1,0:T(8,128)(2,1)} %get-tuple-element.130), channel_id=1, source_target_pairs={{0,4},{4,0},{8,12},{12,8},{16,20},{20,16},{24,28},{28,24},{1,5},{5... | collective-permute-start | bytes 1572872 | tf_op jit(solution)/shard_map/ppermute | solution.py:34
  53.2 14.3 %collective-permute-start.15 = (bf16[4,512,128]{2,1,0:T(8,128)(2,1)}, bf16[4,512,128]{2,1,0:T(8,128)(2,1)S(1)}, u32[]{:S(2)}, u32[]{:S(2)}) collective-permute-start(bf16[4,512,128]{2,1,0:T(8,128)(2,1)} %get-tuple-element.131), channel_id=1, source_target_pairs={{0,8},{4,12},{8,0},{12,4},{16,24},{20,28},{24,16},{28,20},{1,9},{5... | collective-permute-start | bytes 1572872 | tf_op jit(solution)/shard_map/ppermute | solution.py:34
  56.5 17.6 %copy-start.4 = (bf16[3,256,256]{2,1,0:T(8,128)(2,1)S(1)}, bf16[3,256,256]{2,1,0:T(8,128)(2,1)}, u32[]{:S(2)}) copy-start(bf16[3,256,256]{2,1,0:T(8,128)(2,1)} %get-tuple-element.139.refs_0_.refs_2_) | copy-start | bytes 1179652
  57.4 13.2 %all-to-all-start.2 = ((bf16[8,8,1024]{2,1,0:T(8,128)(2,1)}), bf16[8,8,1024]{2,1,0:T(8,128)(2,1)S(1)}, u32[]{:S(2)}, u32[]{:S(2)}) async-start(bf16[8,8,1024]{2,1,0:T(8,128)(2,1)} %bitcast.6), calls=%async_computation.2 | async-start | bytes 262144 | tf_op jit(solution)/shard_map/all_to_all | solution.py:613
  68.6 14.7 %copy-start.2 = (bf16[256,1024]{1,0:T(8,128)(2,1)S(1)}, bf16[256,1024]{1,0:T(8,128)(2,1)}, u32[]{:S(2)}) copy-start(bf16[256,1024]{1,0:T(8,128)(2,1)} %refs_1_.2) | copy-start | bytes 1572868
  70.6 5.1 %collective-permute-start.17 = (bf16[64,1024]{1,0:T(8,128)(2,1)S(1)}, bf16[64,1024]{1,0:T(8,128)(2,1)S(1)}, u32[]{:S(2)}, u32[]{:S(2)}) collective-permute-start(bf16[64,1024]{1,0:T(8,128)(2,1)S(1)} %bitcast.20), channel_id=1, source_target_pairs={{0,2},{1,3},{2,0},{3,1},{4,6},{5,7},{6,4},{7,5},{8,10},{9,11},{10,... | collective-permute-start | bytes 393224 | tf_op jit(solution)/shard_map/ppermute | solution.py:34
  72.1 6.6 %collective-permute-start.19 = (bf16[2,512,128]{2,1,0:T(8,128)(2,1)}, bf16[2,512,128]{2,1,0:T(8,128)(2,1)S(1)}, u32[]{:S(2)}, u32[]{:S(2)}) collective-permute-start(bf16[2,512,128]{2,1,0:T(8,128)(2,1)} %get-tuple-element.146), channel_id=1, source_target_pairs={{0,8},{4,12},{8,0},{12,4},{16,24},{20,28},{24,16},{28,20},{1,9},{5... | collective-permute-start | bytes 786440 | tf_op jit(solution)/shard_map/ppermute | solution.py:34
  72.8 6.6 %collective-permute-start.20 = (bf16[2,512,128]{2,1,0:T(8,128)(2,1)}, bf16[2,512,128]{2,1,0:T(8,128)(2,1)S(1)}, u32[]{:S(2)}, u32[]{:S(2)}) collective-permute-start(bf16[2,512,128]{2,1,0:T(8,128)(2,1)} %get-tuple-element.147), channel_id=1, source_target_pairs={{0,4},{4,0},{8,12},{12,8},{16,20},{20,16},{24,28},{28,24},{1,5},{5... | collective-permute-start | bytes 786440 | tf_op jit(solution)/shard_map/ppermute | solution.py:34
  74.1 2.1 %collective-permute-start.16 = (bf16[64,1024]{1,0:T(8,128)(2,1)S(1)}, bf16[64,1024]{1,0:T(8,128)(2,1)S(1)}, u32[]{:S(2)}, u32[]{:S(2)}) collective-permute-start(bf16[64,1024]{1,0:T(8,128)(2,1)S(1)} %bitcast.21), channel_id=1, source_target_pairs={{0,1},{1,0},{2,3},{3,2},{4,5},{5,4},{6,7},{7,6},{8,9},{9,8},{10,11... | collective-permute-start | bytes 393224 | tf_op jit(solution)/shard_map/ppermute | solution.py:34
  75.7 1.6 %collective-permute-start.18 = (bf16[64,1024]{1,0:T(8,128)(2,1)S(1)}, bf16[64,1024]{1,0:T(8,128)(2,1)S(1)}, u32[]{:S(2)}, u32[]{:S(2)}) collective-permute-start(bf16[64,1024]{1,0:T(8,128)(2,1)S(1)} %collective-permute-done.17.refs_2_), channel_id=1, source_target_pairs={{0,1},{1,0},{2,3},{3,2},{4,5},{5,4},{6,7},{7,6},{8,9},{9,8},{10,11... | collective-permute-start | bytes 393224 | tf_op jit(solution)/shard_map/ppermute | solution.py:34
  80.6 7.0 %copy-start = (bf16[3,1024,256]{2,1,0:T(8,128)(2,1)S(1)}, bf16[3,1024,256]{2,1,0:T(8,128)(2,1)}, u32[]{:S(2)}) copy-start(bf16[3,1024,256]{2,1,0:T(8,128)(2,1)} %refs_1_.3) | copy-start | bytes 4718596
  80.6 13.6 %collective-permute-start.21 = (bf16[1024,128]{1,0:T(8,128)(2,1)S(1)}, bf16[1024,128]{1,0:T(8,128)(2,1)S(1)}, u32[]{:S(2)}, u32[]{:S(2)}) collective-permute-start(bf16[1024,128]{1,0:T(8,128)(2,1)S(1)} %get-tuple-element.161), channel_id=1, source_target_pairs={{0,16},{4,20},{8,24},{12,28},{16,0},{20,4},{24,8},{28,12},{1,17},{... | collective-permute-start | bytes 786440 | tf_op jit(solution)/shard_map/ppermute | solution.py:34
  83.0 11.9 %collective-permute-start.26 = (bf16[4,256,128]{2,1,0:T(8,128)(2,1)S(1)}, bf16[4,256,128]{2,1,0:T(8,128)(2,1)S(1)}, u32[]{:S(2)}, u32[]{:S(2)}) collective-permute-start(bf16[4,256,128]{2,1,0:T(8,128)(2,1)S(1)} %get-tuple-element.170), channel_id=1, source_target_pairs={{0,4},{4,0},{8,12},{12,8},{16,20},{20,16},{24,28},{28,24},{1,5},{5... | collective-permute-start | bytes 786440 | tf_op jit(solution)/shard_map/ppermute | solution.py:34
  85.8 8.4 %copy-start.6 = (bf16[256,1024]{1,0:T(8,128)(2,1)S(1)}, bf16[256,1024]{1,0:T(8,128)(2,1)}, u32[]{:S(2)}) copy-start(bf16[256,1024]{1,0:T(8,128)(2,1)} %get-tuple-element.157.refs_4_.refs_1_) | copy-start | bytes 1572868
  85.8 13.3 %collective-permute-start.25 = (bf16[4,320,128]{2,1,0:T(8,128)(2,1)S(1)}, bf16[4,320,128]{2,1,0:T(8,128)(2,1)S(1)}, u32[]{:S(2)}, u32[]{:S(2)}) collective-permute-start(bf16[4,320,128]{2,1,0:T(8,128)(2,1)S(1)} %get-tuple-element.169), channel_id=1, source_target_pairs={{0,8},{4,12},{8,0},{12,4},{16,24},{20,28},{24,16},{28,20},{1,9},{5... | collective-permute-start | bytes 983048 | tf_op jit(solution)/shard_map/ppermute | solution.py:34
  86.4 12.7 %collective-permute-start.24 = (bf16[4,448,128]{2,1,0:T(8,128)(2,1)S(1)}, bf16[4,448,128]{2,1,0:T(8,128)(2,1)S(1)}, u32[]{:S(2)}, u32[]{:S(2)}) collective-permute-start(bf16[4,448,128]{2,1,0:T(8,128)(2,1)S(1)} %get-tuple-element.168), channel_id=1, source_target_pairs={{0,4},{4,0},{8,12},{12,8},{16,20},{20,16},{24,28},{28,24},{1,5},{5... | collective-permute-start | bytes 1376264 | tf_op jit(solution)/shard_map/ppermute | solution.py:34
  99.4 13.9 %copy-start.5 = (bf16[1,64,1024]{2,1,0:T(8,128)(2,1)S(1)}, bf16[1,64,1024]{2,1,0:T(8,128)(2,1)}, u32[]{:S(2)}) copy-start(bf16[1,64,1024]{2,1,0:T(8,128)(2,1)} %param.7) | copy-start | bytes 393220
  99.4 7.8 %collective-permute-start.27 = (bf16[2,448,128]{2,1,0:T(8,128)(2,1)S(1)}, bf16[2,448,128]{2,1,0:T(8,128)(2,1)S(1)}, u32[]{:S(2)}, u32[]{:S(2)}) collective-permute-start(bf16[2,448,128]{2,1,0:T(8,128)(2,1)S(1)} %get-tuple-element.173), channel_id=1, source_target_pairs={{0,8},{4,12},{8,0},{12,4},{16,24},{20,28},{24,16},{28,20},{1,9},{5... | collective-permute-start | bytes 688136 | tf_op jit(solution)/shard_map/ppermute | solution.py:34
  100.0 8.2 %collective-permute-start.22 = (bf16[2,64,1024]{2,1,0:T(8,128)(2,1)S(1)}, bf16[2,64,1024]{2,1,0:T(8,128)(2,1)S(1)}, u32[]{:S(2)}, u32[]{:S(2)}) collective-permute-start(bf16[2,64,1024]{2,1,0:T(8,128)(2,1)S(1)} %get-tuple-element.163), channel_id=1, source_target_pairs={{0,1},{1,0},{2,3},{3,2},{4,5},{5,4},{6,7},{7,6},{8,9},{9,8},{10,11... | collective-permute-start | bytes 786440 | tf_op jit(solution)/shard_map/ppermute | solution.py:34
  100.0 6.6 %collective-permute-start.28 = (bf16[2,320,128]{2,1,0:T(8,128)(2,1)S(1)}, bf16[2,320,128]{2,1,0:T(8,128)(2,1)S(1)}, u32[]{:S(2)}, u32[]{:S(2)}) collective-permute-start(bf16[2,320,128]{2,1,0:T(8,128)(2,1)S(1)} %get-tuple-element.174), channel_id=1, source_target_pairs={{0,4},{4,0},{8,12},{12,8},{16,20},{20,16},{24,28},{28,24},{1,5},{5... | collective-permute-start | bytes 491528 | tf_op jit(solution)/shard_map/ppermute | solution.py:34
  100.7 9.3 %collective-permute-start.30 = (bf16[2,256,128]{2,1,0:T(8,128)(2,1)S(1)}, bf16[2,256,128]{2,1,0:T(8,128)(2,1)S(1)}, u32[]{:S(2)}, u32[]{:S(2)}) collective-permute-start(bf16[2,256,128]{2,1,0:T(8,128)(2,1)S(1)} %get-tuple-element.178), channel_id=1, source_target_pairs={{0,16},{4,20},{8,24},{12,28},{16,0},{20,4},{24,8},{28,12},{1,17},{... | collective-permute-start | bytes 393224 | tf_op jit(solution)/shard_map/ppermute | solution.py:34
  107.4 11.1 %collective-permute-start.29 = (bf16[768,128]{1,0:T(8,128)(2,1)S(1)}, bf16[768,128]{1,0:T(8,128)(2,1)S(1)}, u32[]{:S(2)}, u32[]{:S(2)}) collective-permute-start(bf16[768,128]{1,0:T(8,128)(2,1)S(1)} %get-tuple-element.176), channel_id=1, source_target_pairs={{0,16},{4,20},{8,24},{12,28},{16,0},{20,4},{24,8},{28,12},{1,17},{... | collective-permute-start | bytes 589832 | tf_op jit(solution)/shard_map/ppermute | solution.py:34
  108.3 5.0 %collective-permute-start.23 = (bf16[64,1024]{1,0:T(8,128)(2,1)S(1)}, bf16[64,1024]{1,0:T(8,128)(2,1)S(1)}, u32[]{:S(2)}, u32[]{:S(2)}) collective-permute-start(bf16[64,1024]{1,0:T(8,128)(2,1)S(1)} %shard_map.123), channel_id=1, source_target_pairs={{0,2},{1,3},{2,0},{3,1},{4,6},{5,7},{6,4},{7,5},{8,10},{9,11},{10,... | collective-permute-start | bytes 393224 | tf_op jit(solution)/shard_map/ppermute | solution.py:34
  110.1 4.6 %collective-permute-start.31 = (bf16[1,256,128]{2,1,0:T(8,128)(2,1)S(1)}, bf16[1,256,128]{2,1,0:T(8,128)(2,1)S(1)}, u32[]{:S(2)}, u32[]{:S(2)}) collective-permute-start(bf16[1,256,128]{2,1,0:T(8,128)(2,1)S(1)} %get-tuple-element.180), channel_id=1, source_target_pairs={{0,8},{4,12},{8,0},{12,4},{16,24},{20,28},{24,16},{28,20},{1,9},{5... | collective-permute-start | bytes 196616 | tf_op jit(solution)/shard_map/ppermute | solution.py:34

commit v4 on v2

--- a/solution.py
+++ b/solution.py
@@ -435,7 +435,7 @@
 
 def qkv_parts(grads):
     flat = jnp.concatenate([grad.T for grad in grads], 0)
-    first = 7 * flat.shape[0] // 12
+    first = 13 * flat.shape[0] // 24
     return flat[:first], flat[first:]
 
 
@@ -446,7 +446,7 @@
 
 
 def qkv_part_shapes(width, dim, groups):
-    first = 7 * 3 * width // 12
+    first = 13 * 3 * width // 24
     return tuple(
         shape((groups // 2, rows, dim // groups)) for rows in (first, 3 * width - first)
     )
@@ -632,15 +632,18 @@
     if halves:
         after = lax.optimization_barrier
         send_x, keep_x = normed_back(s_grads, spatial_qkv, mp)
-        s_grads, t_came = after((s_grads, t_came))
+        o_send, o_keep = halve([o_chunks[1]], [swap(o_chunks[0], "frames", 1)])
+        s_grads, send_x, keep_x, t_came, o_send, o_keep = after(
+            (s_grads, send_x, keep_x, t_came, o_send, o_keep)
+        )
+        o_came = swap(o_send, "frames", 4)
         t_qkv, t_out = last_sums([(t_keep, t_came)])
         s_kept = qkv_keeps(s_grads, normed_x, groups, 50_000_000_000)
         came = [swap(s_sent[0], "frames", 1), swap(s_sent[1], "frames", 2)]
-        came.append(swap(o_chunks[0], "frames", 1))
-        *sends, keep_a, keep_b, o_keep = halve([*s_kept, o_chunks[1]], came)
-        came = [swap(send, "frames", by) for send, by in zip(sends, (2, 1, 4))]
-        s_send, s_keep = halve([keep_a, keep_b], came[:2], merged=True)
-        o_send, o_keep = halve([o_keep], came[2:])
+        send_a, send_b, keep_a, keep_b = halve(s_kept, came)
+        came = [swap(send_a, "frames", 2), swap(send_b, "frames", 1)]
+        s_send, s_keep = halve([keep_a, keep_b], came, merged=True)
+        o_send, o_keep = halve([o_keep], [o_came])
         s_qkv, s_out = last_sums([
             (s_keep, swap(s_send, "frames", 4)), (o_keep, swap(o_send, "frames", 2))
         ])

time: 119 us -> 118 us (level)
  waiting for transfers between devices: 49 us -> 46.3 us
  starting transfers between devices: 41 us -> 42.8 us
    ppermute x32, waiting for transfers between devices: 37 us -> 34.3 us  [swap(): return lax.ppermute(value, axis, [(i, i ^ by) for i in range(size)])]
    ppermute x32, starting transfers between devices: 25.9 us -> 27.7 us  [swap(): return lax.ppermute(value, axis, [(i, i ^ by) for i in range(size)])]
    pallas_call x21 -> x22, Pallas kernels: 27.5 us -> 27.5 us  [run(): pl.pallas_call(wrapped, out_shape=tuple((pltpu.HBM(o.shape, o.dtype) if w...]
  transfers between devices with their start and end apart: 35 -> 35, of which waited for: 22 -> 22; matrix products, arithmetic and copies ran while one was open for 0% -> 0% of each run, Pallas kernels for 16% -> 17%
where the time goes in v4:
time: 118 us
  waiting for transfers between devices  46.3 us (39%)
  starting transfers between devices  42.8 us (36%)
  Pallas kernels  27.5 us (23%)
    ppermute x32, waiting for transfers between devices, swap(): return lax.ppermute(value, axis, [(i, i ^ by) for i in range(size)])  34.3 us
    ppermute x32, starting transfers between devices, swap(): return lax.ppermute(value, axis, [(i, i ^ by) for i in range(size)])  27.7 us
    pallas_call x22, Pallas kernels, run(): pl.pallas_call(wrapped, out_shape=tuple((pltpu.HBM(o.shape, o.dtype) if w...  27.5 us
    all_to_all x1, waiting for transfers between devices, shards(): lax.all_to_all(attn_send.reshape(groups, mp * per, width), 'frames', 0, 0...  6.83 us
    all_to_all x1, starting transfers between devices, shards(): lax.all_to_all(xg.reshape(groups, per, 2 * dim), 'frames', 0, 0, tiled=True)  6.03 us
    all_to_all x1, starting transfers between devices, shards(): lax.all_to_all(attn_send.reshape(groups, mp * per, width), 'frames', 0, 0...  4.78 us
    all_to_all x1, starting transfers between devices, shards(): lax.all_to_all(d_hidden.reshape(groups, per, dim), 'frames', 0, 0, tiled=...  4.24 us
    all_to_all x1, waiting for transfers between devices, shards(): lax.all_to_all(d_hidden.reshape(groups, per, dim), 'frames', 0, 0, tiled=...  3.76 us
  transfers between devices with their start and end apart: 35, of which 22 were waited for; matrix products, arithmetic and copies ran while one was open for 0% of the time, Pallas kernels for 17%

profile of v4, /device:TPU:0, one launch (start us, length us, event | category | flops | bytes accessed | tf_op | source)
XLA Modules:
  0.0 117.7 jit_solution(15389363668316520592)
XLA Ops:
  0.6 3.0 %collective-permute-start.1 = (bf16[64,1024]{1,0:T(8,128)(2,1)}, bf16[64,1024]{1,0:T(8,128)(2,1)S(1)}, u32[]{:S(2)}, u32[]{:S(2)}) collective-permute-start(bf16[64,1024]{1,0:T(8,128)(2,1)} %bitcast.19), channel_id=1, source_target_pairs={{0,2},{1,3},{2,0},{3,1},{4,6},{5,7},{6,4},{7,5},{8,10},{9,11},{10,... | collective-permute-start | bytes 393224 | tf_op jit(solution)/shard_map/ppermute | solution.py:34
  3.7 1.7 %shard_map.110 = bf16[64,2048]{1,0:T(8,128)(2,1)} custom-call(bf16[64,1024]{1,0:T(8,128)(2,1)} %bitcast.21, bf16[64,1024]{1,0:T(8,128)(2,1)} %bitcast.29), custom_call_target="tpu_custom_call" | custom-call | flops 1000 | bytes 1000 | tf_op jit(solution)/shard_map/pallas_call | solution.py:110
  5.4 2.0 %collective-permute-done.1.refs_2_ = bf16[64,1024]{1,0:T(8,128)(2,1)S(1)} collective-permute-done((bf16[64,1024]{1,0:T(8,128)(2,1)}, bf16[64,1024]{1,0:T(8,128)(2,1)S(1)}, u32[]{:S(2)}, u32[]{:S(2)}) %collective-permute-start.1) | collective-permute-done | bytes 131104 | tf_op jit(solution)/shard_map/ppermute | solution.py:34
  7.4 6.0 %all-to-all-start = ((bf16[8,8,2048]{2,1,0:T(8,128)(2,1)}), bf16[8,8,2048]{2,1,0:T(8,128)(2,1)S(1)}, u32[]{:S(2)}, u32[]{:S(2)}) async-start(bf16[8,8,2048]{2,1,0:T(8,128)(2,1)} %bitcast.2), calls=%async_computation | async-start | bytes 524288 | tf_op jit(solution)/shard_map/all_to_all | solution.py:576
  13.4 1.5 %collective-permute-start.2 = (bf16[256,1024]{1,0:T(8,128)(2,1)}, bf16[256,1024]{1,0:T(8,128)(2,1)S(1)}, u32[]{:S(2)}, u32[]{:S(2)}) collective-permute-start(bf16[256,1024]{1,0:T(8,128)(2,1)} %refs_1_.2), channel_id=1, source_target_pairs={{0,2},{1,3},{2,0},{3,1},{4,6},{5,7},{6,4},{7,5},{8,10},{9,11},{10,... | collective-permute-start | bytes 1572872 | tf_op jit(solution)/shard_map/ppermute | solution.py:34
  14.9 0.5 collective-permute-start.9
  15.4 1.0 collective-permute-done.3.refs_3_
  16.4 3.8 %shard_map.111 = (bf16[256,1024]{1,0:T(8,128)(2,1)}, bf16[3,256,256]{2,1,0:T(8,128)(2,1)}, bf16[256,256]{1,0:T(8,128)(2,1)}) custom-call(bf16[64,1024]{1,0:T(8,128)(2,1)} %bitcast.22, bf16[64,1024]{1,0:T(8,128)(2,1)S(1)} %collective-permute-done.refs_1_, bf16[64,1024]{1,0:T(8,128)(2,1)S(1)} %collective-permute-done.1.refs_2_, ...), custom_call_target="tpu_custom_call" | custom-call | flops 1000 | bytes 1000 | tf_op jit(solution)/shard_map/pallas_call | solution.py:110
  20.2 1.4 %all-to-all-done = bf16[8,8,2048]{2,1,0:T(8,128)(2,1)S(1)} async-done(((bf16[8,8,2048]{2,1,0:T(8,128)(2,1)}), bf16[8,8,2048]{2,1,0:T(8,128)(2,1)S(1)}, u32[]{:S(2)}, u32[]{:S(2)}) %all-to-all-start) | async-done | bytes 262176 | tf_op jit(solution)/shard_map/all_to_all | solution.py:576
  21.6 4.8 %all-to-all-start.1 = ((bf16[8,32,256]{2,1,0:T(8,128)(2,1)}), bf16[8,32,256]{2,1,0:T(8,128)(2,1)S(1)}, u32[]{:S(2)}, u32[]{:S(2)}) async-start(bf16[8,32,256]{2,1,0:T(8,128)(2,1)} %bitcast.4), calls=%async_computation.1 | async-start | bytes 262144 | tf_op jit(solution)/shard_map/all_to_all | solution.py:585
  26.4 0.5 collective-permute-start.6
  26.9 6.8 %all-to-all-done.1 = bf16[8,32,256]{2,1,0:T(8,128)(2,1)S(1)} async-done(((bf16[8,32,256]{2,1,0:T(8,128)(2,1)}), bf16[8,32,256]{2,1,0:T(8,128)(2,1)S(1)}, u32[]{:S(2)}, u32[]{:S(2)}) %all-to-all-start.1) | async-done | bytes 131104 | tf_op jit(solution)/shard_map/all_to_all | solution.py:585
  33.8 0.5 collective-permute-start.5
  34.3 0.2 collective-permute-done.6.refs_2_
  34.5 0.5 collective-permute-start.8
  35.0 0.5 collective-permute-start.4
  35.5 0.5 collective-permute-done.5.refs_1_
  36.0 0.6 collective-permute-done.8.refs_6_
  36.6 2.4 %shard_map.112 = (f32[256,1024]{1,0:T(8,128)S(1)}, bf16[256,1024]{1,0:T(8,128)(2,1)S(1)}, bf16[256,256]{1,0:T(8,128)(2,1)S(1)}) custom-call(bf16[64,2048]{1,0:T(8,128)(2,1)S(1)} %bitcast.13, bf16[64,2048]{1,0:T(8,128)(2,1)S(1)} %collective-permute-done.5.refs_1_, bf16[64,2048]{1,0:T(8,128)(2,1)S(1)} %collective-permute-done.6.refs_2_, ...), custom_call_target="tpu_custom_call" | custom-call | flops 1000 | bytes 1000 | tf_op jit(solution)/shard_map/pallas_call | solution.py:110
  39.0 1.4 %collective-permute-done.4.refs_1_ = bf16[256,256]{1,0:T(8,128)(2,1)S(1)} collective-permute-done((bf16[256,256]{1,0:T(8,128)(2,1)S(1)}, bf16[256,256]{1,0:T(8,128)(2,1)S(1)}, u32[]{:S(2)}, u32[]{:S(2)}) %collective-permute-start.4) | collective-permute-done | bytes 131104 | tf_op jit(solution)/shard_map/ppermute | solution.py:34
  40.4 1.3 %collective-permute-done.10.refs_2_ = bf16[256,256]{1,0:T(8,128)(2,1)S(1)} collective-permute-done((bf16[256,256]{1,0:T(8,128)(2,1)S(1)}, bf16[256,256]{1,0:T(8,128)(2,1)S(1)}, u32[]{:S(2)}, u32[]{:S(2)}) %collective-permute-start.10) | collective-permute-done | bytes 131104 | tf_op jit(solution)/shard_map/ppermute | solution.py:34
  41.8 6.4 %shard_map.113 = (bf16[2,64,1024]{2,1,0:T(8,128)(2,1)S(1)}, bf16[2,64,1024]{2,1,0:T(8,128)(2,1)S(1)}, bf16[256,1024]{1,0:T(8,128)(2,1)S(1)}, bf16[64,1024]{1,0:T...) custom-call(s32[4]{0:T(128)S(1)} %copy-done.6, ...), custom_call_target="tpu_custom_call" | custom-call | flops 1000 | bytes 1000 | tf_op jit(solution)/shard_map/pallas_call | solution.py:110
  48.2 0.2 collective-permute-start.12
  48.4 1.8 %collective-permute-start.14 = (bf16[4,512,128]{2,1,0:T(8,128)(2,1)}, bf16[4,512,128]{2,1,0:T(8,128)(2,1)S(1)}, u32[]{:S(2)}, u32[]{:S(2)}) collective-permute-start(bf16[4,512,128]{2,1,0:T(8,128)(2,1)} %get-tuple-element.122), channel_id=1, source_target_pairs={{0,4},{4,0},{8,12},{12,8},{16,20},{20,16},{24,28},{28,24},{1,5},{5... | collective-permute-start | bytes 1572872 | tf_op jit(solution)/shard_map/ppermute | solution.py:34
  50.2 1.5 %collective-permute-start.15 = (bf16[4,512,128]{2,1,0:T(8,128)(2,1)}, bf16[4,512,128]{2,1,0:T(8,128)(2,1)S(1)}, u32[]{:S(2)}, u32[]{:S(2)}) collective-permute-start(bf16[4,512,128]{2,1,0:T(8,128)(2,1)} %get-tuple-element.123), channel_id=1, source_target_pairs={{0,8},{4,12},{8,0},{12,4},{16,24},{20,28},{24,16},{28,20},{1,9},{5... | collective-permute-start | bytes 1572872 | tf_op jit(solution)/shard_map/ppermute | solution.py:34
  51.7 0.6 collective-permute-start.13
  52.3 0.8 shard_map.115
  53.1 3.9 %collective-permute-done.13.refs_2_ = bf16[64,1024]{1,0:T(8,128)(2,1)S(1)} collective-permute-done((bf16[64,1024]{1,0:T(8,128)(2,1)S(1)}, bf16[64,1024]{1,0:T(8,128)(2,1)S(1)}, u32[]{:S(2)}, u32[]{:S(2)}) %collective-permute-start.13) | collective-permute-done | bytes 131104 | tf_op jit(solution)/shard_map/ppermute | solution.py:34
  57.0 0.9 shard_map.116
  57.8 4.2 %all-to-all-start.2 = ((bf16[8,8,1024]{2,1,0:T(8,128)(2,1)}), bf16[8,8,1024]{2,1,0:T(8,128)(2,1)S(1)}, u32[]{:S(2)}, u32[]{:S(2)}) async-start(bf16[8,8,1024]{2,1,0:T(8,128)(2,1)} %bitcast.6), calls=%async_computation.2 | async-start | bytes 262144 | tf_op jit(solution)/shard_map/all_to_all | solution.py:609
  62.1 0.7 collective-permute-done.14.refs_2_
  62.8 1.7 %collective-permute-done.15.refs_3_ = bf16[4,512,128]{2,1,0:T(8,128)(2,1)S(1)} collective-permute-done((bf16[4,512,128]{2,1,0:T(8,128)(2,1)}, bf16[4,512,128]{2,1,0:T(8,128)(2,1)S(1)}, u32[]{:S(2)}, u32[]{:S(2)}) %collective-permute-start.15) | collective-permute-done | bytes 524320 | tf_op jit(solution)/shard_map/ppermute | solution.py:34
  64.5 1.1 shard_map.117
  65.7 3.8 %all-to-all-done.2 = bf16[8,8,1024]{2,1,0:T(8,128)(2,1)S(1)} async-done(((bf16[8,8,1024]{2,1,0:T(8,128)(2,1)}), bf16[8,8,1024]{2,1,0:T(8,128)(2,1)S(1)}, u32[]{:S(2)}, u32[]{:S(2)}) %all-to-all-start.2) | async-done | bytes 131104 | tf_op jit(solution)/shard_map/all_to_all | solution.py:609
  69.4 0.5 collective-permute-start.17
  69.9 1.3 %collective-permute-start.20 = (bf16[2,512,128]{2,1,0:T(8,128)(2,1)}, bf16[2,512,128]{2,1,0:T(8,128)(2,1)S(1)}, u32[]{:S(2)}, u32[]{:S(2)}) collective-permute-start(bf16[2,512,128]{2,1,0:T(8,128)(2,1)} %get-tuple-element.139), channel_id=1, source_target_pairs={{0,4},{4,0},{8,12},{12,8},{16,20},{20,16},{24,28},{28,24},{1,5},{5... | collective-permute-start | bytes 786440 | tf_op jit(solution)/shard_map/ppermute | solution.py:34
  71.3 1.5 %shard_map.118 = (f32[4,256,256]{2,1,0:T(8,128)S(1)}, bf16[256,256]{1,0:T(8,128)(2,1)S(1)}) custom-call(bf16[3,256,256]{2,1,0:T(8,128)(2,1)S(1)} %copy-done.3, bf16[256,256]{1,0:T(8,128)(2,1)} %get-tuple-element.132.refs_1_), custom_call_target="tpu_custom_call" | custom-call | flops 1000 | bytes 1000 | tf_op jit(solution)/shard_map/pallas_call | solution.py:110
  72.8 1.6 %collective-permute-done.17.refs_2_ = bf16[64,1024]{1,0:T(8,128)(2,1)S(1)} collective-permute-done((bf16[64,1024]{1,0:T(8,128)(2,1)S(1)}, bf16[64,1024]{1,0:T(8,128)(2,1)S(1)}, u32[]{:S(2)}, u32[]{:S(2)}) %collective-permute-start.17) | collective-permute-done | bytes 131104 | tf_op jit(solution)/shard_map/ppermute | solution.py:34
  74.4 1.3 %collective-permute-done.18.refs_3_ = bf16[64,1024]{1,0:T(8,128)(2,1)S(1)} collective-permute-done((bf16[64,1024]{1,0:T(8,128)(2,1)S(1)}, bf16[64,1024]{1,0:T(8,128)(2,1)S(1)}, u32[]{:S(2)}, u32[]{:S(2)}) %collective-permute-start.18) | collective-permute-done | bytes 131104 | tf_op jit(solution)/shard_map/ppermute | solution.py:34
  75.7 0.5 shard_map.119
  76.3 0.3 collective-permute-done.19.refs_2_
  76.5 1.3 %collective-permute-start.22 = (bf16[4,256,128]{2,1,0:T(8,128)(2,1)S(1)}, bf16[4,256,128]{2,1,0:T(8,128)(2,1)S(1)}, u32[]{:S(2)}, u32[]{:S(2)}) collective-permute-start(bf16[4,256,128]{2,1,0:T(8,128)(2,1)S(1)} %get-tuple-element.155), channel_id=1, source_target_pairs={{0,4},{4,0},{8,12},{12,8},{16,20},{20,16},{24,28},{28,24},{1,5},{5... | collective-permute-start | bytes 786440 | tf_op jit(solution)/shard_map/ppermute | solution.py:34
  77.8 1.2 shard_map.120
  79.0 1.1 collective-permute-start.21
  80.1 2.4 %shard_map.121 = (bf16[3,256,256]{2,1,0:T(8,128)(2,1)S(1)}, bf16[4,416,128]{2,1,0:T(8,128)(2,1)S(1)}, bf16[4,352,128]{2,1,0:T(8,128)(2,1)S(1)}) custom-call(bf16[256,1024]{1,0:T(8,128)(2,1)S(1)} %get-tuple-element.147.refs_0_, bf16[256,1024]{1,0:T(8,128)(2,1)S(1)} %copy-done.1, bf16[3,256,256]{2,1,0:T(8,128)(2,1)S(1)} %copy-done.3, ...), custom_call_target="tpu_custom_call" | custom-call | flops 1000 | bytes 1000 | tf_op jit(solution)/shard_map/pallas_call | solution.py:110
  82.5 0.4 collective-permute-start.26
  82.9 1.8 %collective-permute-start.25 = (bf16[4,416,128]{2,1,0:T(8,128)(2,1)S(1)}, bf16[4,416,128]{2,1,0:T(8,128)(2,1)S(1)}, u32[]{:S(2)}, u32[]{:S(2)}) collective-permute-start(bf16[4,416,128]{2,1,0:T(8,128)(2,1)S(1)} %get-tuple-element.163), channel_id=1, source_target_pairs={{0,4},{4,0},{8,12},{12,8},{16,20},{20,16},{24,28},{28,24},{1,5},{5... | collective-permute-start | bytes 1277960 | tf_op jit(solution)/shard_map/ppermute | solution.py:34
  84.7 0.7 shard_map.122
  85.5 7.1 %collective-permute-done.21.refs_1_ = bf16[1024,128]{1,0:T(8,128)(2,1)S(1)} collective-permute-done((bf16[1024,128]{1,0:T(8,128)(2,1)S(1)}, bf16[1024,128]{1,0:T(8,128)(2,1)S(1)}, u32[]{:S(2)}, u32[]{:S(2)}) %collective-permute-start.21) | collective-permute-done | bytes 262176 | tf_op jit(solution)/shard_map/ppermute | solution.py:34
  92.6 0.6 shard_map.126
  93.2 2.3 %collective-permute-done.26.refs_3_ = bf16[4,352,128]{2,1,0:T(8,128)(2,1)S(1)} collective-permute-done((bf16[4,352,128]{2,1,0:T(8,128)(2,1)S(1)}, bf16[4,352,128]{2,1,0:T(8,128)(2,1)S(1)}, u32[]{:S(2)}, u32[]{:S(2)}) %collective-permute-start.26) | collective-permute-done | bytes 360480 | tf_op jit(solution)/shard_map/ppermute | solution.py:34
  95.6 0.2 shard_map.127
  95.9 2.4 %collective-permute-start.28 = (bf16[2,352,128]{2,1,0:T(8,128)(2,1)S(1)}, bf16[2,352,128]{2,1,0:T(8,128)(2,1)S(1)}, u32[]{:S(2)}, u32[]{:S(2)}) collective-permute-start(bf16[2,352,128]{2,1,0:T(8,128)(2,1)S(1)} %get-tuple-element.168), channel_id=1, source_target_pairs={{0,4},{4,0},{8,12},{12,8},{16,20},{20,16},{24,28},{28,24},{1,5},{5... | collective-permute-start | bytes 540680 | tf_op jit(solution)/shard_map/ppermute | solution.py:34
  98.4 1.9 %collective-permute-start.30 = (bf16[2,256,128]{2,1,0:T(8,128)(2,1)S(1)}, bf16[2,256,128]{2,1,0:T(8,128)(2,1)S(1)}, u32[]{:S(2)}, u32[]{:S(2)}) collective-permute-start(bf16[2,256,128]{2,1,0:T(8,128)(2,1)S(1)} %get-tuple-element.172), channel_id=1, source_target_pairs={{0,16},{4,20},{8,24},{12,28},{16,0},{20,4},{24,8},{28,12},{1,17},{... | collective-permute-start | bytes 393224 | tf_op jit(solution)/shard_map/ppermute | solution.py:34
  100.3 3.2 %collective-permute-done.28.refs_3_ = bf16[2,352,128]{2,1,0:T(8,128)(2,1)S(1)} collective-permute-done((bf16[2,352,128]{2,1,0:T(8,128)(2,1)S(1)}, bf16[2,352,128]{2,1,0:T(8,128)(2,1)S(1)}, u32[]{:S(2)}, u32[]{:S(2)}) %collective-permute-start.28) | collective-permute-done | bytes 180256 | tf_op jit(solution)/shard_map/ppermute | solution.py:34
  103.5 0.1 shard_map.128
  103.6 3.8 %collective-permute-start.29 = (bf16[768,128]{1,0:T(8,128)(2,1)S(1)}, bf16[768,128]{1,0:T(8,128)(2,1)S(1)}, u32[]{:S(2)}, u32[]{:S(2)}) collective-permute-start(bf16[768,128]{1,0:T(8,128)(2,1)S(1)} %get-tuple-element.170), channel_id=1, source_target_pairs={{0,16},{4,20},{8,24},{12,28},{16,0},{20,4},{24,8},{28,12},{1,17},{... | collective-permute-start | bytes 589832 | tf_op jit(solution)/shard_map/ppermute | solution.py:34
  107.5 1.3 %collective-permute-start.24 = (bf16[64,1024]{1,0:T(8,128)(2,1)S(1)}, bf16[64,1024]{1,0:T(8,128)(2,1)S(1)}, u32[]{:S(2)}, u32[]{:S(2)}) collective-permute-start(bf16[64,1024]{1,0:T(8,128)(2,1)S(1)} %shard_map.124), channel_id=1, source_target_pairs={{0,2},{1,3},{2,0},{3,1},{4,6},{5,7},{6,4},{7,5},{8,10},{9,11},{10,... | collective-permute-start | bytes 393224 | tf_op jit(solution)/shard_map/ppermute | solution.py:34
  108.9 0.6 collective-permute-start.31
  109.5 1.0 shard_map.131
  110.5 2.0 %collective-permute-done.24.refs_2_ = bf16[64,1024]{1,0:T(8,128)(2,1)S(1)} collective-permute-done((bf16[64,1024]{1,0:T(8,128)(2,1)S(1)}, bf16[64,1024]{1,0:T(8,128)(2,1)S(1)}, u32[]{:S(2)}, u32[]{:S(2)}) %collective-permute-start.24) | collective-permute-done | bytes 131104 | tf_op jit(solution)/shard_map/ppermute | solution.py:34
  112.6 0.9 shard_map.125
  113.6 3.0 %collective-permute-done.29.refs_1_ = bf16[768,128]{1,0:T(8,128)(2,1)S(1)} collective-permute-done((bf16[768,128]{1,0:T(8,128)(2,1)S(1)}, bf16[768,128]{1,0:T(8,128)(2,1)S(1)}, u32[]{:S(2)}, u32[]{:S(2)}) %collective-permute-start.29) | collective-permute-done | bytes 196640 | tf_op jit(solution)/shard_map/ppermute | solution.py:34
  116.5 1.0 shard_map.130
  (42 shorter events, 0.6 us)
Async XLA Ops:
  0.6 6.7 %collective-permute-start.1 = (bf16[64,1024]{1,0:T(8,128)(2,1)}, bf16[64,1024]{1,0:T(8,128)(2,1)S(1)}, u32[]{:S(2)}, u32[]{:S(2)}) collective-permute-start(bf16[64,1024]{1,0:T(8,128)(2,1)} %bitcast.19), channel_id=1, source_target_pairs={{0,2},{1,3},{2,0},{3,1},{4,6},{5,7},{6,4},{7,5},{8,10},{9,11},{10,... | collective-permute-start | bytes 393224 | tf_op jit(solution)/shard_map/ppermute | solution.py:34
  3.7 3.7 %collective-permute-start = (bf16[64,1024]{1,0:T(8,128)(2,1)}, bf16[64,1024]{1,0:T(8,128)(2,1)S(1)}, u32[]{:S(2)}, u32[]{:S(2)}) collective-permute-start(bf16[64,1024]{1,0:T(8,128)(2,1)} %bitcast.20), channel_id=1, source_target_pairs={{0,1},{1,0},{2,3},{3,2},{4,5},{5,4},{6,7},{7,6},{8,9},{9,8},{10,11... | collective-permute-start | bytes 393224 | tf_op jit(solution)/shard_map/ppermute | solution.py:34
  7.4 14.3 %all-to-all-start = ((bf16[8,8,2048]{2,1,0:T(8,128)(2,1)}), bf16[8,8,2048]{2,1,0:T(8,128)(2,1)S(1)}, u32[]{:S(2)}, u32[]{:S(2)}) async-start(bf16[8,8,2048]{2,1,0:T(8,128)(2,1)} %bitcast.2), calls=%async_computation | async-start | bytes 524288 | tf_op jit(solution)/shard_map/all_to_all | solution.py:576
  13.4 13.5 %collective-permute-start.2 = (bf16[256,1024]{1,0:T(8,128)(2,1)}, bf16[256,1024]{1,0:T(8,128)(2,1)S(1)}, u32[]{:S(2)}, u32[]{:S(2)}) collective-permute-start(bf16[256,1024]{1,0:T(8,128)(2,1)} %refs_1_.2), channel_id=1, source_target_pairs={{0,2},{1,3},{2,0},{3,1},{4,6},{5,7},{6,4},{7,5},{8,10},{9,11},{10,... | collective-permute-start | bytes 1572872 | tf_op jit(solution)/shard_map/ppermute | solution.py:34
  14.9 1.5 %collective-permute-start.3 = (bf16[64,1024]{1,0:T(8,128)(2,1)S(1)}, bf16[64,1024]{1,0:T(8,128)(2,1)S(1)}, u32[]{:S(2)}, u32[]{:S(2)}) collective-permute-start(bf16[64,1024]{1,0:T(8,128)(2,1)S(1)} %collective-permute-done.1.refs_2_), channel_id=1, source_target_pairs={{0,1},{1,0},{2,3},{3,2},{4,5},{5,4},{6,7},{7,6},{8,9},{9,8},{10,11... | collective-permute-start | bytes 393224 | tf_op jit(solution)/shard_map/ppermute | solution.py:34
  14.9 20.1 %collective-permute-start.9 = (bf16[256,1024]{1,0:T(8,128)(2,1)}, bf16[256,1024]{1,0:T(8,128)(2,1)S(1)}, u32[]{:S(2)}, u32[]{:S(2)}) collective-permute-start(bf16[256,1024]{1,0:T(8,128)(2,1)} %refs_1_.2), channel_id=1, source_target_pairs={{0,1},{1,0},{2,3},{3,2},{4,5},{5,4},{6,7},{7,6},{8,9},{9,8},{10,11... | collective-permute-start | bytes 1572872 | tf_op jit(solution)/shard_map/ppermute | solution.py:34
  21.6 20.1 %copy-start.2 = (bf16[3,1024,256]{2,1,0:T(8,128)(2,1)S(1)}, bf16[3,1024,256]{2,1,0:T(8,128)(2,1)}, u32[]{:S(2)}) copy-start(bf16[3,1024,256]{2,1,0:T(8,128)(2,1)} %refs_7_.3) | copy-start | bytes 4718596
  21.6 20.1 %copy-start.6 = (s32[4]{0:T(128)S(1)}, s32[4]{0:T(128)}, u32[]{:S(2)}) copy-start(s32[4]{0:T(128)} %refs_0_.1) | copy-start | bytes 52
  21.6 12.1 %all-to-all-start.1 = ((bf16[8,32,256]{2,1,0:T(8,128)(2,1)}), bf16[8,32,256]{2,1,0:T(8,128)(2,1)S(1)}, u32[]{:S(2)}, u32[]{:S(2)}) async-start(bf16[8,32,256]{2,1,0:T(8,128)(2,1)} %bitcast.4), calls=%async_computation.1 | async-start | bytes 262144 | tf_op jit(solution)/shard_map/all_to_all | solution.py:585
  26.4 8.1 %collective-permute-start.6 = (bf16[64,2048]{1,0:T(8,128)(2,1)S(1)}, bf16[64,2048]{1,0:T(8,128)(2,1)S(1)}, u32[]{:S(2)}, u32[]{:S(2)}) collective-permute-start(bf16[64,2048]{1,0:T(8,128)(2,1)S(1)} %bitcast.11), channel_id=1, source_target_pairs={{0,2},{1,3},{2,0},{3,1},{4,6},{5,7},{6,4},{7,5},{8,10},{9,11},{10,... | collective-permute-start | bytes 786440 | tf_op jit(solution)/shard_map/ppermute | solution.py:34
  33.8 8.0 %collective-permute-start.11 = (bf16[256,1024]{1,0:T(8,128)(2,1)S(1)}, bf16[256,1024]{1,0:T(8,128)(2,1)S(1)}, u32[]{:S(2)}, u32[]{:S(2)}) collective-permute-start(bf16[256,1024]{1,0:T(8,128)(2,1)S(1)} %collective-permute-done.2.refs_5_), channel_id=1, source_target_pairs={{0,1},{1,0},{2,3},{3,2},{4,5},{5,4},{6,7},{7,6},{8,9},{9,8},{10,11... | collective-permute-start | bytes 1572872 | tf_op jit(solution)/shard_map/ppermute | solution.py:34
  33.8 2.3 %collective-permute-start.5 = (bf16[64,2048]{1,0:T(8,128)(2,1)S(1)}, bf16[64,2048]{1,0:T(8,128)(2,1)S(1)}, u32[]{:S(2)}, u32[]{:S(2)}) collective-permute-start(bf16[64,2048]{1,0:T(8,128)(2,1)S(1)} %bitcast.12), channel_id=1, source_target_pairs={{0,1},{1,0},{2,3},{3,2},{4,5},{5,4},{6,7},{7,6},{8,9},{9,8},{10,11... | collective-permute-start | bytes 786440 | tf_op jit(solution)/shard_map/ppermute | solution.py:34
  34.5 2.1 %collective-permute-start.7 = (bf16[64,2048]{1,0:T(8,128)(2,1)S(1)}, bf16[64,2048]{1,0:T(8,128)(2,1)S(1)}, u32[]{:S(2)}, u32[]{:S(2)}) collective-permute-start(bf16[64,2048]{1,0:T(8,128)(2,1)S(1)} %collective-permute-done.6.refs_2_), channel_id=1, source_target_pairs={{0,1},{1,0},{2,3},{3,2},{4,5},{5,4},{6,7},{7,6},{8,9},{9,8},{10,11... | collective-permute-start | bytes 786440 | tf_op jit(solution)/shard_map/ppermute | solution.py:34
  34.5 2.1 %collective-permute-start.8 = (bf16[256,256]{1,0:T(8,128)(2,1)S(1)}, bf16[256,256]{1,0:T(8,128)(2,1)S(1)}, u32[]{:S(2)}, u32[]{:S(2)}) collective-permute-start(bf16[256,256]{1,0:T(8,128)(2,1)S(1)} %bitcast.24), channel_id=1, source_target_pairs={{0,1},{1,0},{2,3},{3,2},{4,5},{5,4},{6,7},{7,6},{8,9},{9,8},{10,11... | collective-permute-start | bytes 393224 | tf_op jit(solution)/shard_map/ppermute | solution.py:34
  35.0 5.4 %collective-permute-start.4 = (bf16[256,256]{1,0:T(8,128)(2,1)S(1)}, bf16[256,256]{1,0:T(8,128)(2,1)S(1)}, u32[]{:S(2)}, u32[]{:S(2)}) collective-permute-start(bf16[256,256]{1,0:T(8,128)(2,1)S(1)} %bitcast.25), channel_id=1, source_target_pairs={{0,2},{1,3},{2,0},{3,1},{4,6},{5,7},{6,4},{7,5},{8,10},{9,11},{10,... | collective-permute-start | bytes 393224 | tf_op jit(solution)/shard_map/ppermute | solution.py:34
  40.4 1.3 %collective-permute-start.10 = (bf16[256,256]{1,0:T(8,128)(2,1)S(1)}, bf16[256,256]{1,0:T(8,128)(2,1)S(1)}, u32[]{:S(2)}, u32[]{:S(2)}) collective-permute-start(bf16[256,256]{1,0:T(8,128)(2,1)S(1)} %collective-permute-done.4.refs_1_), channel_id=1, source_target_pairs={{0,1},{1,0},{2,3},{3,2},{4,5},{5,4},{6,7},{7,6},{8,9},{9,8},{10,11... | collective-permute-start | bytes 393224 | tf_op jit(solution)/shard_map/ppermute | solution.py:34
  48.2 3.4 %collective-permute-start.12 = (bf16[2,64,1024]{2,1,0:T(8,128)(2,1)S(1)}, bf16[2,64,1024]{2,1,0:T(8,128)(2,1)S(1)}, u32[]{:S(2)}, u32[]{:S(2)}) collective-permute-start(bf16[2,64,1024]{2,1,0:T(8,128)(2,1)S(1)} %get-tuple-element.110), channel_id=1, source_target_pairs={{0,1},{1,0},{2,3},{3,2},{4,5},{5,4},{6,7},{7,6},{8,9},{9,8},{10,11... | collective-permute-start | bytes 786440 | tf_op jit(solution)/shard_map/ppermute | solution.py:34
  48.4 14.4 %collective-permute-start.14 = (bf16[4,512,128]{2,1,0:T(8,128)(2,1)}, bf16[4,512,128]{2,1,0:T(8,128)(2,1)S(1)}, u32[]{:S(2)}, u32[]{:S(2)}) collective-permute-start(bf16[4,512,128]{2,1,0:T(8,128)(2,1)} %get-tuple-element.122), channel_id=1, source_target_pairs={{0,4},{4,0},{8,12},{12,8},{16,20},{20,16},{24,28},{28,24},{1,5},{5... | collective-permute-start | bytes 1572872 | tf_op jit(solution)/shard_map/ppermute | solution.py:34
  50.2 14.4 %collective-permute-start.15 = (bf16[4,512,128]{2,1,0:T(8,128)(2,1)}, bf16[4,512,128]{2,1,0:T(8,128)(2,1)S(1)}, u32[]{:S(2)}, u32[]{:S(2)}) collective-permute-start(bf16[4,512,128]{2,1,0:T(8,128)(2,1)} %get-tuple-element.123), channel_id=1, source_target_pairs={{0,8},{4,12},{8,0},{12,4},{16,24},{20,28},{24,16},{28,20},{1,9},{5... | collective-permute-start | bytes 1572872 | tf_op jit(solution)/shard_map/ppermute | solution.py:34
  51.7 5.3 %collective-permute-start.13 = (bf16[64,1024]{1,0:T(8,128)(2,1)S(1)}, bf16[64,1024]{1,0:T(8,128)(2,1)S(1)}, u32[]{:S(2)}, u32[]{:S(2)}) collective-permute-start(bf16[64,1024]{1,0:T(8,128)(2,1)S(1)} %shard_map.114), channel_id=1, source_target_pairs={{0,2},{1,3},{2,0},{3,1},{4,6},{5,7},{6,4},{7,5},{8,10},{9,11},{10,... | collective-permute-start | bytes 393224 | tf_op jit(solution)/shard_map/ppermute | solution.py:34
  57.0 14.3 %copy-start.3 = (bf16[3,256,256]{2,1,0:T(8,128)(2,1)S(1)}, bf16[3,256,256]{2,1,0:T(8,128)(2,1)}, u32[]{:S(2)}) copy-start(bf16[3,256,256]{2,1,0:T(8,128)(2,1)} %get-tuple-element.131.refs_0_.refs_2_) | copy-start | bytes 1179652
  57.8 11.6 %all-to-all-start.2 = ((bf16[8,8,1024]{2,1,0:T(8,128)(2,1)}), bf16[8,8,1024]{2,1,0:T(8,128)(2,1)S(1)}, u32[]{:S(2)}, u32[]{:S(2)}) async-start(bf16[8,8,1024]{2,1,0:T(8,128)(2,1)} %bitcast.6), calls=%async_computation.2 | async-start | bytes 262144 | tf_op jit(solution)/shard_map/all_to_all | solution.py:609
  65.7 14.4 %copy-start.1 = (bf16[256,1024]{1,0:T(8,128)(2,1)S(1)}, bf16[256,1024]{1,0:T(8,128)(2,1)}, u32[]{:S(2)}) copy-start(bf16[256,1024]{1,0:T(8,128)(2,1)} %refs_1_.2) | copy-start | bytes 1572868
  69.4 5.0 %collective-permute-start.17 = (bf16[64,1024]{1,0:T(8,128)(2,1)S(1)}, bf16[64,1024]{1,0:T(8,128)(2,1)S(1)}, u32[]{:S(2)}, u32[]{:S(2)}) collective-permute-start(bf16[64,1024]{1,0:T(8,128)(2,1)S(1)} %bitcast.15), channel_id=1, source_target_pairs={{0,2},{1,3},{2,0},{3,1},{4,6},{5,7},{6,4},{7,5},{8,10},{9,11},{10,... | collective-permute-start | bytes 393224 | tf_op jit(solution)/shard_map/ppermute | solution.py:34
  69.9 6.6 %collective-permute-start.19 = (bf16[2,512,128]{2,1,0:T(8,128)(2,1)}, bf16[2,512,128]{2,1,0:T(8,128)(2,1)S(1)}, u32[]{:S(2)}, u32[]{:S(2)}) collective-permute-start(bf16[2,512,128]{2,1,0:T(8,128)(2,1)} %get-tuple-element.138), channel_id=1, source_target_pairs={{0,8},{4,12},{8,0},{12,4},{16,24},{20,28},{24,16},{28,20},{1,9},{5... | collective-permute-start | bytes 786440 | tf_op jit(solution)/shard_map/ppermute | solution.py:34
  69.9 6.6 %collective-permute-start.20 = (bf16[2,512,128]{2,1,0:T(8,128)(2,1)}, bf16[2,512,128]{2,1,0:T(8,128)(2,1)S(1)}, u32[]{:S(2)}, u32[]{:S(2)}) collective-permute-start(bf16[2,512,128]{2,1,0:T(8,128)(2,1)} %get-tuple-element.139), channel_id=1, source_target_pairs={{0,4},{4,0},{8,12},{12,8},{16,20},{20,16},{24,28},{28,24},{1,5},{5... | collective-permute-start | bytes 786440 | tf_op jit(solution)/shard_map/ppermute | solution.py:34
  71.2 3.2 %collective-permute-start.16 = (bf16[64,1024]{1,0:T(8,128)(2,1)S(1)}, bf16[64,1024]{1,0:T(8,128)(2,1)S(1)}, u32[]{:S(2)}, u32[]{:S(2)}) collective-permute-start(bf16[64,1024]{1,0:T(8,128)(2,1)S(1)} %bitcast.16), channel_id=1, source_target_pairs={{0,1},{1,0},{2,3},{3,2},{4,5},{5,4},{6,7},{7,6},{8,9},{9,8},{10,11... | collective-permute-start | bytes 393224 | tf_op jit(solution)/shard_map/ppermute | solution.py:34
  74.4 1.3 %collective-permute-start.18 = (bf16[64,1024]{1,0:T(8,128)(2,1)S(1)}, bf16[64,1024]{1,0:T(8,128)(2,1)S(1)}, u32[]{:S(2)}, u32[]{:S(2)}) collective-permute-start(bf16[64,1024]{1,0:T(8,128)(2,1)S(1)} %collective-permute-done.17.refs_2_), channel_id=1, source_target_pairs={{0,1},{1,0},{2,3},{3,2},{4,5},{5,4},{6,7},{7,6},{8,9},{9,8},{10,11... | collective-permute-start | bytes 393224 | tf_op jit(solution)/shard_map/ppermute | solution.py:34
  76.5 8.8 %collective-permute-start.22 = (bf16[4,256,128]{2,1,0:T(8,128)(2,1)S(1)}, bf16[4,256,128]{2,1,0:T(8,128)(2,1)S(1)}, u32[]{:S(2)}, u32[]{:S(2)}) collective-permute-start(bf16[4,256,128]{2,1,0:T(8,128)(2,1)S(1)} %get-tuple-element.155), channel_id=1, source_target_pairs={{0,4},{4,0},{8,12},{12,8},{16,20},{20,16},{24,28},{28,24},{1,5},{5... | collective-permute-start | bytes 786440 | tf_op jit(solution)/shard_map/ppermute | solution.py:34
  79.0 5.7 %copy-start = (bf16[3,1024,256]{2,1,0:T(8,128)(2,1)S(1)}, bf16[3,1024,256]{2,1,0:T(8,128)(2,1)}, u32[]{:S(2)}) copy-start(bf16[3,1024,256]{2,1,0:T(8,128)(2,1)} %refs_1_.3) | copy-start | bytes 4718596
  79.0 13.6 %collective-permute-start.21 = (bf16[1024,128]{1,0:T(8,128)(2,1)S(1)}, bf16[1024,128]{1,0:T(8,128)(2,1)S(1)}, u32[]{:S(2)}, u32[]{:S(2)}) collective-permute-start(bf16[1024,128]{1,0:T(8,128)(2,1)S(1)} %get-tuple-element.153), channel_id=1, source_target_pairs={{0,16},{4,20},{8,24},{12,28},{16,0},{20,4},{24,8},{28,12},{1,17},{... | collective-permute-start | bytes 786440 | tf_op jit(solution)/shard_map/ppermute | solution.py:34
  82.5 10.1 %copy-start.5 = (bf16[256,1024]{1,0:T(8,128)(2,1)S(1)}, bf16[256,1024]{1,0:T(8,128)(2,1)}, u32[]{:S(2)}) copy-start(bf16[256,1024]{1,0:T(8,128)(2,1)} %get-tuple-element.149.refs_4_.refs_1_) | copy-start | bytes 1572868
  82.5 13.1 %collective-permute-start.26 = (bf16[4,352,128]{2,1,0:T(8,128)(2,1)S(1)}, bf16[4,352,128]{2,1,0:T(8,128)(2,1)S(1)}, u32[]{:S(2)}, u32[]{:S(2)}) collective-permute-start(bf16[4,352,128]{2,1,0:T(8,128)(2,1)S(1)} %get-tuple-element.164), channel_id=1, source_target_pairs={{0,8},{4,12},{8,0},{12,4},{16,24},{20,28},{24,16},{28,20},{1,9},{5... | collective-permute-start | bytes 1081352 | tf_op jit(solution)/shard_map/ppermute | solution.py:34
  82.9 12.6 %collective-permute-start.25 = (bf16[4,416,128]{2,1,0:T(8,128)(2,1)S(1)}, bf16[4,416,128]{2,1,0:T(8,128)(2,1)S(1)}, u32[]{:S(2)}, u32[]{:S(2)}) collective-permute-start(bf16[4,416,128]{2,1,0:T(8,128)(2,1)S(1)} %get-tuple-element.163), channel_id=1, source_target_pairs={{0,4},{4,0},{8,12},{12,8},{16,20},{20,16},{24,28},{28,24},{1,5},{5... | collective-permute-start | bytes 1277960 | tf_op jit(solution)/shard_map/ppermute | solution.py:34
  95.6 17.0 %copy-start.4 = (bf16[1,64,1024]{2,1,0:T(8,128)(2,1)S(1)}, bf16[1,64,1024]{2,1,0:T(8,128)(2,1)}, u32[]{:S(2)}) copy-start(bf16[1,64,1024]{2,1,0:T(8,128)(2,1)} %param.7) | copy-start | bytes 393220
  95.8 7.7 %collective-permute-start.27 = (bf16[2,416,128]{2,1,0:T(8,128)(2,1)S(1)}, bf16[2,416,128]{2,1,0:T(8,128)(2,1)S(1)}, u32[]{:S(2)}, u32[]{:S(2)}) collective-permute-start(bf16[2,416,128]{2,1,0:T(8,128)(2,1)S(1)} %get-tuple-element.167), channel_id=1, source_target_pairs={{0,8},{4,12},{8,0},{12,4},{16,24},{20,28},{24,16},{28,20},{1,9},{5... | collective-permute-start | bytes 638984 | tf_op jit(solution)/shard_map/ppermute | solution.py:34
  95.9 11.6 %collective-permute-start.23 = (bf16[2,64,1024]{2,1,0:T(8,128)(2,1)S(1)}, bf16[2,64,1024]{2,1,0:T(8,128)(2,1)S(1)}, u32[]{:S(2)}, u32[]{:S(2)}) collective-permute-start(bf16[2,64,1024]{2,1,0:T(8,128)(2,1)S(1)} %get-tuple-element.159), channel_id=1, source_target_pairs={{0,1},{1,0},{2,3},{3,2},{4,5},{5,4},{6,7},{7,6},{8,9},{9,8},{10,11... | collective-permute-start | bytes 786440 | tf_op jit(solution)/shard_map/ppermute | solution.py:34
  95.9 7.6 %collective-permute-start.28 = (bf16[2,352,128]{2,1,0:T(8,128)(2,1)S(1)}, bf16[2,352,128]{2,1,0:T(8,128)(2,1)S(1)}, u32[]{:S(2)}, u32[]{:S(2)}) collective-permute-start(bf16[2,352,128]{2,1,0:T(8,128)(2,1)S(1)} %get-tuple-element.168), channel_id=1, source_target_pairs={{0,4},{4,0},{8,12},{12,8},{16,20},{20,16},{24,28},{28,24},{1,5},{5... | collective-permute-start | bytes 540680 | tf_op jit(solution)/shard_map/ppermute | solution.py:34
  98.4 10.4 %collective-permute-start.30 = (bf16[2,256,128]{2,1,0:T(8,128)(2,1)S(1)}, bf16[2,256,128]{2,1,0:T(8,128)(2,1)S(1)}, u32[]{:S(2)}, u32[]{:S(2)}) collective-permute-start(bf16[2,256,128]{2,1,0:T(8,128)(2,1)S(1)} %get-tuple-element.172), channel_id=1, source_target_pairs={{0,16},{4,20},{8,24},{12,28},{16,0},{20,4},{24,8},{28,12},{1,17},{... | collective-permute-start | bytes 393224 | tf_op jit(solution)/shard_map/ppermute | solution.py:34
  103.6 12.9 %collective-permute-start.29 = (bf16[768,128]{1,0:T(8,128)(2,1)S(1)}, bf16[768,128]{1,0:T(8,128)(2,1)S(1)}, u32[]{:S(2)}, u32[]{:S(2)}) collective-permute-start(bf16[768,128]{1,0:T(8,128)(2,1)S(1)} %get-tuple-element.170), channel_id=1, source_target_pairs={{0,16},{4,20},{8,24},{12,28},{16,0},{20,4},{24,8},{28,12},{1,17},{... | collective-permute-start | bytes 589832 | tf_op jit(solution)/shard_map/ppermute | solution.py:34
  107.5 5.0 %collective-permute-start.24 = (bf16[64,1024]{1,0:T(8,128)(2,1)S(1)}, bf16[64,1024]{1,0:T(8,128)(2,1)S(1)}, u32[]{:S(2)}, u32[]{:S(2)}) collective-permute-start(bf16[64,1024]{1,0:T(8,128)(2,1)S(1)} %shard_map.124), channel_id=1, source_target_pairs={{0,2},{1,3},{2,0},{3,1},{4,6},{5,7},{6,4},{7,5},{8,10},{9,11},{10,... | collective-permute-start | bytes 393224 | tf_op jit(solution)/shard_map/ppermute | solution.py:34
  108.9 4.7 %collective-permute-start.31 = (bf16[1,256,128]{2,1,0:T(8,128)(2,1)S(1)}, bf16[1,256,128]{2,1,0:T(8,128)(2,1)S(1)}, u32[]{:S(2)}, u32[]{:S(2)}) collective-permute-start(bf16[1,256,128]{2,1,0:T(8,128)(2,1)S(1)} %get-tuple-element.174), channel_id=1, source_target_pairs={{0,8},{4,12},{8,0},{12,4},{16,24},{20,28},{24,16},{28,20},{1,9},{5... | collective-permute-start | bytes 196616 | tf_op jit(solution)/shard_map/ppermute | solution.py:34

commit v5 on v4

--- a/solution.py
+++ b/solution.py
@@ -500,7 +500,7 @@
     )
 
 
-def halve(keeps, cames, keep_in="v", out="v", merged=False):
+def halve(keeps, cames, keep_in="v", out="v", merged=False, flops=1000):
     n, depth = len(keeps), keeps[0].shape[0]
     rows = [keep.shape[1] for keep in keeps]
     chunk = keeps[0].shape[2]
@@ -520,10 +520,10 @@
     else:
         outs = tuple(shape((depth // 2, r, chunk)) for r in rows) * 2
     where = keep_in * n + "v" * n
-    return run(body, (*keeps, *cames), where, outs, out * len(outs))
-
-
-def last_sums(pairs):
+    return run(body, (*keeps, *cames), where, outs, out * len(outs), flops=flops)
+
+
+def last_sums(pairs, flops=1000):
     chunk = pairs[0][0].shape[-1]
     pairs = [tuple(part.reshape(-1, chunk) for part in pair) for pair in pairs]
     width = sum(pair[0].shape[0] for pair in pairs) // 4
@@ -545,7 +545,7 @@
 
     ins = [part for pair in pairs for part in pair]
     outs = (shape((3, chunk, width), F32), shape((width, chunk), F32))
-    return run(body, ins, "v" * len(ins), outs, "hh")
+    return run(body, ins, "v" * len(ins), outs, "hh", flops=flops)
 
 
 def reduce_whole(flat, normed, other):
@@ -637,13 +637,15 @@
             (s_grads, send_x, keep_x, t_came, o_send, o_keep)
         )
         o_came = swap(o_send, "frames", 4)
-        t_qkv, t_out = last_sums([(t_keep, t_came)])
+        t_qkv, t_out = last_sums([(t_keep, t_came)], 50_000_000_000)
         s_kept = qkv_keeps(s_grads, normed_x, groups, 50_000_000_000)
         came = [swap(s_sent[0], "frames", 1), swap(s_sent[1], "frames", 2)]
+        came, t_qkv, t_out = after((came, t_qkv, t_out))
         send_a, send_b, keep_a, keep_b = halve(s_kept, came)
         came = [swap(send_a, "frames", 2), swap(send_b, "frames", 1)]
+        o_send, o_keep = halve([o_keep], [o_came], flops=50_000_000_000)
+        came, o_send, o_keep = after((came, o_send, o_keep))
         s_send, s_keep = halve([keep_a, keep_b], came, merged=True)
-        o_send, o_keep = halve([o_keep], [o_came])
         s_qkv, s_out = last_sums([
             (s_keep, swap(s_send, "frames", 4)), (o_keep, swap(o_send, "frames", 2))
         ])

time: 118 us -> 117 us (level)
  starting transfers between devices: 42.8 us -> 40.7 us
    ppermute x32, starting transfers between devices: 27.7 us -> 25.7 us  [swap(): return lax.ppermute(value, axis, [(i, i ^ by) for i in range(size)])]
  transfers between devices with their start and end apart: 35 -> 35, of which waited for: 22 -> 23; matrix products, arithmetic and copies ran while one was open for 0% -> 0% of each run, Pallas kernels for 17% -> 17%
where the time goes in v5:
time: 117 us; the launch traced here: 116 us
  waiting for transfers between devices  46.9 us (40%)
  starting transfers between devices  40.7 us (35%)
  Pallas kernels  27.5 us (24%)
    ppermute x32, waiting for transfers between devices, swap(): return lax.ppermute(value, axis, [(i, i ^ by) for i in range(size)])  34.9 us
    pallas_call x22, Pallas kernels, run(): pl.pallas_call(wrapped, out_shape=tuple((pltpu.HBM(o.shape, o.dtype) if w...  27.5 us
    ppermute x32, starting transfers between devices, swap(): return lax.ppermute(value, axis, [(i, i ^ by) for i in range(size)])  25.7 us
    all_to_all x1, waiting for transfers between devices, shards(): lax.all_to_all(attn_send.reshape(groups, mp * per, width), 'frames', 0, 0...  6.83 us
    all_to_all x1, starting transfers between devices, shards(): lax.all_to_all(xg.reshape(groups, per, 2 * dim), 'frames', 0, 0, tiled=True)  6.03 us
    all_to_all x1, starting transfers between devices, shards(): lax.all_to_all(attn_send.reshape(groups, mp * per, width), 'frames', 0, 0...  4.78 us
    all_to_all x1, starting transfers between devices, shards(): lax.all_to_all(d_hidden.reshape(groups, per, dim), 'frames', 0, 0, tiled=...  4.24 us
    all_to_all x1, waiting for transfers between devices, shards(): lax.all_to_all(d_hidden.reshape(groups, per, dim), 'frames', 0, 0, tiled=...  3.76 us
  transfers between devices with their start and end apart: 35, of which 23 were waited for; matrix products, arithmetic and copies ran while one was open for 0% of the time, Pallas kernels for 17%

profile of v5, /device:TPU:0, one launch (start us, length us, event | category | flops | bytes accessed | tf_op | source)
XLA Modules:
  0.0 116.2 jit_solution(6896008467213005510)
XLA Ops:
  0.6 3.0 %collective-permute-start.1 = (bf16[64,1024]{1,0:T(8,128)(2,1)}, bf16[64,1024]{1,0:T(8,128)(2,1)S(1)}, u32[]{:S(2)}, u32[]{:S(2)}) collective-permute-start(bf16[64,1024]{1,0:T(8,128)(2,1)} %bitcast.19), channel_id=1, source_target_pairs={{0,2},{1,3},{2,0},{3,1},{4,6},{5,7},{6,4},{7,5},{8,10},{9,11},{10,... | collective-permute-start | bytes 393224 | tf_op jit(solution)/shard_map/ppermute | solution.py:34
  3.7 1.7 %shard_map.110 = bf16[64,2048]{1,0:T(8,128)(2,1)} custom-call(bf16[64,1024]{1,0:T(8,128)(2,1)} %bitcast.21, bf16[64,1024]{1,0:T(8,128)(2,1)} %bitcast.29), custom_call_target="tpu_custom_call" | custom-call | flops 1000 | bytes 1000 | tf_op jit(solution)/shard_map/pallas_call | solution.py:110
  5.4 2.0 %collective-permute-done.1.refs_2_ = bf16[64,1024]{1,0:T(8,128)(2,1)S(1)} collective-permute-done((bf16[64,1024]{1,0:T(8,128)(2,1)}, bf16[64,1024]{1,0:T(8,128)(2,1)S(1)}, u32[]{:S(2)}, u32[]{:S(2)}) %collective-permute-start.1) | collective-permute-done | bytes 131104 | tf_op jit(solution)/shard_map/ppermute | solution.py:34
  7.4 6.0 %all-to-all-start = ((bf16[8,8,2048]{2,1,0:T(8,128)(2,1)}), bf16[8,8,2048]{2,1,0:T(8,128)(2,1)S(1)}, u32[]{:S(2)}, u32[]{:S(2)}) async-start(bf16[8,8,2048]{2,1,0:T(8,128)(2,1)} %bitcast.2), calls=%async_computation | async-start | bytes 524288 | tf_op jit(solution)/shard_map/all_to_all | solution.py:576
  13.4 1.5 %collective-permute-start.2 = (bf16[256,1024]{1,0:T(8,128)(2,1)}, bf16[256,1024]{1,0:T(8,128)(2,1)S(1)}, u32[]{:S(2)}, u32[]{:S(2)}) collective-permute-start(bf16[256,1024]{1,0:T(8,128)(2,1)} %refs_1_.2), channel_id=1, source_target_pairs={{0,2},{1,3},{2,0},{3,1},{4,6},{5,7},{6,4},{7,5},{8,10},{9,11},{10,... | collective-permute-start | bytes 1572872 | tf_op jit(solution)/shard_map/ppermute | solution.py:34
  14.9 0.5 collective-permute-start.9
  15.4 1.0 collective-permute-done.3.refs_3_
  16.4 3.8 %shard_map.111 = (bf16[256,1024]{1,0:T(8,128)(2,1)}, bf16[3,256,256]{2,1,0:T(8,128)(2,1)}, bf16[256,256]{1,0:T(8,128)(2,1)}) custom-call(bf16[64,1024]{1,0:T(8,128)(2,1)} %bitcast.22, bf16[64,1024]{1,0:T(8,128)(2,1)S(1)} %collective-permute-done.refs_1_, bf16[64,1024]{1,0:T(8,128)(2,1)S(1)} %collective-permute-done.1.refs_2_, ...), custom_call_target="tpu_custom_call" | custom-call | flops 1000 | bytes 1000 | tf_op jit(solution)/shard_map/pallas_call | solution.py:110
  20.2 1.4 %all-to-all-done = bf16[8,8,2048]{2,1,0:T(8,128)(2,1)S(1)} async-done(((bf16[8,8,2048]{2,1,0:T(8,128)(2,1)}), bf16[8,8,2048]{2,1,0:T(8,128)(2,1)S(1)}, u32[]{:S(2)}, u32[]{:S(2)}) %all-to-all-start) | async-done | bytes 262176 | tf_op jit(solution)/shard_map/all_to_all | solution.py:576
  21.6 4.8 %all-to-all-start.1 = ((bf16[8,32,256]{2,1,0:T(8,128)(2,1)}), bf16[8,32,256]{2,1,0:T(8,128)(2,1)S(1)}, u32[]{:S(2)}, u32[]{:S(2)}) async-start(bf16[8,32,256]{2,1,0:T(8,128)(2,1)} %bitcast.4), calls=%async_computation.1 | async-start | bytes 262144 | tf_op jit(solution)/shard_map/all_to_all | solution.py:585
  26.4 0.5 collective-permute-start.6
  26.9 6.8 %all-to-all-done.1 = bf16[8,32,256]{2,1,0:T(8,128)(2,1)S(1)} async-done(((bf16[8,32,256]{2,1,0:T(8,128)(2,1)}), bf16[8,32,256]{2,1,0:T(8,128)(2,1)S(1)}, u32[]{:S(2)}, u32[]{:S(2)}) %all-to-all-start.1) | async-done | bytes 131104 | tf_op jit(solution)/shard_map/all_to_all | solution.py:585
  33.8 0.5 collective-permute-start.5
  34.3 0.2 collective-permute-done.6.refs_2_
  34.5 0.5 collective-permute-start.8
  35.0 0.5 collective-permute-start.4
  35.5 0.5 collective-permute-done.5.refs_1_
  36.0 0.6 collective-permute-done.8.refs_6_
  36.6 2.4 %shard_map.112 = (f32[256,1024]{1,0:T(8,128)S(1)}, bf16[256,1024]{1,0:T(8,128)(2,1)S(1)}, bf16[256,256]{1,0:T(8,128)(2,1)S(1)}) custom-call(bf16[64,2048]{1,0:T(8,128)(2,1)S(1)} %bitcast.13, bf16[64,2048]{1,0:T(8,128)(2,1)S(1)} %collective-permute-done.5.refs_1_, bf16[64,2048]{1,0:T(8,128)(2,1)S(1)} %collective-permute-done.6.refs_2_, ...), custom_call_target="tpu_custom_call" | custom-call | flops 1000 | bytes 1000 | tf_op jit(solution)/shard_map/pallas_call | solution.py:110
  39.0 1.4 %collective-permute-done.4.refs_1_ = bf16[256,256]{1,0:T(8,128)(2,1)S(1)} collective-permute-done((bf16[256,256]{1,0:T(8,128)(2,1)S(1)}, bf16[256,256]{1,0:T(8,128)(2,1)S(1)}, u32[]{:S(2)}, u32[]{:S(2)}) %collective-permute-start.4) | collective-permute-done | bytes 131104 | tf_op jit(solution)/shard_map/ppermute | solution.py:34
  40.4 1.3 %collective-permute-done.10.refs_2_ = bf16[256,256]{1,0:T(8,128)(2,1)S(1)} collective-permute-done((bf16[256,256]{1,0:T(8,128)(2,1)S(1)}, bf16[256,256]{1,0:T(8,128)(2,1)S(1)}, u32[]{:S(2)}, u32[]{:S(2)}) %collective-permute-start.10) | collective-permute-done | bytes 131104 | tf_op jit(solution)/shard_map/ppermute | solution.py:34
  41.8 6.4 %shard_map.113 = (bf16[2,64,1024]{2,1,0:T(8,128)(2,1)S(1)}, bf16[2,64,1024]{2,1,0:T(8,128)(2,1)S(1)}, bf16[256,1024]{1,0:T(8,128)(2,1)S(1)}, bf16[64,1024]{1,0:T...) custom-call(s32[4]{0:T(128)S(1)} %copy-done.6, ...), custom_call_target="tpu_custom_call" | custom-call | flops 1000 | bytes 1000 | tf_op jit(solution)/shard_map/pallas_call | solution.py:110
  48.2 0.2 collective-permute-start.12
  48.4 1.8 %collective-permute-start.14 = (bf16[4,512,128]{2,1,0:T(8,128)(2,1)}, bf16[4,512,128]{2,1,0:T(8,128)(2,1)S(1)}, u32[]{:S(2)}, u32[]{:S(2)}) collective-permute-start(bf16[4,512,128]{2,1,0:T(8,128)(2,1)} %get-tuple-element.130), channel_id=1, source_target_pairs={{0,4},{4,0},{8,12},{12,8},{16,20},{20,16},{24,28},{28,24},{1,5},{5... | collective-permute-start | bytes 1572872 | tf_op jit(solution)/shard_map/ppermute | solution.py:34
  50.2 1.5 %collective-permute-start.15 = (bf16[4,512,128]{2,1,0:T(8,128)(2,1)}, bf16[4,512,128]{2,1,0:T(8,128)(2,1)S(1)}, u32[]{:S(2)}, u32[]{:S(2)}) collective-permute-start(bf16[4,512,128]{2,1,0:T(8,128)(2,1)} %get-tuple-element.131), channel_id=1, source_target_pairs={{0,8},{4,12},{8,0},{12,4},{16,24},{20,28},{24,16},{28,20},{1,9},{5... | collective-permute-start | bytes 1572872 | tf_op jit(solution)/shard_map/ppermute | solution.py:34
  51.7 0.6 collective-permute-start.13
  52.3 0.8 shard_map.115
  53.1 3.9 %collective-permute-done.13.refs_2_ = bf16[64,1024]{1,0:T(8,128)(2,1)S(1)} collective-permute-done((bf16[64,1024]{1,0:T(8,128)(2,1)S(1)}, bf16[64,1024]{1,0:T(8,128)(2,1)S(1)}, u32[]{:S(2)}, u32[]{:S(2)}) %collective-permute-start.13) | collective-permute-done | bytes 131104 | tf_op jit(solution)/shard_map/ppermute | solution.py:34
  57.0 0.9 shard_map.116
  57.8 4.2 %all-to-all-start.2 = ((bf16[8,8,1024]{2,1,0:T(8,128)(2,1)}), bf16[8,8,1024]{2,1,0:T(8,128)(2,1)S(1)}, u32[]{:S(2)}, u32[]{:S(2)}) async-start(bf16[8,8,1024]{2,1,0:T(8,128)(2,1)} %bitcast.6), calls=%async_computation.2 | async-start | bytes 262144 | tf_op jit(solution)/shard_map/all_to_all | solution.py:609
  62.1 0.7 collective-permute-done.14.refs_2_
  62.8 1.7 %collective-permute-done.15.refs_3_ = bf16[4,512,128]{2,1,0:T(8,128)(2,1)S(1)} collective-permute-done((bf16[4,512,128]{2,1,0:T(8,128)(2,1)}, bf16[4,512,128]{2,1,0:T(8,128)(2,1)S(1)}, u32[]{:S(2)}, u32[]{:S(2)}) %collective-permute-start.15) | collective-permute-done | bytes 524320 | tf_op jit(solution)/shard_map/ppermute | solution.py:34
  64.5 1.1 shard_map.117
  65.7 3.8 %all-to-all-done.2 = bf16[8,8,1024]{2,1,0:T(8,128)(2,1)S(1)} async-done(((bf16[8,8,1024]{2,1,0:T(8,128)(2,1)}), bf16[8,8,1024]{2,1,0:T(8,128)(2,1)S(1)}, u32[]{:S(2)}, u32[]{:S(2)}) %all-to-all-start.2) | async-done | bytes 131104 | tf_op jit(solution)/shard_map/all_to_all | solution.py:609
  69.4 0.5 collective-permute-start.17
  69.9 1.3 %collective-permute-start.20 = (bf16[2,512,128]{2,1,0:T(8,128)(2,1)}, bf16[2,512,128]{2,1,0:T(8,128)(2,1)S(1)}, u32[]{:S(2)}, u32[]{:S(2)}) collective-permute-start(bf16[2,512,128]{2,1,0:T(8,128)(2,1)} %get-tuple-element.147), channel_id=1, source_target_pairs={{0,4},{4,0},{8,12},{12,8},{16,20},{20,16},{24,28},{28,24},{1,5},{5... | collective-permute-start | bytes 786440 | tf_op jit(solution)/shard_map/ppermute | solution.py:34
  71.3 1.5 %shard_map.118 = (f32[4,256,256]{2,1,0:T(8,128)S(1)}, bf16[256,256]{1,0:T(8,128)(2,1)S(1)}) custom-call(bf16[3,256,256]{2,1,0:T(8,128)(2,1)S(1)} %copy-done.3, bf16[256,256]{1,0:T(8,128)(2,1)} %get-tuple-element.140.refs_1_), custom_call_target="tpu_custom_call" | custom-call | flops 1000 | bytes 1000 | tf_op jit(solution)/shard_map/pallas_call | solution.py:110
  72.8 1.6 %collective-permute-done.17.refs_2_ = bf16[64,1024]{1,0:T(8,128)(2,1)S(1)} collective-permute-done((bf16[64,1024]{1,0:T(8,128)(2,1)S(1)}, bf16[64,1024]{1,0:T(8,128)(2,1)S(1)}, u32[]{:S(2)}, u32[]{:S(2)}) %collective-permute-start.17) | collective-permute-done | bytes 131104 | tf_op jit(solution)/shard_map/ppermute | solution.py:34
  74.4 1.3 %collective-permute-done.18.refs_3_ = bf16[64,1024]{1,0:T(8,128)(2,1)S(1)} collective-permute-done((bf16[64,1024]{1,0:T(8,128)(2,1)S(1)}, bf16[64,1024]{1,0:T(8,128)(2,1)S(1)}, u32[]{:S(2)}, u32[]{:S(2)}) %collective-permute-start.18) | collective-permute-done | bytes 131104 | tf_op jit(solution)/shard_map/ppermute | solution.py:34
  75.7 0.5 shard_map.119
  76.3 0.3 collective-permute-done.19.refs_2_
  76.5 1.3 %collective-permute-start.22 = (bf16[4,256,128]{2,1,0:T(8,128)(2,1)S(1)}, bf16[4,256,128]{2,1,0:T(8,128)(2,1)S(1)}, u32[]{:S(2)}, u32[]{:S(2)}) collective-permute-start(bf16[4,256,128]{2,1,0:T(8,128)(2,1)S(1)} %get-tuple-element.163), channel_id=1, source_target_pairs={{0,4},{4,0},{8,12},{12,8},{16,20},{20,16},{24,28},{28,24},{1,5},{5... | collective-permute-start | bytes 786440 | tf_op jit(solution)/shard_map/ppermute | solution.py:34
  77.8 1.2 shard_map.120
  79.0 1.1 collective-permute-start.21
  80.1 2.4 %shard_map.121 = (bf16[3,256,256]{2,1,0:T(8,128)(2,1)S(1)}, bf16[4,416,128]{2,1,0:T(8,128)(2,1)S(1)}, bf16[4,352,128]{2,1,0:T(8,128)(2,1)S(1)}) custom-call(bf16[256,1024]{1,0:T(8,128)(2,1)S(1)} %get-tuple-element.155.refs_0_, bf16[256,1024]{1,0:T(8,128)(2,1)S(1)} %copy-done.1, bf16[3,256,256]{2,1,0:T(8,128)(2,1)S(1)} %copy-done.3, ...), custom_call_target="tpu_custom_call" | custom-call | flops 1000 | bytes 1000 | tf_op jit(solution)/shard_map/pallas_call | solution.py:110
  82.5 0.4 collective-permute-start.26
  82.9 1.8 %collective-permute-start.25 = (bf16[4,416,128]{2,1,0:T(8,128)(2,1)S(1)}, bf16[4,416,128]{2,1,0:T(8,128)(2,1)S(1)}, u32[]{:S(2)}, u32[]{:S(2)}) collective-permute-start(bf16[4,416,128]{2,1,0:T(8,128)(2,1)S(1)} %get-tuple-element.171), channel_id=1, source_target_pairs={{0,4},{4,0},{8,12},{12,8},{16,20},{20,16},{24,28},{28,24},{1,5},{5... | collective-permute-start | bytes 1277960 | tf_op jit(solution)/shard_map/ppermute | solution.py:34
  84.7 0.7 shard_map.122
  85.5 7.1 %collective-permute-done.21.refs_1_ = bf16[1024,128]{1,0:T(8,128)(2,1)S(1)} collective-permute-done((bf16[1024,128]{1,0:T(8,128)(2,1)S(1)}, bf16[1024,128]{1,0:T(8,128)(2,1)S(1)}, u32[]{:S(2)}, u32[]{:S(2)}) %collective-permute-start.21) | collective-permute-done | bytes 262176 | tf_op jit(solution)/shard_map/ppermute | solution.py:34
  92.6 0.6 shard_map.126
  93.3 1.0 shard_map.127
  94.3 1.4 %collective-permute-done.26.refs_3_ = bf16[4,352,128]{2,1,0:T(8,128)(2,1)S(1)} collective-permute-done((bf16[4,352,128]{2,1,0:T(8,128)(2,1)S(1)}, bf16[4,352,128]{2,1,0:T(8,128)(2,1)S(1)}, u32[]{:S(2)}, u32[]{:S(2)}) %collective-permute-start.26) | collective-permute-done | bytes 360480 | tf_op jit(solution)/shard_map/ppermute | solution.py:34
  95.7 0.2 shard_map.128
  95.9 2.6 %collective-permute-start.28 = (bf16[2,352,128]{2,1,0:T(8,128)(2,1)S(1)}, bf16[2,352,128]{2,1,0:T(8,128)(2,1)S(1)}, u32[]{:S(2)}, u32[]{:S(2)}) collective-permute-start(bf16[2,352,128]{2,1,0:T(8,128)(2,1)S(1)} %get-tuple-element.182), channel_id=1, source_target_pairs={{0,4},{4,0},{8,12},{12,8},{16,20},{20,16},{24,28},{28,24},{1,5},{5... | collective-permute-start | bytes 540680 | tf_op jit(solution)/shard_map/ppermute | solution.py:34
  98.5 2.2 %collective-permute-done.29.refs_1_ = bf16[2,256,128]{2,1,0:T(8,128)(2,1)S(1)} collective-permute-done((bf16[2,256,128]{2,1,0:T(8,128)(2,1)S(1)}, bf16[2,256,128]{2,1,0:T(8,128)(2,1)S(1)}, u32[]{:S(2)}, u32[]{:S(2)}) %collective-permute-start.29) | collective-permute-done | bytes 131104 | tf_op jit(solution)/shard_map/ppermute | solution.py:34
  100.8 1.2 %collective-permute-done.28.refs_3_ = bf16[2,352,128]{2,1,0:T(8,128)(2,1)S(1)} collective-permute-done((bf16[2,352,128]{2,1,0:T(8,128)(2,1)S(1)}, bf16[2,352,128]{2,1,0:T(8,128)(2,1)S(1)}, u32[]{:S(2)}, u32[]{:S(2)}) %collective-permute-start.28) | collective-permute-done | bytes 180256 | tf_op jit(solution)/shard_map/ppermute | solution.py:34
  102.0 3.1 %collective-permute-done.27.refs_2_ = bf16[2,416,128]{2,1,0:T(8,128)(2,1)S(1)} collective-permute-done((bf16[2,416,128]{2,1,0:T(8,128)(2,1)S(1)}, bf16[2,416,128]{2,1,0:T(8,128)(2,1)S(1)}, u32[]{:S(2)}, u32[]{:S(2)}) %collective-permute-start.27) | collective-permute-done | bytes 213024 | tf_op jit(solution)/shard_map/ppermute | solution.py:34
  105.3 2.1 %collective-permute-start.30 = (bf16[768,128]{1,0:T(8,128)(2,1)S(1)}, bf16[768,128]{1,0:T(8,128)(2,1)S(1)}, u32[]{:S(2)}, u32[]{:S(2)}) collective-permute-start(bf16[768,128]{1,0:T(8,128)(2,1)S(1)} %get-tuple-element.190), channel_id=1, source_target_pairs={{0,16},{4,20},{8,24},{12,28},{16,0},{20,4},{24,8},{28,12},{1,17},{... | collective-permute-start | bytes 589832 | tf_op jit(solution)/shard_map/ppermute | solution.py:34
  107.5 1.4 %collective-permute-start.24 = (bf16[64,1024]{1,0:T(8,128)(2,1)S(1)}, bf16[64,1024]{1,0:T(8,128)(2,1)S(1)}, u32[]{:S(2)}, u32[]{:S(2)}) collective-permute-start(bf16[64,1024]{1,0:T(8,128)(2,1)S(1)} %shard_map.124), channel_id=1, source_target_pairs={{0,2},{1,3},{2,0},{3,1},{4,6},{5,7},{6,4},{7,5},{8,10},{9,11},{10,... | collective-permute-start | bytes 393224 | tf_op jit(solution)/shard_map/ppermute | solution.py:34
  108.9 1.9 %collective-permute-start.31 = (bf16[1,256,128]{2,1,0:T(8,128)(2,1)S(1)}, bf16[1,256,128]{2,1,0:T(8,128)(2,1)S(1)}, u32[]{:S(2)}, u32[]{:S(2)}) collective-permute-start(bf16[1,256,128]{2,1,0:T(8,128)(2,1)S(1)} %get-tuple-element.192), channel_id=1, source_target_pairs={{0,8},{4,12},{8,0},{12,4},{16,24},{20,28},{24,16},{28,20},{1,9},{5... | collective-permute-start | bytes 196616 | tf_op jit(solution)/shard_map/ppermute | solution.py:34
  110.8 1.7 %collective-permute-done.24.refs_2_ = bf16[64,1024]{1,0:T(8,128)(2,1)S(1)} collective-permute-done((bf16[64,1024]{1,0:T(8,128)(2,1)S(1)}, bf16[64,1024]{1,0:T(8,128)(2,1)S(1)}, u32[]{:S(2)}, u32[]{:S(2)}) %collective-permute-start.24) | collective-permute-done | bytes 131104 | tf_op jit(solution)/shard_map/ppermute | solution.py:34
  112.6 0.9 shard_map.125
  113.5 1.6 %collective-permute-done.31 = bf16[1,256,128]{2,1,0:T(8,128)(2,1)S(1)} collective-permute-done((bf16[1,256,128]{2,1,0:T(8,128)(2,1)S(1)}, bf16[1,256,128]{2,1,0:T(8,128)(2,1)S(1)}, u32[]{:S(2)}, u32[]{:S(2)}) %collective-permute-start.31) | collective-permute-done | bytes 65568 | tf_op jit(solution)/shard_map/ppermute | solution.py:34
  115.0 1.0 shard_map.131
  (42 shorter events, 0.6 us)
Async XLA Ops:
  0.6 6.7 %collective-permute-start.1 = (bf16[64,1024]{1,0:T(8,128)(2,1)}, bf16[64,1024]{1,0:T(8,128)(2,1)S(1)}, u32[]{:S(2)}, u32[]{:S(2)}) collective-permute-start(bf16[64,1024]{1,0:T(8,128)(2,1)} %bitcast.19), channel_id=1, source_target_pairs={{0,2},{1,3},{2,0},{3,1},{4,6},{5,7},{6,4},{7,5},{8,10},{9,11},{10,... | collective-permute-start | bytes 393224 | tf_op jit(solution)/shard_map/ppermute | solution.py:34
  3.7 3.7 %collective-permute-start = (bf16[64,1024]{1,0:T(8,128)(2,1)}, bf16[64,1024]{1,0:T(8,128)(2,1)S(1)}, u32[]{:S(2)}, u32[]{:S(2)}) collective-permute-start(bf16[64,1024]{1,0:T(8,128)(2,1)} %bitcast.20), channel_id=1, source_target_pairs={{0,1},{1,0},{2,3},{3,2},{4,5},{5,4},{6,7},{7,6},{8,9},{9,8},{10,11... | collective-permute-start | bytes 393224 | tf_op jit(solution)/shard_map/ppermute | solution.py:34
  7.4 14.3 %all-to-all-start = ((bf16[8,8,2048]{2,1,0:T(8,128)(2,1)}), bf16[8,8,2048]{2,1,0:T(8,128)(2,1)S(1)}, u32[]{:S(2)}, u32[]{:S(2)}) async-start(bf16[8,8,2048]{2,1,0:T(8,128)(2,1)} %bitcast.2), calls=%async_computation | async-start | bytes 524288 | tf_op jit(solution)/shard_map/all_to_all | solution.py:576
  13.4 13.5 %collective-permute-start.2 = (bf16[256,1024]{1,0:T(8,128)(2,1)}, bf16[256,1024]{1,0:T(8,128)(2,1)S(1)}, u32[]{:S(2)}, u32[]{:S(2)}) collective-permute-start(bf16[256,1024]{1,0:T(8,128)(2,1)} %refs_1_.2), channel_id=1, source_target_pairs={{0,2},{1,3},{2,0},{3,1},{4,6},{5,7},{6,4},{7,5},{8,10},{9,11},{10,... | collective-permute-start | bytes 1572872 | tf_op jit(solution)/shard_map/ppermute | solution.py:34
  14.9 1.5 %collective-permute-start.3 = (bf16[64,1024]{1,0:T(8,128)(2,1)S(1)}, bf16[64,1024]{1,0:T(8,128)(2,1)S(1)}, u32[]{:S(2)}, u32[]{:S(2)}) collective-permute-start(bf16[64,1024]{1,0:T(8,128)(2,1)S(1)} %collective-permute-done.1.refs_2_), channel_id=1, source_target_pairs={{0,1},{1,0},{2,3},{3,2},{4,5},{5,4},{6,7},{7,6},{8,9},{9,8},{10,11... | collective-permute-start | bytes 393224 | tf_op jit(solution)/shard_map/ppermute | solution.py:34
  14.9 20.1 %collective-permute-start.9 = (bf16[256,1024]{1,0:T(8,128)(2,1)}, bf16[256,1024]{1,0:T(8,128)(2,1)S(1)}, u32[]{:S(2)}, u32[]{:S(2)}) collective-permute-start(bf16[256,1024]{1,0:T(8,128)(2,1)} %refs_1_.2), channel_id=1, source_target_pairs={{0,1},{1,0},{2,3},{3,2},{4,5},{5,4},{6,7},{7,6},{8,9},{9,8},{10,11... | collective-permute-start | bytes 1572872 | tf_op jit(solution)/shard_map/ppermute | solution.py:34
  21.6 20.1 %copy-start.2 = (bf16[3,1024,256]{2,1,0:T(8,128)(2,1)S(1)}, bf16[3,1024,256]{2,1,0:T(8,128)(2,1)}, u32[]{:S(2)}) copy-start(bf16[3,1024,256]{2,1,0:T(8,128)(2,1)} %refs_7_.3) | copy-start | bytes 4718596
  21.6 20.1 %copy-start.6 = (s32[4]{0:T(128)S(1)}, s32[4]{0:T(128)}, u32[]{:S(2)}) copy-start(s32[4]{0:T(128)} %refs_0_.1) | copy-start | bytes 52
  21.6 12.1 %all-to-all-start.1 = ((bf16[8,32,256]{2,1,0:T(8,128)(2,1)}), bf16[8,32,256]{2,1,0:T(8,128)(2,1)S(1)}, u32[]{:S(2)}, u32[]{:S(2)}) async-start(bf16[8,32,256]{2,1,0:T(8,128)(2,1)} %bitcast.4), calls=%async_computation.1 | async-start | bytes 262144 | tf_op jit(solution)/shard_map/all_to_all | solution.py:585
  26.4 8.1 %collective-permute-start.6 = (bf16[64,2048]{1,0:T(8,128)(2,1)S(1)}, bf16[64,2048]{1,0:T(8,128)(2,1)S(1)}, u32[]{:S(2)}, u32[]{:S(2)}) collective-permute-start(bf16[64,2048]{1,0:T(8,128)(2,1)S(1)} %bitcast.11), channel_id=1, source_target_pairs={{0,2},{1,3},{2,0},{3,1},{4,6},{5,7},{6,4},{7,5},{8,10},{9,11},{10,... | collective-permute-start | bytes 786440 | tf_op jit(solution)/shard_map/ppermute | solution.py:34
  33.8 8.0 %collective-permute-start.11 = (bf16[256,1024]{1,0:T(8,128)(2,1)S(1)}, bf16[256,1024]{1,0:T(8,128)(2,1)S(1)}, u32[]{:S(2)}, u32[]{:S(2)}) collective-permute-start(bf16[256,1024]{1,0:T(8,128)(2,1)S(1)} %collective-permute-done.2.refs_5_), channel_id=1, source_target_pairs={{0,1},{1,0},{2,3},{3,2},{4,5},{5,4},{6,7},{7,6},{8,9},{9,8},{10,11... | collective-permute-start | bytes 1572872 | tf_op jit(solution)/shard_map/ppermute | solution.py:34
  33.8 2.3 %collective-permute-start.5 = (bf16[64,2048]{1,0:T(8,128)(2,1)S(1)}, bf16[64,2048]{1,0:T(8,128)(2,1)S(1)}, u32[]{:S(2)}, u32[]{:S(2)}) collective-permute-start(bf16[64,2048]{1,0:T(8,128)(2,1)S(1)} %bitcast.12), channel_id=1, source_target_pairs={{0,1},{1,0},{2,3},{3,2},{4,5},{5,4},{6,7},{7,6},{8,9},{9,8},{10,11... | collective-permute-start | bytes 786440 | tf_op jit(solution)/shard_map/ppermute | solution.py:34
  34.5 2.1 %collective-permute-start.7 = (bf16[64,2048]{1,0:T(8,128)(2,1)S(1)}, bf16[64,2048]{1,0:T(8,128)(2,1)S(1)}, u32[]{:S(2)}, u32[]{:S(2)}) collective-permute-start(bf16[64,2048]{1,0:T(8,128)(2,1)S(1)} %collective-permute-done.6.refs_2_), channel_id=1, source_target_pairs={{0,1},{1,0},{2,3},{3,2},{4,5},{5,4},{6,7},{7,6},{8,9},{9,8},{10,11... | collective-permute-start | bytes 786440 | tf_op jit(solution)/shard_map/ppermute | solution.py:34
  34.5 2.1 %collective-permute-start.8 = (bf16[256,256]{1,0:T(8,128)(2,1)S(1)}, bf16[256,256]{1,0:T(8,128)(2,1)S(1)}, u32[]{:S(2)}, u32[]{:S(2)}) collective-permute-start(bf16[256,256]{1,0:T(8,128)(2,1)S(1)} %bitcast.24), channel_id=1, source_target_pairs={{0,1},{1,0},{2,3},{3,2},{4,5},{5,4},{6,7},{7,6},{8,9},{9,8},{10,11... | collective-permute-start | bytes 393224 | tf_op jit(solution)/shard_map/ppermute | solution.py:34
  35.0 5.4 %collective-permute-start.4 = (bf16[256,256]{1,0:T(8,128)(2,1)S(1)}, bf16[256,256]{1,0:T(8,128)(2,1)S(1)}, u32[]{:S(2)}, u32[]{:S(2)}) collective-permute-start(bf16[256,256]{1,0:T(8,128)(2,1)S(1)} %bitcast.25), channel_id=1, source_target_pairs={{0,2},{1,3},{2,0},{3,1},{4,6},{5,7},{6,4},{7,5},{8,10},{9,11},{10,... | collective-permute-start | bytes 393224 | tf_op jit(solution)/shard_map/ppermute | solution.py:34
  40.4 1.3 %collective-permute-start.10 = (bf16[256,256]{1,0:T(8,128)(2,1)S(1)}, bf16[256,256]{1,0:T(8,128)(2,1)S(1)}, u32[]{:S(2)}, u32[]{:S(2)}) collective-permute-start(bf16[256,256]{1,0:T(8,128)(2,1)S(1)} %collective-permute-done.4.refs_1_), channel_id=1, source_target_pairs={{0,1},{1,0},{2,3},{3,2},{4,5},{5,4},{6,7},{7,6},{8,9},{9,8},{10,11... | collective-permute-start | bytes 393224 | tf_op jit(solution)/shard_map/ppermute | solution.py:34
  48.2 3.4 %collective-permute-start.12 = (bf16[2,64,1024]{2,1,0:T(8,128)(2,1)S(1)}, bf16[2,64,1024]{2,1,0:T(8,128)(2,1)S(1)}, u32[]{:S(2)}, u32[]{:S(2)}) collective-permute-start(bf16[2,64,1024]{2,1,0:T(8,128)(2,1)S(1)} %get-tuple-element.118), channel_id=1, source_target_pairs={{0,1},{1,0},{2,3},{3,2},{4,5},{5,4},{6,7},{7,6},{8,9},{9,8},{10,11... | collective-permute-start | bytes 786440 | tf_op jit(solution)/shard_map/ppermute | solution.py:34
  48.4 14.4 %collective-permute-start.14 = (bf16[4,512,128]{2,1,0:T(8,128)(2,1)}, bf16[4,512,128]{2,1,0:T(8,128)(2,1)S(1)}, u32[]{:S(2)}, u32[]{:S(2)}) collective-permute-start(bf16[4,512,128]{2,1,0:T(8,128)(2,1)} %get-tuple-element.130), channel_id=1, source_target_pairs={{0,4},{4,0},{8,12},{12,8},{16,20},{20,16},{24,28},{28,24},{1,5},{5... | collective-permute-start | bytes 1572872 | tf_op jit(solution)/shard_map/ppermute | solution.py:34
  50.2 14.4 %collective-permute-start.15 = (bf16[4,512,128]{2,1,0:T(8,128)(2,1)}, bf16[4,512,128]{2,1,0:T(8,128)(2,1)S(1)}, u32[]{:S(2)}, u32[]{:S(2)}) collective-permute-start(bf16[4,512,128]{2,1,0:T(8,128)(2,1)} %get-tuple-element.131), channel_id=1, source_target_pairs={{0,8},{4,12},{8,0},{12,4},{16,24},{20,28},{24,16},{28,20},{1,9},{5... | collective-permute-start | bytes 1572872 | tf_op jit(solution)/shard_map/ppermute | solution.py:34
  51.7 5.3 %collective-permute-start.13 = (bf16[64,1024]{1,0:T(8,128)(2,1)S(1)}, bf16[64,1024]{1,0:T(8,128)(2,1)S(1)}, u32[]{:S(2)}, u32[]{:S(2)}) collective-permute-start(bf16[64,1024]{1,0:T(8,128)(2,1)S(1)} %shard_map.114), channel_id=1, source_target_pairs={{0,2},{1,3},{2,0},{3,1},{4,6},{5,7},{6,4},{7,5},{8,10},{9,11},{10,... | collective-permute-start | bytes 393224 | tf_op jit(solution)/shard_map/ppermute | solution.py:34
  57.0 14.3 %copy-start.3 = (bf16[3,256,256]{2,1,0:T(8,128)(2,1)S(1)}, bf16[3,256,256]{2,1,0:T(8,128)(2,1)}, u32[]{:S(2)}) copy-start(bf16[3,256,256]{2,1,0:T(8,128)(2,1)} %get-tuple-element.139.refs_0_.refs_2_) | copy-start | bytes 1179652
  57.8 11.6 %all-to-all-start.2 = ((bf16[8,8,1024]{2,1,0:T(8,128)(2,1)}), bf16[8,8,1024]{2,1,0:T(8,128)(2,1)S(1)}, u32[]{:S(2)}, u32[]{:S(2)}) async-start(bf16[8,8,1024]{2,1,0:T(8,128)(2,1)} %bitcast.6), calls=%async_computation.2 | async-start | bytes 262144 | tf_op jit(solution)/shard_map/all_to_all | solution.py:609
  65.7 14.4 %copy-start.1 = (bf16[256,1024]{1,0:T(8,128)(2,1)S(1)}, bf16[256,1024]{1,0:T(8,128)(2,1)}, u32[]{:S(2)}) copy-start(bf16[256,1024]{1,0:T(8,128)(2,1)} %refs_1_.2) | copy-start | bytes 1572868
  69.4 5.0 %collective-permute-start.17 = (bf16[64,1024]{1,0:T(8,128)(2,1)S(1)}, bf16[64,1024]{1,0:T(8,128)(2,1)S(1)}, u32[]{:S(2)}, u32[]{:S(2)}) collective-permute-start(bf16[64,1024]{1,0:T(8,128)(2,1)S(1)} %bitcast.15), channel_id=1, source_target_pairs={{0,2},{1,3},{2,0},{3,1},{4,6},{5,7},{6,4},{7,5},{8,10},{9,11},{10,... | collective-permute-start | bytes 393224 | tf_op jit(solution)/shard_map/ppermute | solution.py:34
  69.9 6.6 %collective-permute-start.19 = (bf16[2,512,128]{2,1,0:T(8,128)(2,1)}, bf16[2,512,128]{2,1,0:T(8,128)(2,1)S(1)}, u32[]{:S(2)}, u32[]{:S(2)}) collective-permute-start(bf16[2,512,128]{2,1,0:T(8,128)(2,1)} %get-tuple-element.146), channel_id=1, source_target_pairs={{0,8},{4,12},{8,0},{12,4},{16,24},{20,28},{24,16},{28,20},{1,9},{5... | collective-permute-start | bytes 786440 | tf_op jit(solution)/shard_map/ppermute | solution.py:34
  69.9 6.6 %collective-permute-start.20 = (bf16[2,512,128]{2,1,0:T(8,128)(2,1)}, bf16[2,512,128]{2,1,0:T(8,128)(2,1)S(1)}, u32[]{:S(2)}, u32[]{:S(2)}) collective-permute-start(bf16[2,512,128]{2,1,0:T(8,128)(2,1)} %get-tuple-element.147), channel_id=1, source_target_pairs={{0,4},{4,0},{8,12},{12,8},{16,20},{20,16},{24,28},{28,24},{1,5},{5... | collective-permute-start | bytes 786440 | tf_op jit(solution)/shard_map/ppermute | solution.py:34
  71.2 3.2 %collective-permute-start.16 = (bf16[64,1024]{1,0:T(8,128)(2,1)S(1)}, bf16[64,1024]{1,0:T(8,128)(2,1)S(1)}, u32[]{:S(2)}, u32[]{:S(2)}) collective-permute-start(bf16[64,1024]{1,0:T(8,128)(2,1)S(1)} %bitcast.16), channel_id=1, source_target_pairs={{0,1},{1,0},{2,3},{3,2},{4,5},{5,4},{6,7},{7,6},{8,9},{9,8},{10,11... | collective-permute-start | bytes 393224 | tf_op jit(solution)/shard_map/ppermute | solution.py:34
  74.4 1.3 %collective-permute-start.18 = (bf16[64,1024]{1,0:T(8,128)(2,1)S(1)}, bf16[64,1024]{1,0:T(8,128)(2,1)S(1)}, u32[]{:S(2)}, u32[]{:S(2)}) collective-permute-start(bf16[64,1024]{1,0:T(8,128)(2,1)S(1)} %collective-permute-done.17.refs_2_), channel_id=1, source_target_pairs={{0,1},{1,0},{2,3},{3,2},{4,5},{5,4},{6,7},{7,6},{8,9},{9,8},{10,11... | collective-permute-start | bytes 393224 | tf_op jit(solution)/shard_map/ppermute | solution.py:34
  76.5 8.8 %collective-permute-start.22 = (bf16[4,256,128]{2,1,0:T(8,128)(2,1)S(1)}, bf16[4,256,128]{2,1,0:T(8,128)(2,1)S(1)}, u32[]{:S(2)}, u32[]{:S(2)}) collective-permute-start(bf16[4,256,128]{2,1,0:T(8,128)(2,1)S(1)} %get-tuple-element.163), channel_id=1, source_target_pairs={{0,4},{4,0},{8,12},{12,8},{16,20},{20,16},{24,28},{28,24},{1,5},{5... | collective-permute-start | bytes 786440 | tf_op jit(solution)/shard_map/ppermute | solution.py:34
  79.0 5.7 %copy-start = (bf16[3,1024,256]{2,1,0:T(8,128)(2,1)S(1)}, bf16[3,1024,256]{2,1,0:T(8,128)(2,1)}, u32[]{:S(2)}) copy-start(bf16[3,1024,256]{2,1,0:T(8,128)(2,1)} %refs_1_.3) | copy-start | bytes 4718596
  79.0 13.6 %collective-permute-start.21 = (bf16[1024,128]{1,0:T(8,128)(2,1)S(1)}, bf16[1024,128]{1,0:T(8,128)(2,1)S(1)}, u32[]{:S(2)}, u32[]{:S(2)}) collective-permute-start(bf16[1024,128]{1,0:T(8,128)(2,1)S(1)} %get-tuple-element.161), channel_id=1, source_target_pairs={{0,16},{4,20},{8,24},{12,28},{16,0},{20,4},{24,8},{28,12},{1,17},{... | collective-permute-start | bytes 786440 | tf_op jit(solution)/shard_map/ppermute | solution.py:34
  82.5 10.1 %copy-start.5 = (bf16[256,1024]{1,0:T(8,128)(2,1)S(1)}, bf16[256,1024]{1,0:T(8,128)(2,1)}, u32[]{:S(2)}) copy-start(bf16[256,1024]{1,0:T(8,128)(2,1)} %get-tuple-element.157.refs_4_.refs_1_) | copy-start | bytes 1572868
  82.5 13.2 %collective-permute-start.26 = (bf16[4,352,128]{2,1,0:T(8,128)(2,1)S(1)}, bf16[4,352,128]{2,1,0:T(8,128)(2,1)S(1)}, u32[]{:S(2)}, u32[]{:S(2)}) collective-permute-start(bf16[4,352,128]{2,1,0:T(8,128)(2,1)S(1)} %get-tuple-element.172), channel_id=1, source_target_pairs={{0,8},{4,12},{8,0},{12,4},{16,24},{20,28},{24,16},{28,20},{1,9},{5... | collective-permute-start | bytes 1081352 | tf_op jit(solution)/shard_map/ppermute | solution.py:34
  82.9 12.7 %collective-permute-start.25 = (bf16[4,416,128]{2,1,0:T(8,128)(2,1)S(1)}, bf16[4,416,128]{2,1,0:T(8,128)(2,1)S(1)}, u32[]{:S(2)}, u32[]{:S(2)}) collective-permute-start(bf16[4,416,128]{2,1,0:T(8,128)(2,1)S(1)} %get-tuple-element.171), channel_id=1, source_target_pairs={{0,4},{4,0},{8,12},{12,8},{16,20},{20,16},{24,28},{28,24},{1,5},{5... | collective-permute-start | bytes 1277960 | tf_op jit(solution)/shard_map/ppermute | solution.py:34
  92.6 8.1 %collective-permute-start.29 = (bf16[2,256,128]{2,1,0:T(8,128)(2,1)S(1)}, bf16[2,256,128]{2,1,0:T(8,128)(2,1)S(1)}, u32[]{:S(2)}, u32[]{:S(2)}) collective-permute-start(bf16[2,256,128]{2,1,0:T(8,128)(2,1)S(1)} %get-tuple-element.184), channel_id=1, source_target_pairs={{0,16},{4,20},{8,24},{12,28},{16,0},{20,4},{24,8},{28,12},{1,17},{... | collective-permute-start | bytes 393224 | tf_op jit(solution)/shard_map/ppermute | solution.py:34
  93.2 14.2 %collective-permute-start.23 = (bf16[2,64,1024]{2,1,0:T(8,128)(2,1)S(1)}, bf16[2,64,1024]{2,1,0:T(8,128)(2,1)S(1)}, u32[]{:S(2)}, u32[]{:S(2)}) collective-permute-start(bf16[2,64,1024]{2,1,0:T(8,128)(2,1)S(1)} %get-tuple-element.167), channel_id=1, source_target_pairs={{0,1},{1,0},{2,3},{3,2},{4,5},{5,4},{6,7},{7,6},{8,9},{9,8},{10,11... | collective-permute-start | bytes 786440 | tf_op jit(solution)/shard_map/ppermute | solution.py:34
  95.9 6.1 %collective-permute-start.28 = (bf16[2,352,128]{2,1,0:T(8,128)(2,1)S(1)}, bf16[2,352,128]{2,1,0:T(8,128)(2,1)S(1)}, u32[]{:S(2)}, u32[]{:S(2)}) collective-permute-start(bf16[2,352,128]{2,1,0:T(8,128)(2,1)S(1)} %get-tuple-element.182), channel_id=1, source_target_pairs={{0,4},{4,0},{8,12},{12,8},{16,20},{20,16},{24,28},{28,24},{1,5},{5... | collective-permute-start | bytes 540680 | tf_op jit(solution)/shard_map/ppermute | solution.py:34
  98.5 14.0 %copy-start.4 = (bf16[1,64,1024]{2,1,0:T(8,128)(2,1)S(1)}, bf16[1,64,1024]{2,1,0:T(8,128)(2,1)}, u32[]{:S(2)}) copy-start(bf16[1,64,1024]{2,1,0:T(8,128)(2,1)} %param.7) | copy-start | bytes 393220
  98.5 6.6 %collective-permute-start.27 = (bf16[2,416,128]{2,1,0:T(8,128)(2,1)S(1)}, bf16[2,416,128]{2,1,0:T(8,128)(2,1)S(1)}, u32[]{:S(2)}, u32[]{:S(2)}) collective-permute-start(bf16[2,416,128]{2,1,0:T(8,128)(2,1)S(1)} %get-tuple-element.181), channel_id=1, source_target_pairs={{0,8},{4,12},{8,0},{12,4},{16,24},{20,28},{24,16},{28,20},{1,9},{5... | collective-permute-start | bytes 638984 | tf_op jit(solution)/shard_map/ppermute | solution.py:34
  105.3 9.7 %collective-permute-start.30 = (bf16[768,128]{1,0:T(8,128)(2,1)S(1)}, bf16[768,128]{1,0:T(8,128)(2,1)S(1)}, u32[]{:S(2)}, u32[]{:S(2)}) collective-permute-start(bf16[768,128]{1,0:T(8,128)(2,1)S(1)} %get-tuple-element.190), channel_id=1, source_target_pairs={{0,16},{4,20},{8,24},{12,28},{16,0},{20,4},{24,8},{28,12},{1,17},{... | collective-permute-start | bytes 589832 | tf_op jit(solution)/shard_map/ppermute | solution.py:34
  107.5 5.0 %collective-permute-start.24 = (bf16[64,1024]{1,0:T(8,128)(2,1)S(1)}, bf16[64,1024]{1,0:T(8,128)(2,1)S(1)}, u32[]{:S(2)}, u32[]{:S(2)}) collective-permute-start(bf16[64,1024]{1,0:T(8,128)(2,1)S(1)} %shard_map.124), channel_id=1, source_target_pairs={{0,2},{1,3},{2,0},{3,1},{4,6},{5,7},{6,4},{7,5},{8,10},{9,11},{10,... | collective-permute-start | bytes 393224 | tf_op jit(solution)/shard_map/ppermute | solution.py:34
  108.9 6.1 %collective-permute-start.31 = (bf16[1,256,128]{2,1,0:T(8,128)(2,1)S(1)}, bf16[1,256,128]{2,1,0:T(8,128)(2,1)S(1)}, u32[]{:S(2)}, u32[]{:S(2)}) collective-permute-start(bf16[1,256,128]{2,1,0:T(8,128)(2,1)S(1)} %get-tuple-element.192), channel_id=1, source_target_pairs={{0,8},{4,12},{8,0},{12,4},{16,24},{20,28},{24,16},{28,20},{1,9},{5... | collective-permute-start | bytes 196616 | tf_op jit(solution)/shard_map/ppermute | solution.py:34

commit v6 on v5

--- a/solution.py
+++ b/solution.py
@@ -435,7 +435,7 @@
 
 def qkv_parts(grads):
     flat = jnp.concatenate([grad.T for grad in grads], 0)
-    first = 13 * flat.shape[0] // 24
+    first = 7 * flat.shape[0] // 12
     return flat[:first], flat[first:]
 
 
@@ -446,7 +446,7 @@
 
 
 def qkv_part_shapes(width, dim, groups):
-    first = 13 * 3 * width // 24
+    first = 7 * 3 * width // 12
     return tuple(
         shape((groups // 2, rows, dim // groups)) for rows in (first, 3 * width - first)
     )
@@ -637,11 +637,13 @@
             (s_grads, send_x, keep_x, t_came, o_send, o_keep)
         )
         o_came = swap(o_send, "frames", 4)
+        s_kept = qkv_keeps(s_grads, normed_x, groups, 50_000_000_000)
+        came_a, came_b = swap(s_sent[0], "frames", 1), swap(s_sent[1], "frames", 2)
+        send_a, keep_a = halve([s_kept[0]], [came_a])
+        send_a, keep_a, t_keep = after((send_a, keep_a, t_keep))
         t_qkv, t_out = last_sums([(t_keep, t_came)], 50_000_000_000)
-        s_kept = qkv_keeps(s_grads, normed_x, groups, 50_000_000_000)
-        came = [swap(s_sent[0], "frames", 1), swap(s_sent[1], "frames", 2)]
-        came, t_qkv, t_out = after((came, t_qkv, t_out))
-        send_a, send_b, keep_a, keep_b = halve(s_kept, came)
+        came_b, t_qkv, t_out = after((came_b, t_qkv, t_out))
+        send_b, keep_b = halve([s_kept[1]], [came_b])
         came = [swap(send_a, "frames", 2), swap(send_b, "frames", 1)]
         o_send, o_keep = halve([o_keep], [o_came], flops=50_000_000_000)
         came, o_send, o_keep = after((came, o_send, o_keep))

time: 117 us -> 117 us (level)
  waiting for transfers between devices: 46.9 us -> 48.7 us
  starting transfers between devices: 40.7 us -> 39.3 us
    ppermute x32, waiting for transfers between devices: 34.9 us -> 36.7 us  [swap(): return lax.ppermute(value, axis, [(i, i ^ by) for i in range(size)])]
    ppermute x32, starting transfers between devices: 25.7 us -> 24.3 us  [swap(): return lax.ppermute(value, axis, [(i, i ^ by) for i in range(size)])]
    pallas_call x22 -> x23, Pallas kernels: 27.5 us -> 27.5 us  [run(): pl.pallas_call(wrapped, out_shape=tuple((pltpu.HBM(o.shape, o.dtype) if w...]
  transfers between devices with their start and end apart: 35 -> 35, of which waited for: 23 -> 24; matrix products, arithmetic and copies ran while one was open for 0% -> 0% of each run, Pallas kernels for 17% -> 17%
where the time goes in v6:
time: 117 us
  waiting for transfers between devices  48.7 us (42%)
  starting transfers between devices  39.3 us (34%)
  Pallas kernels  27.5 us (24%)
    ppermute x32, waiting for transfers between devices, swap(): return lax.ppermute(value, axis, [(i, i ^ by) for i in range(size)])  36.7 us
    pallas_call x23, Pallas kernels, run(): pl.pallas_call(wrapped, out_shape=tuple((pltpu.HBM(o.shape, o.dtype) if w...  27.5 us
    ppermute x32, starting transfers between devices, swap(): return lax.ppermute(value, axis, [(i, i ^ by) for i in range(size)])  24.3 us
    all_to_all x1, waiting for transfers between devices, shards(): lax.all_to_all(attn_send.reshape(groups, mp * per, width), 'frames', 0, 0...  6.83 us
    all_to_all x1, starting transfers between devices, shards(): lax.all_to_all(xg.reshape(groups, per, 2 * dim), 'frames', 0, 0, tiled=True)  6.03 us
    all_to_all x1, starting transfers between devices, shards(): lax.all_to_all(attn_send.reshape(groups, mp * per, width), 'frames', 0, 0...  4.78 us
    all_to_all x1, starting transfers between devices, shards(): lax.all_to_all(d_hidden.reshape(groups, per, dim), 'frames', 0, 0, tiled=...  4.24 us
    all_to_all x1, waiting for transfers between devices, shards(): lax.all_to_all(d_hidden.reshape(groups, per, dim), 'frames', 0, 0, tiled=...  3.77 us
  transfers between devices with their start and end apart: 35, of which 24 were waited for; matrix products, arithmetic and copies ran while one was open for 0% of the time, Pallas kernels for 17%

profile of v6, /device:TPU:0, one launch (start us, length us, event | category | flops | bytes accessed | tf_op | source)
XLA Modules:
  0.0 116.6 jit_solution(9558856430558205283)
XLA Ops:
  0.6 3.0 %collective-permute-start.1 = (bf16[64,1024]{1,0:T(8,128)(2,1)}, bf16[64,1024]{1,0:T(8,128)(2,1)S(1)}, u32[]{:S(2)}, u32[]{:S(2)}) collective-permute-start(bf16[64,1024]{1,0:T(8,128)(2,1)} %bitcast.19), channel_id=1, source_target_pairs={{0,2},{1,3},{2,0},{3,1},{4,6},{5,7},{6,4},{7,5},{8,10},{9,11},{10,... | collective-permute-start | bytes 393224 | tf_op jit(solution)/shard_map/ppermute | solution.py:34
  3.7 1.7 %shard_map.110 = bf16[64,2048]{1,0:T(8,128)(2,1)} custom-call(bf16[64,1024]{1,0:T(8,128)(2,1)} %bitcast.21, bf16[64,1024]{1,0:T(8,128)(2,1)} %bitcast.29), custom_call_target="tpu_custom_call" | custom-call | flops 1000 | bytes 1000 | tf_op jit(solution)/shard_map/pallas_call | solution.py:110
  5.4 2.0 %collective-permute-done.1.refs_2_ = bf16[64,1024]{1,0:T(8,128)(2,1)S(1)} collective-permute-done((bf16[64,1024]{1,0:T(8,128)(2,1)}, bf16[64,1024]{1,0:T(8,128)(2,1)S(1)}, u32[]{:S(2)}, u32[]{:S(2)}) %collective-permute-start.1) | collective-permute-done | bytes 131104 | tf_op jit(solution)/shard_map/ppermute | solution.py:34
  7.4 6.0 %all-to-all-start = ((bf16[8,8,2048]{2,1,0:T(8,128)(2,1)}), bf16[8,8,2048]{2,1,0:T(8,128)(2,1)S(1)}, u32[]{:S(2)}, u32[]{:S(2)}) async-start(bf16[8,8,2048]{2,1,0:T(8,128)(2,1)} %bitcast.2), calls=%async_computation | async-start | bytes 524288 | tf_op jit(solution)/shard_map/all_to_all | solution.py:576
  13.4 1.5 %collective-permute-start.2 = (bf16[256,1024]{1,0:T(8,128)(2,1)}, bf16[256,1024]{1,0:T(8,128)(2,1)S(1)}, u32[]{:S(2)}, u32[]{:S(2)}) collective-permute-start(bf16[256,1024]{1,0:T(8,128)(2,1)} %refs_1_.2), channel_id=1, source_target_pairs={{0,2},{1,3},{2,0},{3,1},{4,6},{5,7},{6,4},{7,5},{8,10},{9,11},{10,... | collective-permute-start | bytes 1572872 | tf_op jit(solution)/shard_map/ppermute | solution.py:34
  14.9 0.5 collective-permute-start.9
  15.4 1.0 collective-permute-done.3.refs_3_
  16.4 3.8 %shard_map.111 = (bf16[256,1024]{1,0:T(8,128)(2,1)}, bf16[3,256,256]{2,1,0:T(8,128)(2,1)}, bf16[256,256]{1,0:T(8,128)(2,1)}) custom-call(bf16[64,1024]{1,0:T(8,128)(2,1)} %bitcast.22, bf16[64,1024]{1,0:T(8,128)(2,1)S(1)} %collective-permute-done.refs_1_, bf16[64,1024]{1,0:T(8,128)(2,1)S(1)} %collective-permute-done.1.refs_2_, ...), custom_call_target="tpu_custom_call" | custom-call | flops 1000 | bytes 1000 | tf_op jit(solution)/shard_map/pallas_call | solution.py:110
  20.2 1.4 %all-to-all-done = bf16[8,8,2048]{2,1,0:T(8,128)(2,1)S(1)} async-done(((bf16[8,8,2048]{2,1,0:T(8,128)(2,1)}), bf16[8,8,2048]{2,1,0:T(8,128)(2,1)S(1)}, u32[]{:S(2)}, u32[]{:S(2)}) %all-to-all-start) | async-done | bytes 262176 | tf_op jit(solution)/shard_map/all_to_all | solution.py:576
  21.6 4.8 %all-to-all-start.1 = ((bf16[8,32,256]{2,1,0:T(8,128)(2,1)}), bf16[8,32,256]{2,1,0:T(8,128)(2,1)S(1)}, u32[]{:S(2)}, u32[]{:S(2)}) async-start(bf16[8,32,256]{2,1,0:T(8,128)(2,1)} %bitcast.4), calls=%async_computation.1 | async-start | bytes 262144 | tf_op jit(solution)/shard_map/all_to_all | solution.py:585
  26.4 0.5 collective-permute-start.6
  26.9 6.8 %all-to-all-done.1 = bf16[8,32,256]{2,1,0:T(8,128)(2,1)S(1)} async-done(((bf16[8,32,256]{2,1,0:T(8,128)(2,1)}), bf16[8,32,256]{2,1,0:T(8,128)(2,1)S(1)}, u32[]{:S(2)}, u32[]{:S(2)}) %all-to-all-start.1) | async-done | bytes 131104 | tf_op jit(solution)/shard_map/all_to_all | solution.py:585
  33.8 0.5 collective-permute-start.5
  34.3 0.2 collective-permute-done.6.refs_2_
  34.5 0.5 collective-permute-start.8
  35.0 0.5 collective-permute-start.4
  35.5 0.5 collective-permute-done.5.refs_1_
  36.0 0.6 collective-permute-done.8.refs_6_
  36.6 2.4 %shard_map.112 = (f32[256,1024]{1,0:T(8,128)S(1)}, bf16[256,1024]{1,0:T(8,128)(2,1)S(1)}, bf16[256,256]{1,0:T(8,128)(2,1)S(1)}) custom-call(bf16[64,2048]{1,0:T(8,128)(2,1)S(1)} %bitcast.13, bf16[64,2048]{1,0:T(8,128)(2,1)S(1)} %collective-permute-done.5.refs_1_, bf16[64,2048]{1,0:T(8,128)(2,1)S(1)} %collective-permute-done.6.refs_2_, ...), custom_call_target="tpu_custom_call" | custom-call | flops 1000 | bytes 1000 | tf_op jit(solution)/shard_map/pallas_call | solution.py:110
  39.0 1.4 %collective-permute-done.4.refs_1_ = bf16[256,256]{1,0:T(8,128)(2,1)S(1)} collective-permute-done((bf16[256,256]{1,0:T(8,128)(2,1)S(1)}, bf16[256,256]{1,0:T(8,128)(2,1)S(1)}, u32[]{:S(2)}, u32[]{:S(2)}) %collective-permute-start.4) | collective-permute-done | bytes 131104 | tf_op jit(solution)/shard_map/ppermute | solution.py:34
  40.4 1.3 %collective-permute-done.10.refs_2_ = bf16[256,256]{1,0:T(8,128)(2,1)S(1)} collective-permute-done((bf16[256,256]{1,0:T(8,128)(2,1)S(1)}, bf16[256,256]{1,0:T(8,128)(2,1)S(1)}, u32[]{:S(2)}, u32[]{:S(2)}) %collective-permute-start.10) | collective-permute-done | bytes 131104 | tf_op jit(solution)/shard_map/ppermute | solution.py:34
  41.8 6.4 %shard_map.113 = (bf16[2,64,1024]{2,1,0:T(8,128)(2,1)S(1)}, bf16[2,64,1024]{2,1,0:T(8,128)(2,1)S(1)}, bf16[256,1024]{1,0:T(8,128)(2,1)S(1)}, bf16[64,1024]{1,0:T...) custom-call(s32[4]{0:T(128)S(1)} %copy-done.6, ...), custom_call_target="tpu_custom_call" | custom-call | flops 1000 | bytes 1000 | tf_op jit(solution)/shard_map/pallas_call | solution.py:110
  48.4 1.8 %collective-permute-start.14 = (bf16[4,512,128]{2,1,0:T(8,128)(2,1)}, bf16[4,512,128]{2,1,0:T(8,128)(2,1)S(1)}, u32[]{:S(2)}, u32[]{:S(2)}) collective-permute-start(bf16[4,512,128]{2,1,0:T(8,128)(2,1)} %get-tuple-element.132), channel_id=1, source_target_pairs={{0,4},{4,0},{8,12},{12,8},{16,20},{20,16},{24,28},{28,24},{1,5},{5... | collective-permute-start | bytes 1572872 | tf_op jit(solution)/shard_map/ppermute | solution.py:34
  50.2 1.5 %collective-permute-start.15 = (bf16[4,512,128]{2,1,0:T(8,128)(2,1)}, bf16[4,512,128]{2,1,0:T(8,128)(2,1)S(1)}, u32[]{:S(2)}, u32[]{:S(2)}) collective-permute-start(bf16[4,512,128]{2,1,0:T(8,128)(2,1)} %get-tuple-element.133), channel_id=1, source_target_pairs={{0,8},{4,12},{8,0},{12,4},{16,24},{20,28},{24,16},{28,20},{1,9},{5... | collective-permute-start | bytes 1572872 | tf_op jit(solution)/shard_map/ppermute | solution.py:34
  51.7 0.6 collective-permute-start.13
  52.3 0.8 shard_map.115
  53.1 3.9 %collective-permute-done.13.refs_2_ = bf16[64,1024]{1,0:T(8,128)(2,1)S(1)} collective-permute-done((bf16[64,1024]{1,0:T(8,128)(2,1)S(1)}, bf16[64,1024]{1,0:T(8,128)(2,1)S(1)}, u32[]{:S(2)}, u32[]{:S(2)}) %collective-permute-start.13) | collective-permute-done | bytes 131104 | tf_op jit(solution)/shard_map/ppermute | solution.py:34
  57.0 0.9 shard_map.116
  57.8 4.2 %all-to-all-start.2 = ((bf16[8,8,1024]{2,1,0:T(8,128)(2,1)}), bf16[8,8,1024]{2,1,0:T(8,128)(2,1)S(1)}, u32[]{:S(2)}, u32[]{:S(2)}) async-start(bf16[8,8,1024]{2,1,0:T(8,128)(2,1)} %bitcast.6), calls=%async_computation.2 | async-start | bytes 262144 | tf_op jit(solution)/shard_map/all_to_all | solution.py:609
  62.1 0.7 collective-permute-done.14.refs_2_
  62.8 1.7 %collective-permute-done.15.refs_3_ = bf16[4,512,128]{2,1,0:T(8,128)(2,1)S(1)} collective-permute-done((bf16[4,512,128]{2,1,0:T(8,128)(2,1)}, bf16[4,512,128]{2,1,0:T(8,128)(2,1)S(1)}, u32[]{:S(2)}, u32[]{:S(2)}) %collective-permute-start.15) | collective-permute-done | bytes 524320 | tf_op jit(solution)/shard_map/ppermute | solution.py:34
  64.5 1.1 shard_map.117
  65.7 3.8 %all-to-all-done.2 = bf16[8,8,1024]{2,1,0:T(8,128)(2,1)S(1)} async-done(((bf16[8,8,1024]{2,1,0:T(8,128)(2,1)}), bf16[8,8,1024]{2,1,0:T(8,128)(2,1)S(1)}, u32[]{:S(2)}, u32[]{:S(2)}) %all-to-all-start.2) | async-done | bytes 131104 | tf_op jit(solution)/shard_map/all_to_all | solution.py:609
  69.4 0.5 collective-permute-start.17
  69.9 1.3 %collective-permute-start.20 = (bf16[2,512,128]{2,1,0:T(8,128)(2,1)}, bf16[2,512,128]{2,1,0:T(8,128)(2,1)S(1)}, u32[]{:S(2)}, u32[]{:S(2)}) collective-permute-start(bf16[2,512,128]{2,1,0:T(8,128)(2,1)} %get-tuple-element.149), channel_id=1, source_target_pairs={{0,4},{4,0},{8,12},{12,8},{16,20},{20,16},{24,28},{28,24},{1,5},{5... | collective-permute-start | bytes 786440 | tf_op jit(solution)/shard_map/ppermute | solution.py:34
  71.3 1.5 %shard_map.118 = (f32[4,256,256]{2,1,0:T(8,128)S(1)}, bf16[256,256]{1,0:T(8,128)(2,1)S(1)}) custom-call(bf16[3,256,256]{2,1,0:T(8,128)(2,1)S(1)} %copy-done.3, bf16[256,256]{1,0:T(8,128)(2,1)} %get-tuple-element.142.refs_1_), custom_call_target="tpu_custom_call" | custom-call | flops 1000 | bytes 1000 | tf_op jit(solution)/shard_map/pallas_call | solution.py:110
  72.8 1.6 %collective-permute-done.17.refs_2_ = bf16[64,1024]{1,0:T(8,128)(2,1)S(1)} collective-permute-done((bf16[64,1024]{1,0:T(8,128)(2,1)S(1)}, bf16[64,1024]{1,0:T(8,128)(2,1)S(1)}, u32[]{:S(2)}, u32[]{:S(2)}) %collective-permute-start.17) | collective-permute-done | bytes 131104 | tf_op jit(solution)/shard_map/ppermute | solution.py:34
  74.4 1.3 %collective-permute-done.18.refs_3_ = bf16[64,1024]{1,0:T(8,128)(2,1)S(1)} collective-permute-done((bf16[64,1024]{1,0:T(8,128)(2,1)S(1)}, bf16[64,1024]{1,0:T(8,128)(2,1)S(1)}, u32[]{:S(2)}, u32[]{:S(2)}) %collective-permute-start.18) | collective-permute-done | bytes 131104 | tf_op jit(solution)/shard_map/ppermute | solution.py:34
  75.7 0.5 shard_map.119
  76.3 0.3 collective-permute-done.19.refs_2_
  76.5 1.3 %collective-permute-start.22 = (bf16[4,256,128]{2,1,0:T(8,128)(2,1)S(1)}, bf16[4,256,128]{2,1,0:T(8,128)(2,1)S(1)}, u32[]{:S(2)}, u32[]{:S(2)}) collective-permute-start(bf16[4,256,128]{2,1,0:T(8,128)(2,1)S(1)} %get-tuple-element.165), channel_id=1, source_target_pairs={{0,4},{4,0},{8,12},{12,8},{16,20},{20,16},{24,28},{28,24},{1,5},{5... | collective-permute-start | bytes 786440 | tf_op jit(solution)/shard_map/ppermute | solution.py:34
  77.8 1.2 shard_map.120
  79.0 1.1 collective-permute-start.21
  80.1 2.4 %shard_map.121 = (bf16[3,256,256]{2,1,0:T(8,128)(2,1)S(1)}, bf16[4,448,128]{2,1,0:T(8,128)(2,1)S(1)}, bf16[4,320,128]{2,1,0:T(8,128)(2,1)S(1)}) custom-call(bf16[256,1024]{1,0:T(8,128)(2,1)S(1)} %get-tuple-element.157.refs_0_, bf16[256,1024]{1,0:T(8,128)(2,1)S(1)} %copy-done.1, bf16[3,256,256]{2,1,0:T(8,128)(2,1)S(1)} %copy-done.3, ...), custom_call_target="tpu_custom_call" | custom-call | flops 1000 | bytes 1000 | tf_op jit(solution)/shard_map/pallas_call | solution.py:110
  82.5 0.4 collective-permute-start.26
  82.9 1.8 %collective-permute-start.25 = (bf16[4,448,128]{2,1,0:T(8,128)(2,1)S(1)}, bf16[4,448,128]{2,1,0:T(8,128)(2,1)S(1)}, u32[]{:S(2)}, u32[]{:S(2)}) collective-permute-start(bf16[4,448,128]{2,1,0:T(8,128)(2,1)S(1)} %get-tuple-element.172), channel_id=1, source_target_pairs={{0,4},{4,0},{8,12},{12,8},{16,20},{20,16},{24,28},{28,24},{1,5},{5... | collective-permute-start | bytes 1376264 | tf_op jit(solution)/shard_map/ppermute | solution.py:34
  84.7 0.7 shard_map.122
  85.5 7.1 %collective-permute-done.21.refs_1_ = bf16[1024,128]{1,0:T(8,128)(2,1)S(1)} collective-permute-done((bf16[1024,128]{1,0:T(8,128)(2,1)S(1)}, bf16[1024,128]{1,0:T(8,128)(2,1)S(1)}, u32[]{:S(2)}, u32[]{:S(2)}) %collective-permute-start.21) | collective-permute-done | bytes 262176 | tf_op jit(solution)/shard_map/ppermute | solution.py:34
  92.6 0.6 shard_map.126
  93.3 1.2 %collective-permute-done.25.refs_1_ = bf16[4,448,128]{2,1,0:T(8,128)(2,1)S(1)} collective-permute-done((bf16[4,448,128]{2,1,0:T(8,128)(2,1)S(1)}, bf16[4,448,128]{2,1,0:T(8,128)(2,1)S(1)}, u32[]{:S(2)}, u32[]{:S(2)}) %collective-permute-start.25) | collective-permute-done | bytes 458784 | tf_op jit(solution)/shard_map/ppermute | solution.py:34
  94.7 0.7 collective-permute-start.27
  95.3 1.0 shard_map.128
  96.5 1.2 %collective-permute-start.28 = (bf16[2,320,128]{2,1,0:T(8,128)(2,1)S(1)}, bf16[2,320,128]{2,1,0:T(8,128)(2,1)S(1)}, u32[]{:S(2)}, u32[]{:S(2)}) collective-permute-start(bf16[2,320,128]{2,1,0:T(8,128)(2,1)S(1)} %get-tuple-element.186), channel_id=1, source_target_pairs={{0,4},{4,0},{8,12},{12,8},{16,20},{20,16},{24,28},{28,24},{1,5},{5... | collective-permute-start | bytes 491528 | tf_op jit(solution)/shard_map/ppermute | solution.py:34
  97.7 2.7 %collective-permute-done.29.refs_1_ = bf16[2,256,128]{2,1,0:T(8,128)(2,1)S(1)} collective-permute-done((bf16[2,256,128]{2,1,0:T(8,128)(2,1)S(1)}, bf16[2,256,128]{2,1,0:T(8,128)(2,1)S(1)}, u32[]{:S(2)}, u32[]{:S(2)}) %collective-permute-start.29) | collective-permute-done | bytes 131104 | tf_op jit(solution)/shard_map/ppermute | solution.py:34
  100.4 2.4 %collective-permute-done.28.refs_3_ = bf16[2,320,128]{2,1,0:T(8,128)(2,1)S(1)} collective-permute-done((bf16[2,320,128]{2,1,0:T(8,128)(2,1)S(1)}, bf16[2,320,128]{2,1,0:T(8,128)(2,1)S(1)}, u32[]{:S(2)}, u32[]{:S(2)}) %collective-permute-start.28) | collective-permute-done | bytes 163872 | tf_op jit(solution)/shard_map/ppermute | solution.py:34
  102.9 1.5 %collective-permute-done.27.refs_2_ = bf16[2,448,128]{2,1,0:T(8,128)(2,1)S(1)} collective-permute-done((bf16[2,448,128]{2,1,0:T(8,128)(2,1)S(1)}, bf16[2,448,128]{2,1,0:T(8,128)(2,1)S(1)}, u32[]{:S(2)}, u32[]{:S(2)}) %collective-permute-start.27) | collective-permute-done | bytes 229408 | tf_op jit(solution)/shard_map/ppermute | solution.py:34
  104.4 0.7 collective-permute-start.30
  105.2 0.9 collective-permute-start.24
  106.1 3.3 %collective-permute-start.31 = (bf16[1,256,128]{2,1,0:T(8,128)(2,1)S(1)}, bf16[1,256,128]{2,1,0:T(8,128)(2,1)S(1)}, u32[]{:S(2)}, u32[]{:S(2)}) collective-permute-start(bf16[1,256,128]{2,1,0:T(8,128)(2,1)S(1)} %get-tuple-element.196), channel_id=1, source_target_pairs={{0,8},{4,12},{8,0},{12,4},{16,24},{20,28},{24,16},{28,20},{1,9},{5... | collective-permute-start | bytes 196616 | tf_op jit(solution)/shard_map/ppermute | solution.py:34
  109.4 1.0 collective-permute-done.24.refs_2_
  110.3 0.9 shard_map.125
  111.3 0.4 collective-permute-done.31
  111.7 3.8 %collective-permute-done.30.refs_1_ = bf16[768,128]{1,0:T(8,128)(2,1)S(1)} collective-permute-done((bf16[768,128]{1,0:T(8,128)(2,1)S(1)}, bf16[768,128]{1,0:T(8,128)(2,1)S(1)}, u32[]{:S(2)}, u32[]{:S(2)}) %collective-permute-start.30) | collective-permute-done | bytes 196640 | tf_op jit(solution)/shard_map/ppermute | solution.py:34
  115.5 1.0 shard_map.132
  (43 shorter events, 1.0 us)
Async XLA Ops:
  0.6 6.7 %collective-permute-start.1 = (bf16[64,1024]{1,0:T(8,128)(2,1)}, bf16[64,1024]{1,0:T(8,128)(2,1)S(1)}, u32[]{:S(2)}, u32[]{:S(2)}) collective-permute-start(bf16[64,1024]{1,0:T(8,128)(2,1)} %bitcast.19), channel_id=1, source_target_pairs={{0,2},{1,3},{2,0},{3,1},{4,6},{5,7},{6,4},{7,5},{8,10},{9,11},{10,... | collective-permute-start | bytes 393224 | tf_op jit(solution)/shard_map/ppermute | solution.py:34
  3.7 3.7 %collective-permute-start = (bf16[64,1024]{1,0:T(8,128)(2,1)}, bf16[64,1024]{1,0:T(8,128)(2,1)S(1)}, u32[]{:S(2)}, u32[]{:S(2)}) collective-permute-start(bf16[64,1024]{1,0:T(8,128)(2,1)} %bitcast.20), channel_id=1, source_target_pairs={{0,1},{1,0},{2,3},{3,2},{4,5},{5,4},{6,7},{7,6},{8,9},{9,8},{10,11... | collective-permute-start | bytes 393224 | tf_op jit(solution)/shard_map/ppermute | solution.py:34
  7.4 14.3 %all-to-all-start = ((bf16[8,8,2048]{2,1,0:T(8,128)(2,1)}), bf16[8,8,2048]{2,1,0:T(8,128)(2,1)S(1)}, u32[]{:S(2)}, u32[]{:S(2)}) async-start(bf16[8,8,2048]{2,1,0:T(8,128)(2,1)} %bitcast.2), calls=%async_computation | async-start | bytes 524288 | tf_op jit(solution)/shard_map/all_to_all | solution.py:576
  13.4 13.5 %collective-permute-start.2 = (bf16[256,1024]{1,0:T(8,128)(2,1)}, bf16[256,1024]{1,0:T(8,128)(2,1)S(1)}, u32[]{:S(2)}, u32[]{:S(2)}) collective-permute-start(bf16[256,1024]{1,0:T(8,128)(2,1)} %refs_1_.2), channel_id=1, source_target_pairs={{0,2},{1,3},{2,0},{3,1},{4,6},{5,7},{6,4},{7,5},{8,10},{9,11},{10,... | collective-permute-start | bytes 1572872 | tf_op jit(solution)/shard_map/ppermute | solution.py:34
  14.9 1.5 %collective-permute-start.3 = (bf16[64,1024]{1,0:T(8,128)(2,1)S(1)}, bf16[64,1024]{1,0:T(8,128)(2,1)S(1)}, u32[]{:S(2)}, u32[]{:S(2)}) collective-permute-start(bf16[64,1024]{1,0:T(8,128)(2,1)S(1)} %collective-permute-done.1.refs_2_), channel_id=1, source_target_pairs={{0,1},{1,0},{2,3},{3,2},{4,5},{5,4},{6,7},{7,6},{8,9},{9,8},{10,11... | collective-permute-start | bytes 393224 | tf_op jit(solution)/shard_map/ppermute | solution.py:34
  14.9 20.1 %collective-permute-start.9 = (bf16[256,1024]{1,0:T(8,128)(2,1)}, bf16[256,1024]{1,0:T(8,128)(2,1)S(1)}, u32[]{:S(2)}, u32[]{:S(2)}) collective-permute-start(bf16[256,1024]{1,0:T(8,128)(2,1)} %refs_1_.2), channel_id=1, source_target_pairs={{0,1},{1,0},{2,3},{3,2},{4,5},{5,4},{6,7},{7,6},{8,9},{9,8},{10,11... | collective-permute-start | bytes 1572872 | tf_op jit(solution)/shard_map/ppermute | solution.py:34
  21.6 20.1 %copy-start.2 = (bf16[3,1024,256]{2,1,0:T(8,128)(2,1)S(1)}, bf16[3,1024,256]{2,1,0:T(8,128)(2,1)}, u32[]{:S(2)}) copy-start(bf16[3,1024,256]{2,1,0:T(8,128)(2,1)} %refs_7_.3) | copy-start | bytes 4718596
  21.6 20.1 %copy-start.6 = (s32[4]{0:T(128)S(1)}, s32[4]{0:T(128)}, u32[]{:S(2)}) copy-start(s32[4]{0:T(128)} %refs_0_.1) | copy-start | bytes 52
  21.6 12.1 %all-to-all-start.1 = ((bf16[8,32,256]{2,1,0:T(8,128)(2,1)}), bf16[8,32,256]{2,1,0:T(8,128)(2,1)S(1)}, u32[]{:S(2)}, u32[]{:S(2)}) async-start(bf16[8,32,256]{2,1,0:T(8,128)(2,1)} %bitcast.4), calls=%async_computation.1 | async-start | bytes 262144 | tf_op jit(solution)/shard_map/all_to_all | solution.py:585
  26.4 8.1 %collective-permute-start.6 = (bf16[64,2048]{1,0:T(8,128)(2,1)S(1)}, bf16[64,2048]{1,0:T(8,128)(2,1)S(1)}, u32[]{:S(2)}, u32[]{:S(2)}) collective-permute-start(bf16[64,2048]{1,0:T(8,128)(2,1)S(1)} %bitcast.11), channel_id=1, source_target_pairs={{0,2},{1,3},{2,0},{3,1},{4,6},{5,7},{6,4},{7,5},{8,10},{9,11},{10,... | collective-permute-start | bytes 786440 | tf_op jit(solution)/shard_map/ppermute | solution.py:34
  33.8 8.0 %collective-permute-start.11 = (bf16[256,1024]{1,0:T(8,128)(2,1)S(1)}, bf16[256,1024]{1,0:T(8,128)(2,1)S(1)}, u32[]{:S(2)}, u32[]{:S(2)}) collective-permute-start(bf16[256,1024]{1,0:T(8,128)(2,1)S(1)} %collective-permute-done.2.refs_5_), channel_id=1, source_target_pairs={{0,1},{1,0},{2,3},{3,2},{4,5},{5,4},{6,7},{7,6},{8,9},{9,8},{10,11... | collective-permute-start | bytes 1572872 | tf_op jit(solution)/shard_map/ppermute | solution.py:34
  33.8 2.3 %collective-permute-start.5 = (bf16[64,2048]{1,0:T(8,128)(2,1)S(1)}, bf16[64,2048]{1,0:T(8,128)(2,1)S(1)}, u32[]{:S(2)}, u32[]{:S(2)}) collective-permute-start(bf16[64,2048]{1,0:T(8,128)(2,1)S(1)} %bitcast.12), channel_id=1, source_target_pairs={{0,1},{1,0},{2,3},{3,2},{4,5},{5,4},{6,7},{7,6},{8,9},{9,8},{10,11... | collective-permute-start | bytes 786440 | tf_op jit(solution)/shard_map/ppermute | solution.py:34
  34.5 2.1 %collective-permute-start.7 = (bf16[64,2048]{1,0:T(8,128)(2,1)S(1)}, bf16[64,2048]{1,0:T(8,128)(2,1)S(1)}, u32[]{:S(2)}, u32[]{:S(2)}) collective-permute-start(bf16[64,2048]{1,0:T(8,128)(2,1)S(1)} %collective-permute-done.6.refs_2_), channel_id=1, source_target_pairs={{0,1},{1,0},{2,3},{3,2},{4,5},{5,4},{6,7},{7,6},{8,9},{9,8},{10,11... | collective-permute-start | bytes 786440 | tf_op jit(solution)/shard_map/ppermute | solution.py:34
  34.5 2.1 %collective-permute-start.8 = (bf16[256,256]{1,0:T(8,128)(2,1)S(1)}, bf16[256,256]{1,0:T(8,128)(2,1)S(1)}, u32[]{:S(2)}, u32[]{:S(2)}) collective-permute-start(bf16[256,256]{1,0:T(8,128)(2,1)S(1)} %bitcast.24), channel_id=1, source_target_pairs={{0,1},{1,0},{2,3},{3,2},{4,5},{5,4},{6,7},{7,6},{8,9},{9,8},{10,11... | collective-permute-start | bytes 393224 | tf_op jit(solution)/shard_map/ppermute | solution.py:34
  35.0 5.4 %collective-permute-start.4 = (bf16[256,256]{1,0:T(8,128)(2,1)S(1)}, bf16[256,256]{1,0:T(8,128)(2,1)S(1)}, u32[]{:S(2)}, u32[]{:S(2)}) collective-permute-start(bf16[256,256]{1,0:T(8,128)(2,1)S(1)} %bitcast.25), channel_id=1, source_target_pairs={{0,2},{1,3},{2,0},{3,1},{4,6},{5,7},{6,4},{7,5},{8,10},{9,11},{10,... | collective-permute-start | bytes 393224 | tf_op jit(solution)/shard_map/ppermute | solution.py:34
  40.4 1.3 %collective-permute-start.10 = (bf16[256,256]{1,0:T(8,128)(2,1)S(1)}, bf16[256,256]{1,0:T(8,128)(2,1)S(1)}, u32[]{:S(2)}, u32[]{:S(2)}) collective-permute-start(bf16[256,256]{1,0:T(8,128)(2,1)S(1)} %collective-permute-done.4.refs_1_), channel_id=1, source_target_pairs={{0,1},{1,0},{2,3},{3,2},{4,5},{5,4},{6,7},{7,6},{8,9},{9,8},{10,11... | collective-permute-start | bytes 393224 | tf_op jit(solution)/shard_map/ppermute | solution.py:34
  48.2 3.4 %collective-permute-start.12 = (bf16[2,64,1024]{2,1,0:T(8,128)(2,1)S(1)}, bf16[2,64,1024]{2,1,0:T(8,128)(2,1)S(1)}, u32[]{:S(2)}, u32[]{:S(2)}) collective-permute-start(bf16[2,64,1024]{2,1,0:T(8,128)(2,1)S(1)} %get-tuple-element.120), channel_id=1, source_target_pairs={{0,1},{1,0},{2,3},{3,2},{4,5},{5,4},{6,7},{7,6},{8,9},{9,8},{10,11... | collective-permute-start | bytes 786440 | tf_op jit(solution)/shard_map/ppermute | solution.py:34
  48.4 14.4 %collective-permute-start.14 = (bf16[4,512,128]{2,1,0:T(8,128)(2,1)}, bf16[4,512,128]{2,1,0:T(8,128)(2,1)S(1)}, u32[]{:S(2)}, u32[]{:S(2)}) collective-permute-start(bf16[4,512,128]{2,1,0:T(8,128)(2,1)} %get-tuple-element.132), channel_id=1, source_target_pairs={{0,4},{4,0},{8,12},{12,8},{16,20},{20,16},{24,28},{28,24},{1,5},{5... | collective-permute-start | bytes 1572872 | tf_op jit(solution)/shard_map/ppermute | solution.py:34
  50.2 14.4 %collective-permute-start.15 = (bf16[4,512,128]{2,1,0:T(8,128)(2,1)}, bf16[4,512,128]{2,1,0:T(8,128)(2,1)S(1)}, u32[]{:S(2)}, u32[]{:S(2)}) collective-permute-start(bf16[4,512,128]{2,1,0:T(8,128)(2,1)} %get-tuple-element.133), channel_id=1, source_target_pairs={{0,8},{4,12},{8,0},{12,4},{16,24},{20,28},{24,16},{28,20},{1,9},{5... | collective-permute-start | bytes 1572872 | tf_op jit(solution)/shard_map/ppermute | solution.py:34
  51.7 5.3 %collective-permute-start.13 = (bf16[64,1024]{1,0:T(8,128)(2,1)S(1)}, bf16[64,1024]{1,0:T(8,128)(2,1)S(1)}, u32[]{:S(2)}, u32[]{:S(2)}) collective-permute-start(bf16[64,1024]{1,0:T(8,128)(2,1)S(1)} %shard_map.114), channel_id=1, source_target_pairs={{0,2},{1,3},{2,0},{3,1},{4,6},{5,7},{6,4},{7,5},{8,10},{9,11},{10,... | collective-permute-start | bytes 393224 | tf_op jit(solution)/shard_map/ppermute | solution.py:34
  57.0 14.3 %copy-start.3 = (bf16[3,256,256]{2,1,0:T(8,128)(2,1)S(1)}, bf16[3,256,256]{2,1,0:T(8,128)(2,1)}, u32[]{:S(2)}) copy-start(bf16[3,256,256]{2,1,0:T(8,128)(2,1)} %get-tuple-element.141.refs_0_.refs_2_) | copy-start | bytes 1179652
  57.8 11.6 %all-to-all-start.2 = ((bf16[8,8,1024]{2,1,0:T(8,128)(2,1)}), bf16[8,8,1024]{2,1,0:T(8,128)(2,1)S(1)}, u32[]{:S(2)}, u32[]{:S(2)}) async-start(bf16[8,8,1024]{2,1,0:T(8,128)(2,1)} %bitcast.6), calls=%async_computation.2 | async-start | bytes 262144 | tf_op jit(solution)/shard_map/all_to_all | solution.py:609
  65.6 14.4 %copy-start.1 = (bf16[256,1024]{1,0:T(8,128)(2,1)S(1)}, bf16[256,1024]{1,0:T(8,128)(2,1)}, u32[]{:S(2)}) copy-start(bf16[256,1024]{1,0:T(8,128)(2,1)} %refs_1_.2) | copy-start | bytes 1572868
  69.4 5.0 %collective-permute-start.17 = (bf16[64,1024]{1,0:T(8,128)(2,1)S(1)}, bf16[64,1024]{1,0:T(8,128)(2,1)S(1)}, u32[]{:S(2)}, u32[]{:S(2)}) collective-permute-start(bf16[64,1024]{1,0:T(8,128)(2,1)S(1)} %bitcast.15), channel_id=1, source_target_pairs={{0,2},{1,3},{2,0},{3,1},{4,6},{5,7},{6,4},{7,5},{8,10},{9,11},{10,... | collective-permute-start | bytes 393224 | tf_op jit(solution)/shard_map/ppermute | solution.py:34
  69.9 6.6 %collective-permute-start.19 = (bf16[2,512,128]{2,1,0:T(8,128)(2,1)}, bf16[2,512,128]{2,1,0:T(8,128)(2,1)S(1)}, u32[]{:S(2)}, u32[]{:S(2)}) collective-permute-start(bf16[2,512,128]{2,1,0:T(8,128)(2,1)} %get-tuple-element.148), channel_id=1, source_target_pairs={{0,8},{4,12},{8,0},{12,4},{16,24},{20,28},{24,16},{28,20},{1,9},{5... | collective-permute-start | bytes 786440 | tf_op jit(solution)/shard_map/ppermute | solution.py:34
  69.9 6.6 %collective-permute-start.20 = (bf16[2,512,128]{2,1,0:T(8,128)(2,1)}, bf16[2,512,128]{2,1,0:T(8,128)(2,1)S(1)}, u32[]{:S(2)}, u32[]{:S(2)}) collective-permute-start(bf16[2,512,128]{2,1,0:T(8,128)(2,1)} %get-tuple-element.149), channel_id=1, source_target_pairs={{0,4},{4,0},{8,12},{12,8},{16,20},{20,16},{24,28},{28,24},{1,5},{5... | collective-permute-start | bytes 786440 | tf_op jit(solution)/shard_map/ppermute | solution.py:34
  71.2 3.2 %collective-permute-start.16 = (bf16[64,1024]{1,0:T(8,128)(2,1)S(1)}, bf16[64,1024]{1,0:T(8,128)(2,1)S(1)}, u32[]{:S(2)}, u32[]{:S(2)}) collective-permute-start(bf16[64,1024]{1,0:T(8,128)(2,1)S(1)} %bitcast.16), channel_id=1, source_target_pairs={{0,1},{1,0},{2,3},{3,2},{4,5},{5,4},{6,7},{7,6},{8,9},{9,8},{10,11... | collective-permute-start | bytes 393224 | tf_op jit(solution)/shard_map/ppermute | solution.py:34
  74.4 1.3 %collective-permute-start.18 = (bf16[64,1024]{1,0:T(8,128)(2,1)S(1)}, bf16[64,1024]{1,0:T(8,128)(2,1)S(1)}, u32[]{:S(2)}, u32[]{:S(2)}) collective-permute-start(bf16[64,1024]{1,0:T(8,128)(2,1)S(1)} %collective-permute-done.17.refs_2_), channel_id=1, source_target_pairs={{0,1},{1,0},{2,3},{3,2},{4,5},{5,4},{6,7},{7,6},{8,9},{9,8},{10,11... | collective-permute-start | bytes 393224 | tf_op jit(solution)/shard_map/ppermute | solution.py:34
  76.5 8.8 %collective-permute-start.22 = (bf16[4,256,128]{2,1,0:T(8,128)(2,1)S(1)}, bf16[4,256,128]{2,1,0:T(8,128)(2,1)S(1)}, u32[]{:S(2)}, u32[]{:S(2)}) collective-permute-start(bf16[4,256,128]{2,1,0:T(8,128)(2,1)S(1)} %get-tuple-element.165), channel_id=1, source_target_pairs={{0,4},{4,0},{8,12},{12,8},{16,20},{20,16},{24,28},{28,24},{1,5},{5... | collective-permute-start | bytes 786440 | tf_op jit(solution)/shard_map/ppermute | solution.py:34
  79.0 5.7 %copy-start = (bf16[3,1024,256]{2,1,0:T(8,128)(2,1)S(1)}, bf16[3,1024,256]{2,1,0:T(8,128)(2,1)}, u32[]{:S(2)}) copy-start(bf16[3,1024,256]{2,1,0:T(8,128)(2,1)} %refs_1_.3) | copy-start | bytes 4718596
  79.0 13.6 %collective-permute-start.21 = (bf16[1024,128]{1,0:T(8,128)(2,1)S(1)}, bf16[1024,128]{1,0:T(8,128)(2,1)S(1)}, u32[]{:S(2)}, u32[]{:S(2)}) collective-permute-start(bf16[1024,128]{1,0:T(8,128)(2,1)S(1)} %get-tuple-element.163), channel_id=1, source_target_pairs={{0,16},{4,20},{8,24},{12,28},{16,0},{20,4},{24,8},{28,12},{1,17},{... | collective-permute-start | bytes 786440 | tf_op jit(solution)/shard_map/ppermute | solution.py:34
  82.5 10.1 %copy-start.5 = (bf16[256,1024]{1,0:T(8,128)(2,1)S(1)}, bf16[256,1024]{1,0:T(8,128)(2,1)}, u32[]{:S(2)}) copy-start(bf16[256,1024]{1,0:T(8,128)(2,1)} %get-tuple-element.159.refs_4_.refs_1_) | copy-start | bytes 1572868
  82.5 13.9 %collective-permute-start.26 = (bf16[4,320,128]{2,1,0:T(8,128)(2,1)S(1)}, bf16[4,320,128]{2,1,0:T(8,128)(2,1)S(1)}, u32[]{:S(2)}, u32[]{:S(2)}) collective-permute-start(bf16[4,320,128]{2,1,0:T(8,128)(2,1)S(1)} %get-tuple-element.178), channel_id=1, source_target_pairs={{0,8},{4,12},{8,0},{12,4},{16,24},{20,28},{24,16},{28,20},{1,9},{5... | collective-permute-start | bytes 983048 | tf_op jit(solution)/shard_map/ppermute | solution.py:34
  82.9 11.6 %collective-permute-start.25 = (bf16[4,448,128]{2,1,0:T(8,128)(2,1)S(1)}, bf16[4,448,128]{2,1,0:T(8,128)(2,1)S(1)}, u32[]{:S(2)}, u32[]{:S(2)}) collective-permute-start(bf16[4,448,128]{2,1,0:T(8,128)(2,1)S(1)} %get-tuple-element.172), channel_id=1, source_target_pairs={{0,4},{4,0},{8,12},{12,8},{16,20},{20,16},{24,28},{28,24},{1,5},{5... | collective-permute-start | bytes 1376264 | tf_op jit(solution)/shard_map/ppermute | solution.py:34
  92.6 7.8 %collective-permute-start.29 = (bf16[2,256,128]{2,1,0:T(8,128)(2,1)S(1)}, bf16[2,256,128]{2,1,0:T(8,128)(2,1)S(1)}, u32[]{:S(2)}, u32[]{:S(2)}) collective-permute-start(bf16[2,256,128]{2,1,0:T(8,128)(2,1)S(1)} %get-tuple-element.188), channel_id=1, source_target_pairs={{0,16},{4,20},{8,24},{12,28},{16,0},{20,4},{24,8},{28,12},{1,17},{... | collective-permute-start | bytes 393224 | tf_op jit(solution)/shard_map/ppermute | solution.py:34
  93.2 11.9 %collective-permute-start.23 = (bf16[2,64,1024]{2,1,0:T(8,128)(2,1)S(1)}, bf16[2,64,1024]{2,1,0:T(8,128)(2,1)S(1)}, u32[]{:S(2)}, u32[]{:S(2)}) collective-permute-start(bf16[2,64,1024]{2,1,0:T(8,128)(2,1)S(1)} %get-tuple-element.169), channel_id=1, source_target_pairs={{0,1},{1,0},{2,3},{3,2},{4,5},{5,4},{6,7},{7,6},{8,9},{9,8},{10,11... | collective-permute-start | bytes 786440 | tf_op jit(solution)/shard_map/ppermute | solution.py:34
  94.7 9.6 %collective-permute-start.27 = (bf16[2,448,128]{2,1,0:T(8,128)(2,1)S(1)}, bf16[2,448,128]{2,1,0:T(8,128)(2,1)S(1)}, u32[]{:S(2)}, u32[]{:S(2)}) collective-permute-start(bf16[2,448,128]{2,1,0:T(8,128)(2,1)S(1)} %get-tuple-element.185), channel_id=1, source_target_pairs={{0,8},{4,12},{8,0},{12,4},{16,24},{20,28},{24,16},{28,20},{1,9},{5... | collective-permute-start | bytes 688136 | tf_op jit(solution)/shard_map/ppermute | solution.py:34
  96.5 13.9 %copy-start.4 = (bf16[1,64,1024]{2,1,0:T(8,128)(2,1)S(1)}, bf16[1,64,1024]{2,1,0:T(8,128)(2,1)}, u32[]{:S(2)}) copy-start(bf16[1,64,1024]{2,1,0:T(8,128)(2,1)} %param.7) | copy-start | bytes 393220
  96.5 6.4 %collective-permute-start.28 = (bf16[2,320,128]{2,1,0:T(8,128)(2,1)S(1)}, bf16[2,320,128]{2,1,0:T(8,128)(2,1)S(1)}, u32[]{:S(2)}, u32[]{:S(2)}) collective-permute-start(bf16[2,320,128]{2,1,0:T(8,128)(2,1)S(1)} %get-tuple-element.186), channel_id=1, source_target_pairs={{0,4},{4,0},{8,12},{12,8},{16,20},{20,16},{24,28},{28,24},{1,5},{5... | collective-permute-start | bytes 491528 | tf_op jit(solution)/shard_map/ppermute | solution.py:34
  104.4 11.1 %collective-permute-start.30 = (bf16[768,128]{1,0:T(8,128)(2,1)S(1)}, bf16[768,128]{1,0:T(8,128)(2,1)S(1)}, u32[]{:S(2)}, u32[]{:S(2)}) collective-permute-start(bf16[768,128]{1,0:T(8,128)(2,1)S(1)} %get-tuple-element.194), channel_id=1, source_target_pairs={{0,16},{4,20},{8,24},{12,28},{16,0},{20,4},{24,8},{28,12},{1,17},{... | collective-permute-start | bytes 589832 | tf_op jit(solution)/shard_map/ppermute | solution.py:34
  105.2 5.1 %collective-permute-start.24 = (bf16[64,1024]{1,0:T(8,128)(2,1)S(1)}, bf16[64,1024]{1,0:T(8,128)(2,1)S(1)}, u32[]{:S(2)}, u32[]{:S(2)}) collective-permute-start(bf16[64,1024]{1,0:T(8,128)(2,1)S(1)} %shard_map.124), channel_id=1, source_target_pairs={{0,2},{1,3},{2,0},{3,1},{4,6},{5,7},{6,4},{7,5},{8,10},{9,11},{10,... | collective-permute-start | bytes 393224 | tf_op jit(solution)/shard_map/ppermute | solution.py:34
  106.1 5.6 %collective-permute-start.31 = (bf16[1,256,128]{2,1,0:T(8,128)(2,1)S(1)}, bf16[1,256,128]{2,1,0:T(8,128)(2,1)S(1)}, u32[]{:S(2)}, u32[]{:S(2)}) collective-permute-start(bf16[1,256,128]{2,1,0:T(8,128)(2,1)S(1)} %get-tuple-element.196), channel_id=1, source_target_pairs={{0,8},{4,12},{8,0},{12,4},{16,24},{20,28},{24,16},{28,20},{1,9},{5... | collective-permute-start | bytes 196616 | tf_op jit(solution)/shard_map/ppermute | solution.py:34

commit v7 on v6

--- a/solution.py
+++ b/solution.py
@@ -435,7 +435,7 @@
 
 def qkv_parts(grads):
     flat = jnp.concatenate([grad.T for grad in grads], 0)
-    first = 7 * flat.shape[0] // 12
+    first = 13 * flat.shape[0] // 24
     return flat[:first], flat[first:]
 
 
@@ -446,7 +446,7 @@
 
 
 def qkv_part_shapes(width, dim, groups):
-    first = 7 * 3 * width // 12
+    first = 13 * 3 * width // 24
     return tuple(
         shape((groups // 2, rows, dim // groups)) for rows in (first, 3 * width - first)
     )

time: 117 us -> 117 us (level)
  waiting for transfers between devices: 48.7 us -> 44.4 us
  starting transfers between devices: 39.3 us -> 43.3 us
    ppermute x32, waiting for transfers between devices: 36.7 us -> 32.4 us  [swap(): return lax.ppermute(value, axis, [(i, i ^ by) for i in range(size)])]
    ppermute x32, starting transfers between devices: 24.3 us -> 28.3 us  [swap(): return lax.ppermute(value, axis, [(i, i ^ by) for i in range(size)])]
  transfers between devices with their start and end apart: 35 -> 35, of which waited for: 24 -> 23; matrix products, arithmetic and copies ran while one was open for 0% -> 0% of each run, Pallas kernels for 17% -> 17%
where the time goes in v7:
time: 117 us; the launch traced here: 116 us
  waiting for transfers between devices  44.4 us (38%)
  starting transfers between devices  43.3 us (37%)
  Pallas kernels  27.5 us (24%)
    ppermute x32, waiting for transfers between devices, swap(): return lax.ppermute(value, axis, [(i, i ^ by) for i in range(size)])  32.4 us
    ppermute x32, starting transfers between devices, swap(): return lax.ppermute(value, axis, [(i, i ^ by) for i in range(size)])  28.3 us
    pallas_call x23, Pallas kernels, run(): pl.pallas_call(wrapped, out_shape=tuple((pltpu.HBM(o.shape, o.dtype) if w...  27.5 us
    all_to_all x1, waiting for transfers between devices, shards(): lax.all_to_all(attn_send.reshape(groups, mp * per, width), 'frames', 0, 0...  6.83 us
    all_to_all x1, starting transfers between devices, shards(): lax.all_to_all(xg.reshape(groups, per, 2 * dim), 'frames', 0, 0, tiled=True)  6.03 us
    all_to_all x1, starting transfers between devices, shards(): lax.all_to_all(attn_send.reshape(groups, mp * per, width), 'frames', 0, 0...  4.78 us
    all_to_all x1, starting transfers between devices, shards(): lax.all_to_all(d_hidden.reshape(groups, per, dim), 'frames', 0, 0, tiled=...  4.24 us
    all_to_all x1, waiting for transfers between devices, shards(): lax.all_to_all(d_hidden.reshape(groups, per, dim), 'frames', 0, 0, tiled=...  3.77 us
  transfers between devices with their start and end apart: 35, of which 23 were waited for; matrix products, arithmetic and copies ran while one was open for 0% of the time, Pallas kernels for 17%

profile of v7, /device:TPU:0, one launch (start us, length us, event | category | flops | bytes accessed | tf_op | source)
XLA Modules:
  0.0 116.3 jit_solution(17787798177988451215)
XLA Ops:
  0.6 3.0 %collective-permute-start.1 = (bf16[64,1024]{1,0:T(8,128)(2,1)}, bf16[64,1024]{1,0:T(8,128)(2,1)S(1)}, u32[]{:S(2)}, u32[]{:S(2)}) collective-permute-start(bf16[64,1024]{1,0:T(8,128)(2,1)} %bitcast.19), channel_id=1, source_target_pairs={{0,2},{1,3},{2,0},{3,1},{4,6},{5,7},{6,4},{7,5},{8,10},{9,11},{10,... | collective-permute-start | bytes 393224 | tf_op jit(solution)/shard_map/ppermute | solution.py:34
  3.7 1.7 %shard_map.110 = bf16[64,2048]{1,0:T(8,128)(2,1)} custom-call(bf16[64,1024]{1,0:T(8,128)(2,1)} %bitcast.21, bf16[64,1024]{1,0:T(8,128)(2,1)} %bitcast.29), custom_call_target="tpu_custom_call" | custom-call | flops 1000 | bytes 1000 | tf_op jit(solution)/shard_map/pallas_call | solution.py:110
  5.4 2.0 %collective-permute-done.1.refs_2_ = bf16[64,1024]{1,0:T(8,128)(2,1)S(1)} collective-permute-done((bf16[64,1024]{1,0:T(8,128)(2,1)}, bf16[64,1024]{1,0:T(8,128)(2,1)S(1)}, u32[]{:S(2)}, u32[]{:S(2)}) %collective-permute-start.1) | collective-permute-done | bytes 131104 | tf_op jit(solution)/shard_map/ppermute | solution.py:34
  7.4 6.0 %all-to-all-start = ((bf16[8,8,2048]{2,1,0:T(8,128)(2,1)}), bf16[8,8,2048]{2,1,0:T(8,128)(2,1)S(1)}, u32[]{:S(2)}, u32[]{:S(2)}) async-start(bf16[8,8,2048]{2,1,0:T(8,128)(2,1)} %bitcast.2), calls=%async_computation | async-start | bytes 524288 | tf_op jit(solution)/shard_map/all_to_all | solution.py:576
  13.4 1.5 %collective-permute-start.2 = (bf16[256,1024]{1,0:T(8,128)(2,1)}, bf16[256,1024]{1,0:T(8,128)(2,1)S(1)}, u32[]{:S(2)}, u32[]{:S(2)}) collective-permute-start(bf16[256,1024]{1,0:T(8,128)(2,1)} %refs_1_.2), channel_id=1, source_target_pairs={{0,2},{1,3},{2,0},{3,1},{4,6},{5,7},{6,4},{7,5},{8,10},{9,11},{10,... | collective-permute-start | bytes 1572872 | tf_op jit(solution)/shard_map/ppermute | solution.py:34
  14.9 0.5 collective-permute-start.9
  15.4 1.0 collective-permute-done.3.refs_3_
  16.4 3.8 %shard_map.111 = (bf16[256,1024]{1,0:T(8,128)(2,1)}, bf16[3,256,256]{2,1,0:T(8,128)(2,1)}, bf16[256,256]{1,0:T(8,128)(2,1)}) custom-call(bf16[64,1024]{1,0:T(8,128)(2,1)} %bitcast.22, bf16[64,1024]{1,0:T(8,128)(2,1)S(1)} %collective-permute-done.refs_1_, bf16[64,1024]{1,0:T(8,128)(2,1)S(1)} %collective-permute-done.1.refs_2_, ...), custom_call_target="tpu_custom_call" | custom-call | flops 1000 | bytes 1000 | tf_op jit(solution)/shard_map/pallas_call | solution.py:110
  20.2 1.4 %all-to-all-done = bf16[8,8,2048]{2,1,0:T(8,128)(2,1)S(1)} async-done(((bf16[8,8,2048]{2,1,0:T(8,128)(2,1)}), bf16[8,8,2048]{2,1,0:T(8,128)(2,1)S(1)}, u32[]{:S(2)}, u32[]{:S(2)}) %all-to-all-start) | async-done | bytes 262176 | tf_op jit(solution)/shard_map/all_to_all | solution.py:576
  21.6 4.8 %all-to-all-start.1 = ((bf16[8,32,256]{2,1,0:T(8,128)(2,1)}), bf16[8,32,256]{2,1,0:T(8,128)(2,1)S(1)}, u32[]{:S(2)}, u32[]{:S(2)}) async-start(bf16[8,32,256]{2,1,0:T(8,128)(2,1)} %bitcast.4), calls=%async_computation.1 | async-start | bytes 262144 | tf_op jit(solution)/shard_map/all_to_all | solution.py:585
  26.4 0.5 collective-permute-start.6
  26.9 6.8 %all-to-all-done.1 = bf16[8,32,256]{2,1,0:T(8,128)(2,1)S(1)} async-done(((bf16[8,32,256]{2,1,0:T(8,128)(2,1)}), bf16[8,32,256]{2,1,0:T(8,128)(2,1)S(1)}, u32[]{:S(2)}, u32[]{:S(2)}) %all-to-all-start.1) | async-done | bytes 131104 | tf_op jit(solution)/shard_map/all_to_all | solution.py:585
  33.8 0.5 collective-permute-start.5
  34.3 0.2 collective-permute-done.6.refs_2_
  34.5 0.5 collective-permute-start.8
  35.0 0.5 collective-permute-start.4
  35.5 0.5 collective-permute-done.5.refs_1_
  36.0 0.6 collective-permute-done.8.refs_6_
  36.6 2.4 %shard_map.112 = (f32[256,1024]{1,0:T(8,128)S(1)}, bf16[256,1024]{1,0:T(8,128)(2,1)S(1)}, bf16[256,256]{1,0:T(8,128)(2,1)S(1)}) custom-call(bf16[64,2048]{1,0:T(8,128)(2,1)S(1)} %bitcast.13, bf16[64,2048]{1,0:T(8,128)(2,1)S(1)} %collective-permute-done.5.refs_1_, bf16[64,2048]{1,0:T(8,128)(2,1)S(1)} %collective-permute-done.6.refs_2_, ...), custom_call_target="tpu_custom_call" | custom-call | flops 1000 | bytes 1000 | tf_op jit(solution)/shard_map/pallas_call | solution.py:110
  39.0 1.4 %collective-permute-done.4.refs_1_ = bf16[256,256]{1,0:T(8,128)(2,1)S(1)} collective-permute-done((bf16[256,256]{1,0:T(8,128)(2,1)S(1)}, bf16[256,256]{1,0:T(8,128)(2,1)S(1)}, u32[]{:S(2)}, u32[]{:S(2)}) %collective-permute-start.4) | collective-permute-done | bytes 131104 | tf_op jit(solution)/shard_map/ppermute | solution.py:34
  40.4 1.3 %collective-permute-done.10.refs_2_ = bf16[256,256]{1,0:T(8,128)(2,1)S(1)} collective-permute-done((bf16[256,256]{1,0:T(8,128)(2,1)S(1)}, bf16[256,256]{1,0:T(8,128)(2,1)S(1)}, u32[]{:S(2)}, u32[]{:S(2)}) %collective-permute-start.10) | collective-permute-done | bytes 131104 | tf_op jit(solution)/shard_map/ppermute | solution.py:34
  41.8 6.4 %shard_map.113 = (bf16[2,64,1024]{2,1,0:T(8,128)(2,1)S(1)}, bf16[2,64,1024]{2,1,0:T(8,128)(2,1)S(1)}, bf16[256,1024]{1,0:T(8,128)(2,1)S(1)}, bf16[64,1024]{1,0:T...) custom-call(s32[4]{0:T(128)S(1)} %copy-done.6, ...), custom_call_target="tpu_custom_call" | custom-call | flops 1000 | bytes 1000 | tf_op jit(solution)/shard_map/pallas_call | solution.py:110
  48.2 0.2 collective-permute-start.12
  48.4 1.8 %collective-permute-start.14 = (bf16[4,512,128]{2,1,0:T(8,128)(2,1)}, bf16[4,512,128]{2,1,0:T(8,128)(2,1)S(1)}, u32[]{:S(2)}, u32[]{:S(2)}) collective-permute-start(bf16[4,512,128]{2,1,0:T(8,128)(2,1)} %get-tuple-element.132), channel_id=1, source_target_pairs={{0,4},{4,0},{8,12},{12,8},{16,20},{20,16},{24,28},{28,24},{1,5},{5... | collective-permute-start | bytes 1572872 | tf_op jit(solution)/shard_map/ppermute | solution.py:34
  50.2 1.5 %collective-permute-start.15 = (bf16[4,512,128]{2,1,0:T(8,128)(2,1)}, bf16[4,512,128]{2,1,0:T(8,128)(2,1)S(1)}, u32[]{:S(2)}, u32[]{:S(2)}) collective-permute-start(bf16[4,512,128]{2,1,0:T(8,128)(2,1)} %get-tuple-element.133), channel_id=1, source_target_pairs={{0,8},{4,12},{8,0},{12,4},{16,24},{20,28},{24,16},{28,20},{1,9},{5... | collective-permute-start | bytes 1572872 | tf_op jit(solution)/shard_map/ppermute | solution.py:34
  51.7 0.6 collective-permute-start.13
  52.3 0.8 shard_map.115
  53.1 3.9 %collective-permute-done.13.refs_2_ = bf16[64,1024]{1,0:T(8,128)(2,1)S(1)} collective-permute-done((bf16[64,1024]{1,0:T(8,128)(2,1)S(1)}, bf16[64,1024]{1,0:T(8,128)(2,1)S(1)}, u32[]{:S(2)}, u32[]{:S(2)}) %collective-permute-start.13) | collective-permute-done | bytes 131104 | tf_op jit(solution)/shard_map/ppermute | solution.py:34
  57.0 0.9 shard_map.116
  57.8 4.2 %all-to-all-start.2 = ((bf16[8,8,1024]{2,1,0:T(8,128)(2,1)}), bf16[8,8,1024]{2,1,0:T(8,128)(2,1)S(1)}, u32[]{:S(2)}, u32[]{:S(2)}) async-start(bf16[8,8,1024]{2,1,0:T(8,128)(2,1)} %bitcast.6), calls=%async_computation.2 | async-start | bytes 262144 | tf_op jit(solution)/shard_map/all_to_all | solution.py:609
  62.1 0.7 collective-permute-done.14.refs_2_
  62.8 1.7 %collective-permute-done.15.refs_3_ = bf16[4,512,128]{2,1,0:T(8,128)(2,1)S(1)} collective-permute-done((bf16[4,512,128]{2,1,0:T(8,128)(2,1)}, bf16[4,512,128]{2,1,0:T(8,128)(2,1)S(1)}, u32[]{:S(2)}, u32[]{:S(2)}) %collective-permute-start.15) | collective-permute-done | bytes 524320 | tf_op jit(solution)/shard_map/ppermute | solution.py:34
  64.5 1.1 shard_map.117
  65.7 3.8 %all-to-all-done.2 = bf16[8,8,1024]{2,1,0:T(8,128)(2,1)S(1)} async-done(((bf16[8,8,1024]{2,1,0:T(8,128)(2,1)}), bf16[8,8,1024]{2,1,0:T(8,128)(2,1)S(1)}, u32[]{:S(2)}, u32[]{:S(2)}) %all-to-all-start.2) | async-done | bytes 131104 | tf_op jit(solution)/shard_map/all_to_all | solution.py:609
  69.4 0.5 collective-permute-start.17
  69.9 1.3 %collective-permute-start.20 = (bf16[2,512,128]{2,1,0:T(8,128)(2,1)}, bf16[2,512,128]{2,1,0:T(8,128)(2,1)S(1)}, u32[]{:S(2)}, u32[]{:S(2)}) collective-permute-start(bf16[2,512,128]{2,1,0:T(8,128)(2,1)} %get-tuple-element.149), channel_id=1, source_target_pairs={{0,4},{4,0},{8,12},{12,8},{16,20},{20,16},{24,28},{28,24},{1,5},{5... | collective-permute-start | bytes 786440 | tf_op jit(solution)/shard_map/ppermute | solution.py:34
  71.3 1.5 %shard_map.118 = (f32[4,256,256]{2,1,0:T(8,128)S(1)}, bf16[256,256]{1,0:T(8,128)(2,1)S(1)}) custom-call(bf16[3,256,256]{2,1,0:T(8,128)(2,1)S(1)} %copy-done.3, bf16[256,256]{1,0:T(8,128)(2,1)} %get-tuple-element.142.refs_1_), custom_call_target="tpu_custom_call" | custom-call | flops 1000 | bytes 1000 | tf_op jit(solution)/shard_map/pallas_call | solution.py:110
  72.8 1.6 %collective-permute-done.17.refs_2_ = bf16[64,1024]{1,0:T(8,128)(2,1)S(1)} collective-permute-done((bf16[64,1024]{1,0:T(8,128)(2,1)S(1)}, bf16[64,1024]{1,0:T(8,128)(2,1)S(1)}, u32[]{:S(2)}, u32[]{:S(2)}) %collective-permute-start.17) | collective-permute-done | bytes 131104 | tf_op jit(solution)/shard_map/ppermute | solution.py:34
  74.4 1.3 %collective-permute-done.18.refs_3_ = bf16[64,1024]{1,0:T(8,128)(2,1)S(1)} collective-permute-done((bf16[64,1024]{1,0:T(8,128)(2,1)S(1)}, bf16[64,1024]{1,0:T(8,128)(2,1)S(1)}, u32[]{:S(2)}, u32[]{:S(2)}) %collective-permute-start.18) | collective-permute-done | bytes 131104 | tf_op jit(solution)/shard_map/ppermute | solution.py:34
  75.7 0.5 shard_map.119
  76.3 0.3 collective-permute-done.19.refs_2_
  76.5 1.3 %collective-permute-start.22 = (bf16[4,256,128]{2,1,0:T(8,128)(2,1)S(1)}, bf16[4,256,128]{2,1,0:T(8,128)(2,1)S(1)}, u32[]{:S(2)}, u32[]{:S(2)}) collective-permute-start(bf16[4,256,128]{2,1,0:T(8,128)(2,1)S(1)} %get-tuple-element.165), channel_id=1, source_target_pairs={{0,4},{4,0},{8,12},{12,8},{16,20},{20,16},{24,28},{28,24},{1,5},{5... | collective-permute-start | bytes 786440 | tf_op jit(solution)/shard_map/ppermute | solution.py:34
  77.8 1.2 shard_map.120
  79.0 1.1 collective-permute-start.21
  80.1 2.4 %shard_map.121 = (bf16[3,256,256]{2,1,0:T(8,128)(2,1)S(1)}, bf16[4,416,128]{2,1,0:T(8,128)(2,1)S(1)}, bf16[4,352,128]{2,1,0:T(8,128)(2,1)S(1)}) custom-call(bf16[256,1024]{1,0:T(8,128)(2,1)S(1)} %get-tuple-element.157.refs_0_, bf16[256,1024]{1,0:T(8,128)(2,1)S(1)} %copy-done.1, bf16[3,256,256]{2,1,0:T(8,128)(2,1)S(1)} %copy-done.3, ...), custom_call_target="tpu_custom_call" | custom-call | flops 1000 | bytes 1000 | tf_op jit(solution)/shard_map/pallas_call | solution.py:110
  82.5 0.4 collective-permute-start.26
  82.9 1.8 %collective-permute-start.25 = (bf16[4,416,128]{2,1,0:T(8,128)(2,1)S(1)}, bf16[4,416,128]{2,1,0:T(8,128)(2,1)S(1)}, u32[]{:S(2)}, u32[]{:S(2)}) collective-permute-start(bf16[4,416,128]{2,1,0:T(8,128)(2,1)S(1)} %get-tuple-element.172), channel_id=1, source_target_pairs={{0,4},{4,0},{8,12},{12,8},{16,20},{20,16},{24,28},{28,24},{1,5},{5... | collective-permute-start | bytes 1277960 | tf_op jit(solution)/shard_map/ppermute | solution.py:34
  84.7 0.7 shard_map.122
  85.5 7.1 %collective-permute-done.21.refs_1_ = bf16[1024,128]{1,0:T(8,128)(2,1)S(1)} collective-permute-done((bf16[1024,128]{1,0:T(8,128)(2,1)S(1)}, bf16[1024,128]{1,0:T(8,128)(2,1)S(1)}, u32[]{:S(2)}, u32[]{:S(2)}) %collective-permute-start.21) | collective-permute-done | bytes 262176 | tf_op jit(solution)/shard_map/ppermute | solution.py:34
  92.6 0.6 shard_map.126
  93.3 0.5 collective-permute-done.25.refs_1_
  94.0 1.4 %collective-permute-start.27 = (bf16[2,416,128]{2,1,0:T(8,128)(2,1)S(1)}, bf16[2,416,128]{2,1,0:T(8,128)(2,1)S(1)}, u32[]{:S(2)}, u32[]{:S(2)}) collective-permute-start(bf16[2,416,128]{2,1,0:T(8,128)(2,1)S(1)} %get-tuple-element.185), channel_id=1, source_target_pairs={{0,8},{4,12},{8,0},{12,4},{16,24},{20,28},{24,16},{28,20},{1,9},{5... | collective-permute-start | bytes 638984 | tf_op jit(solution)/shard_map/ppermute | solution.py:34
  95.3 1.0 shard_map.128
  96.5 2.4 %collective-permute-start.28 = (bf16[2,352,128]{2,1,0:T(8,128)(2,1)S(1)}, bf16[2,352,128]{2,1,0:T(8,128)(2,1)S(1)}, u32[]{:S(2)}, u32[]{:S(2)}) collective-permute-start(bf16[2,352,128]{2,1,0:T(8,128)(2,1)S(1)} %get-tuple-element.186), channel_id=1, source_target_pairs={{0,4},{4,0},{8,12},{12,8},{16,20},{20,16},{24,28},{28,24},{1,5},{5... | collective-permute-start | bytes 540680 | tf_op jit(solution)/shard_map/ppermute | solution.py:34
  98.9 1.8 %collective-permute-done.29.refs_1_ = bf16[2,256,128]{2,1,0:T(8,128)(2,1)S(1)} collective-permute-done((bf16[2,256,128]{2,1,0:T(8,128)(2,1)S(1)}, bf16[2,256,128]{2,1,0:T(8,128)(2,1)S(1)}, u32[]{:S(2)}, u32[]{:S(2)}) %collective-permute-start.29) | collective-permute-done | bytes 131104 | tf_op jit(solution)/shard_map/ppermute | solution.py:34
  100.8 2.4 %collective-permute-done.28.refs_3_ = bf16[2,352,128]{2,1,0:T(8,128)(2,1)S(1)} collective-permute-done((bf16[2,352,128]{2,1,0:T(8,128)(2,1)S(1)}, bf16[2,352,128]{2,1,0:T(8,128)(2,1)S(1)}, u32[]{:S(2)}, u32[]{:S(2)}) %collective-permute-start.28) | collective-permute-done | bytes 180256 | tf_op jit(solution)/shard_map/ppermute | solution.py:34
  103.2 0.4 collective-permute-done.27.refs_2_
  103.7 1.4 %collective-permute-start.30 = (bf16[768,128]{1,0:T(8,128)(2,1)S(1)}, bf16[768,128]{1,0:T(8,128)(2,1)S(1)}, u32[]{:S(2)}, u32[]{:S(2)}) collective-permute-start(bf16[768,128]{1,0:T(8,128)(2,1)S(1)} %get-tuple-element.194), channel_id=1, source_target_pairs={{0,16},{4,20},{8,24},{12,28},{16,0},{20,4},{24,8},{28,12},{1,17},{... | collective-permute-start | bytes 589832 | tf_op jit(solution)/shard_map/ppermute | solution.py:34
  105.2 3.1 %collective-permute-start.24 = (bf16[64,1024]{1,0:T(8,128)(2,1)S(1)}, bf16[64,1024]{1,0:T(8,128)(2,1)S(1)}, u32[]{:S(2)}, u32[]{:S(2)}) collective-permute-start(bf16[64,1024]{1,0:T(8,128)(2,1)S(1)} %shard_map.124), channel_id=1, source_target_pairs={{0,2},{1,3},{2,0},{3,1},{4,6},{5,7},{6,4},{7,5},{8,10},{9,11},{10,... | collective-permute-start | bytes 393224 | tf_op jit(solution)/shard_map/ppermute | solution.py:34
  108.2 2.5 %collective-permute-start.31 = (bf16[1,256,128]{2,1,0:T(8,128)(2,1)S(1)}, bf16[1,256,128]{2,1,0:T(8,128)(2,1)S(1)}, u32[]{:S(2)}, u32[]{:S(2)}) collective-permute-start(bf16[1,256,128]{2,1,0:T(8,128)(2,1)S(1)} %get-tuple-element.196), channel_id=1, source_target_pairs={{0,8},{4,12},{8,0},{12,4},{16,24},{20,28},{24,16},{28,20},{1,9},{5... | collective-permute-start | bytes 196616 | tf_op jit(solution)/shard_map/ppermute | solution.py:34
  110.7 0.5 collective-permute-done.24.refs_2_
  111.2 0.9 shard_map.125
  112.1 3.0 %collective-permute-done.31 = bf16[1,256,128]{2,1,0:T(8,128)(2,1)S(1)} collective-permute-done((bf16[1,256,128]{2,1,0:T(8,128)(2,1)S(1)}, bf16[1,256,128]{2,1,0:T(8,128)(2,1)S(1)}, u32[]{:S(2)}, u32[]{:S(2)}) %collective-permute-start.31) | collective-permute-done | bytes 65568 | tf_op jit(solution)/shard_map/ppermute | solution.py:34
  115.1 1.0 shard_map.132
  (43 shorter events, 0.8 us)
Async XLA Ops:
  0.6 6.7 %collective-permute-start.1 = (bf16[64,1024]{1,0:T(8,128)(2,1)}, bf16[64,1024]{1,0:T(8,128)(2,1)S(1)}, u32[]{:S(2)}, u32[]{:S(2)}) collective-permute-start(bf16[64,1024]{1,0:T(8,128)(2,1)} %bitcast.19), channel_id=1, source_target_pairs={{0,2},{1,3},{2,0},{3,1},{4,6},{5,7},{6,4},{7,5},{8,10},{9,11},{10,... | collective-permute-start | bytes 393224 | tf_op jit(solution)/shard_map/ppermute | solution.py:34
  3.7 3.7 %collective-permute-start = (bf16[64,1024]{1,0:T(8,128)(2,1)}, bf16[64,1024]{1,0:T(8,128)(2,1)S(1)}, u32[]{:S(2)}, u32[]{:S(2)}) collective-permute-start(bf16[64,1024]{1,0:T(8,128)(2,1)} %bitcast.20), channel_id=1, source_target_pairs={{0,1},{1,0},{2,3},{3,2},{4,5},{5,4},{6,7},{7,6},{8,9},{9,8},{10,11... | collective-permute-start | bytes 393224 | tf_op jit(solution)/shard_map/ppermute | solution.py:34
  7.4 14.3 %all-to-all-start = ((bf16[8,8,2048]{2,1,0:T(8,128)(2,1)}), bf16[8,8,2048]{2,1,0:T(8,128)(2,1)S(1)}, u32[]{:S(2)}, u32[]{:S(2)}) async-start(bf16[8,8,2048]{2,1,0:T(8,128)(2,1)} %bitcast.2), calls=%async_computation | async-start | bytes 524288 | tf_op jit(solution)/shard_map/all_to_all | solution.py:576
  13.4 13.5 %collective-permute-start.2 = (bf16[256,1024]{1,0:T(8,128)(2,1)}, bf16[256,1024]{1,0:T(8,128)(2,1)S(1)}, u32[]{:S(2)}, u32[]{:S(2)}) collective-permute-start(bf16[256,1024]{1,0:T(8,128)(2,1)} %refs_1_.2), channel_id=1, source_target_pairs={{0,2},{1,3},{2,0},{3,1},{4,6},{5,7},{6,4},{7,5},{8,10},{9,11},{10,... | collective-permute-start | bytes 1572872 | tf_op jit(solution)/shard_map/ppermute | solution.py:34
  14.9 1.5 %collective-permute-start.3 = (bf16[64,1024]{1,0:T(8,128)(2,1)S(1)}, bf16[64,1024]{1,0:T(8,128)(2,1)S(1)}, u32[]{:S(2)}, u32[]{:S(2)}) collective-permute-start(bf16[64,1024]{1,0:T(8,128)(2,1)S(1)} %collective-permute-done.1.refs_2_), channel_id=1, source_target_pairs={{0,1},{1,0},{2,3},{3,2},{4,5},{5,4},{6,7},{7,6},{8,9},{9,8},{10,11... | collective-permute-start | bytes 393224 | tf_op jit(solution)/shard_map/ppermute | solution.py:34
  14.9 20.1 %collective-permute-start.9 = (bf16[256,1024]{1,0:T(8,128)(2,1)}, bf16[256,1024]{1,0:T(8,128)(2,1)S(1)}, u32[]{:S(2)}, u32[]{:S(2)}) collective-permute-start(bf16[256,1024]{1,0:T(8,128)(2,1)} %refs_1_.2), channel_id=1, source_target_pairs={{0,1},{1,0},{2,3},{3,2},{4,5},{5,4},{6,7},{7,6},{8,9},{9,8},{10,11... | collective-permute-start | bytes 1572872 | tf_op jit(solution)/shard_map/ppermute | solution.py:34
  21.6 20.1 %copy-start.2 = (bf16[3,1024,256]{2,1,0:T(8,128)(2,1)S(1)}, bf16[3,1024,256]{2,1,0:T(8,128)(2,1)}, u32[]{:S(2)}) copy-start(bf16[3,1024,256]{2,1,0:T(8,128)(2,1)} %refs_7_.3) | copy-start | bytes 4718596
  21.6 20.1 %copy-start.6 = (s32[4]{0:T(128)S(1)}, s32[4]{0:T(128)}, u32[]{:S(2)}) copy-start(s32[4]{0:T(128)} %refs_0_.1) | copy-start | bytes 52
  21.6 12.1 %all-to-all-start.1 = ((bf16[8,32,256]{2,1,0:T(8,128)(2,1)}), bf16[8,32,256]{2,1,0:T(8,128)(2,1)S(1)}, u32[]{:S(2)}, u32[]{:S(2)}) async-start(bf16[8,32,256]{2,1,0:T(8,128)(2,1)} %bitcast.4), calls=%async_computation.1 | async-start | bytes 262144 | tf_op jit(solution)/shard_map/all_to_all | solution.py:585
  26.4 8.1 %collective-permute-start.6 = (bf16[64,2048]{1,0:T(8,128)(2,1)S(1)}, bf16[64,2048]{1,0:T(8,128)(2,1)S(1)}, u32[]{:S(2)}, u32[]{:S(2)}) collective-permute-start(bf16[64,2048]{1,0:T(8,128)(2,1)S(1)} %bitcast.11), channel_id=1, source_target_pairs={{0,2},{1,3},{2,0},{3,1},{4,6},{5,7},{6,4},{7,5},{8,10},{9,11},{10,... | collective-permute-start | bytes 786440 | tf_op jit(solution)/shard_map/ppermute | solution.py:34
  33.8 8.0 %collective-permute-start.11 = (bf16[256,1024]{1,0:T(8,128)(2,1)S(1)}, bf16[256,1024]{1,0:T(8,128)(2,1)S(1)}, u32[]{:S(2)}, u32[]{:S(2)}) collective-permute-start(bf16[256,1024]{1,0:T(8,128)(2,1)S(1)} %collective-permute-done.2.refs_5_), channel_id=1, source_target_pairs={{0,1},{1,0},{2,3},{3,2},{4,5},{5,4},{6,7},{7,6},{8,9},{9,8},{10,11... | collective-permute-start | bytes 1572872 | tf_op jit(solution)/shard_map/ppermute | solution.py:34
  33.8 2.3 %collective-permute-start.5 = (bf16[64,2048]{1,0:T(8,128)(2,1)S(1)}, bf16[64,2048]{1,0:T(8,128)(2,1)S(1)}, u32[]{:S(2)}, u32[]{:S(2)}) collective-permute-start(bf16[64,2048]{1,0:T(8,128)(2,1)S(1)} %bitcast.12), channel_id=1, source_target_pairs={{0,1},{1,0},{2,3},{3,2},{4,5},{5,4},{6,7},{7,6},{8,9},{9,8},{10,11... | collective-permute-start | bytes 786440 | tf_op jit(solution)/shard_map/ppermute | solution.py:34
  34.5 2.1 %collective-permute-start.7 = (bf16[64,2048]{1,0:T(8,128)(2,1)S(1)}, bf16[64,2048]{1,0:T(8,128)(2,1)S(1)}, u32[]{:S(2)}, u32[]{:S(2)}) collective-permute-start(bf16[64,2048]{1,0:T(8,128)(2,1)S(1)} %collective-permute-done.6.refs_2_), channel_id=1, source_target_pairs={{0,1},{1,0},{2,3},{3,2},{4,5},{5,4},{6,7},{7,6},{8,9},{9,8},{10,11... | collective-permute-start | bytes 786440 | tf_op jit(solution)/shard_map/ppermute | solution.py:34
  34.5 2.1 %collective-permute-start.8 = (bf16[256,256]{1,0:T(8,128)(2,1)S(1)}, bf16[256,256]{1,0:T(8,128)(2,1)S(1)}, u32[]{:S(2)}, u32[]{:S(2)}) collective-permute-start(bf16[256,256]{1,0:T(8,128)(2,1)S(1)} %bitcast.24), channel_id=1, source_target_pairs={{0,1},{1,0},{2,3},{3,2},{4,5},{5,4},{6,7},{7,6},{8,9},{9,8},{10,11... | collective-permute-start | bytes 393224 | tf_op jit(solution)/shard_map/ppermute | solution.py:34
  35.0 5.4 %collective-permute-start.4 = (bf16[256,256]{1,0:T(8,128)(2,1)S(1)}, bf16[256,256]{1,0:T(8,128)(2,1)S(1)}, u32[]{:S(2)}, u32[]{:S(2)}) collective-permute-start(bf16[256,256]{1,0:T(8,128)(2,1)S(1)} %bitcast.25), channel_id=1, source_target_pairs={{0,2},{1,3},{2,0},{3,1},{4,6},{5,7},{6,4},{7,5},{8,10},{9,11},{10,... | collective-permute-start | bytes 393224 | tf_op jit(solution)/shard_map/ppermute | solution.py:34
  40.4 1.3 %collective-permute-start.10 = (bf16[256,256]{1,0:T(8,128)(2,1)S(1)}, bf16[256,256]{1,0:T(8,128)(2,1)S(1)}, u32[]{:S(2)}, u32[]{:S(2)}) collective-permute-start(bf16[256,256]{1,0:T(8,128)(2,1)S(1)} %collective-permute-done.4.refs_1_), channel_id=1, source_target_pairs={{0,1},{1,0},{2,3},{3,2},{4,5},{5,4},{6,7},{7,6},{8,9},{9,8},{10,11... | collective-permute-start | bytes 393224 | tf_op jit(solution)/shard_map/ppermute | solution.py:34
  48.2 3.4 %collective-permute-start.12 = (bf16[2,64,1024]{2,1,0:T(8,128)(2,1)S(1)}, bf16[2,64,1024]{2,1,0:T(8,128)(2,1)S(1)}, u32[]{:S(2)}, u32[]{:S(2)}) collective-permute-start(bf16[2,64,1024]{2,1,0:T(8,128)(2,1)S(1)} %get-tuple-element.120), channel_id=1, source_target_pairs={{0,1},{1,0},{2,3},{3,2},{4,5},{5,4},{6,7},{7,6},{8,9},{9,8},{10,11... | collective-permute-start | bytes 786440 | tf_op jit(solution)/shard_map/ppermute | solution.py:34
  48.4 14.4 %collective-permute-start.14 = (bf16[4,512,128]{2,1,0:T(8,128)(2,1)}, bf16[4,512,128]{2,1,0:T(8,128)(2,1)S(1)}, u32[]{:S(2)}, u32[]{:S(2)}) collective-permute-start(bf16[4,512,128]{2,1,0:T(8,128)(2,1)} %get-tuple-element.132), channel_id=1, source_target_pairs={{0,4},{4,0},{8,12},{12,8},{16,20},{20,16},{24,28},{28,24},{1,5},{5... | collective-permute-start | bytes 1572872 | tf_op jit(solution)/shard_map/ppermute | solution.py:34
  50.2 14.4 %collective-permute-start.15 = (bf16[4,512,128]{2,1,0:T(8,128)(2,1)}, bf16[4,512,128]{2,1,0:T(8,128)(2,1)S(1)}, u32[]{:S(2)}, u32[]{:S(2)}) collective-permute-start(bf16[4,512,128]{2,1,0:T(8,128)(2,1)} %get-tuple-element.133), channel_id=1, source_target_pairs={{0,8},{4,12},{8,0},{12,4},{16,24},{20,28},{24,16},{28,20},{1,9},{5... | collective-permute-start | bytes 1572872 | tf_op jit(solution)/shard_map/ppermute | solution.py:34
  51.7 5.3 %collective-permute-start.13 = (bf16[64,1024]{1,0:T(8,128)(2,1)S(1)}, bf16[64,1024]{1,0:T(8,128)(2,1)S(1)}, u32[]{:S(2)}, u32[]{:S(2)}) collective-permute-start(bf16[64,1024]{1,0:T(8,128)(2,1)S(1)} %shard_map.114), channel_id=1, source_target_pairs={{0,2},{1,3},{2,0},{3,1},{4,6},{5,7},{6,4},{7,5},{8,10},{9,11},{10,... | collective-permute-start | bytes 393224 | tf_op jit(solution)/shard_map/ppermute | solution.py:34
  57.0 14.3 %copy-start.3 = (bf16[3,256,256]{2,1,0:T(8,128)(2,1)S(1)}, bf16[3,256,256]{2,1,0:T(8,128)(2,1)}, u32[]{:S(2)}) copy-start(bf16[3,256,256]{2,1,0:T(8,128)(2,1)} %get-tuple-element.141.refs_0_.refs_2_) | copy-start | bytes 1179652
  57.8 11.6 %all-to-all-start.2 = ((bf16[8,8,1024]{2,1,0:T(8,128)(2,1)}), bf16[8,8,1024]{2,1,0:T(8,128)(2,1)S(1)}, u32[]{:S(2)}, u32[]{:S(2)}) async-start(bf16[8,8,1024]{2,1,0:T(8,128)(2,1)} %bitcast.6), calls=%async_computation.2 | async-start | bytes 262144 | tf_op jit(solution)/shard_map/all_to_all | solution.py:609
  65.6 14.4 %copy-start.1 = (bf16[256,1024]{1,0:T(8,128)(2,1)S(1)}, bf16[256,1024]{1,0:T(8,128)(2,1)}, u32[]{:S(2)}) copy-start(bf16[256,1024]{1,0:T(8,128)(2,1)} %refs_1_.2) | copy-start | bytes 1572868
  69.4 5.0 %collective-permute-start.17 = (bf16[64,1024]{1,0:T(8,128)(2,1)S(1)}, bf16[64,1024]{1,0:T(8,128)(2,1)S(1)}, u32[]{:S(2)}, u32[]{:S(2)}) collective-permute-start(bf16[64,1024]{1,0:T(8,128)(2,1)S(1)} %bitcast.15), channel_id=1, source_target_pairs={{0,2},{1,3},{2,0},{3,1},{4,6},{5,7},{6,4},{7,5},{8,10},{9,11},{10,... | collective-permute-start | bytes 393224 | tf_op jit(solution)/shard_map/ppermute | solution.py:34
  69.9 6.6 %collective-permute-start.19 = (bf16[2,512,128]{2,1,0:T(8,128)(2,1)}, bf16[2,512,128]{2,1,0:T(8,128)(2,1)S(1)}, u32[]{:S(2)}, u32[]{:S(2)}) collective-permute-start(bf16[2,512,128]{2,1,0:T(8,128)(2,1)} %get-tuple-element.148), channel_id=1, source_target_pairs={{0,8},{4,12},{8,0},{12,4},{16,24},{20,28},{24,16},{28,20},{1,9},{5... | collective-permute-start | bytes 786440 | tf_op jit(solution)/shard_map/ppermute | solution.py:34
  69.9 6.6 %collective-permute-start.20 = (bf16[2,512,128]{2,1,0:T(8,128)(2,1)}, bf16[2,512,128]{2,1,0:T(8,128)(2,1)S(1)}, u32[]{:S(2)}, u32[]{:S(2)}) collective-permute-start(bf16[2,512,128]{2,1,0:T(8,128)(2,1)} %get-tuple-element.149), channel_id=1, source_target_pairs={{0,4},{4,0},{8,12},{12,8},{16,20},{20,16},{24,28},{28,24},{1,5},{5... | collective-permute-start | bytes 786440 | tf_op jit(solution)/shard_map/ppermute | solution.py:34
  71.2 3.2 %collective-permute-start.16 = (bf16[64,1024]{1,0:T(8,128)(2,1)S(1)}, bf16[64,1024]{1,0:T(8,128)(2,1)S(1)}, u32[]{:S(2)}, u32[]{:S(2)}) collective-permute-start(bf16[64,1024]{1,0:T(8,128)(2,1)S(1)} %bitcast.16), channel_id=1, source_target_pairs={{0,1},{1,0},{2,3},{3,2},{4,5},{5,4},{6,7},{7,6},{8,9},{9,8},{10,11... | collective-permute-start | bytes 393224 | tf_op jit(solution)/shard_map/ppermute | solution.py:34
  74.4 1.3 %collective-permute-start.18 = (bf16[64,1024]{1,0:T(8,128)(2,1)S(1)}, bf16[64,1024]{1,0:T(8,128)(2,1)S(1)}, u32[]{:S(2)}, u32[]{:S(2)}) collective-permute-start(bf16[64,1024]{1,0:T(8,128)(2,1)S(1)} %collective-permute-done.17.refs_2_), channel_id=1, source_target_pairs={{0,1},{1,0},{2,3},{3,2},{4,5},{5,4},{6,7},{7,6},{8,9},{9,8},{10,11... | collective-permute-start | bytes 393224 | tf_op jit(solution)/shard_map/ppermute | solution.py:34
  76.5 8.8 %collective-permute-start.22 = (bf16[4,256,128]{2,1,0:T(8,128)(2,1)S(1)}, bf16[4,256,128]{2,1,0:T(8,128)(2,1)S(1)}, u32[]{:S(2)}, u32[]{:S(2)}) collective-permute-start(bf16[4,256,128]{2,1,0:T(8,128)(2,1)S(1)} %get-tuple-element.165), channel_id=1, source_target_pairs={{0,4},{4,0},{8,12},{12,8},{16,20},{20,16},{24,28},{28,24},{1,5},{5... | collective-permute-start | bytes 786440 | tf_op jit(solution)/shard_map/ppermute | solution.py:34
  79.0 5.7 %copy-start = (bf16[3,1024,256]{2,1,0:T(8,128)(2,1)S(1)}, bf16[3,1024,256]{2,1,0:T(8,128)(2,1)}, u32[]{:S(2)}) copy-start(bf16[3,1024,256]{2,1,0:T(8,128)(2,1)} %refs_1_.3) | copy-start | bytes 4718596
  79.0 13.6 %collective-permute-start.21 = (bf16[1024,128]{1,0:T(8,128)(2,1)S(1)}, bf16[1024,128]{1,0:T(8,128)(2,1)S(1)}, u32[]{:S(2)}, u32[]{:S(2)}) collective-permute-start(bf16[1024,128]{1,0:T(8,128)(2,1)S(1)} %get-tuple-element.163), channel_id=1, source_target_pairs={{0,16},{4,20},{8,24},{12,28},{16,0},{20,4},{24,8},{28,12},{1,17},{... | collective-permute-start | bytes 786440 | tf_op jit(solution)/shard_map/ppermute | solution.py:34
  82.5 10.1 %copy-start.5 = (bf16[256,1024]{1,0:T(8,128)(2,1)S(1)}, bf16[256,1024]{1,0:T(8,128)(2,1)}, u32[]{:S(2)}) copy-start(bf16[256,1024]{1,0:T(8,128)(2,1)} %get-tuple-element.159.refs_4_.refs_1_) | copy-start | bytes 1572868
  82.5 13.8 %collective-permute-start.26 = (bf16[4,352,128]{2,1,0:T(8,128)(2,1)S(1)}, bf16[4,352,128]{2,1,0:T(8,128)(2,1)S(1)}, u32[]{:S(2)}, u32[]{:S(2)}) collective-permute-start(bf16[4,352,128]{2,1,0:T(8,128)(2,1)S(1)} %get-tuple-element.178), channel_id=1, source_target_pairs={{0,8},{4,12},{8,0},{12,4},{16,24},{20,28},{24,16},{28,20},{1,9},{5... | collective-permute-start | bytes 1081352 | tf_op jit(solution)/shard_map/ppermute | solution.py:34
  82.9 10.9 %collective-permute-start.25 = (bf16[4,416,128]{2,1,0:T(8,128)(2,1)S(1)}, bf16[4,416,128]{2,1,0:T(8,128)(2,1)S(1)}, u32[]{:S(2)}, u32[]{:S(2)}) collective-permute-start(bf16[4,416,128]{2,1,0:T(8,128)(2,1)S(1)} %get-tuple-element.172), channel_id=1, source_target_pairs={{0,4},{4,0},{8,12},{12,8},{16,20},{20,16},{24,28},{28,24},{1,5},{5... | collective-permute-start | bytes 1277960 | tf_op jit(solution)/shard_map/ppermute | solution.py:34
  92.6 8.1 %collective-permute-start.29 = (bf16[2,256,128]{2,1,0:T(8,128)(2,1)S(1)}, bf16[2,256,128]{2,1,0:T(8,128)(2,1)S(1)}, u32[]{:S(2)}, u32[]{:S(2)}) collective-permute-start(bf16[2,256,128]{2,1,0:T(8,128)(2,1)S(1)} %get-tuple-element.188), channel_id=1, source_target_pairs={{0,16},{4,20},{8,24},{12,28},{16,0},{20,4},{24,8},{28,12},{1,17},{... | collective-permute-start | bytes 393224 | tf_op jit(solution)/shard_map/ppermute | solution.py:34
  93.2 11.8 %collective-permute-start.23 = (bf16[2,64,1024]{2,1,0:T(8,128)(2,1)S(1)}, bf16[2,64,1024]{2,1,0:T(8,128)(2,1)S(1)}, u32[]{:S(2)}, u32[]{:S(2)}) collective-permute-start(bf16[2,64,1024]{2,1,0:T(8,128)(2,1)S(1)} %get-tuple-element.169), channel_id=1, source_target_pairs={{0,1},{1,0},{2,3},{3,2},{4,5},{5,4},{6,7},{7,6},{8,9},{9,8},{10,11... | collective-permute-start | bytes 786440 | tf_op jit(solution)/shard_map/ppermute | solution.py:34
  94.0 9.6 %collective-permute-start.27 = (bf16[2,416,128]{2,1,0:T(8,128)(2,1)S(1)}, bf16[2,416,128]{2,1,0:T(8,128)(2,1)S(1)}, u32[]{:S(2)}, u32[]{:S(2)}) collective-permute-start(bf16[2,416,128]{2,1,0:T(8,128)(2,1)S(1)} %get-tuple-element.185), channel_id=1, source_target_pairs={{0,8},{4,12},{8,0},{12,4},{16,24},{20,28},{24,16},{28,20},{1,9},{5... | collective-permute-start | bytes 638984 | tf_op jit(solution)/shard_map/ppermute | solution.py:34
  96.5 14.7 %copy-start.4 = (bf16[1,64,1024]{2,1,0:T(8,128)(2,1)S(1)}, bf16[1,64,1024]{2,1,0:T(8,128)(2,1)}, u32[]{:S(2)}) copy-start(bf16[1,64,1024]{2,1,0:T(8,128)(2,1)} %param.7) | copy-start | bytes 393220
  96.5 6.7 %collective-permute-start.28 = (bf16[2,352,128]{2,1,0:T(8,128)(2,1)S(1)}, bf16[2,352,128]{2,1,0:T(8,128)(2,1)S(1)}, u32[]{:S(2)}, u32[]{:S(2)}) collective-permute-start(bf16[2,352,128]{2,1,0:T(8,128)(2,1)S(1)} %get-tuple-element.186), channel_id=1, source_target_pairs={{0,4},{4,0},{8,12},{12,8},{16,20},{20,16},{24,28},{28,24},{1,5},{5... | collective-permute-start | bytes 540680 | tf_op jit(solution)/shard_map/ppermute | solution.py:34
  103.7 11.4 %collective-permute-start.30 = (bf16[768,128]{1,0:T(8,128)(2,1)S(1)}, bf16[768,128]{1,0:T(8,128)(2,1)S(1)}, u32[]{:S(2)}, u32[]{:S(2)}) collective-permute-start(bf16[768,128]{1,0:T(8,128)(2,1)S(1)} %get-tuple-element.194), channel_id=1, source_target_pairs={{0,16},{4,20},{8,24},{12,28},{16,0},{20,4},{24,8},{28,12},{1,17},{... | collective-permute-start | bytes 589832 | tf_op jit(solution)/shard_map/ppermute | solution.py:34
  105.2 6.0 %collective-permute-start.24 = (bf16[64,1024]{1,0:T(8,128)(2,1)S(1)}, bf16[64,1024]{1,0:T(8,128)(2,1)S(1)}, u32[]{:S(2)}, u32[]{:S(2)}) collective-permute-start(bf16[64,1024]{1,0:T(8,128)(2,1)S(1)} %shard_map.124), channel_id=1, source_target_pairs={{0,2},{1,3},{2,0},{3,1},{4,6},{5,7},{6,4},{7,5},{8,10},{9,11},{10,... | collective-permute-start | bytes 393224 | tf_op jit(solution)/shard_map/ppermute | solution.py:34
  108.2 6.9 %collective-permute-start.31 = (bf16[1,256,128]{2,1,0:T(8,128)(2,1)S(1)}, bf16[1,256,128]{2,1,0:T(8,128)(2,1)S(1)}, u32[]{:S(2)}, u32[]{:S(2)}) collective-permute-start(bf16[1,256,128]{2,1,0:T(8,128)(2,1)S(1)} %get-tuple-element.196), channel_id=1, source_target_pairs={{0,8},{4,12},{8,0},{12,4},{16,24},{20,28},{24,16},{28,20},{1,9},{5... | collective-permute-start | bytes 196616 | tf_op jit(solution)/shard_map/ppermute | solution.py:34
